TPU v7x, 128 devices: a whole 4x4x4 slice. The times are simulated.
128 devices in a mesh: section: 2 (over z_lo), dp: 8 (over x, z_hi), head: 8 (over y, core).
Axes of the slice: x: 4, y: 4, z: 4 (z_hi: 2, z_lo: 2; z = z_hi * 2 + z_lo), core: 2. Of those that a mesh axis runs over, the one named last changes fastest.
Arguments:
- images: bfloat16 [16, 1024, 1024], P('dp', 'head'), may hold values from -6 to 6
- key_mask: int32 [16, 1024], P('dp'), may hold values from 0 to 1, as said below
- image_order: int32 [16], P('dp'), may hold values from 0 to 15, as said below
- attn_norm_gain: bfloat16 [2, 1024], P('section', ('dp', 'head')), may hold values from 0.5 to 1.5
- attn_norm_bias: bfloat16 [2, 1024], P('section', ('dp', 'head')), may hold values from -0.625 to 0.625
- qkv_weight: bfloat16 [2, 1024, 3072], P('section', ('dp', 'head')), may hold values from -0.1875 to 0.1875
- query_bias: bfloat16 [2, 1024], P('section', ('dp', 'head')), may hold values from -0.625 to 0.625
- value_bias: bfloat16 [2, 1024], P('section', ('dp', 'head')), may hold values from -0.625 to 0.625
- proj_weight: bfloat16 [2, 1024, 1024], P('section', ('dp', 'head')), may hold values from -3.5 to 3.5
- proj_bias: bfloat16 [2, 1024], P('section', ('dp', 'head')), may hold values from -0.625 to 0.625
- attn_scale: bfloat16 [2, 1024], P('section', ('dp', 'head')), may hold values from 0.3984375 to 1.1953125
- mlp_norm_gain: bfloat16 [2, 1024], P('section', ('dp', 'head')), may hold values from 0.5 to 1.5
- mlp_norm_bias: bfloat16 [2, 1024], P('section', ('dp', 'head')), may hold values from -0.625 to 0.625
- fc1_weight: bfloat16 [2, 1024, 4096], P('section', ('dp', 'head')), may hold values from -0.1875 to 0.1875
- fc1_bias: bfloat16 [2, 4096], P('section', ('dp', 'head')), may hold values from -0.625 to 0.625
- fc2_weight: bfloat16 [2, 4096, 1024], P('section', ('dp', 'head')), may hold values from -0.09375 to 0.09375
- fc2_bias: bfloat16 [2, 1024], P('section', ('dp', 'head')), may hold values from -0.625 to 0.625
- mlp_scale: bfloat16 [2, 1024], P('section', ('dp', 'head')), may hold values from 0.3984375 to 1.1953125
- cotangent: bfloat16 [16, 1024, 1024], P('dp', 'head'), may hold values from -6 to 6
Outputs:
- layer_out: bfloat16 [2, 16, 1024, 1024], P('section', 'dp', 'head')
- input_grad: bfloat16 [2, 16, 1024, 1024], P('section', 'dp', 'head')
- grad_attn_norm_gain: float32 [2, 1024], P('section', ('dp', 'head'))
- grad_attn_norm_bias: float32 [2, 1024], P('section', ('dp', 'head'))
- grad_qkv_weight: float32 [2, 1024, 3072], P('section', ('dp', 'head'))
- grad_query_bias: float32 [2, 1024], P('section', ('dp', 'head'))
- grad_value_bias: float32 [2, 1024], P('section', ('dp', 'head'))
- grad_proj_weight: float32 [2, 1024, 1024], P('section', ('dp', 'head'))
- grad_proj_bias: float32 [2, 1024], P('section', ('dp', 'head'))
- grad_attn_scale: float32 [2, 1024], P('section', ('dp', 'head'))
- grad_mlp_norm_gain: float32 [2, 1024], P('section', ('dp', 'head'))
- grad_mlp_norm_bias: float32 [2, 1024], P('section', ('dp', 'head'))
- grad_fc1_weight: float32 [2, 1024, 4096], P('section', ('dp', 'head'))
- grad_fc1_bias: float32 [2, 4096], P('section', ('dp', 'head'))
- grad_fc2_weight: float32 [2, 4096, 1024], P('section', ('dp', 'head'))
- grad_fc2_bias: float32 [2, 1024], P('section', ('dp', 'head'))
- grad_mlp_scale: float32 [2, 1024], P('section', ('dp', 'head'))
Inputs may be any that keep to these rules, and one draw needn't show every extreme that they name: `key_mask`: the ones of each image form a prefix of its 1024 tokens, its first token among them, and its zeros the rest. `image_order`: each aligned block of 2 entries, the images of one index of dp, is a permutation of that block's own positions; micro-batch k of that index takes the block's entries k * 1 to (k + 1) - 1.
All inputs are finite; a program needn't handle non-finite values.
Results may differ from a plain program's by a relative error of at most 0.022.
Values may be sent and summed in bfloat16 or wider, within the bound.
No kernel may reach another device: no remote copies, remote signals or barrier semaphores. Data moves between devices by JAX's collectives and lax.ppermute only.
A program may use at most 512 MiB of HBM per device.

v0:
```python
import jax
import jax.numpy as jnp
from jax import lax
from jax.sharding import PartitionSpec as P

DH = 64
MICRO = 2


MASKED_SCORE = -1e30
NORM_EPSILON = 1e-06
ROOT_HALF = 0.7071067811865476
DENSITY_SCALE = 0.3989422804014327


def shifted(block, axis, distance):
    devices = range(lax.axis_size(axis))
    route = [(i - distance, i) for i in devices if i - distance in devices]
    return lax.ppermute(block, axis, route)


def gated_call(active, function, *operands):

    def skipped(*values):
        return jax.tree.map(jnp.zeros_like, function(*values))

    return lax.cond(active, function, skipped, *operands)


def norm_stats(flat_rows):
    centre = flat_rows - jnp.mean(flat_rows, axis=-1, keepdims=True)
    inverse = lax.rsqrt(jnp.mean(centre * centre, axis=-1, keepdims=True) + NORM_EPSILON)
    return (centre * inverse, inverse)


def norm_back(grad_norm, scaled, inverse):
    first_mean = jnp.mean(grad_norm, axis=-1, keepdims=True)
    second_mean = jnp.mean(grad_norm * scaled, axis=-1, keepdims=True)
    return inverse * (grad_norm - first_mean - scaled * second_mean)


def gelu_slope(hidden):
    return (
        0.5 * (1.0 + lax.erf(hidden * ROOT_HALF))
        + hidden * jnp.exp(-0.5 * hidden * hidden) * DENSITY_SCALE
    )


def row_product(left_rows, right_rows):
    return lax.dot_general(
        left_rows, right_rows, (((0,), (0,)), ((), ())), preferred_element_type=jnp.float32
    )


def right_product(left_rows, right_rows):
    return lax.dot_general(
        left_rows, right_rows, (((1,), (1,)), ((), ())), preferred_element_type=jnp.float32
    )


def weight_products(row_pairs):
    return tuple((row_product(pair_item[0], pair_item[1]) for pair_item in row_pairs))


def empty_slots(fresh_tree):
    return jax.tree.map(
        lambda fresh_leaf: jnp.zeros((MICRO,) + fresh_leaf.shape, fresh_leaf.dtype), fresh_tree
    )


def put_slot(stacked, fresh_tree, slot_index, active):

    def place_leaf(stacked_leaf, fresh_leaf):
        current = lax.dynamic_index_in_dim(stacked_leaf, slot_index, 0, keepdims=False)
        return lax.dynamic_update_index_in_dim(
            stacked_leaf, jnp.where(active, fresh_leaf, current), slot_index, 0
        )

    return jax.tree.map(place_leaf, stacked, fresh_tree)


def take_slot(stacked, slot_index):
    return jax.tree.map(
        lambda stacked_leaf: lax.dynamic_index_in_dim(stacked_leaf, slot_index, 0, keepdims=False),
        stacked,
    )


def masked_scores(queries, key_vectors, valid_keys):
    scores = jnp.einsum(
        "qhd,khd->hqk", queries, key_vectors, preferred_element_type=jnp.float32
    ) * DH ** (-0.5)
    return jnp.where(valid_keys[None, None, :] > 0, scores, MASKED_SCORE)


def on_device(
    images,
    key_mask,
    image_order,
    attn_norm_gain,
    attn_norm_bias,
    qkv_weight,
    query_bias,
    value_bias,
    proj_weight,
    proj_bias,
    attn_scale,
    mlp_norm_gain,
    mlp_norm_bias,
    fc1_weight,
    fc1_bias,
    fc2_weight,
    fc2_bias,
    mlp_scale,
    cotangent,
):
    section_index = lax.axis_index("section")
    section_count = lax.axis_size("section")
    local_images, tokens_here, features = images.shape
    seq_len = key_mask.shape[1]
    per_micro = local_images // MICRO
    row_count = per_micro * tokens_here
    local_order = image_order - lax.axis_index("dp") * local_images
    inverse_order = jnp.argsort(local_order)
    gathered = (
        lax.all_gather(attn_norm_gain[0], ("dp", "head"), axis=0, tiled=True),
        lax.all_gather(attn_norm_bias[0], ("dp", "head"), axis=0, tiled=True),
        lax.all_gather(qkv_weight[0], ("dp", "head"), axis=0, tiled=True),
        lax.all_gather(query_bias[0], ("dp", "head"), axis=0, tiled=True),
        lax.all_gather(value_bias[0], ("dp", "head"), axis=0, tiled=True),
        lax.all_gather(proj_weight[0], ("dp", "head"), axis=0, tiled=True),
        lax.all_gather(proj_bias[0], ("dp", "head"), axis=0, tiled=True),
        lax.all_gather(attn_scale[0], ("dp", "head"), axis=0, tiled=True),
        lax.all_gather(mlp_norm_gain[0], ("dp", "head"), axis=0, tiled=True),
        lax.all_gather(mlp_norm_bias[0], ("dp", "head"), axis=0, tiled=True),
        lax.all_gather(fc1_weight[0], ("dp", "head"), axis=0, tiled=True),
        lax.all_gather(fc1_bias[0], ("dp", "head"), axis=0, tiled=True),
        lax.all_gather(fc2_weight[0], ("dp", "head"), axis=0, tiled=True),
        lax.all_gather(fc2_bias[0], ("dp", "head"), axis=0, tiled=True),
        lax.all_gather(mlp_scale[0], ("dp", "head"), axis=0, tiled=True),
    )
    (
        attn_gain,
        attn_shift,
        qkv_full,
        query_add,
        value_add,
        proj_full,
        proj_add,
        attn_layer,
        mlp_gain,
        mlp_shift,
        fc1_full,
        fc1_add,
        fc2_full,
        fc2_add,
        mlp_layer,
    ) = gathered
    (
        attn_gain,
        attn_shift,
        query_add,
        value_add,
        proj_add,
        attn_layer,
        mlp_gain,
        mlp_shift,
        fc1_add,
        fc2_add,
        mlp_layer,
    ) = tuple(
        (
            member.astype(jnp.float32)
            for member in (
                attn_gain,
                attn_shift,
                query_add,
                value_add,
                proj_add,
                attn_layer,
                mlp_gain,
                mlp_shift,
                fc1_add,
                fc2_add,
                mlp_layer,
            )
        )
    )
    qkv_add = jnp.concatenate([query_add, jnp.zeros_like(query_add), value_add])
    picked = [
        local_order[micro_id * per_micro : (micro_id + 1) * per_micro] for micro_id in range(MICRO)
    ]
    section_inputs = jnp.stack([jnp.take(images, chosen, axis=0) for chosen in picked])
    section_masks = jnp.stack([jnp.take(key_mask, chosen, axis=0) for chosen in picked])
    cotangents = cotangent.reshape(MICRO, per_micro, tokens_here, features)

    def front_part(section_input):
        flat_rows = section_input.reshape(row_count, features).astype(jnp.float32)
        scaled, inverse = norm_stats(flat_rows)
        normed = (scaled * attn_gain + attn_shift).astype(jnp.bfloat16)
        mixed_qkv = jnp.dot(normed, qkv_full, preferred_element_type=jnp.float32) + qkv_add
        return (
            mixed_qkv.astype(jnp.bfloat16).reshape(per_micro, tokens_here, 3, features),
            normed,
            scaled,
            inverse,
        )

    def attend(heads_in, mask_rows):

        def one_image(item_pair):
            block_in, valid_keys = item_pair
            local_width = block_in.shape[-1]
            split_qkv = block_in.reshape(seq_len, 3, local_width // DH, DH)
            scores = masked_scores(split_qkv[:, 0], split_qkv[:, 1], valid_keys)
            totals = jax.nn.logsumexp(scores, axis=-1, keepdims=True)
            attention = jnp.exp(scores - totals).astype(jnp.bfloat16)
            mixed_heads = jnp.einsum(
                "hqk,khd->qhd", attention, split_qkv[:, 2], preferred_element_type=jnp.float32
            )
            return (mixed_heads.reshape(seq_len, local_width).astype(jnp.bfloat16), totals[..., 0])

        return lax.map(one_image, (heads_in, mask_rows))

    def rear_part(section_input, attn_tokens):
        flat_rows = section_input.reshape(row_count, features).astype(jnp.float32)
        attn_rows = attn_tokens.reshape(row_count, features)
        branch = jnp.dot(attn_rows, proj_full, preferred_element_type=jnp.float32) + proj_add
        middle = flat_rows + attn_layer * branch
        scaled_mid, inverse_mid = norm_stats(middle)
        normed_mid = (scaled_mid * mlp_gain + mlp_shift).astype(jnp.bfloat16)
        hidden = jnp.dot(normed_mid, fc1_full, preferred_element_type=jnp.float32) + fc1_add
        active_units = jax.nn.gelu(hidden, approximate=False).astype(jnp.bfloat16)
        mlp_out = jnp.dot(active_units, fc2_full, preferred_element_type=jnp.float32) + fc2_add
        result = (
            (middle + mlp_layer * mlp_out)
            .astype(jnp.bfloat16)
            .reshape(per_micro, tokens_here, features)
        )
        return (
            result,
            (branch, scaled_mid, inverse_mid, normed_mid, hidden, active_units, mlp_out),
        )

    def rear_back(
        grad_out,
        attn_tokens,
        branch,
        scaled_mid,
        inverse_mid,
        normed_mid,
        hidden,
        active_units,
        mlp_out,
    ):
        grad_rows = grad_out.reshape(row_count, features).astype(jnp.float32)
        grad_mlp_layer = jnp.sum(grad_rows * mlp_out, axis=0)
        grad_mlp = mlp_layer * grad_rows
        grad_fc2_add = jnp.sum(grad_mlp, axis=0)
        grad_mlp_low = grad_mlp.astype(jnp.bfloat16)
        grad_hidden = right_product(grad_mlp_low, fc2_full) * gelu_slope(hidden)
        grad_fc1_add = jnp.sum(grad_hidden, axis=0)
        grad_hidden_low = grad_hidden.astype(jnp.bfloat16)
        grad_normed = right_product(grad_hidden_low, fc1_full)
        grad_mlp_gain = jnp.sum(grad_normed * scaled_mid, axis=0)
        grad_mlp_shift = jnp.sum(grad_normed, axis=0)
        grad_middle = grad_rows + norm_back(grad_normed * mlp_gain, scaled_mid, inverse_mid)
        grad_attn_layer = jnp.sum(grad_middle * branch, axis=0)
        grad_branch = attn_layer * grad_middle
        grad_proj_add = jnp.sum(grad_branch, axis=0)
        grad_branch_low = grad_branch.astype(jnp.bfloat16)
        grad_attn = right_product(grad_branch_low, proj_full).astype(jnp.bfloat16)
        smalls = (
            grad_proj_add,
            grad_attn_layer,
            grad_mlp_gain,
            grad_mlp_shift,
            grad_fc1_add,
            grad_fc2_add,
            grad_mlp_layer,
        )
        row_pairs = (
            (attn_tokens.reshape(row_count, features), grad_branch_low),
            (normed_mid, grad_hidden_low),
            (active_units, grad_mlp_low),
        )
        return (grad_attn.reshape(per_micro, tokens_here, features), grad_middle, smalls, row_pairs)

    def attend_back(grad_heads, heads_in, totals, mask_rows):

        def one_image(item_group):
            grad_block, block_in, lse_rows, valid_keys = item_group
            local_width = block_in.shape[-1]
            local_heads = local_width // DH
            split_qkv = block_in.reshape(seq_len, 3, local_heads, DH)
            queries = split_qkv[:, 0]
            key_vectors = split_qkv[:, 1]
            grad_mixed = grad_block.reshape(seq_len, local_heads, DH)
            scores = masked_scores(queries, key_vectors, valid_keys)
            attention = jnp.exp(scores - lse_rows[..., None])
            attention_low = attention.astype(jnp.bfloat16)
            grad_probs = jnp.einsum(
                "qhd,khd->hqk", grad_mixed, split_qkv[:, 2], preferred_element_type=jnp.float32
            )
            row_dot = jnp.sum(attention * grad_probs, axis=-1, keepdims=True)
            grad_scores = (attention * (grad_probs - row_dot)).astype(jnp.bfloat16)
            grad_query = (
                jnp.einsum(
                    "hqk,khd->qhd", grad_scores, key_vectors, preferred_element_type=jnp.float32
                )
                * DH ** (-0.5)
            ).astype(jnp.bfloat16)
            grad_keys = (
                jnp.einsum("hqk,qhd->khd", grad_scores, queries, preferred_element_type=jnp.float32)
                * DH ** (-0.5)
            ).astype(jnp.bfloat16)
            grad_values = jnp.einsum(
                "hqk,qhd->khd", attention_low, grad_mixed, preferred_element_type=jnp.float32
            ).astype(jnp.bfloat16)
            return jnp.stack([grad_query, grad_keys, grad_values], axis=1).reshape(
                seq_len, 3, local_width
            )

        return lax.map(one_image, (grad_heads, heads_in, totals, mask_rows))

    def front_back(grad_qkv, grad_middle, normed, scaled, inverse):
        grad_rows = grad_qkv.reshape(row_count, 3 * features)
        grad_query_add = jnp.sum(grad_rows[:, :features].astype(jnp.float32), axis=0)
        grad_value_add = jnp.sum(grad_rows[:, 2 * features :].astype(jnp.float32), axis=0)
        grad_normed = right_product(grad_rows, qkv_full)
        grad_attn_gain = jnp.sum(grad_normed * scaled, axis=0)
        grad_attn_shift = jnp.sum(grad_normed, axis=0)
        grad_input = grad_middle + norm_back(grad_normed * attn_gain, scaled, inverse)
        smalls = (grad_attn_gain, grad_attn_shift, grad_query_add, grad_value_add)
        return (
            grad_input.astype(jnp.bfloat16).reshape(per_micro, tokens_here, features),
            smalls,
            (normed, grad_rows),
        )

    received = jnp.zeros((per_micro, tokens_here, features), jnp.bfloat16)
    kept_state = None
    produced = None
    for moment in range(MICRO + section_count - 1):
        micro_now = moment - section_index
        active = (micro_now >= 0) & (micro_now < MICRO)
        slot_index = jnp.clip(micro_now, 0, MICRO - 1)
        section_input = jnp.where(
            section_index == 0, section_inputs[min(moment, MICRO - 1)], received
        )
        mask_now = lax.dynamic_index_in_dim(section_masks, slot_index, 0, keepdims=False)
        qkv_tokens, normed, scaled, inverse = gated_call(active, front_part, section_input)
        heads_in = lax.all_to_all(qkv_tokens, "head", split_axis=3, concat_axis=1, tiled=True)
        attn_heads, totals = gated_call(active, attend, heads_in, mask_now)
        attn_tokens = lax.all_to_all(attn_heads, "head", split_axis=1, concat_axis=2, tiled=True)
        result, rear_state = gated_call(active, rear_part, section_input, attn_tokens)
        record = (normed, scaled, inverse, heads_in, totals, attn_tokens) + rear_state
        if kept_state is None:
            kept_state = empty_slots(record)
            produced = empty_slots(result)
        kept_state = put_slot(kept_state, record, slot_index, active)
        produced = put_slot(produced, result, slot_index, active)
        if moment < MICRO + section_count - 2:
            received = shifted(result, "section", 1)
    grad_received = jnp.zeros((per_micro, tokens_here, features), jnp.bfloat16)
    input_grads = None
    summed = None
    for moment in range(MICRO + section_count - 1):
        micro_now = moment - (section_count - 1 - section_index)
        active = (micro_now >= 0) & (micro_now < MICRO)
        slot_index = jnp.clip(micro_now, 0, MICRO - 1)
        grad_in = jnp.where(
            section_index == section_count - 1, cotangents[min(moment, MICRO - 1)], grad_received
        )
        mask_now = lax.dynamic_index_in_dim(section_masks, slot_index, 0, keepdims=False)
        (
            normed,
            scaled,
            inverse,
            heads_in,
            totals,
            attn_tokens,
            branch,
            scaled_mid,
            inverse_mid,
            normed_mid,
            hidden,
            active_units,
            mlp_out,
        ) = take_slot(kept_state, slot_index)
        grad_attn, grad_middle, rear_small, rear_pairs = gated_call(
            active,
            rear_back,
            grad_in,
            attn_tokens,
            branch,
            scaled_mid,
            inverse_mid,
            normed_mid,
            hidden,
            active_units,
            mlp_out,
        )
        grad_heads = lax.all_to_all(grad_attn, "head", split_axis=2, concat_axis=1, tiled=True)
        grad_qkv_heads = gated_call(active, attend_back, grad_heads, heads_in, totals, mask_now)
        grad_qkv = lax.all_to_all(grad_qkv_heads, "head", split_axis=1, concat_axis=3, tiled=True)
        grad_input, front_small, front_pair = gated_call(
            active, front_back, grad_qkv, grad_middle, normed, scaled, inverse
        )
        if input_grads is None:
            input_grads = empty_slots(grad_input)
        input_grads = put_slot(input_grads, grad_input, slot_index, active)
        full_pairs = (front_pair, rear_pairs[0], rear_pairs[1], rear_pairs[2])
        made_qkv, made_proj, made_fc1, made_fc2 = gated_call(active, weight_products, full_pairs)
        shares = (
            lax.psum_scatter(front_small[0], ("dp", "head"), scatter_dimension=0, tiled=True),
            lax.psum_scatter(front_small[1], ("dp", "head"), scatter_dimension=0, tiled=True),
            lax.psum_scatter(made_qkv, ("dp", "head"), scatter_dimension=0, tiled=True),
            lax.psum_scatter(front_small[2], ("dp", "head"), scatter_dimension=0, tiled=True),
            lax.psum_scatter(front_small[3], ("dp", "head"), scatter_dimension=0, tiled=True),
            lax.psum_scatter(made_proj, ("dp", "head"), scatter_dimension=0, tiled=True),
            lax.psum_scatter(rear_small[0], ("dp", "head"), scatter_dimension=0, tiled=True),
            lax.psum_scatter(rear_small[1], ("dp", "head"), scatter_dimension=0, tiled=True),
            lax.psum_scatter(rear_small[2], ("dp", "head"), scatter_dimension=0, tiled=True),
            lax.psum_scatter(rear_small[3], ("dp", "head"), scatter_dimension=0, tiled=True),
            lax.psum_scatter(made_fc1, ("dp", "head"), scatter_dimension=0, tiled=True),
            lax.psum_scatter(rear_small[4], ("dp", "head"), scatter_dimension=0, tiled=True),
            lax.psum_scatter(made_fc2, ("dp", "head"), scatter_dimension=0, tiled=True),
            lax.psum_scatter(rear_small[5], ("dp", "head"), scatter_dimension=0, tiled=True),
            lax.psum_scatter(rear_small[6], ("dp", "head"), scatter_dimension=0, tiled=True),
        )
        summed = shares if summed is None else jax.tree.map(jnp.add, summed, shares)
        if moment < MICRO + section_count - 2:
            grad_received = shifted(grad_input, "section", -1)
    layer_flat = produced.reshape(local_images, tokens_here, features)
    grad_flat = input_grads.reshape(local_images, tokens_here, features)
    input_grad = jnp.where(
        section_index == 0, jnp.take(grad_flat, inverse_order, axis=0), grad_flat
    )
    return (layer_flat[None], input_grad[None]) + tuple((member[None] for member in summed))


def solution(mesh):
    in_specs = (
        P("dp", "head", None),
        P("dp", None),
        P("dp"),
        P("section", ("dp", "head")),
        P("section", ("dp", "head")),
        P("section", ("dp", "head"), None),
        P("section", ("dp", "head")),
        P("section", ("dp", "head")),
        P("section", ("dp", "head"), None),
        P("section", ("dp", "head")),
        P("section", ("dp", "head")),
        P("section", ("dp", "head")),
        P("section", ("dp", "head")),
        P("section", ("dp", "head"), None),
        P("section", ("dp", "head")),
        P("section", ("dp", "head"), None),
        P("section", ("dp", "head")),
        P("section", ("dp", "head")),
        P("dp", "head", None),
    )
    out_specs = (
        P("section", "dp", "head", None),
        P("section", "dp", "head", None),
        P("section", ("dp", "head")),
        P("section", ("dp", "head")),
        P("section", ("dp", "head"), None),
        P("section", ("dp", "head")),
        P("section", ("dp", "head")),
        P("section", ("dp", "head"), None),
        P("section", ("dp", "head")),
        P("section", ("dp", "head")),
        P("section", ("dp", "head")),
        P("section", ("dp", "head")),
        P("section", ("dp", "head"), None),
        P("section", ("dp", "head")),
        P("section", ("dp", "head"), None),
        P("section", ("dp", "head")),
        P("section", ("dp", "head")),
    )
    return jax.shard_map(
        on_device, mesh=mesh, in_specs=in_specs, out_specs=out_specs, check_vma=False
    )
```

profile of v0, /device:TPU:1, one launch (start us, length us, event | category | flops | bytes accessed | tf_op | source)
XLA Modules:
  0.0 2323.7 jit_solution(7843579987965048721)
XLA Ops:
  27.6 326.4 %all-reduce.23 = (bf16[1024]{0:T(1024)(128)(2,1)S(1)}, bf16[1024]{0:T(1024)(128)(2,1)S(1)}, bf16[1024]{0:T(1024)(128)(2,1)S(1)}, bf16[1024]{0:T(1024)(128)(2,1)S...) all-reduce(bf16[1024]{0:T(1024)(128)(2,1)S(1)} %dynamic-update-slic, ...), channel_id=2, replica_groups=mesh['section'=2,'dp'=8,'head'=8] {'dp','head'}, use_global_device_ids=true, to_apply=%add | all-reduce | flops 14336 | bytes 57344
  357.0 6.7 conditional.21
  365.4 11.7 all-to-all-start
  379.2 13.0 all-to-all-done
  392.3 10.0 conditional.22
  419.7 24.2 %conditional.23 = (f32[128,1024]{1,0:T(8,128)}, f32[128,1024]{1,0:T(8,128)}, f32[128,1]{0,1:T(1,128)S(1)}, bf16[128,1024]{1,0:T(8,128)(2,1)}, f32[128,4096]{1,0:...) conditional(s32[]{:T(128)} %convert_element_type.462, ...), branch_computations={%region_8.11_spmd, %region_9.14_spmd} | conditional | flops 2453929984 | bytes 55633008 | solution.py:27
  428.5 8.9 fusion.8
  486.5 10.6 all-to-all-done.2
  498.4 6.8 conditional.25
  523.9 24.2 %conditional.26 = (f32[128,1024]{1,0:T(8,128)}, f32[128,1024]{1,0:T(8,128)}, f32[128,1]{0,1:T(1,128)S(1)}, bf16[128,1024]{1,0:T(8,128)(2,1)}, f32[128,4096]{1,0:...) conditional(s32[]{:T(128)} %convert_element_type.474, ...), branch_computations={%region_20.23_spmd, %region_21.26_spmd} | conditional | flops 2453929984 | bytes 56681612 | solution.py:27
  531.6 9.3 fusion.29
  585.9 9.6 all-to-all-done.4
  623.3 6.9 conditional.29
  638.7 10.7 conditional.30
  683.3 12.1 all-to-all-done.7
  704.1 88.2 %collective-permute-done.2 = bf16[1,128,1024]{2,1,0:T(8,128)(2,1)} collective-permute-done((bf16[1,128,1024]{2,1,0:T(8,128)(2,1)}, bf16[1,128,1024]{2,1,0:T(8,128)(2,1)}, u32[]{:S(2)}, u32[]{:S(2)}) %collective-permute-start.2) | collective-permute-done | bytes 262176 | tf_op jit(solution)/shard_map/ppermute | solution.py:19
  792.3 31.1 %conditional.33 = (bf16[1,128,1024]{2,1,0:T(8,128)(2,1)}, f32[128,1024]{1,0:T(8,128)}, f32[1024]{0:T(1024)}, f32[1024]{0:T(1024)}, f32[1024]{0:T(1024)}, /*index...) conditional(s32[]{:T(128)} %convert_element_type.477, ...), branch_computations={%region_59.62_spmd, %region_60.72_spmd} | conditional | flops 2425608192 | bytes 69932824 | solution.py:27
  798.8 8.9 fusion.236
  836.8 6.6 all-to-all-done.8
  847.0 22.8 conditional.34
  877.6 15.2 all-to-all-done.9
  894.1 17.8 conditional.35
  900.5 6.0 fusion.110
  913.2 7.9 collective-permute-done.3
  921.0 26.8 %conditional.36 = (bf16[1,128,1024]{2,1,0:T(8,128)(2,1)}, f32[128,1024]{1,0:T(8,128)}, f32[1024]{0:T(1024)S(1)}, f32[1024]{0:T(1024)S(1)}, f32[1024]{0:T(1024)S(...) conditional(s32[]{:T(128)} %convert_element_type.478, ...), branch_computations={%region_81.84_spmd, %region_82.94_spmd} | conditional | flops 2425608192 | bytes 69932824 | solution.py:27
  927.4 8.3 fusion.237
  958.6 6.5 all-to-all-done.10
  965.5 15.1 conditional.37
  987.2 17.1 conditional.39
  988.1 6.1 broadcast.1286
  996.3 7.8 broadcast.1288
  1011.4 30.1 %conditional.40 = (f32[1024,3072]{1,0:T(8,128)}, f32[1024,1024]{1,0:T(8,128)}, f32[1024,4096]{1,0:T(8,128)}, f32[4096,1024]{1,0:T(8,128)}) conditional(s32[]{:T(128)} %convert_element_type.477, () %tuple.264, (bf16[128,1024]{1,0:T(8,128)(2,1)}, bf16[128,3072]{1,0:T(8,128)(2,1)}, bf16[128,1024]{1,0:T(8,128)(2,1)}, bf16[128,1024]{1,0:T(8,128)(2,1)}, ...), branch_computations={%region_112.115_spmd, %region_113.116_spmd} | conditional | flops 3221225472 | bytes 54525984 | solution.py:27
  1015.1 7.6 fusion.244
  1022.7 9.4 fusion.246
  1032.1 9.4 fusion.247
  1042.8 10.7 conditional.38
  1053.5 28.3 %conditional.41 = (f32[1024,3072]{1,0:T(8,128)}, f32[1024,1024]{1,0:T(8,128)S(1)}, f32[1024,4096]{1,0:T(8,128)}, f32[4096,1024]{1,0:T(8,128)}) conditional(s32[]{:T(128)} %convert_element_type.478, () %tuple.266, (bf16[128,1024]{1,0:T(8,128)(2,1)S(1)}, bf16[128,3072]{1,0:T(8,128)(2,1)}, bf16[128,1024]{1,0:T(8,128)(2,1)S(1)}, ...), branch_computations={%region_115.118_spmd, %region_116.119_spmd} | conditional | flops 3221225472 | bytes 54525984 | solution.py:27
  1055.5 7.4 fusion.248
  1062.9 9.5 fusion.250
  1072.4 9.5 fusion.251
  1081.8 7.0 add_add_fusion.3
  1089.1 19.0 add_add_fusion.2
  1108.2 23.3 %add_add_fusion.1 = f32[1024,4096]{1,0:T(8,128)} fusion(f32[1024,4096]{1,0:T(8,128)} %get-tuple-element.1545, f32[1024,4096]{1,0:T(8,128)} %get-tuple-element.1543, f32[1024,4096]{1,0:T(8,128)} %get-tuple-element.1544), kind=kLoop, calls=%fused_computation.438 | loop fusion | flops 8388608 | bytes 67108864 | tf_op jit(solution)/shard_map/add | solution.py:432
  1131.6 23.9 %add_add_fusion = f32[4096,1024]{1,0:T(8,128)} fusion(f32[4096,1024]{1,0:T(8,128)} %get-tuple-element.1551, f32[4096,1024]{1,0:T(8,128)} %copy-done.1, f32[4096,1024]{1,0:T(8,128)} %get-tuple-element.1550), kind=kLoop, calls=%fused_computation.437 | loop fusion | flops 8388608 | bytes 67108864 | tf_op jit(solution)/shard_map/add | solution.py:432
  1169.7 315.6 %all-reduce.22 = (f32[1024]{0:T(1024)S(1)}, f32[1024]{0:T(1024)S(1)}, f32[1024]{0:T(1024)S(1)}, f32[1024]{0:T(1024)S(1)}, f32[1024]{0:T(1024)S(1)}, /*index=5*/f...) all-reduce(f32[1024]{0:T(1024)S(1)} %add_add_fusion.14, ...), channel_id=47, replica_groups=mesh['section'=2,'dp'=8,'head'=8] {'dp','head'}, use_global_device_ids=true, to_apply=%region_103.106.clone | all-reduce | flops 14336 | bytes 114688
  1491.7 113.5 %reduce-scatter.5.cloned.1.call-done = f32[16,3072]{1,0:T(8,128)} async-done(((f32[1024,3072]{1,0:T(8,128)}), f32[16,3072]{1,0:T(8,128)}) %reduce-scatter.5.cloned.1.call-update) | async-done | bytes 196624 | tf_op jit(solution)/shard_map/reduce_scatter | solution.py:418
  1605.2 354.4 %reduce-scatter.9.cloned.1.call-done = f32[16,4096]{1,0:T(8,128)} async-done(((f32[1024,4096]{1,0:T(8,128)}), f32[16,4096]{1,0:T(8,128)}) %reduce-scatter.9.cloned.1.call-update) | async-done | bytes 262160 | tf_op jit(solution)/shard_map/reduce_scatter | solution.py:426
  1959.6 357.0 %reduce-scatter.11.cloned.1.call-done = f32[64,1024]{1,0:T(8,128)} async-done(((f32[4096,1024]{1,0:T(8,128)}), f32[64,1024]{1,0:T(8,128)}) %reduce-scatter.11.cloned.1.call-update) | async-done | bytes 262160 | tf_op jit(solution)/shard_map/reduce_scatter | solution.py:428
  (609 shorter events, 484.3 us)
Async XLA Ops:
  7.2 349.0 %copy-start.84 = (s32[2,1024]{1,0:T(2,128)S(1)}, s32[2,1024]{1,0:T(2,128)}, u32[]{:S(2)}) copy-start(s32[2,1024]{1,0:T(2,128)} %param.66) | copy-start | bytes 24580
  7.2 349.8 %all-gather.20.cloned.1.call-start = ((), (), s32[]{:S(2)}) async-start(), calls=%async_computation.16 | async-start | bytes 6389760 | tf_op jit(solution)/shard_map/all_gather | solution.py:128
  7.9 411.8 %all-gather.22.cloned.1.call-start = ((), (), s32[]{:S(2)}) async-start(), calls=%async_computation.17 | async-start | bytes 2129920 | tf_op jit(solution)/shard_map/all_gather | solution.py:131
  8.7 411.0 %all-gather.24.cloned.1.call-start = ((), (), s32[]{:S(2)}) async-start(), calls=%async_computation.18 | async-start | bytes 8519680 | tf_op jit(solution)/shard_map/all_gather | solution.py:136
  9.4 410.3 %all-gather.26.cloned.1.call-start = ((), (), s32[]{:S(2)}) async-start(), calls=%async_computation.19 | async-start | bytes 8519680 | tf_op jit(solution)/shard_map/all_gather | solution.py:138
  356.3 240.6 %copy-start.66 = (s32[2,1,1024]{2,1,0:T(1,128)}, s32[2,1,1024]{2,1,0:T(1,128)S(1)}, u32[]{:S(2)}) copy-start(s32[2,1,1024]{2,1,0:T(1,128)S(1)} %pad_add_fusion) | copy-start | bytes 24580
  365.4 26.8 %all-to-all-start = ((bf16[1,128,3,1024]{1,2,0,3:T(4,128)(2,1)}), bf16[1,128,3,1024]{1,2,0,3:T(4,128)(2,1)S(1)}, u32[]{:S(2)}, u32[]{:S(2)}) async-start(bf16[1,128,3,1024]{1,2,0,3:T(4,128)(2,1)} %copy.176), calls=%async_computation | async-start | bytes 2097152 | tf_op jit(solution)/shard_map/all_to_all | solution.py:353
  406.2 10.7 all-to-all-start.1
  426.2 11.2 slice-start
  428.5 8.9 slice-start.1
  443.9 25.6 %collective-permute-start = (bf16[1,128,1024]{1,2,0:T(8,128)(2,1)S(1)}, bf16[1,128,1024]{1,2,0:T(8,128)(2,1)S(1)}, u32[]{:S(2)}, u32[]{:S(2)}) collective-permute-start(bf16[1,128,1024]{1,2,0:T(8,128)(2,1)S(1)} %get-tuple-element.2112), channel_id=1, source_target_pairs={{0,64},{1,65},{2,66},{3,67},{4,68},{5,69},{6,70},{7,71},{8,72},{9,... | collective-permute-start | bytes 786440 | tf_op jit(solution)/shard_map/ppermute | solution.py:19
  477.1 20.0 all-to-all-start.2
  482.1 15.2 copy-start.90
  508.7 11.6 all-to-all-start.3
  513.7 10.2 copy-start
  529.4 11.5 slice-start.2
  531.6 9.3 slice-start.3
  548.1 19.9 collective-permute-start.1
  572.3 10.5 copy-start.88
  575.1 20.4 all-to-all-start.4
  598.7 14.4 copy-start.70
  598.7 12.3 copy-start.53
  606.3 11.4 all-to-all-start.5
  649.4 15.1 copy-start.54
  657.0 11.6 all-to-all-start.6
  672.7 8.8 copy-start.57
  675.1 20.4 all-to-all-start.7
  701.9 90.5 %collective-permute-start.2 = (bf16[1,128,1024]{2,1,0:T(8,128)(2,1)}, bf16[1,128,1024]{2,1,0:T(8,128)(2,1)}, u32[]{:S(2)}, u32[]{:S(2)}) collective-permute-start(bf16[1,128,1024]{2,1,0:T(8,128)(2,1)} %get-tuple-element.1482), channel_id=1, source_target_pairs={{64,0},{65,1},{66,2},{67,3},{68,4},{69,5},{70,6},{71,7},{72,8},{73... | collective-permute-start | bytes 786440 | tf_op jit(solution)/shard_map/ppermute | solution.py:19
  796.2 11.5 slice-start.8
  798.8 8.9 slice-start.9
  830.9 12.4 all-to-all-start.8
  872.2 20.5 all-to-all-start.9
  911.9 9.2 collective-permute-start.3
  924.8 10.9 slice-start.10
  927.4 8.3 slice-start.11
  949.2 16.2 copy-start.76
  949.2 16.2 copy-start.78
  949.2 16.2 copy-start.80
  949.2 16.2 copy-start.82
  949.2 16.2 copy-start.67
  953.5 11.6 all-to-all-start.10
  982.0 59.5 %all-to-all-start.11 = ((bf16[1,1024,3,128]{3,2,0,1:T(4,128)(2,1)}), bf16[1,1024,3,128]{3,2,0,1:T(4,128)(2,1)}, u32[]{:S(2)}, u32[]{:S(2)}) async-start(bf16[1,1024,3,128]{3,2,0,1:T(4,128)(2,1)} %copy.229), calls=%async_computation.11 | async-start | bytes 2097152 | tf_op jit(solution)/shard_map/all_to_all | solution.py:406
  987.1 504.6 %reduce-scatter.7.cloned.1.call-start = ((), (), s32[]{:S(2)}) async-start(), calls=%async_computation.21 | async-start | bytes 4259840 | tf_op jit(solution)/shard_map/reduce_scatter | solution.py:421
  1004.3 38.5 %copy-start.91 = (f32[2,128,1]{1,2,0:T(1,128)S(1)}, f32[2,128,1]{1,2,0:T(1,128)}, u32[]{:S(2)}) copy-start(f32[2,128,1]{1,2,0:T(1,128)} %constant_dynamic-update-slice_fusion.12) | copy-start | bytes 3076
  1042.8 10.7 copy-start.56
  1088.8 516.4 %reduce-scatter.5.cloned.1.call-start = ((), (), s32[]{:S(2)}) async-start(), calls=%async_computation.20 | async-start | bytes 12779520 | tf_op jit(solution)/shard_map/reduce_scatter | solution.py:418
  1108.1 851.5 %reduce-scatter.9.cloned.1.call-start = ((), (), s32[]{:S(2)}) async-start(), calls=%async_computation.22 | async-start | bytes 17039360 | tf_op jit(solution)/shard_map/reduce_scatter | solution.py:426
  1131.6 1185.1 %reduce-scatter.11.cloned.1.call-start = ((), (), s32[]{:S(2)}) async-start(), calls=%async_computation.23 | async-start | bytes 17039360 | tf_op jit(solution)/shard_map/reduce_scatter | solution.py:428
  (68 other events, 226.8 us)
Sparse Core Ops, SparseCore 0:
  11.2 82.1 all-gather.19
  96.6 65.0 all-gather.21
  164.9 80.6 all-gather.23
  248.5 80.5 all-gather.25
  1089.0 327.0 reduce-scatter.6
  1423.3 181.8 reduce-scatter.4
  1608.3 351.2 reduce-scatter.8
  1962.7 353.8 reduce-scatter.10
where the time goes:
time: 2340 us; the launch traced here: 2320 us
  waiting for transfers between devices  1010 us (43%)
  blocking collectives  642 us (27%)
  local copies, waits for them, and re-layouts  215 us (9%)
  other arithmetic  195 us (8%)
  matrix products  165 us (7%)
  starting transfers between devices  74.1 us (3%)
    unnamed x2, blocking collectives  642 us
    reduce_scatter x1, waiting for transfers between devices, on_device(): lax.psum_scatter(made_fc2, ('dp', 'head'), scatter_dimension=0, tiled=True)  357 us
    reduce_scatter x1, waiting for transfers between devices, on_device(): lax.psum_scatter(made_fc1, ('dp', 'head'), scatter_dimension=0, tiled=True)  354 us
    reduce_scatter x1, waiting for transfers between devices, on_device(): lax.psum_scatter(made_qkv, ('dp', 'head'), scatter_dimension=0, tiled=True)  113 us
    ppermute x4, waiting for transfers between devices, shifted(): return lax.ppermute(block, axis, route)  96 us
    add x15, other arithmetic, on_device(): summed = shares if summed is None else jax.tree.map(jnp.add, summed, shares)  80.9 us
    another operation x71, local copies, waits for them, and re-layouts  64.6 us
    dot_general x8, matrix products, row_product(): lax.dot_general(left_rows, right_rows, (((0,), (0,)), ((), ())), preferre...  58.1 us
  transfers between devices with their start and end apart: 24, of which 16 were waited for; matrix products, arithmetic and copies ran while one was open for 10% of the time, Pallas kernels for 0%

commit v1 on v0

v1 whole, which is shorter than its diff:
```python
import functools

import jax
import jax.numpy as jnp
from jax import lax
from jax.experimental import pallas as pl
from jax.experimental.pallas import tpu as pltpu
from jax.sharding import PartitionSpec as P

DH = 64
MASKED_SCORE = -1e30
NORM_EPSILON = 1e-06
ROOT_HALF = 0.7071067811865476
DENSITY_SCALE = 0.3989422804014327
SCORE_SCALE = DH ** (-0.5)
SLAB = 16
QUERY_ROWS = 256
VMEM_LIMIT = 60 * 1024 * 1024

(
    ATTN_GAIN,
    ATTN_SHIFT,
    QUERY_ADD,
    VALUE_ADD,
    PROJ_ADD,
    ATTN_LAYER,
    MLP_GAIN,
    MLP_SHIFT,
    FC2_ADD,
    MLP_LAYER,
) = range(10)
HIDDEN_ROW = 10
TABLE_ROWS = 16


def hop(block, axis, places):
    size = lax.axis_size(axis)
    return lax.ppermute(block, axis, [(i, (i + 2 * places) % size) for i in range(size)])


def swap(block, axis):
    size = lax.axis_size(axis)
    return lax.ppermute(block, axis, [(i, i ^ 1) for i in range(size)])


def coordinates():
    dp_index, head_index = lax.axis_index("dp"), lax.axis_index("head")
    return dp_index // 2, dp_index % 2, head_index // 2, head_index % 2


def spread(shard, last_axis):
    x_me, z_me, y_me, core_me = coordinates()
    x_size, y_size = lax.axis_size("dp") // 2, lax.axis_size("head") // 2
    across = swap(shard, "dp")
    pair = jnp.where(z_me == 0, jnp.stack([shard, across]), jnp.stack([across, shard]))
    zeros = (0,) * shard.ndim
    if last_axis == "dp":
        first_axis, first_me, first_size = "head", y_me, y_size
        last_me, last_size = x_me, x_size
        lane = jnp.zeros((2, y_size) + shard.shape, shard.dtype)
    else:
        first_axis, first_me, first_size = "dp", x_me, x_size
        last_me, last_size = y_me, y_size
        lane = jnp.zeros((x_size, 2) + shard.shape, shard.dtype)
    for places in range(first_size):
        came = pair if places == 0 else hop(pair, first_axis, places)
        source = (first_me - places) % first_size
        if last_axis == "dp":
            lane = lax.dynamic_update_slice(lane, came[:, None], (0, source) + zeros)
        else:
            lane = lax.dynamic_update_slice(lane, came[None], (source, 0) + zeros)
    whole = jnp.zeros((x_size, 2, y_size, 2) + shard.shape, shard.dtype)
    arrived = [
        lane if places == 0 else hop(lane, last_axis, places) for places in range(last_size)
    ]
    for places, came in enumerate(arrived):
        source = (last_me - places) % last_size
        for core, block in ((core_me, came), (1 - core_me, swap(came, "head"))):
            if last_axis == "dp":
                whole = lax.dynamic_update_slice(
                    whole, block[None, :, :, None], (source, 0, 0, core) + zeros
                )
            else:
                whole = lax.dynamic_update_slice(
                    whole, block[:, :, None, None], (0, 0, source, core) + zeros
                )
    return whole.reshape((x_size * 2 * y_size * 2,) + shard.shape)


def ring_sum(terms, axis, dim, me, size):
    own = lax.dynamic_index_in_dim(terms, me, dim, keepdims=False).astype(jnp.float32)
    for places in range(1, size):
        block = lax.dynamic_index_in_dim(terms, (me + places) % size, dim, keepdims=False)
        own = own + hop(block, axis, places).astype(jnp.float32)
    return own


def collect(mine, other, first_axis):
    x_me, z_me, y_me, core_me = coordinates()
    x_size, y_size = lax.axis_size("dp") // 2, lax.axis_size("head") // 2
    chip_sum = mine.astype(jnp.float32) + swap(other, "head").astype(jnp.float32)
    terms = chip_sum.astype(jnp.bfloat16).reshape((x_size, 2, y_size) + mine.shape[1:])
    if first_axis == "dp":
        terms = ring_sum(terms, "dp", 0, x_me, x_size).astype(jnp.bfloat16)
        terms = ring_sum(terms, "head", 1, y_me, y_size)
    else:
        terms = ring_sum(terms, "head", 2, y_me, y_size).astype(jnp.bfloat16)
        terms = ring_sum(terms, "dp", 0, x_me, x_size)
    away = lax.dynamic_index_in_dim(terms, 1 - z_me, 0, keepdims=False).astype(jnp.bfloat16)
    own = lax.dynamic_index_in_dim(terms, z_me, 0, keepdims=False)
    return own + swap(away, "dp").astype(jnp.float32)


def to_peers(blocks):
    return lax.all_to_all(blocks, "head", split_axis=0, concat_axis=0, tiled=True)


def shifted(block, distance):
    size = lax.axis_size("section")
    route = [(i, i + distance) for i in range(size) if 0 <= i + distance < size]
    return lax.ppermute(block, "section", route)


def norm_stats(rows):
    centre = rows - jnp.mean(rows, axis=-1, keepdims=True)
    inverse = lax.rsqrt(jnp.mean(centre * centre, axis=-1, keepdims=True) + NORM_EPSILON)
    return centre * inverse, inverse


def norm_back(grad_norm, scaled, inverse):
    first_mean = jnp.mean(grad_norm, axis=-1, keepdims=True)
    second_mean = jnp.mean(grad_norm * scaled, axis=-1, keepdims=True)
    return inverse * (grad_norm - first_mean - scaled * second_mean)


def product(left, right):
    return jnp.dot(left, right, preferred_element_type=jnp.float32)


def product_nt(left, right):
    return lax.dot_general(
        left, right, (((1,), (1,)), ((), ())), preferred_element_type=jnp.float32
    )


def product_tn(left, right):
    return lax.dot_general(
        left, right, (((0,), (0,)), ((), ())), preferred_element_type=jnp.float32
    )


def flat(block):
    return block.reshape(-1, block.shape[-1])


def column_sum(rows):
    return jnp.sum(rows, axis=0, keepdims=True)


def vector(table_ref, row):
    return table_ref[row : row + 1, :]


def side_by_side(blocks_ref, start=0):
    return jnp.concatenate(
        [blocks_ref[peer, :, start : start + 128] for peer in range(blocks_ref.shape[0])], axis=1
    )


def put_side_by_side(blocks_ref, rows, start=0):
    for peer in range(blocks_ref.shape[0]):
        blocks_ref[peer, :, start : start + 128] = rows[:, peer * 128 : (peer + 1) * 128].astype(
            blocks_ref.dtype
        )


def attn_normed(rows, table_ref):
    scaled, inverse = norm_stats(rows)
    normed = (scaled * vector(table_ref, ATTN_GAIN) + vector(table_ref, ATTN_SHIFT)).astype(
        jnp.bfloat16
    )
    return normed, scaled, inverse


def mlp_normed(middle, table_ref):
    scaled, inverse = norm_stats(middle)
    normed = (scaled * vector(table_ref, MLP_GAIN) + vector(table_ref, MLP_SHIFT)).astype(
        jnp.bfloat16
    )
    return normed, scaled, inverse


def cumulative(hidden):
    return 0.5 * (1.0 + lax.erf(hidden * ROOT_HALF))


def front_kernel(x_ref, table_ref, qk_ref, v_ref, out_ref):
    normed, _, _ = attn_normed(x_ref[...].astype(jnp.float32), table_ref)
    queries = product(normed, flat(qk_ref[:, :SLAB])) + vector(table_ref, QUERY_ADD)
    put_side_by_side(out_ref, queries, 0)
    put_side_by_side(out_ref, product(normed, flat(qk_ref[:, SLAB:])), 128)
    values = product(normed, flat(v_ref[...])) + vector(table_ref, VALUE_ADD)
    put_side_by_side(out_ref, values, 256)


def valid_rows(count, like):
    return lax.broadcasted_iota(jnp.int32, like.shape, 0) < count


def attend_kernel(count_ref, heads_ref, out_ref, lse_ref):
    count = count_ref[pl.program_id(0)]
    block = flat(heads_ref[:, 0])
    seq_len = block.shape[0]
    for start in range(0, seq_len, QUERY_ROWS):
        outs = []
        for head in range(2):
            low = head * DH
            keys = block[:, 128 + low : 128 + low + DH]
            values = block[:, 256 + low : 256 + low + DH]
            queries = block[start : start + QUERY_ROWS, low : low + DH]
            scores = product_nt(keys, queries)
            scores = jnp.where(valid_rows(count, scores), scores * SCORE_SCALE, MASKED_SCORE)
            largest = jnp.max(scores, axis=0, keepdims=True)
            weights = jnp.exp(scores - largest)
            total = jnp.sum(weights, axis=0, keepdims=True)
            mixed = product_tn(values, weights.astype(jnp.bfloat16)) / total
            outs.append(mixed.T)
            lse_ref[0, head : head + 1, start : start + QUERY_ROWS] = largest + jnp.log(total)
        rows = jnp.concatenate(outs, axis=1).astype(jnp.bfloat16)
        peers = QUERY_ROWS // 128
        out_ref[start // 128 : start // 128 + peers, 0] = rows.reshape(peers, 128, 128)


def attend_back_kernel(count_ref, grad_ref, heads_ref, lse_ref, out_ref):
    count = count_ref[pl.program_id(0)]
    block = flat(heads_ref[:, 0])
    grads = flat(grad_ref[:, 0])
    seq_len = block.shape[0]
    peers = QUERY_ROWS // 128
    key_sums = [jnp.zeros((seq_len, DH), jnp.float32) for _ in range(2)]
    value_sums = [jnp.zeros((seq_len, DH), jnp.float32) for _ in range(2)]
    for start in range(0, seq_len, QUERY_ROWS):
        outs = []
        for head in range(2):
            low = head * DH
            keys = block[:, 128 + low : 128 + low + DH]
            values = block[:, 256 + low : 256 + low + DH]
            queries = block[start : start + QUERY_ROWS, low : low + DH]
            grad_rows = grads[start : start + QUERY_ROWS, low : low + DH]
            lse = lse_ref[0, head : head + 1, start : start + QUERY_ROWS]
            scores = product_nt(keys, queries)
            scores = jnp.where(valid_rows(count, scores), scores * SCORE_SCALE, MASKED_SCORE)
            weights = jnp.exp(scores - lse)
            grad_weights = product_nt(values, grad_rows)
            dots = jnp.sum(weights * grad_weights, axis=0, keepdims=True)
            grad_scores = (weights * (grad_weights - dots)).astype(jnp.bfloat16)
            value_sums[head] += product(weights.astype(jnp.bfloat16), grad_rows)
            key_sums[head] += product(grad_scores, queries)
            outs.append((product_tn(keys, grad_scores) * SCORE_SCALE).T)
        rows = jnp.concatenate(outs, axis=1).astype(jnp.bfloat16)
        out_ref[start // 128 : start // 128 + peers, 0, :, :128] = rows.reshape(peers, 128, 128)
    key_rows = (jnp.concatenate(key_sums, axis=1) * SCORE_SCALE).astype(jnp.bfloat16)
    value_rows = jnp.concatenate(value_sums, axis=1).astype(jnp.bfloat16)
    out_ref[:, 0, :, 128:256] = key_rows.reshape(-1, 128, 128)
    out_ref[:, 0, :, 256:] = value_rows.reshape(-1, 128, 128)


def rear_kernel(keep, x_ref, attn_ref, table_ref, proj_ref, fc1_ref, fc2_ref, *rest):
    if keep:
        result_ref, branch_ref, hidden_ref, mlp_ref, normed, middle, total = rest
    else:
        result_ref, normed, middle, total = rest
    step = pl.program_id(0)

    @pl.when(step == 0)
    def _():
        branch = product(side_by_side(attn_ref), flat(proj_ref[...])) + vector(table_ref, PROJ_ADD)
        if keep:
            branch_ref[...] = branch
        middle[...] = x_ref[...].astype(jnp.float32) + vector(table_ref, ATTN_LAYER) * branch
        normed[...] = mlp_normed(middle[...], table_ref)[0]
        total[...] = jnp.broadcast_to(vector(table_ref, FC2_ADD), total.shape)

    hidden = product(normed[...], flat(fc1_ref[...])) + table_ref[pl.ds(HIDDEN_ROW + step, 1), :]
    if keep:
        hidden_ref[...] = hidden
    active = (hidden * cumulative(hidden)).astype(jnp.bfloat16)
    total[...] += product(active, flat(fc2_ref[...]))

    @pl.when(step == pl.num_programs(0) - 1)
    def _():
        if keep:
            mlp_ref[...] = total[...]
        result = middle[...] + vector(table_ref, MLP_LAYER) * total[...]
        result_ref[...] = result.astype(jnp.bfloat16)


def rear_back_kernel(
    keep,
    grad_ref,
    x_ref,
    branch_ref,
    hidden_ref,
    mlp_ref,
    table_ref,
    proj_ref,
    fc1_ref,
    fc2_ref,
    attn_grad_ref,
    middle_grad_ref,
    *rest,
):
    if keep:
        mlp_low_ref, hidden_low_ref, active_ref, normed_ref, branch_low_ref, sums_ref = rest[:6]
    mlp_low, total = rest[-2:]
    step = pl.program_id(0)

    @pl.when(step == 0)
    def _():
        grad_mlp = vector(table_ref, MLP_LAYER) * grad_ref[...].astype(jnp.float32)
        mlp_low[...] = grad_mlp.astype(jnp.bfloat16)
        total[...] = jnp.zeros_like(total)
        if keep:
            sums_ref[...] = jnp.zeros_like(sums_ref)
            sums_ref[FC2_ADD : FC2_ADD + 1, :] = column_sum(grad_mlp)
            mlp_low_ref[...] = mlp_low[...]

    hidden = hidden_ref[...]
    below = cumulative(hidden)
    slope = below + hidden * (jnp.exp(-0.5 * hidden * hidden) * DENSITY_SCALE)
    grad_hidden = product_nt(mlp_low[...], flat(fc2_ref[...])) * slope
    hidden_low = grad_hidden.astype(jnp.bfloat16)
    total[...] += product_nt(hidden_low, flat(fc1_ref[...]))
    if keep:
        sums_ref[pl.ds(HIDDEN_ROW + step, 1), :] = column_sum(grad_hidden)
        hidden_low_ref[...] = hidden_low
        active_ref[...] = (hidden * below).astype(jnp.bfloat16)

    @pl.when(step == pl.num_programs(0) - 1)
    def _():
        grad_rows = grad_ref[...].astype(jnp.float32)
        branch = branch_ref[...]
        middle = x_ref[...].astype(jnp.float32) + vector(table_ref, ATTN_LAYER) * branch
        normed, scaled, inverse = mlp_normed(middle, table_ref)
        grad_normed = total[...]
        grad_middle = grad_rows + norm_back(
            grad_normed * vector(table_ref, MLP_GAIN), scaled, inverse
        )
        middle_grad_ref[...] = grad_middle
        grad_branch = vector(table_ref, ATTN_LAYER) * grad_middle
        branch_low = grad_branch.astype(jnp.bfloat16)
        put_side_by_side(attn_grad_ref, product_nt(branch_low, flat(proj_ref[...])))
        if keep:
            normed_ref[...] = normed
            branch_low_ref[...] = branch_low
            for row, rows in (
                (MLP_LAYER, grad_rows * mlp_ref[...]),
                (MLP_GAIN, grad_normed * scaled),
                (MLP_SHIFT, grad_normed),
                (ATTN_LAYER, grad_middle * branch),
                (PROJ_ADD, grad_branch),
            ):
                sums_ref[row : row + 1, :] = column_sum(rows)


def front_back_kernel(keep, grad_ref, middle_grad_ref, x_ref, table_ref, qk_ref, v_ref, *rest):
    if keep:
        out_ref, sums_ref = rest
    else:
        (out_ref,) = rest
    queries, keys, values = (side_by_side(grad_ref, start) for start in (0, 128, 256))
    grad_normed = product_nt(queries, flat(qk_ref[:, :SLAB]))
    grad_normed += product_nt(keys, flat(qk_ref[:, SLAB:]))
    grad_normed += product_nt(values, flat(v_ref[...]))
    _, scaled, inverse = attn_normed(x_ref[...].astype(jnp.float32), table_ref)
    grad_input = middle_grad_ref[...] + norm_back(
        grad_normed * vector(table_ref, ATTN_GAIN), scaled, inverse
    )
    out_ref[...] = grad_input.astype(jnp.bfloat16)
    if keep:
        sums_ref[...] = jnp.zeros_like(sums_ref)
        for row, rows in (
            (ATTN_GAIN, grad_normed * scaled),
            (ATTN_SHIFT, grad_normed),
            (QUERY_ADD, queries.astype(jnp.float32)),
            (VALUE_ADD, values.astype(jnp.float32)),
        ):
            sums_ref[row : row + 1, :] = column_sum(rows)


def put_by_core(core, mine_ref, other_ref, rows, start, count):
    pairs = rows.astype(jnp.bfloat16).reshape(-1, 2, count, rows.shape[-1])
    first, second = pairs[:, 0], pairs[:, 1]
    here = core == 0
    mine_ref[:, start : start + count] = jnp.where(here, first, second)
    other_ref[:, start : start + count] = jnp.where(here, second, first)


def mlp_weights_kernel(
    core_ref,
    normed_ref,
    hidden_low_ref,
    active_ref,
    mlp_low_ref,
    fc1_mine_ref,
    fc1_other_ref,
    fc2_mine_ref,
    fc2_other_ref,
):
    core = core_ref[0]
    fc2_grad = product_tn(active_ref[...], mlp_low_ref[...])
    put_by_core(core, fc2_mine_ref, fc2_other_ref, fc2_grad, 0, fc2_mine_ref.shape[1])
    fc1_grad = product_tn(normed_ref[...], hidden_low_ref[...])
    put_by_core(core, fc1_mine_ref, fc1_other_ref, fc1_grad, 0, SLAB)


def attn_weights_kernel(
    core_ref,
    x_ref,
    table_ref,
    grad_ref,
    attn_ref,
    branch_low_ref,
    small_ref,
    first_mine_ref,
    first_other_ref,
    second_mine_ref,
    second_other_ref,
):
    core = core_ref[0]
    normed, _, _ = attn_normed(x_ref[...].astype(jnp.float32), table_ref)
    for at in range(2):
        grad = product_tn(normed, side_by_side(grad_ref, at * 128))
        put_by_core(core, first_mine_ref, first_other_ref, grad, at * SLAB, SLAB)
    grad = product_tn(normed, side_by_side(grad_ref, 256))
    put_by_core(core, second_mine_ref, second_other_ref, grad, 0, SLAB)
    grad = product_tn(side_by_side(attn_ref), branch_low_ref[...])
    put_by_core(core, second_mine_ref, second_other_ref, grad, SLAB, SLAB)
    put_by_core(core, second_mine_ref, second_other_ref, flat(small_ref[...]), 2 * SLAB, SLAB)


def like(*shape, dtype=jnp.bfloat16):
    return jax.ShapeDtypeStruct(shape, dtype)


def whole_block(array):
    ndim = len(array.shape)
    return pl.BlockSpec(array.shape, lambda *_: (0,) * ndim)


def params():
    return pltpu.CompilerParams(vmem_limit_bytes=VMEM_LIMIT)


SCALARS = pl.BlockSpec(memory_space=pltpu.SMEM)


def call_front(x, table, early):
    rows, width = x.shape
    devices = early[0].shape[0]
    return pl.pallas_call(
        front_kernel,
        grid=(1,),
        in_specs=[
            whole_block(x),
            whole_block(table),
            whole_block(early[0]),
            pl.BlockSpec((devices, SLAB, width), lambda i: (0, 0, 0)),
        ],
        out_specs=pl.BlockSpec((8, rows, 384), lambda i: (0, 0, 0)),
        out_shape=like(8, rows, 384),
        compiler_params=params(),
    )(x, table, *early)


def call_attend(counts, heads):
    images = counts.shape[0]
    heads = heads.reshape(8, images, -1, 384)
    tokens = heads.shape[2]
    out, lse = pl.pallas_call(
        attend_kernel,
        grid=(images,),
        in_specs=[SCALARS, pl.BlockSpec((8, 1, tokens, 384), lambda i: (0, i, 0, 0))],
        out_specs=[
            pl.BlockSpec((8, 1, tokens, 128), lambda i: (0, i, 0, 0)),
            pl.BlockSpec((1, 2, 8 * tokens), lambda i: (i, 0, 0)),
        ],
        out_shape=[
            like(8, images, tokens, 128),
            like(images, 2, 8 * tokens, dtype=jnp.float32),
        ],
        compiler_params=params(),
    )(counts, heads)
    return out.reshape(8, images * tokens, 128), lse


def call_attend_back(counts, grads, heads, lse):
    images = counts.shape[0]
    heads = heads.reshape(8, images, -1, 384)
    tokens = heads.shape[2]
    out = pl.pallas_call(
        attend_back_kernel,
        grid=(images,),
        in_specs=[
            SCALARS,
            pl.BlockSpec((8, 1, tokens, 128), lambda i: (0, i, 0, 0)),
            pl.BlockSpec((8, 1, tokens, 384), lambda i: (0, i, 0, 0)),
            pl.BlockSpec((1, 2, 8 * tokens), lambda i: (i, 0, 0)),
        ],
        out_specs=pl.BlockSpec((8, 1, tokens, 384), lambda i: (0, i, 0, 0)),
        out_shape=like(*heads.shape),
        compiler_params=params(),
    )(counts, grads.reshape(8, images, tokens, 128), heads, lse)
    return out.reshape(8, images * tokens, 384)


def rear_weight_specs(late):
    fc1, fc2_proj = late
    devices, _, width = fc1.shape
    fc2_rows = fc2_proj.shape[1] - SLAB
    steps = fc1.shape[1] // SLAB
    return steps, [
        pl.BlockSpec((devices, SLAB, width), lambda j: (0, fc2_rows // SLAB, 0)),
        pl.BlockSpec((devices, SLAB, width), lambda j: (0, j, 0)),
        pl.BlockSpec((devices // steps, fc2_rows, width), lambda j: (j, 0, 0)),
    ]


def call_rear(keep, x, attn, table, late):
    rows, width = x.shape
    steps, weight_specs = rear_weight_specs(late)
    full = like(rows, width, dtype=jnp.float32)
    column = pl.BlockSpec((rows, width), lambda j: (0, j))
    out_shape, out_specs = [like(rows, width)], [whole_block(x)]
    if keep:
        out_shape += [full, like(rows, steps * width, dtype=jnp.float32), full]
        out_specs += [whole_block(x), column, whole_block(x)]
    return pl.pallas_call(
        functools.partial(rear_kernel, keep),
        grid=(steps,),
        in_specs=[whole_block(x), whole_block(attn), whole_block(table)] + weight_specs,
        out_specs=out_specs,
        out_shape=out_shape,
        scratch_shapes=[
            pltpu.VMEM((rows, width), jnp.bfloat16),
            pltpu.VMEM((rows, width), jnp.float32),
            pltpu.VMEM((rows, width), jnp.float32),
        ],
        compiler_params=params(),
    )(x, attn, table, late[1], late[0], late[1])


def call_rear_back(keep, grad, x, branch, hidden, mlp, table, late):
    rows, width = x.shape
    steps, weight_specs = rear_weight_specs(late)
    column = pl.BlockSpec((rows, width), lambda j: (0, j))
    out_shape = [like(8, rows, 128), like(rows, width, dtype=jnp.float32)]
    out_specs = [pl.BlockSpec((8, rows, 128), lambda j: (0, 0, 0)), whole_block(x)]
    if keep:
        wide = like(rows, steps * width)
        out_shape += [like(rows, width), wide, wide, like(rows, width), like(rows, width)]
        out_specs += [whole_block(x), column, column, whole_block(x), whole_block(x)]
        out_shape += [like(*table.shape, dtype=jnp.float32)]
        out_specs += [whole_block(table)]
    return pl.pallas_call(
        functools.partial(rear_back_kernel, keep),
        grid=(steps,),
        in_specs=[
            whole_block(grad),
            whole_block(x),
            whole_block(branch),
            column,
            whole_block(mlp),
            whole_block(table),
        ]
        + weight_specs,
        out_specs=out_specs,
        out_shape=out_shape,
        scratch_shapes=[
            pltpu.VMEM((rows, width), jnp.bfloat16),
            pltpu.VMEM((rows, width), jnp.float32),
        ],
        compiler_params=params(),
    )(grad, x, branch, hidden, mlp, table, late[1], late[0], late[1])


def call_front_back(keep, grad_qkv, grad_middle, x, table, early):
    rows, width = x.shape
    devices = early[0].shape[0]
    out_shape, out_specs = [like(rows, width)], [whole_block(x)]
    if keep:
        out_shape += [like(*table.shape, dtype=jnp.float32)]
        out_specs += [whole_block(table)]
    return pl.pallas_call(
        functools.partial(front_back_kernel, keep),
        grid=(1,),
        in_specs=[
            whole_block(grad_qkv),
            whole_block(grad_middle),
            whole_block(x),
            whole_block(table),
            whole_block(early[0]),
            pl.BlockSpec((devices, SLAB, width), lambda i: (0, 0, 0)),
        ],
        out_specs=out_specs,
        out_shape=out_shape,
        compiler_params=params(),
    )(grad_qkv, grad_middle, x, table, *early)


def call_mlp_weights(core, normed, hidden_low, active, mlp_low, late):
    rows, width = normed.shape
    chips = late[0].shape[0] // 2
    steps = late[0].shape[1] // SLAB
    owned = late[0].shape[1]
    column = pl.BlockSpec((rows, width), lambda j: (0, j))
    fc1_spec = pl.BlockSpec((chips, SLAB, width), lambda j: (0, j, 0))
    fc2_spec = pl.BlockSpec((chips // steps, owned, width), lambda j: (j, 0, 0))
    return pl.pallas_call(
        mlp_weights_kernel,
        grid=(steps,),
        in_specs=[SCALARS, whole_block(normed), column, column, whole_block(mlp_low)],
        out_specs=[fc1_spec, fc1_spec, fc2_spec, fc2_spec],
        out_shape=[like(chips, owned, width)] * 4,
        compiler_params=params(),
    )(core, normed, hidden_low, active, mlp_low)


def call_attn_weights(core, x, table, grad_qkv, attn, branch_low, small):
    width = x.shape[1]
    chips = small.shape[0] // 2
    first, second = like(chips, 2 * SLAB, width), like(chips, 3 * SLAB, width)
    operands = (x, table, grad_qkv, attn, branch_low, small)
    return pl.pallas_call(
        attn_weights_kernel,
        grid=(1,),
        in_specs=[SCALARS] + [whole_block(operand) for operand in operands],
        out_specs=[whole_block(shape) for shape in (first, first, second, second)],
        out_shape=[first, first, second, second],
        compiler_params=params(),
    )(core, *operands)


def small_slab(vectors, hidden_vector):
    lead = vectors.shape[:-2]
    row = jnp.concatenate([vectors.reshape(lead + (-1,)), hidden_vector], axis=-1)
    return jnp.pad(
        row[..., None, :], [(0, 0)] * len(lead) + [(0, SLAB - 1), (0, 1024 - row.shape[-1])]
    )


def table_of(slabs):
    row = slabs[:, 0, :].astype(jnp.float32)
    vectors = row[:, : HIDDEN_ROW * SLAB].reshape(-1, HIDDEN_ROW, SLAB)
    vectors = vectors.transpose(1, 0, 2).reshape(HIDDEN_ROW, -1)
    start = HIDDEN_ROW * SLAB
    hidden = row[:, start : start + 64].reshape(-1, vectors.shape[1])
    return jnp.pad(
        jnp.concatenate([vectors, hidden]),
        [(0, TABLE_ROWS - HIDDEN_ROW - hidden.shape[0]), (0, 0)],
    )


def slabs_of(sums, devices):
    vectors = sums[:HIDDEN_ROW].reshape(HIDDEN_ROW, devices, SLAB).transpose(1, 0, 2)
    hidden = sums[HIDDEN_ROW : HIDDEN_ROW + 4].reshape(devices, -1)
    return small_slab(vectors, hidden).astype(jnp.bfloat16)


def column_slabs(rows):
    count = rows.shape[1] // 1024
    return rows.reshape(SLAB, count, 1024).transpose(1, 0, 2).reshape(count * SLAB, 1024)


def from_column_slabs(rows):
    count = rows.shape[0] // SLAB
    return rows.reshape(count, SLAB, 1024).transpose(1, 0, 2).reshape(SLAB, count * 1024)


def on_device(
    images,
    key_mask,
    image_order,
    attn_norm_gain,
    attn_norm_bias,
    qkv_weight,
    query_bias,
    value_bias,
    proj_weight,
    proj_bias,
    attn_scale,
    mlp_norm_gain,
    mlp_norm_bias,
    fc1_weight,
    fc1_bias,
    fc2_weight,
    fc2_bias,
    mlp_scale,
    cotangent,
):
    section_index = lax.axis_index("section")
    local_images, tokens_here, features = images.shape
    rows = local_images * tokens_here
    reversed_order = image_order[0] > image_order[1]
    core = (lax.axis_index("head") % 2).astype(jnp.int32).reshape(1)

    vectors = jnp.concatenate(
        [
            attn_norm_gain,
            attn_norm_bias,
            query_bias,
            value_bias,
            proj_bias,
            attn_scale,
            mlp_norm_gain,
            mlp_norm_bias,
            fc2_bias,
            mlp_scale,
        ]
    )
    qkv_slabs = column_slabs(qkv_weight[0])
    early = (
        spread(qkv_slabs[: 2 * SLAB], "dp"),
        spread(
            jnp.concatenate([qkv_slabs[2 * SLAB :], small_slab(vectors, fc1_bias[0])]), "head"
        ),
    )
    late = (
        spread(column_slabs(fc1_weight[0]), "dp"),
        spread(jnp.concatenate([fc2_weight[0], proj_weight[0]]), "head"),
    )
    table = table_of(early[1][:, SLAB:])
    devices = early[0].shape[0]

    own_images = jnp.where(reversed_order, images[::-1], images).reshape(rows, features)
    counts = jnp.sum(key_mask, axis=1, dtype=jnp.int32)
    counts = jnp.where(reversed_order, counts[::-1], counts)

    def forward(x, keep):
        heads = to_peers(call_front(x, table, early))
        attn_heads, lse = call_attend(counts, heads)
        attn = to_peers(attn_heads)
        return (heads, lse, attn), call_rear(keep, x, attn, table, late)

    def backward(grad, x, attn_state, rear_state, keep):
        heads, lse, _ = attn_state
        _, branch, hidden, mlp = rear_state
        rear = call_rear_back(keep, grad, x, branch, hidden, mlp, table, late)
        grad_heads = to_peers(rear[0])
        grad_qkv = to_peers(call_attend_back(counts, grad_heads, heads, lse))
        front = call_front_back(keep, grad_qkv, rear[1], x, table, early)
        return rear, grad_qkv, front

    _, (passed,) = forward(own_images, False)
    x = jnp.where(section_index == 0, own_images, shifted(passed, 1))
    attn_state, rear_state = forward(x, True)

    own_grad = cotangent.reshape(rows, features)
    _, _, (passed_back,) = backward(own_grad, x, attn_state, rear_state, False)
    grad = jnp.where(section_index == 0, shifted(passed_back, -1), own_grad)
    rear, grad_qkv, (input_grad, front_sums) = backward(grad, x, attn_state, rear_state, True)
    _, _, mlp_low, hidden_low, active, normed, branch_low, rear_sums = rear

    fc1_mine, fc1_other, fc2_mine, fc2_other = call_mlp_weights(
        core, normed, hidden_low, active, mlp_low, late
    )
    fc1_grad = collect(fc1_mine, fc1_other, "dp")
    fc2_grad = collect(fc2_mine, fc2_other, "head")
    small = slabs_of(rear_sums + front_sums, devices)
    first_mine, first_other, second_mine, second_other = call_attn_weights(
        core, x, table, grad_qkv, attn_state[2], branch_low, small
    )
    first_grad = collect(first_mine, first_other, "dp")
    second_grad = collect(second_mine, second_other, "head")
    qkv_grad = from_column_slabs(jnp.concatenate([first_grad, second_grad[:SLAB]]))
    proj_grad = second_grad[SLAB : 2 * SLAB]
    row = second_grad[2 * SLAB]
    small_grads = row[: HIDDEN_ROW * SLAB].reshape(HIDDEN_ROW, SLAB)
    fc1_bias_grad = row[HIDDEN_ROW * SLAB : HIDDEN_ROW * SLAB + 64]

    layer_out = rear_state[0].reshape(images.shape)
    input_grad = input_grad.reshape(images.shape)
    input_grad = jnp.where(
        (section_index == 0) & reversed_order, input_grad[::-1], input_grad
    )
    outs = (
        layer_out,
        input_grad,
        small_grads[ATTN_GAIN],
        small_grads[ATTN_SHIFT],
        qkv_grad,
        small_grads[QUERY_ADD],
        small_grads[VALUE_ADD],
        proj_grad,
        small_grads[PROJ_ADD],
        small_grads[ATTN_LAYER],
        small_grads[MLP_GAIN],
        small_grads[MLP_SHIFT],
        from_column_slabs(fc1_grad),
        fc1_bias_grad,
        fc2_grad,
        small_grads[FC2_ADD],
        small_grads[MLP_LAYER],
    )
    return tuple(member[None] for member in outs)


def solution(mesh):
    tokens = P("dp", "head", None)
    vec = P("section", ("dp", "head"))
    mat = P("section", ("dp", "head"), None)
    in_specs = (
        (tokens, P("dp", None), P("dp"), vec, vec, mat, vec, vec, mat, vec, vec, vec, vec)
        + (mat, vec, mat, vec, vec, tokens)
    )
    out_tokens = P("section", "dp", "head", None)
    out_specs = (
        (out_tokens, out_tokens, vec, vec, mat, vec, vec, mat, vec, vec, vec, vec, mat, vec)
        + (mat, vec, vec)
    )
    return jax.shard_map(
        on_device, mesh=mesh, in_specs=in_specs, out_specs=out_specs, check_vma=False
    )
```

time: 2340 us -> 732 us (0.31)
  waiting for transfers between devices: 1010 us -> 236 us
  blocking collectives: 642 us -> 97.1 us
  matrix products: 165 us -> 0 us
  other arithmetic: 195 us -> 30.4 us
  Pallas kernels: 0 us -> 163 us
  local copies, waits for them, and re-layouts: 215 us -> 76 us
  starting transfers between devices: 74.1 us -> 116 us
    reduce_scatter x4 -> x0, waiting for transfers between devices: 825 us -> none  [the longest x1 357 us: on_device(): lax.psum_scatter(made_fc2, ('dp', 'head'), scatter_dimension=0, tiled=True)]
    unnamed x2 -> x0, blocking collectives: 642 us -> none
    dot_general x38 -> x0, matrix products: 165 us -> none  [the longest x8 58.1 us: row_product(): lax.dot_general(left_rows, right_rows, (((0,), (0,)), ((), ())), preferre...]
    pallas_call x0 -> x14, Pallas kernels: none -> 163 us  [the longest x2 33.2 us: call_attend_back(): pl.pallas_call(attend_back_kernel, grid=(images,), in_specs=[SCALARS, pl....]
    ppermute x4 -> x78, waiting for transfers between devices: 96 us -> 225 us  [the longest x48 190 us: hop(): lax.ppermute(block, axis, [(i, (i + 2 * places) % size) for i in range(si...]
    all_to_all x0 -> x5, blocking collectives: none -> 97.1 us  [to_peers(): lax.all_to_all(blocks, 'head', split_axis=0, concat_axis=0, tiled=True)]
    ppermute x4 -> x78, starting transfers between devices: 6.14 us -> 94.2 us  [the longest x48 53.5 us: hop(): lax.ppermute(block, axis, [(i, (i + 2 * places) % size) for i in range(si...]
    add x19 -> x7, other arithmetic: 80.9 us -> 0.56 us  [the longest x4 0.5 us: ring_sum(): own = own + hop(block, axis, places).astype(jnp.float32)]
  transfers between devices with their start and end apart: 24 -> 81, of which waited for: 16 -> 33; matrix products, arithmetic and copies ran while one was open for 10% -> 13% of each run, Pallas kernels for 0% -> 6%
where the time goes in v1:
time: 732 us; the launch traced here: 722 us
  waiting for transfers between devices  236 us (32%)
  Pallas kernels  163 us (22%)
  starting transfers between devices  116 us (16%)
  blocking collectives  97.1 us (13%)
  local copies, waits for them, and re-layouts  76 us (10%)
  other arithmetic  30.4 us (4%)
    ppermute x48, waiting for transfers between devices, hop(): lax.ppermute(block, axis, [(i, (i + 2 * places) % size) for i in range(si...  190 us
    all_to_all x5, blocking collectives, to_peers(): lax.all_to_all(blocks, 'head', split_axis=0, concat_axis=0, tiled=True)  97.1 us
    ppermute x48, starting transfers between devices, hop(): lax.ppermute(block, axis, [(i, (i + 2 * places) % size) for i in range(si...  53.5 us
    ppermute x28, starting transfers between devices, swap(): return lax.ppermute(block, axis, [(i, i ^ 1) for i in range(size)])  36.2 us
    pallas_call x2, Pallas kernels, call_attend_back(): pl.pallas_call(attend_back_kernel, grid=(images,), in_specs=[SCALARS, pl....  33.2 us
    pallas_call x2, Pallas kernels, call_rear_back(): pl.pallas_call(functools.partial(rear_back_kernel, keep), grid=(steps,),...  30.6 us
    pallas_call x2, Pallas kernels, call_attend(): pl.pallas_call(attend_kernel, grid=(images,), in_specs=[SCALARS, pl.Block...  28.7 us
    pallas_call x2, Pallas kernels, call_rear(): pl.pallas_call(functools.partial(rear_kernel, keep), grid=(steps,), in_sp...  26 us
  transfers between devices with their start and end apart: 81, of which 33 were waited for; matrix products, arithmetic and copies ran while one was open for 13% of the time, Pallas kernels for 6%

profile of v1, /device:TPU:1, one launch (start us, length us, event | category | flops | bytes accessed | tf_op | source)
XLA Modules:
  0.0 721.8 jit_solution(2888676004872489262)
XLA Ops:
  4.1 4.5 collective-permute-start
  46.6 4.1 collective-permute-start.4
  54.2 4.3 broadcast_in_dim.209
  64.7 5.3 broadcast_in_dim.196
  74.6 5.3 collective-permute-done.7
  80.5 16.8 %collective-permute-done.16 = bf16[2,4,32,1024]{3,2,1,0:T(8,128)(2,1)S(1)} collective-permute-done((bf16[2,4,32,1024]{3,2,1,0:T(8,128)(2,1)S(1)}, bf16[2,4,32,1024]{3,2,1,0:T(8,128)(2,1)S(1)}, u32[]{:S(2)}, u32[]{:S(2)}) %collective-permute-start.16) | collective-permute-done | bytes 524320 | tf_op jit(solution)/shard_map/ppermute | solution.py:38
  110.5 38.1 %collective-permute-done.38 = bf16[2,4,64,1024]{3,2,1,0:T(8,128)(2,1)S(1)} collective-permute-done((bf16[2,4,64,1024]{3,2,1,0:T(8,128)(2,1)}, bf16[2,4,64,1024]{3,2,1,0:T(8,128)(2,1)S(1)}, u32[]{:S(2)}, u32[]{:S(2)}) %collective-permute-start.38) | collective-permute-done | bytes 1048608 | tf_op jit(solution)/shard_map/ppermute | solution.py:38
  154.9 6.4 shard_map.314
  161.3 5.0 all-to-all-start
  179.6 3.5 collective-permute-start.28
  183.1 24.1 %collective-permute-done.31 = bf16[4,2,80,1024]{3,2,1,0:T(8,128)(2,1)} collective-permute-done((bf16[4,2,80,1024]{3,2,1,0:T(8,128)(2,1)S(1)}, bf16[4,2,80,1024]{3,2,1,0:T(8,128)(2,1)}, u32[]{:S(2)}, u32[]{:S(2)}) %collective-permute-start.31) | collective-permute-done | bytes 1310752 | tf_op jit(solution)/shard_map/ppermute | solution.py:38
  218.8 14.3 %shard_map.315 = (bf16[8,2,128,128]{3,2,1,0:T(8,128)(2,1)}, f32[2,2,1024]{2,1,0:T(2,128)}) custom-call(s32[2]{0:T(128)} %broadcast_select_fusion.2.count_ref, bf16[8,2,128,384]{3,2,1,0:T(8,128)(2,1)} %bitcast.348), custom_call_target="tpu_custom_call" | custom-call | tf_op jit(solution)/shard_map/pallas_call | solution.py:480
  233.1 12.0 %all-to-all-start.1 = ((bf16[8,256,128]{2,1,0:T(8,128)(2,1)}), bf16[8,256,128]{2,1,0:T(8,128)(2,1)S(1)}, u32[]{:S(2)}, u32[]{:S(2)}) async-start(bf16[8,256,128]{2,1,0:T(8,128)(2,1)} %bitcast.368), calls=%async_computation.1 | async-start | bytes 1048576 | tf_op jit(solution)/shard_map/all_to_all | solution.py:115
  258.4 12.5 %shard_map.316 = bf16[256,1024]{1,0:T(8,128)(2,1)} custom-call(bf16[256,1024]{1,0:T(8,128)(2,1)} %bitcast.346, bf16[8,256,128]{2,1,0:T(8,128)(2,1)} %copy-done.8, f32[16,1024]{1,0:T(8,128)} %select_maximum_fusion.table_ref, bf16[64,80,1024]{2,1,0:T(8,128)(2,1)} %bitcast.82.proj_ref.fc2_ref, bf16[64,64,1024]{2,1,0:T(8,128)(2,1)} %bitcast.109.fc1_ref, ...), custom_call_target="tpu_custom_call" | custom-call | tf_op jit(solution)/shard_map/pallas_call | solution.py:538
  273.8 11.6 %collective-permute-done.44 = bf16[256,1024]{1,0:T(8,128)(2,1)S(1)} collective-permute-done((bf16[256,1024]{1,0:T(8,128)(2,1)}, bf16[256,1024]{1,0:T(8,128)(2,1)S(1)}, u32[]{:S(2)}, u32[]{:S(2)}) %collective-permute-start.44) | collective-permute-done | bytes 524320 | tf_op jit(solution)/shard_map/ppermute | solution.py:121
  286.3 6.4 shard_map.317
  292.7 26.3 %all_to_all.40 = bf16[8,256,384]{2,1,0:T(8,128)(2,1)} all-to-all(bf16[8,256,384]{2,1,0:T(8,128)(2,1)} %shard_map.317), channel_id=1, replica_groups=mesh['section'=2,'dp'=8,'head'=8] {'head'}, dimensions={0} | all-to-all | bytes 3145728 | tf_op jit(solution)/shard_map/all_to_all | solution.py:115
  319.0 14.3 %shard_map.318 = (bf16[8,2,128,128]{3,2,1,0:T(8,128)(2,1)}, f32[2,2,1024]{2,1,0:T(2,128)}) custom-call(s32[2]{0:T(128)} %broadcast_select_fusion.2.count_ref, bf16[8,2,128,384]{3,2,1,0:T(8,128)(2,1)} %bitcast.336), custom_call_target="tpu_custom_call" | custom-call | tf_op jit(solution)/shard_map/pallas_call | solution.py:480
  333.3 14.5 %all_to_all.41.attn_ref = bf16[8,256,128]{2,1,0:T(8,128)(2,1)} all-to-all(bf16[8,256,128]{2,1,0:T(8,128)(2,1)} %bitcast.370), channel_id=1, replica_groups=mesh['section'=2,'dp'=8,'head'=8] {'head'}, dimensions={0} | all-to-all | bytes 1048576 | tf_op jit(solution)/shard_map/all_to_all | solution.py:115
  347.8 13.5 %shard_map.319 = (bf16[256,1024]{1,0:T(8,128)(2,1)}, f32[256,1024]{1,0:T(8,128)}, f32[256,4096]{1,0:T(8,128)}, f32[256,1024]{1,0:T(8,128)}) custom-call(bf16[256,1024]{1,0:T(8,128)(2,1)} %broadcast_select_fusion.1.x_ref, bf16[8,256,128]{2,1,0:T(8,128)(2,1)} %all_to_all.41.attn_ref, f32[16,1024]{1,0:T(8,128)} %select_maximum_fusion.table_ref, ...), custom_call_target="tpu_custom_call" | custom-call | tf_op jit(solution)/shard_map/pallas_call | solution.py:538
  361.3 14.1 %shard_map.320 = (bf16[8,256,128]{2,1,0:T(8,128)(2,1)}, f32[256,1024]{1,0:T(8,128)}) custom-call(bf16[256,1024]{1,0:T(8,128)(2,1)} %bitcast.351, bf16[256,1024]{1,0:T(8,128)(2,1)} %broadcast_select_fusion.1.x_ref, f32[256,1024]{1,0:T(8,128)} %get-tuple-element.47.branch_ref, f32[256,4096]{1,0:T(8,128)} %get-tuple-element.48.hidden_ref, ...), custom_call_target="tpu_custom_call" | custom-call | tf_op jit(solution)/shard_map/pallas_call | solution.py:565
  375.4 14.7 %all_to_all.42 = bf16[8,256,128]{2,1,0:T(8,128)(2,1)} all-to-all(bf16[8,256,128]{2,1,0:T(8,128)(2,1)} %get-tuple-element.50), channel_id=1, replica_groups=mesh['section'=2,'dp'=8,'head'=8] {'head'}, dimensions={0} | all-to-all | bytes 1048576 | tf_op jit(solution)/shard_map/all_to_all | solution.py:115
  390.2 16.6 %shard_map.321 = bf16[8,2,128,384]{3,2,1,0:T(8,128)(2,1)} custom-call(s32[2]{0:T(128)} %broadcast_select_fusion.2.count_ref, bf16[8,2,128,128]{3,2,1,0:T(8,128)(2,1)} %bitcast.353, bf16[8,2,128,384]{3,2,1,0:T(8,128)(2,1)} %bitcast.337, f32[2,2,1024]{2,1,0:T(2,128)} %get-tuple-element.51.lse_ref), custom_call_target="tpu_custom_call" | custom-call | tf_op jit(solution)/shard_map/pallas_call | solution.py:501
  406.8 26.1 %all_to_all.43.grad_ref = bf16[8,256,384]{2,1,0:T(8,128)(2,1)} all-to-all(bf16[8,256,384]{2,1,0:T(8,128)(2,1)} %bitcast.350), channel_id=1, replica_groups=mesh['section'=2,'dp'=8,'head'=8] {'head'}, dimensions={0} | all-to-all | bytes 3145728 | tf_op jit(solution)/shard_map/all_to_all | solution.py:115
  432.8 6.8 shard_map.322
  441.3 12.8 %collective-permute-done.45 = bf16[256,1024]{1,0:T(8,128)(2,1)S(1)} collective-permute-done((bf16[256,1024]{1,0:T(8,128)(2,1)}, bf16[256,1024]{1,0:T(8,128)(2,1)S(1)}, u32[]{:S(2)}, u32[]{:S(2)}) %collective-permute-start.45) | collective-permute-done | bytes 524320 | tf_op jit(solution)/shard_map/ppermute | solution.py:121
  455.0 16.5 %shard_map.323 = (bf16[8,256,128]{2,1,0:T(8,128)(2,1)}, f32[256,1024]{1,0:T(8,128)}, bf16[256,1024]{1,0:T(8,128)(2,1)}, bf16[256,4096]{1,0:T(8,128)(2,1)}, bf16[...) custom-call(bf16[256,1024]{1,0:T(8,128)(2,1)} %broadcast_select_fusion.grad_re, ...), custom_call_target="tpu_custom_call" | custom-call | tf_op jit(solution)/shard_map/pallas_call | solution.py:565
  471.5 15.4 %all_to_all.44 = bf16[8,256,128]{2,1,0:T(8,128)(2,1)} all-to-all(bf16[8,256,128]{2,1,0:T(8,128)(2,1)} %get-tuple-element.53), channel_id=1, replica_groups=mesh['section'=2,'dp'=8,'head'=8] {'head'}, dimensions={0} | all-to-all | bytes 1048576 | tf_op jit(solution)/shard_map/all_to_all | solution.py:115
  486.9 16.6 %shard_map.324 = bf16[8,2,128,384]{3,2,1,0:T(8,128)(2,1)} custom-call(s32[2]{0:T(128)} %broadcast_select_fusion.2.count_ref, bf16[8,2,128,128]{3,2,1,0:T(8,128)(2,1)} %bitcast.352, bf16[8,2,128,384]{3,2,1,0:T(8,128)(2,1)} %bitcast.338, f32[2,2,1024]{2,1,0:T(2,128)} %get-tuple-element.51.lse_ref), custom_call_target="tpu_custom_call" | custom-call | tf_op jit(solution)/shard_map/pallas_call | solution.py:501
  503.6 4.5 all-to-all-start.7
  508.1 10.1 %shard_map.327 = (bf16[32,64,1024]{2,1,0:T(8,128)(2,1)}, bf16[32,64,1024]{2,1,0:T(8,128)(2,1)}, bf16[32,64,1024]{2,1,0:T(8,128)(2,1)}, bf16[32,64,1024]{2,1,0:T(8,128)(2,1)}) custom-call(s32[1]{0:T(128)} %bitcast.120.core_ref, bf16[256,1024]{1,0:T(8,128)(2,1)} %get-tuple-element.63.normed_ref, bf16[256,4096]{1,0:T(8,128)(2,1)} %get-tuple-element.64.hidden_low_ref, ...), custom_call_target="tpu_custom_call" | custom-call | tf_op jit(solution)/shard_map/pallas_call | solution.py:619
  518.8 10.0 %all-to-all-done.7.grad_ref = bf16[8,256,384]{2,1,0:T(8,128)(2,1)S(1)} async-done(((bf16[8,256,384]{2,1,0:T(8,128)(2,1)}), bf16[8,256,384]{2,1,0:T(8,128)(2,1)S(1)}, u32[]{:S(2)}, u32[]{:S(2)}) %all-to-all-start.7) | async-done | bytes 1572896 | tf_op jit(solution)/shard_map/all_to_all | solution.py:115
  530.0 6.9 shard_map.325
  539.9 8.1 %shard_map.326 = (bf16[32,32,1024]{2,1,0:T(8,128)(2,1)}, bf16[32,32,1024]{2,1,0:T(8,128)(2,1)}, bf16[32,48,1024]{2,1,0:T(8,128)(2,1)}, bf16[32,48,1024]{2,1,0:T(8,128)(2,1)}) custom-call(s32[1]{0:T(128)} %bitcast.120.core_ref, bf16[256,1024]{1,0:T(8,128)(2,1)} %broadcast_select_fusion.1.x_ref, f32[16,1024]{1,0:T(8,128)} %select_maximum_fusion.table_ref, ...), custom_call_target="tpu_custom_call" | custom-call | tf_op jit(solution)/shard_map/pallas_call | solution.py:634
  549.0 7.1 collective-permute-done.54
  562.9 4.3 add_convert_fusion.1
  567.7 5.2 collective-permute-done.57
  575.4 11.9 %collective-permute-done.55 = bf16[2,4,32,1024]{3,2,0,1:T(8,128)(2,1)S(1)} collective-permute-done((bf16[2,4,32,1024]{3,2,0,1:T(8,128)(2,1)}, bf16[2,4,32,1024]{3,2,0,1:T(8,128)(2,1)S(1)}, u32[]{:S(2)}, u32[]{:S(2)}) %collective-permute-start.55) | collective-permute-done | bytes 524320 | tf_op jit(solution)/shard_map/ppermute | solution.py:38
  595.1 4.3 add_convert_fusion
  601.6 3.5 collective-permute-done.58
  608.8 8.1 %collective-permute-done.64 = bf16[2,4,64,1024]{3,2,1,0:T(8,128)(2,1)S(1)} collective-permute-done((bf16[2,4,64,1024]{3,2,1,0:T(8,128)(2,1)S(1)}, bf16[2,4,64,1024]{3,2,1,0:T(8,128)(2,1)S(1)}, u32[]{:S(2)}, u32[]{:S(2)}) %collective-permute-start.64) | collective-permute-done | bytes 1048608 | tf_op jit(solution)/shard_map/ppermute | solution.py:38
  620.3 19.7 %collective-permute-done.63 = bf16[2,4,64,1024]{3,2,1,0:T(8,128)(2,1)} collective-permute-done((bf16[2,4,64,1024]{3,2,1,0:T(8,128)(2,1)S(1)}, bf16[2,4,64,1024]{3,2,1,0:T(8,128)(2,1)}, u32[]{:S(2)}, u32[]{:S(2)}) %collective-permute-start.63) | collective-permute-done | bytes 1048608 | tf_op jit(solution)/shard_map/ppermute | solution.py:38
  644.6 4.9 collective-permute-start.66
  649.6 8.4 %collective-permute-done.71 = bf16[4,2,64,1024]{3,2,1,0:T(8,128)(2,1)S(1)} collective-permute-done((bf16[4,2,64,1024]{3,2,1,0:T(8,128)(2,1)S(1)}, bf16[4,2,64,1024]{3,2,1,0:T(8,128)(2,1)S(1)}, u32[]{:S(2)}, u32[]{:S(2)}) %collective-permute-start.71) | collective-permute-done | bytes 1048608 | tf_op jit(solution)/shard_map/ppermute | solution.py:38
  666.4 5.1 collective-permute-done.75
  681.3 18.0 %collective-permute-done.47 = bf16[4,2,48,1024]{3,2,1,0:T(8,128)(2,1)S(1)} collective-permute-done((bf16[4,2,48,1024]{3,2,1,0:T(8,128)(2,1)S(1)}, bf16[4,2,48,1024]{3,2,1,0:T(8,128)(2,1)S(1)}, u32[]{:S(2)}, u32[]{:S(2)}) %collective-permute-start.47) | collective-permute-done | bytes 786464 | tf_op jit(solution)/shard_map/ppermute | solution.py:38
  706.9 5.6 collective-permute-done.50
  712.7 3.4 collective-permute-start.53
  (303 shorter events, 186.7 us)
Async XLA Ops:
  9.8 18.9 %collective-permute-start.22 = (bf16[80,1024]{1,0:T(8,128)(2,1)S(1)}, bf16[80,1024]{1,0:T(8,128)(2,1)S(1)}, u32[]{:S(2)}, u32[]{:S(2)}) collective-permute-start(bf16[80,1024]{1,0:T(8,128)(2,1)S(1)} %get-tuple-element.110), channel_id=1, source_target_pairs={{0,8},{8,0},{16,24},{24,16},{32,40},{40,32},{48,56},{56,48},{1,9},... | collective-permute-start | bytes 491528 | tf_op jit(solution)/shard_map/ppermute | solution.py:43
  34.8 16.7 %collective-permute-start.36 = (bf16[2,64,1024]{2,1,0:T(8,128)(2,1)S(1)}, bf16[2,64,1024]{2,1,0:T(8,128)(2,1)S(1)}, u32[]{:S(2)}, u32[]{:S(2)}) collective-permute-start(bf16[2,64,1024]{2,1,0:T(8,128)(2,1)S(1)} %maximum_select_fusion.3), channel_id=1, source_target_pairs={{0,6},{1,7},{2,0},{3,1},{4,2},{5,3},{6,4},{7,5},{8,14},{9,15},{10,... | collective-permute-start | bytes 786440 | tf_op jit(solution)/shard_map/ppermute | solution.py:38
  36.5 24.3 %collective-permute-start.23 = (bf16[2,80,1024]{2,1,0:T(8,128)(2,1)S(1)}, bf16[2,80,1024]{2,1,0:T(8,128)(2,1)S(1)}, u32[]{:S(2)}, u32[]{:S(2)}) collective-permute-start(bf16[2,80,1024]{2,1,0:T(8,128)(2,1)S(1)} %maximum_select_fusion.1), channel_id=1, source_target_pairs={{0,16},{8,24},{16,32},{24,40},{32,48},{40,56},{48,0},{56,8},{1,17}... | collective-permute-start | bytes 983048 | tf_op jit(solution)/shard_map/ppermute | solution.py:38
  36.9 27.0 %collective-permute-start.24 = (bf16[2,80,1024]{2,1,0:T(8,128)(2,1)S(1)}, bf16[2,80,1024]{2,1,0:T(8,128)(2,1)S(1)}, u32[]{:S(2)}, u32[]{:S(2)}) collective-permute-start(bf16[2,80,1024]{2,1,0:T(8,128)(2,1)S(1)} %maximum_select_fusion.1), channel_id=1, source_target_pairs={{0,32},{8,40},{16,48},{24,56},{32,0},{40,8},{48,16},{56,24},{1,33}... | collective-permute-start | bytes 983048 | tf_op jit(solution)/shard_map/ppermute | solution.py:38
  41.3 22.8 %collective-permute-start.25 = (bf16[2,80,1024]{2,1,0:T(8,128)(2,1)S(1)}, bf16[2,80,1024]{2,1,0:T(8,128)(2,1)S(1)}, u32[]{:S(2)}, u32[]{:S(2)}) collective-permute-start(bf16[2,80,1024]{2,1,0:T(8,128)(2,1)S(1)} %maximum_select_fusion.1), channel_id=1, source_target_pairs={{0,48},{8,56},{16,0},{24,8},{32,16},{40,24},{48,32},{56,40},{1,49}... | collective-permute-start | bytes 983048 | tf_op jit(solution)/shard_map/ppermute | solution.py:38
  46.6 24.7 %collective-permute-start.4 = (bf16[4,2,32,1024]{3,2,1,0:T(8,128)(2,1)S(1)}, bf16[4,2,32,1024]{3,2,1,0:T(8,128)(2,1)S(1)}, u32[]{:S(2)}, u32[]{:S(2)}) collective-permute-start(bf16[4,2,32,1024]{3,2,1,0:T(8,128)(2,1)S(1)} %bitcast_dynamic-update-slice_fusion.41), channel_id=1, source_target_pairs={{0,1},{1,0},{2,3},{3,2},{4,5},{5,4},{6,7},{7,6},{8,9},{9,8},{10,11... | collective-permute-start | bytes 1572872 | tf_op jit(solution)/shard_map/ppermute | solution.py:43
  51.5 19.8 %collective-permute-start.5 = (bf16[4,2,32,1024]{3,2,1,0:T(8,128)(2,1)S(1)}, bf16[4,2,32,1024]{3,2,1,0:T(8,128)(2,1)S(1)}, u32[]{:S(2)}, u32[]{:S(2)}) collective-permute-start(bf16[4,2,32,1024]{3,2,1,0:T(8,128)(2,1)S(1)} %bitcast_dynamic-update-slice_fusion.41), channel_id=1, source_target_pairs={{0,2},{1,3},{2,4},{3,5},{4,6},{5,7},{6,0},{7,1},{8,10},{9,11},{10,... | collective-permute-start | bytes 1572872 | tf_op jit(solution)/shard_map/ppermute | solution.py:38
  60.8 19.1 %collective-permute-start.7 = (bf16[4,2,32,1024]{3,2,1,0:T(8,128)(2,1)S(1)}, bf16[4,2,32,1024]{3,2,1,0:T(8,128)(2,1)S(1)}, u32[]{:S(2)}, u32[]{:S(2)}) collective-permute-start(bf16[4,2,32,1024]{3,2,1,0:T(8,128)(2,1)S(1)} %bitcast_dynamic-update-slice_fusion.41), channel_id=1, source_target_pairs={{0,4},{1,5},{2,6},{3,7},{4,0},{5,1},{6,2},{7,3},{8,12},{9,13},{10,... | collective-permute-start | bytes 1572872 | tf_op jit(solution)/shard_map/ppermute | solution.py:38
  63.9 35.0 %collective-permute-start.9 = (bf16[4,2,32,1024]{3,2,1,0:T(8,128)(2,1)S(1)}, bf16[4,2,32,1024]{3,2,1,0:T(8,128)(2,1)S(1)}, u32[]{:S(2)}, u32[]{:S(2)}) collective-permute-start(bf16[4,2,32,1024]{3,2,1,0:T(8,128)(2,1)S(1)} %bitcast_dynamic-update-slice_fusion.41), channel_id=1, source_target_pairs={{0,6},{1,7},{2,0},{3,1},{4,2},{5,3},{6,4},{7,5},{8,14},{9,15},{10,... | collective-permute-start | bytes 1572872 | tf_op jit(solution)/shard_map/ppermute | solution.py:38
  71.3 26.1 %collective-permute-start.16 = (bf16[2,4,32,1024]{3,2,1,0:T(8,128)(2,1)S(1)}, bf16[2,4,32,1024]{3,2,1,0:T(8,128)(2,1)S(1)}, u32[]{:S(2)}, u32[]{:S(2)}) collective-permute-start(bf16[2,4,32,1024]{3,2,1,0:T(8,128)(2,1)S(1)} %bitcast_dynamic-update-slice_fusion.38), channel_id=1, source_target_pairs={{0,16},{8,24},{16,32},{24,40},{32,48},{40,56},{48,0},{56,8},{1,17}... | collective-permute-start | bytes 1572872 | tf_op jit(solution)/shard_map/ppermute | solution.py:38
  71.3 27.7 %collective-permute-start.6 = (bf16[4,2,32,1024]{3,2,1,0:T(8,128)(2,1)S(1)}, bf16[4,2,32,1024]{3,2,1,0:T(8,128)(2,1)S(1)}, u32[]{:S(2)}, u32[]{:S(2)}) collective-permute-start(bf16[4,2,32,1024]{3,2,1,0:T(8,128)(2,1)S(1)} %collective-permute-done.5), channel_id=1, source_target_pairs={{0,1},{1,0},{2,3},{3,2},{4,5},{5,4},{6,7},{7,6},{8,9},{9,8},{10,11... | collective-permute-start | bytes 1572872 | tf_op jit(solution)/shard_map/ppermute | solution.py:43
  71.5 28.6 %collective-permute-start.18 = (bf16[2,4,32,1024]{3,2,1,0:T(8,128)(2,1)S(1)}, bf16[2,4,32,1024]{3,2,1,0:T(8,128)(2,1)S(1)}, u32[]{:S(2)}, u32[]{:S(2)}) collective-permute-start(bf16[2,4,32,1024]{3,2,1,0:T(8,128)(2,1)S(1)} %bitcast_dynamic-update-slice_fusion.38), channel_id=1, source_target_pairs={{0,32},{8,40},{16,48},{24,56},{32,0},{40,8},{48,16},{56,24},{1,33}... | collective-permute-start | bytes 1572872 | tf_op jit(solution)/shard_map/ppermute | solution.py:38
  79.9 22.7 %collective-permute-start.20 = (bf16[2,4,32,1024]{3,2,1,0:T(8,128)(2,1)S(1)}, bf16[2,4,32,1024]{3,2,1,0:T(8,128)(2,1)S(1)}, u32[]{:S(2)}, u32[]{:S(2)}) collective-permute-start(bf16[2,4,32,1024]{3,2,1,0:T(8,128)(2,1)S(1)} %bitcast_dynamic-update-slice_fusion.38), channel_id=1, source_target_pairs={{0,48},{8,56},{16,0},{24,8},{32,16},{40,24},{48,32},{56,40},{1,49}... | collective-permute-start | bytes 1572872 | tf_op jit(solution)/shard_map/ppermute | solution.py:38
  100.1 48.5 %collective-permute-start.38 = (bf16[2,4,64,1024]{3,2,1,0:T(8,128)(2,1)}, bf16[2,4,64,1024]{3,2,1,0:T(8,128)(2,1)S(1)}, u32[]{:S(2)}, u32[]{:S(2)}) collective-permute-start(bf16[2,4,64,1024]{3,2,1,0:T(8,128)(2,1)} %bitcast_dynamic-update-slice_fusion.37), channel_id=1, source_target_pairs={{0,16},{8,24},{16,32},{24,40},{32,48},{40,56},{48,0},{56,8},{1,17}... | collective-permute-start | bytes 3145736 | tf_op jit(solution)/shard_map/ppermute | solution.py:38
  102.6 47.2 %collective-permute-start.40 = (bf16[2,4,64,1024]{3,2,1,0:T(8,128)(2,1)}, bf16[2,4,64,1024]{3,2,1,0:T(8,128)(2,1)S(1)}, u32[]{:S(2)}, u32[]{:S(2)}) collective-permute-start(bf16[2,4,64,1024]{3,2,1,0:T(8,128)(2,1)} %bitcast_dynamic-update-slice_fusion.37), channel_id=1, source_target_pairs={{0,32},{8,40},{16,48},{24,56},{32,0},{40,8},{48,16},{56,24},{1,33}... | collective-permute-start | bytes 3145736 | tf_op jit(solution)/shard_map/ppermute | solution.py:38
  104.9 61.5 %collective-permute-start.42 = (bf16[2,4,64,1024]{3,2,1,0:T(8,128)(2,1)}, bf16[2,4,64,1024]{3,2,1,0:T(8,128)(2,1)}, u32[]{:S(2)}, u32[]{:S(2)}) collective-permute-start(bf16[2,4,64,1024]{3,2,1,0:T(8,128)(2,1)} %bitcast_dynamic-update-slice_fusion.37), channel_id=1, source_target_pairs={{0,48},{8,56},{16,0},{24,8},{32,16},{40,24},{48,32},{56,40},{1,49}... | collective-permute-start | bytes 3145736 | tf_op jit(solution)/shard_map/ppermute | solution.py:38
  106.6 64.6 %collective-permute-start.26 = (bf16[4,2,80,1024]{3,2,1,0:T(8,128)(2,1)S(1)}, bf16[4,2,80,1024]{3,2,1,0:T(8,128)(2,1)}, u32[]{:S(2)}, u32[]{:S(2)}) collective-permute-start(bf16[4,2,80,1024]{3,2,1,0:T(8,128)(2,1)S(1)} %bitcast_dynamic-update-slice_fusion.32), channel_id=1, source_target_pairs={{0,1},{1,0},{2,3},{3,2},{4,5},{5,4},{6,7},{7,6},{8,9},{9,8},{10,11... | collective-permute-start | bytes 3932168 | tf_op jit(solution)/shard_map/ppermute | solution.py:43
  107.9 66.2 %collective-permute-start.27 = (bf16[4,2,80,1024]{3,2,1,0:T(8,128)(2,1)S(1)}, bf16[4,2,80,1024]{3,2,1,0:T(8,128)(2,1)}, u32[]{:S(2)}, u32[]{:S(2)}) collective-permute-start(bf16[4,2,80,1024]{3,2,1,0:T(8,128)(2,1)S(1)} %bitcast_dynamic-update-slice_fusion.32), channel_id=1, source_target_pairs={{0,2},{1,3},{2,4},{3,5},{4,6},{5,7},{6,0},{7,1},{8,10},{9,11},{10,... | collective-permute-start | bytes 3932168 | tf_op jit(solution)/shard_map/ppermute | solution.py:38
  148.6 30.9 %collective-permute-start.29 = (bf16[4,2,80,1024]{3,2,1,0:T(8,128)(2,1)S(1)}, bf16[4,2,80,1024]{3,2,1,0:T(8,128)(2,1)}, u32[]{:S(2)}, u32[]{:S(2)}) collective-permute-start(bf16[4,2,80,1024]{3,2,1,0:T(8,128)(2,1)S(1)} %bitcast_dynamic-update-slice_fusion.32), channel_id=1, source_target_pairs={{0,4},{1,5},{2,6},{3,7},{4,0},{5,1},{6,2},{7,3},{8,12},{9,13},{10,... | collective-permute-start | bytes 3932168 | tf_op jit(solution)/shard_map/ppermute | solution.py:38
  149.8 57.4 %collective-permute-start.31 = (bf16[4,2,80,1024]{3,2,1,0:T(8,128)(2,1)S(1)}, bf16[4,2,80,1024]{3,2,1,0:T(8,128)(2,1)}, u32[]{:S(2)}, u32[]{:S(2)}) collective-permute-start(bf16[4,2,80,1024]{3,2,1,0:T(8,128)(2,1)S(1)} %bitcast_dynamic-update-slice_fusion.32), channel_id=1, source_target_pairs={{0,6},{1,7},{2,0},{3,1},{4,2},{5,3},{6,4},{7,5},{8,14},{9,15},{10,... | collective-permute-start | bytes 3932168 | tf_op jit(solution)/shard_map/ppermute | solution.py:38
  161.3 56.2 %all-to-all-start = ((bf16[8,256,384]{2,1,0:T(8,128)(2,1)}), bf16[8,256,384]{2,1,0:T(8,128)(2,1)S(1)}, u32[]{:S(2)}, u32[]{:S(2)}) async-start(bf16[8,256,384]{2,1,0:T(8,128)(2,1)} %shard_map.314), calls=%async_computation | async-start | bytes 3145728 | tf_op jit(solution)/shard_map/all_to_all | solution.py:115
  166.4 43.1 %collective-permute-start.39 = (bf16[2,4,64,1024]{3,2,1,0:T(8,128)(2,1)}, bf16[2,4,64,1024]{3,2,1,0:T(8,128)(2,1)S(1)}, u32[]{:S(2)}, u32[]{:S(2)}) collective-permute-start(bf16[2,4,64,1024]{3,2,1,0:T(8,128)(2,1)} %copy-done.9), channel_id=1, source_target_pairs={{0,1},{1,0},{2,3},{3,2},{4,5},{5,4},{6,7},{7,6},{8,9},{9,8},{10,11... | collective-permute-start | bytes 3145736 | tf_op jit(solution)/shard_map/ppermute | solution.py:43
  171.3 40.8 %collective-permute-start.41 = (bf16[2,4,64,1024]{3,2,1,0:T(8,128)(2,1)S(1)}, bf16[2,4,64,1024]{3,2,1,0:T(8,128)(2,1)S(1)}, u32[]{:S(2)}, u32[]{:S(2)}) collective-permute-start(bf16[2,4,64,1024]{3,2,1,0:T(8,128)(2,1)S(1)} %copy-done.12), channel_id=1, source_target_pairs={{0,1},{1,0},{2,3},{3,2},{4,5},{5,4},{6,7},{7,6},{8,9},{9,8},{10,11... | collective-permute-start | bytes 3145736 | tf_op jit(solution)/shard_map/ppermute | solution.py:43
  174.1 41.4 %collective-permute-start.43 = (bf16[2,4,64,1024]{3,2,1,0:T(8,128)(2,1)}, bf16[2,4,64,1024]{3,2,1,0:T(8,128)(2,1)S(1)}, u32[]{:S(2)}, u32[]{:S(2)}) collective-permute-start(bf16[2,4,64,1024]{3,2,1,0:T(8,128)(2,1)} %collective-permute-done.42), channel_id=1, source_target_pairs={{0,1},{1,0},{2,3},{3,2},{4,5},{5,4},{6,7},{7,6},{8,9},{9,8},{10,11... | collective-permute-start | bytes 3145736 | tf_op jit(solution)/shard_map/ppermute | solution.py:43
  179.6 65.6 %collective-permute-start.28 = (bf16[4,2,80,1024]{3,2,1,0:T(8,128)(2,1)}, bf16[4,2,80,1024]{3,2,1,0:T(8,128)(2,1)}, u32[]{:S(2)}, u32[]{:S(2)}) collective-permute-start(bf16[4,2,80,1024]{3,2,1,0:T(8,128)(2,1)} %collective-permute-done.27), channel_id=1, source_target_pairs={{0,1},{1,0},{2,3},{3,2},{4,5},{5,4},{6,7},{7,6},{8,9},{9,8},{10,11... | collective-permute-start | bytes 3932168 | tf_op jit(solution)/shard_map/ppermute | solution.py:43
  207.2 43.0 %collective-permute-start.30 = (bf16[4,2,80,1024]{3,2,1,0:T(8,128)(2,1)}, bf16[4,2,80,1024]{3,2,1,0:T(8,128)(2,1)}, u32[]{:S(2)}, u32[]{:S(2)}) collective-permute-start(bf16[4,2,80,1024]{3,2,1,0:T(8,128)(2,1)} %collective-permute-done.29), channel_id=1, source_target_pairs={{0,1},{1,0},{2,3},{3,2},{4,5},{5,4},{6,7},{7,6},{8,9},{9,8},{10,11... | collective-permute-start | bytes 3932168 | tf_op jit(solution)/shard_map/ppermute | solution.py:43
  209.5 45.6 %collective-permute-start.32 = (bf16[4,2,80,1024]{3,2,1,0:T(8,128)(2,1)}, bf16[4,2,80,1024]{3,2,1,0:T(8,128)(2,1)}, u32[]{:S(2)}, u32[]{:S(2)}) collective-permute-start(bf16[4,2,80,1024]{3,2,1,0:T(8,128)(2,1)} %collective-permute-done.31), channel_id=1, source_target_pairs={{0,1},{1,0},{2,3},{3,2},{4,5},{5,4},{6,7},{7,6},{8,9},{9,8},{10,11... | collective-permute-start | bytes 3932168 | tf_op jit(solution)/shard_map/ppermute | solution.py:43
  233.1 24.5 %all-to-all-start.1 = ((bf16[8,256,128]{2,1,0:T(8,128)(2,1)}), bf16[8,256,128]{2,1,0:T(8,128)(2,1)S(1)}, u32[]{:S(2)}, u32[]{:S(2)}) async-start(bf16[8,256,128]{2,1,0:T(8,128)(2,1)} %bitcast.368), calls=%async_computation.1 | async-start | bytes 1048576 | tf_op jit(solution)/shard_map/all_to_all | solution.py:115
  503.6 25.3 %all-to-all-start.7 = ((bf16[8,256,384]{2,1,0:T(8,128)(2,1)}), bf16[8,256,384]{2,1,0:T(8,128)(2,1)S(1)}, u32[]{:S(2)}, u32[]{:S(2)}) async-start(bf16[8,256,384]{2,1,0:T(8,128)(2,1)} %bitcast.349), calls=%async_computation.7 | async-start | bytes 3145728 | tf_op jit(solution)/shard_map/all_to_all | solution.py:115
  518.2 43.2 %collective-permute-start.62 = (bf16[32,64,1024]{2,1,0:T(8,128)(2,1)}, bf16[32,64,1024]{2,1,0:T(8,128)(2,1)}, u32[]{:S(2)}, u32[]{:S(2)}) collective-permute-start(bf16[32,64,1024]{2,1,0:T(8,128)(2,1)} %get-tuple-element.68), channel_id=1, source_target_pairs={{0,1},{1,0},{2,3},{3,2},{4,5},{5,4},{6,7},{7,6},{8,9},{9,8},{10,11... | collective-permute-start | bytes 12582920 | tf_op jit(solution)/shard_map/ppermute | solution.py:43
  518.5 73.0 %collective-permute-start.70 = (bf16[32,64,1024]{2,1,0:T(8,128)(2,1)}, bf16[32,64,1024]{2,1,0:T(8,128)(2,1)}, u32[]{:S(2)}, u32[]{:S(2)}) collective-permute-start(bf16[32,64,1024]{2,1,0:T(8,128)(2,1)} %get-tuple-element.70), channel_id=1, source_target_pairs={{0,1},{1,0},{2,3},{3,2},{4,5},{5,4},{6,7},{7,6},{8,9},{9,8},{10,11... | collective-permute-start | bytes 12582920 | tf_op jit(solution)/shard_map/ppermute | solution.py:43
  549.0 57.1 %collective-permute-start.46 = (bf16[32,48,1024]{2,1,0:T(8,128)(2,1)}, bf16[32,48,1024]{2,1,0:T(8,128)(2,1)S(1)}, u32[]{:S(2)}, u32[]{:S(2)}) collective-permute-start(bf16[32,48,1024]{2,1,0:T(8,128)(2,1)} %get-tuple-element.60), channel_id=1, source_target_pairs={{0,1},{1,0},{2,3},{3,2},{4,5},{5,4},{6,7},{7,6},{8,9},{9,8},{10,11... | collective-permute-start | bytes 9437192 | tf_op jit(solution)/shard_map/ppermute | solution.py:43
  561.4 25.9 %collective-permute-start.55 = (bf16[2,4,32,1024]{3,2,0,1:T(8,128)(2,1)}, bf16[2,4,32,1024]{3,2,0,1:T(8,128)(2,1)S(1)}, u32[]{:S(2)}, u32[]{:S(2)}) collective-permute-start(bf16[2,4,32,1024]{3,2,0,1:T(8,128)(2,1)} %bitcast.326), channel_id=1, source_target_pairs={{0,16},{8,24},{16,32},{24,40},{32,48},{40,56},{48,0},{56,8},{1,17}... | collective-permute-start | bytes 1572872 | tf_op jit(solution)/shard_map/ppermute | solution.py:38
  572.8 34.4 %collective-permute-start.65 = (bf16[2,4,64,1024]{3,2,1,0:T(8,128)(2,1)S(1)}, bf16[2,4,64,1024]{3,2,1,0:T(8,128)(2,1)S(1)}, u32[]{:S(2)}, u32[]{:S(2)}) collective-permute-start(bf16[2,4,64,1024]{3,2,1,0:T(8,128)(2,1)S(1)} %get-tuple-element.75), channel_id=1, source_target_pairs={{0,48},{8,56},{16,0},{24,8},{32,16},{40,24},{48,32},{56,40},{1,49}... | collective-permute-start | bytes 3145736 | tf_op jit(solution)/shard_map/ppermute | solution.py:38
  591.5 25.5 %collective-permute-start.64 = (bf16[2,4,64,1024]{3,2,1,0:T(8,128)(2,1)S(1)}, bf16[2,4,64,1024]{3,2,1,0:T(8,128)(2,1)S(1)}, u32[]{:S(2)}, u32[]{:S(2)}) collective-permute-start(bf16[2,4,64,1024]{3,2,1,0:T(8,128)(2,1)S(1)} %get-tuple-element.76), channel_id=1, source_target_pairs={{0,32},{8,40},{16,48},{24,56},{32,0},{40,8},{48,16},{56,24},{1,33}... | collective-permute-start | bytes 3145736 | tf_op jit(solution)/shard_map/ppermute | solution.py:38
  591.5 48.5 %collective-permute-start.63 = (bf16[2,4,64,1024]{3,2,1,0:T(8,128)(2,1)S(1)}, bf16[2,4,64,1024]{3,2,1,0:T(8,128)(2,1)}, u32[]{:S(2)}, u32[]{:S(2)}) collective-permute-start(bf16[2,4,64,1024]{3,2,1,0:T(8,128)(2,1)S(1)} %get-tuple-element.74), channel_id=1, source_target_pairs={{0,16},{8,24},{16,32},{24,40},{32,48},{40,56},{48,0},{56,8},{1,17}... | collective-permute-start | bytes 3145736 | tf_op jit(solution)/shard_map/ppermute | solution.py:38
  605.2 37.2 %collective-permute-start.73 = (bf16[4,2,64,1024]{3,2,1,0:T(8,128)(2,1)S(1)}, bf16[4,2,64,1024]{3,2,1,0:T(8,128)(2,1)S(1)}, u32[]{:S(2)}, u32[]{:S(2)}) collective-permute-start(bf16[4,2,64,1024]{3,2,1,0:T(8,128)(2,1)S(1)} %get-tuple-element.72), channel_id=1, source_target_pairs={{0,6},{1,7},{2,0},{3,1},{4,2},{5,3},{6,4},{7,5},{8,14},{9,15},{10,... | collective-permute-start | bytes 3145736 | tf_op jit(solution)/shard_map/ppermute | solution.py:38
  606.1 38.6 %collective-permute-start.72 = (bf16[4,2,64,1024]{3,2,1,0:T(8,128)(2,1)S(1)}, bf16[4,2,64,1024]{3,2,1,0:T(8,128)(2,1)S(1)}, u32[]{:S(2)}, u32[]{:S(2)}) collective-permute-start(bf16[4,2,64,1024]{3,2,1,0:T(8,128)(2,1)S(1)} %get-tuple-element.73), channel_id=1, source_target_pairs={{0,4},{1,5},{2,6},{3,7},{4,0},{5,1},{6,2},{7,3},{8,12},{9,13},{10,... | collective-permute-start | bytes 3145736 | tf_op jit(solution)/shard_map/ppermute | solution.py:38
  607.2 50.7 %collective-permute-start.71 = (bf16[4,2,64,1024]{3,2,1,0:T(8,128)(2,1)S(1)}, bf16[4,2,64,1024]{3,2,1,0:T(8,128)(2,1)S(1)}, u32[]{:S(2)}, u32[]{:S(2)}) collective-permute-start(bf16[4,2,64,1024]{3,2,1,0:T(8,128)(2,1)S(1)} %get-tuple-element.71), channel_id=1, source_target_pairs={{0,2},{1,3},{2,4},{3,5},{4,6},{5,7},{6,0},{7,1},{8,10},{9,11},{10,... | collective-permute-start | bytes 3145736 | tf_op jit(solution)/shard_map/ppermute | solution.py:38
  617.0 42.3 %collective-permute-start.61 = (bf16[32,1024]{1,0:T(8,128)(2,1)S(1)}, bf16[32,1024]{1,0:T(8,128)(2,1)S(1)}, u32[]{:S(2)}, u32[]{:S(2)}) collective-permute-start(bf16[32,1024]{1,0:T(8,128)(2,1)S(1)} %fusion.31), channel_id=1, source_target_pairs={{0,8},{8,0},{16,24},{24,16},{32,40},{40,32},{48,56},{56,48},{1,9},... | collective-permute-start | bytes 196616 | tf_op jit(solution)/shard_map/ppermute | solution.py:43
  642.2 17.8 %collective-permute-start.68 = (bf16[2,64,1024]{2,1,0:T(8,128)(2,1)S(1)}, bf16[2,64,1024]{2,1,0:T(8,128)(2,1)S(1)}, u32[]{:S(2)}, u32[]{:S(2)}) collective-permute-start(bf16[2,64,1024]{2,1,0:T(8,128)(2,1)S(1)} %get-tuple-element.88), channel_id=1, source_target_pairs={{0,6},{1,7},{2,0},{3,1},{4,2},{5,3},{6,4},{7,5},{8,14},{9,15},{10,... | collective-permute-start | bytes 786440 | tf_op jit(solution)/shard_map/ppermute | solution.py:38
  642.3 18.7 %collective-permute-start.67 = (bf16[2,64,1024]{2,1,0:T(8,128)(2,1)S(1)}, bf16[2,64,1024]{2,1,0:T(8,128)(2,1)S(1)}, u32[]{:S(2)}, u32[]{:S(2)}) collective-permute-start(bf16[2,64,1024]{2,1,0:T(8,128)(2,1)S(1)} %get-tuple-element.89), channel_id=1, source_target_pairs={{0,4},{1,5},{2,6},{3,7},{4,0},{5,1},{6,2},{7,3},{8,12},{9,13},{10,... | collective-permute-start | bytes 786440 | tf_op jit(solution)/shard_map/ppermute | solution.py:38
  644.6 19.9 %collective-permute-start.66 = (bf16[2,64,1024]{2,1,0:T(8,128)(2,1)S(1)}, bf16[2,64,1024]{2,1,0:T(8,128)(2,1)S(1)}, u32[]{:S(2)}, u32[]{:S(2)}) collective-permute-start(bf16[2,64,1024]{2,1,0:T(8,128)(2,1)S(1)} %get-tuple-element.87), channel_id=1, source_target_pairs={{0,2},{1,3},{2,4},{3,5},{4,6},{5,7},{6,0},{7,1},{8,10},{9,11},{10,... | collective-permute-start | bytes 786440 | tf_op jit(solution)/shard_map/ppermute | solution.py:38
  659.3 20.2 %collective-permute-start.49 = (bf16[4,2,48,1024]{3,2,1,0:T(8,128)(2,1)S(1)}, bf16[4,2,48,1024]{3,2,1,0:T(8,128)(2,1)S(1)}, u32[]{:S(2)}, u32[]{:S(2)}) collective-permute-start(bf16[4,2,48,1024]{3,2,1,0:T(8,128)(2,1)S(1)} %get-tuple-element.78), channel_id=1, source_target_pairs={{0,6},{1,7},{2,0},{3,1},{4,2},{5,3},{6,4},{7,5},{8,14},{9,15},{10,... | collective-permute-start | bytes 2359304 | tf_op jit(solution)/shard_map/ppermute | solution.py:38
  660.0 21.4 %collective-permute-start.48 = (bf16[4,2,48,1024]{3,2,1,0:T(8,128)(2,1)S(1)}, bf16[4,2,48,1024]{3,2,1,0:T(8,128)(2,1)S(1)}, u32[]{:S(2)}, u32[]{:S(2)}) collective-permute-start(bf16[4,2,48,1024]{3,2,1,0:T(8,128)(2,1)S(1)} %get-tuple-element.79), channel_id=1, source_target_pairs={{0,4},{1,5},{2,6},{3,7},{4,0},{5,1},{6,2},{7,3},{8,12},{9,13},{10,... | collective-permute-start | bytes 2359304 | tf_op jit(solution)/shard_map/ppermute | solution.py:38
  661.1 38.3 %collective-permute-start.47 = (bf16[4,2,48,1024]{3,2,1,0:T(8,128)(2,1)S(1)}, bf16[4,2,48,1024]{3,2,1,0:T(8,128)(2,1)S(1)}, u32[]{:S(2)}, u32[]{:S(2)}) collective-permute-start(bf16[4,2,48,1024]{3,2,1,0:T(8,128)(2,1)S(1)} %get-tuple-element.77), channel_id=1, source_target_pairs={{0,2},{1,3},{2,4},{3,5},{4,6},{5,7},{6,0},{7,1},{8,10},{9,11},{10,... | collective-permute-start | bytes 2359304 | tf_op jit(solution)/shard_map/ppermute | solution.py:38
  671.6 30.5 %collective-permute-start.69 = (bf16[64,1024]{1,0:T(8,128)(2,1)S(1)}, bf16[64,1024]{1,0:T(8,128)(2,1)S(1)}, u32[]{:S(2)}, u32[]{:S(2)}) collective-permute-start(bf16[64,1024]{1,0:T(8,128)(2,1)S(1)} %fusion.24), channel_id=1, source_target_pairs={{0,8},{8,0},{16,24},{24,16},{32,40},{40,32},{48,56},{56,48},{1,9},... | collective-permute-start | bytes 393224 | tf_op jit(solution)/shard_map/ppermute | solution.py:43
  675.1 41.0 %collective-permute-start.77 = (bf16[64,1024]{1,0:T(8,128)(2,1)S(1)}, bf16[64,1024]{1,0:T(8,128)(2,1)S(1)}, u32[]{:S(2)}, u32[]{:S(2)}) collective-permute-start(bf16[64,1024]{1,0:T(8,128)(2,1)S(1)} %fusion.25), channel_id=1, source_target_pairs={{0,8},{8,0},{16,24},{24,16},{32,40},{40,32},{48,56},{56,48},{1,9},... | collective-permute-start | bytes 393224 | tf_op jit(solution)/shard_map/ppermute | solution.py:43
  (49 other events, 466.1 us)

commit v2 on v1

--- a/solution.py
+++ b/solution.py
@@ -14,6 +14,7 @@
 DENSITY_SCALE = 0.3989422804014327
 SCORE_SCALE = DH ** (-0.5)
 SLAB = 16
+SMALL_WIDTH = 512
 QUERY_ROWS = 256
 VMEM_LIMIT = 60 * 1024 * 1024
 
@@ -48,67 +49,142 @@
     return dp_index // 2, dp_index % 2, head_index // 2, head_index % 2
 
 
-def spread(shard, last_axis):
-    x_me, z_me, y_me, core_me = coordinates()
+def after(value, *others):
+    return lax.optimization_barrier((value,) + others)[0]
+
+
+def blank(shape, given):
+    def kernel(given_ref, out_ref):
+        pass
+
+    anywhere = pl.BlockSpec(memory_space=pl.ANY)
+    return pl.pallas_call(
+        kernel,
+        in_specs=[anywhere],
+        out_specs=anywhere,
+        out_shape=jax.ShapeDtypeStruct(shape, given.dtype),
+    )(given)
+
+
+def by_core(core, mine, other, axis):
+    return jnp.where(
+        core == 0,
+        jnp.concatenate([mine, other], axis=axis),
+        jnp.concatenate([other, mine], axis=axis),
+    )
+
+
+def spread_chip(shard):
+    _, z_me, _, core_me = coordinates()
+    half = shard.shape[1] // 2
+    first, second = shard[:, :half], shard[:, half:]
+    mine = jnp.where(core_me == 0, first, second)[None]
+    cores = by_core(core_me, mine, swap(jnp.where(core_me == 0, second, first), "head")[None], 0)
+    return by_core(z_me, cores[None], swap(cores, "dp")[None], 0)
+
+
+def spread_lane(pair, last_axis):
+    x_me, _, y_me, _ = coordinates()
     x_size, y_size = lax.axis_size("dp") // 2, lax.axis_size("head") // 2
-    across = swap(shard, "dp")
-    pair = jnp.where(z_me == 0, jnp.stack([shard, across]), jnp.stack([across, shard]))
-    zeros = (0,) * shard.ndim
-    if last_axis == "dp":
-        first_axis, first_me, first_size = "head", y_me, y_size
-        last_me, last_size = x_me, x_size
-        lane = jnp.zeros((2, y_size) + shard.shape, shard.dtype)
-    else:
-        first_axis, first_me, first_size = "dp", x_me, x_size
-        last_me, last_size = y_me, y_size
-        lane = jnp.zeros((x_size, 2) + shard.shape, shard.dtype)
-    for places in range(first_size):
-        came = pair if places == 0 else hop(pair, first_axis, places)
-        source = (first_me - places) % first_size
-        if last_axis == "dp":
+    shape = pair.shape[1:]
+    zeros = (0,) * len(shape)
+    along_y = last_axis == "dp"
+    axis, me, size = ("head", y_me, y_size) if along_y else ("dp", x_me, x_size)
+    lane = blank(((2, size) if along_y else (size, 2)) + shape, pair)
+    for places in range(size):
+        came = pair if places == 0 else hop(pair, axis, places)
+        source = (me - places) % size
+        if along_y:
             lane = lax.dynamic_update_slice(lane, came[:, None], (0, source) + zeros)
         else:
             lane = lax.dynamic_update_slice(lane, came[None], (source, 0) + zeros)
-    whole = jnp.zeros((x_size, 2, y_size, 2) + shard.shape, shard.dtype)
-    arrived = [
-        lane if places == 0 else hop(lane, last_axis, places) for places in range(last_size)
-    ]
-    for places, came in enumerate(arrived):
-        source = (last_me - places) % last_size
-        for core, block in ((core_me, came), (1 - core_me, swap(came, "head"))):
-            if last_axis == "dp":
-                whole = lax.dynamic_update_slice(
-                    whole, block[None, :, :, None], (source, 0, 0, core) + zeros
-                )
-            else:
-                whole = lax.dynamic_update_slice(
-                    whole, block[:, :, None, None], (0, 0, source, core) + zeros
-                )
-    return whole.reshape((x_size * 2 * y_size * 2,) + shard.shape)
-
-
-def ring_sum(terms, axis, dim, me, size):
-    own = lax.dynamic_index_in_dim(terms, me, dim, keepdims=False).astype(jnp.float32)
-    for places in range(1, size):
-        block = lax.dynamic_index_in_dim(terms, (me + places) % size, dim, keepdims=False)
-        own = own + hop(block, axis, places).astype(jnp.float32)
+    return lane
+
+
+def spread_ends(lane, last_axis):
+    return hop(lane, last_axis, 1), hop(lane, last_axis, -1)
+
+
+def spread_rest(lane, ends, last_axis):
+    x_me, _, y_me, _ = coordinates()
+    x_size, y_size = lax.axis_size("dp") // 2, lax.axis_size("head") // 2
+    along_x = last_axis == "dp"
+    me, size = (x_me, x_size) if along_x else (y_me, y_size)
+    low, high = ends
+    half = lane.shape[0] // 2
+    far = (hop(low[:half], last_axis, 1), hop(high[half:], last_axis, -1))
+    shape = lane.shape[2:]
+    zeros = (0,) * len(shape)
+    near = blank((x_size, 2, y_size) + shape, lane)
+    for places, at, block in (
+        (0, 0, lane),
+        (1, 0, low),
+        (-1, 0, high),
+        (2, 0, far[0]),
+        (2, half, far[1]),
+    ):
+        source = (me - places) % size
+        if along_x:
+            near = lax.dynamic_update_slice(near, block[None], (source, at, 0) + zeros)
+        else:
+            near = lax.dynamic_update_slice(near, block[:, :, None], (at, 0, source) + zeros)
+    near = near.reshape((-1,) + shape[1:])
+    return near, swap(near, "head")
+
+
+def piece(terms, at, dim):
+    return lax.dynamic_index_in_dim(terms, at, dim, keepdims=False)
+
+
+def core_sum(mine, other):
+    x_size, y_size = lax.axis_size("dp") // 2, lax.axis_size("head") // 2
+    total = mine.astype(jnp.float32) + swap(other, "head").astype(jnp.float32)
+    return total.astype(jnp.bfloat16).reshape((x_size, 2, y_size, 2) + mine.shape[1:])
+
+
+def ring_halves(terms, axis):
+    x_me, _, y_me, _ = coordinates()
+    dim, me, size = (0, x_me, 4) if axis == "dp" else (2, y_me, 4)
+    far = piece(terms, (me + 2) % size, dim)
+    half = far.shape[0] // 2
+    return hop(far[:half], axis, 1), hop(far[half:], axis, -1)
+
+
+def ring_rest(terms, halves, axis):
+    x_me, _, y_me, _ = coordinates()
+    dim, me, size = (0, x_me, 4) if axis == "dp" else (2, y_me, 4)
+    low, high = (part.astype(jnp.float32) for part in halves)
+    up = piece(terms, (me + 1) % size, dim).astype(jnp.float32)
+    down = piece(terms, (me - 1) % size, dim).astype(jnp.float32)
+    half = up.shape[0] // 2
+    up = jnp.concatenate([up[:half] + low, up[half:]]).astype(jnp.bfloat16)
+    down = jnp.concatenate([down[:half], down[half:] + high]).astype(jnp.bfloat16)
+    total = piece(terms, me, dim).astype(jnp.float32)
+    total = total + hop(up, axis, 1).astype(jnp.float32)
+    return total + hop(down, axis, -1).astype(jnp.float32)
+
+
+def ring_direct(terms, axis, dim, me):
+    own = piece(terms, me, dim).astype(jnp.float32)
+    for places in (1, 2, 3):
+        own = own + hop(piece(terms, (me + places) % 4, dim), axis, places).astype(jnp.float32)
     return own
 
 
-def collect(mine, other, first_axis):
-    x_me, z_me, y_me, core_me = coordinates()
-    x_size, y_size = lax.axis_size("dp") // 2, lax.axis_size("head") // 2
-    chip_sum = mine.astype(jnp.float32) + swap(other, "head").astype(jnp.float32)
-    terms = chip_sum.astype(jnp.bfloat16).reshape((x_size, 2, y_size) + mine.shape[1:])
+def second_ring(terms, first_axis):
+    x_me, _, y_me, _ = coordinates()
+    terms = terms.astype(jnp.bfloat16)
     if first_axis == "dp":
-        terms = ring_sum(terms, "dp", 0, x_me, x_size).astype(jnp.bfloat16)
-        terms = ring_sum(terms, "head", 1, y_me, y_size)
-    else:
-        terms = ring_sum(terms, "head", 2, y_me, y_size).astype(jnp.bfloat16)
-        terms = ring_sum(terms, "dp", 0, x_me, x_size)
-    away = lax.dynamic_index_in_dim(terms, 1 - z_me, 0, keepdims=False).astype(jnp.bfloat16)
-    own = lax.dynamic_index_in_dim(terms, z_me, 0, keepdims=False)
-    return own + swap(away, "dp").astype(jnp.float32)
+        return ring_direct(terms, "head", 1, y_me)
+    return ring_direct(terms, "dp", 0, x_me)
+
+
+def collect_rest(terms):
+    _, z_me, _, core_me = coordinates()
+    away = piece(terms, 1 - z_me, 0).astype(jnp.bfloat16)
+    cores = piece(terms, z_me, 0) + swap(away, "dp").astype(jnp.float32)
+    got = swap(piece(cores, 1 - core_me, 0).astype(jnp.bfloat16), "head").astype(jnp.float32)
+    return by_core(core_me, piece(cores, core_me, 0), got, 1)
 
 
 def to_peers(blocks):
@@ -161,17 +237,23 @@
     return table_ref[row : row + 1, :]
 
 
-def side_by_side(blocks_ref, start=0):
+def side_by_side(blocks_ref, start=0, first=0, count=8):
     return jnp.concatenate(
-        [blocks_ref[peer, :, start : start + 128] for peer in range(blocks_ref.shape[0])], axis=1
-    )
-
-
-def put_side_by_side(blocks_ref, rows, start=0):
-    for peer in range(blocks_ref.shape[0]):
-        blocks_ref[peer, :, start : start + 128] = rows[:, peer * 128 : (peer + 1) * 128].astype(
-            blocks_ref.dtype
-        )
+        [blocks_ref[first + peer, :, start : start + 128] for peer in range(count)], axis=1
+    )
+
+
+def put_side_by_side(blocks_ref, rows, start=0, first=0):
+    for peer in range(rows.shape[1] // 128):
+        blocks_ref[first + peer, :, start : start + 128] = rows[
+            :, peer * 128 : (peer + 1) * 128
+        ].astype(blocks_ref.dtype)
+
+
+def halves(core, rows):
+    half = rows.shape[1] // 2
+    first, second = rows[:, :half], rows[:, half:]
+    return jnp.where(core == 0, first, second), jnp.where(core == 0, second, first)
 
 
 def attn_normed(rows, table_ref):
@@ -194,13 +276,22 @@
     return 0.5 * (1.0 + lax.erf(hidden * ROOT_HALF))
 
 
-def front_kernel(x_ref, table_ref, qk_ref, v_ref, out_ref):
+def front_kernel(
+    core_ref, x_ref, table_ref, qk_mine_ref, v_mine_ref, qk_other_ref, v_other_ref, out_ref
+):
+    core = core_ref[0]
     normed, _, _ = attn_normed(x_ref[...].astype(jnp.float32), table_ref)
-    queries = product(normed, flat(qk_ref[:, :SLAB])) + vector(table_ref, QUERY_ADD)
-    put_side_by_side(out_ref, queries, 0)
-    put_side_by_side(out_ref, product(normed, flat(qk_ref[:, SLAB:])), 128)
-    values = product(normed, flat(v_ref[...])) + vector(table_ref, VALUE_ADD)
-    put_side_by_side(out_ref, values, 256)
+    query_adds = halves(core, vector(table_ref, QUERY_ADD))
+    value_adds = halves(core, vector(table_ref, VALUE_ADD))
+    for at, (qk_ref, v_ref) in enumerate(
+        ((qk_mine_ref, v_mine_ref), (qk_other_ref, v_other_ref))
+    ):
+        first = (core if at == 0 else 1 - core) * 4
+        queries = product(normed, flat(qk_ref[:, :SLAB])) + query_adds[at]
+        put_side_by_side(out_ref, queries, 0, first)
+        put_side_by_side(out_ref, product(normed, flat(qk_ref[:, SLAB:])), 128, first)
+        values = product(normed, flat(v_ref[...])) + value_adds[at]
+        put_side_by_side(out_ref, values, 256, first)
 
 
 def valid_rows(count, like):
@@ -363,15 +454,35 @@
                 sums_ref[row : row + 1, :] = column_sum(rows)
 
 
-def front_back_kernel(keep, grad_ref, middle_grad_ref, x_ref, table_ref, qk_ref, v_ref, *rest):
+def front_back_kernel(
+    keep,
+    core_ref,
+    grad_ref,
+    middle_grad_ref,
+    x_ref,
+    table_ref,
+    qk_mine_ref,
+    v_mine_ref,
+    qk_other_ref,
+    v_other_ref,
+    *rest,
+):
     if keep:
         out_ref, sums_ref = rest
     else:
         (out_ref,) = rest
-    queries, keys, values = (side_by_side(grad_ref, start) for start in (0, 128, 256))
-    grad_normed = product_nt(queries, flat(qk_ref[:, :SLAB]))
-    grad_normed += product_nt(keys, flat(qk_ref[:, SLAB:]))
-    grad_normed += product_nt(values, flat(v_ref[...]))
+    core = core_ref[0]
+    grad_normed = 0.0
+    for at, (qk_ref, v_ref) in enumerate(
+        ((qk_mine_ref, v_mine_ref), (qk_other_ref, v_other_ref))
+    ):
+        first = (core if at == 0 else 1 - core) * 4
+        queries, keys, values = (
+            side_by_side(grad_ref, start, first, 4) for start in (0, 128, 256)
+        )
+        grad_normed += product_nt(queries, flat(qk_ref[:, :SLAB]))
+        grad_normed += product_nt(keys, flat(qk_ref[:, SLAB:]))
+        grad_normed += product_nt(values, flat(v_ref[...]))
     _, scaled, inverse = attn_normed(x_ref[...].astype(jnp.float32), table_ref)
     grad_input = middle_grad_ref[...] + norm_back(
         grad_normed * vector(table_ref, ATTN_GAIN), scaled, inverse
@@ -382,18 +493,16 @@
         for row, rows in (
             (ATTN_GAIN, grad_normed * scaled),
             (ATTN_SHIFT, grad_normed),
-            (QUERY_ADD, queries.astype(jnp.float32)),
-            (VALUE_ADD, values.astype(jnp.float32)),
+            (QUERY_ADD, side_by_side(grad_ref, 0).astype(jnp.float32)),
+            (VALUE_ADD, side_by_side(grad_ref, 256).astype(jnp.float32)),
         ):
             sums_ref[row : row + 1, :] = column_sum(rows)
 
 
-def put_by_core(core, mine_ref, other_ref, rows, start, count):
-    pairs = rows.astype(jnp.bfloat16).reshape(-1, 2, count, rows.shape[-1])
-    first, second = pairs[:, 0], pairs[:, 1]
-    here = core == 0
-    mine_ref[:, start : start + count] = jnp.where(here, first, second)
-    other_ref[:, start : start + count] = jnp.where(here, second, first)
+def put_products(core, mine_ref, other_ref, left, right, start, count):
+    for ref, part in zip((mine_ref, other_ref), halves(core, right)):
+        grad = product_tn(left, part).astype(jnp.bfloat16)
+        ref[:, start : start + count] = grad.reshape(-1, count, part.shape[1])
 
 
 def mlp_weights_kernel(
@@ -402,41 +511,40 @@
     hidden_low_ref,
     active_ref,
     mlp_low_ref,
+    attn_ref,
+    branch_low_ref,
     fc1_mine_ref,
     fc1_other_ref,
     fc2_mine_ref,
     fc2_other_ref,
+    proj_mine_ref,
+    proj_other_ref,
 ):
     core = core_ref[0]
-    fc2_grad = product_tn(active_ref[...], mlp_low_ref[...])
-    put_by_core(core, fc2_mine_ref, fc2_other_ref, fc2_grad, 0, fc2_mine_ref.shape[1])
-    fc1_grad = product_tn(normed_ref[...], hidden_low_ref[...])
-    put_by_core(core, fc1_mine_ref, fc1_other_ref, fc1_grad, 0, SLAB)
-
-
-def attn_weights_kernel(
-    core_ref,
-    x_ref,
-    table_ref,
-    grad_ref,
-    attn_ref,
-    branch_low_ref,
-    small_ref,
-    first_mine_ref,
-    first_other_ref,
-    second_mine_ref,
-    second_other_ref,
-):
+    owned = fc2_mine_ref.shape[1]
+    put_products(core, fc2_mine_ref, fc2_other_ref, active_ref[...], mlp_low_ref[...], 0, owned)
+    put_products(core, fc1_mine_ref, fc1_other_ref, normed_ref[...], hidden_low_ref[...], 0, SLAB)
+
+    @pl.when(pl.program_id(0) == 0)
+    def _():
+        attn = side_by_side(attn_ref)
+        put_products(core, proj_mine_ref, proj_other_ref, attn, branch_low_ref[...], 0, SLAB)
+
+
+def query_key_weights_kernel(core_ref, x_ref, table_ref, grad_ref, mine_ref, other_ref):
+    normed, _, _ = attn_normed(x_ref[...].astype(jnp.float32), table_ref)
+    for at in range(2):
+        grads = side_by_side(grad_ref, at * 128)
+        put_products(core_ref[0], mine_ref, other_ref, normed, grads, at * SLAB, SLAB)
+
+
+def value_weights_kernel(core_ref, x_ref, table_ref, grad_ref, small_ref, mine_ref, other_ref):
     core = core_ref[0]
     normed, _, _ = attn_normed(x_ref[...].astype(jnp.float32), table_ref)
-    for at in range(2):
-        grad = product_tn(normed, side_by_side(grad_ref, at * 128))
-        put_by_core(core, first_mine_ref, first_other_ref, grad, at * SLAB, SLAB)
-    grad = product_tn(normed, side_by_side(grad_ref, 256))
-    put_by_core(core, second_mine_ref, second_other_ref, grad, 0, SLAB)
-    grad = product_tn(side_by_side(attn_ref), branch_low_ref[...])
-    put_by_core(core, second_mine_ref, second_other_ref, grad, SLAB, SLAB)
-    put_by_core(core, second_mine_ref, second_other_ref, flat(small_ref[...]), 2 * SLAB, SLAB)
+    put_products(core, mine_ref, other_ref, normed, side_by_side(grad_ref, 256), 0, SLAB)
+    small = small_ref[...]
+    mine_ref[:, SLAB:] = jnp.where(core == 0, small, jnp.zeros_like(small))
+    other_ref[:, SLAB:] = jnp.where(core == 0, jnp.zeros_like(small), small)
 
 
 def like(*shape, dtype=jnp.bfloat16):
@@ -452,25 +560,32 @@
     return pltpu.CompilerParams(vmem_limit_bytes=VMEM_LIMIT)
 
 
+def takes(microseconds):
+    return pl.CostEstimate(
+        flops=int(microseconds * 1.15e9), transcendentals=0, bytes_accessed=int(microseconds * 3e6)
+    )
+
+
 SCALARS = pl.BlockSpec(memory_space=pltpu.SMEM)
 
 
-def call_front(x, table, early):
-    rows, width = x.shape
-    devices = early[0].shape[0]
+def early_specs(early):
+    devices, _, half = early[0].shape
+    values = pl.BlockSpec((devices, SLAB, half), lambda i: (0, 0, 0))
+    return [whole_block(early[0]), values, whole_block(early[0]), values]
+
+
+def call_front(core, x, table, early):
+    rows, _ = x.shape
     return pl.pallas_call(
         front_kernel,
         grid=(1,),
-        in_specs=[
-            whole_block(x),
-            whole_block(table),
-            whole_block(early[0]),
-            pl.BlockSpec((devices, SLAB, width), lambda i: (0, 0, 0)),
-        ],
+        in_specs=[SCALARS, whole_block(x), whole_block(table)] + early_specs(early),
         out_specs=pl.BlockSpec((8, rows, 384), lambda i: (0, 0, 0)),
         out_shape=like(8, rows, 384),
         compiler_params=params(),
-    )(x, table, *early)
+        cost_estimate=takes(6.5),
+    )(core, x, table, *early)
 
 
 def call_attend(counts, heads):
@@ -490,6 +605,7 @@
             like(images, 2, 8 * tokens, dtype=jnp.float32),
         ],
         compiler_params=params(),
+        cost_estimate=takes(14.3),
     )(counts, heads)
     return out.reshape(8, images * tokens, 128), lse
 
@@ -510,18 +626,18 @@
         out_specs=pl.BlockSpec((8, 1, tokens, 384), lambda i: (0, i, 0, 0)),
         out_shape=like(*heads.shape),
         compiler_params=params(),
+        cost_estimate=takes(16.5),
     )(counts, grads.reshape(8, images, tokens, 128), heads, lse)
     return out.reshape(8, images * tokens, 384)
 
 
 def rear_weight_specs(late):
-    fc1, fc2_proj = late
-    devices, _, width = fc1.shape
-    fc2_rows = fc2_proj.shape[1] - SLAB
-    steps = fc1.shape[1] // SLAB
+    devices, owned, width = late.shape
+    fc2_rows = (owned - SLAB) // 2
+    steps = fc2_rows // SLAB
     return steps, [
-        pl.BlockSpec((devices, SLAB, width), lambda j: (0, fc2_rows // SLAB, 0)),
-        pl.BlockSpec((devices, SLAB, width), lambda j: (0, j, 0)),
+        pl.BlockSpec((devices, SLAB, width), lambda j: (0, 2 * steps, 0)),
+        pl.BlockSpec((devices, SLAB, width), lambda j: (0, steps + j, 0)),
         pl.BlockSpec((devices // steps, fc2_rows, width), lambda j: (j, 0, 0)),
     ]
 
@@ -538,7 +654,7 @@
     return pl.pallas_call(
         functools.partial(rear_kernel, keep),
         grid=(steps,),
-        in_specs=[whole_block(x), whole_block(attn), whole_block(table)] + weight_specs,
+        in_specs=[whole_block(member) for member in (x, attn, table)] + weight_specs,
         out_specs=out_specs,
         out_shape=out_shape,
         scratch_shapes=[
@@ -547,15 +663,17 @@
             pltpu.VMEM((rows, width), jnp.float32),
         ],
         compiler_params=params(),
-    )(x, attn, table, late[1], late[0], late[1])
+        cost_estimate=takes(13),
+    )(x, attn, table, late, late, late)
 
 
 def call_rear_back(keep, grad, x, branch, hidden, mlp, table, late):
     rows, width = x.shape
     steps, weight_specs = rear_weight_specs(late)
     column = pl.BlockSpec((rows, width), lambda j: (0, j))
-    out_shape = [like(8, rows, 128), like(rows, width, dtype=jnp.float32)]
-    out_specs = [pl.BlockSpec((8, rows, 128), lambda j: (0, 0, 0)), whole_block(x)]
+    attn_grad = like(8, rows, 128)
+    out_shape = [attn_grad, like(rows, width, dtype=jnp.float32)]
+    out_specs = [whole_block(attn_grad), whole_block(x)]
     if keep:
         wide = like(rows, steps * width)
         out_shape += [like(rows, width), wide, wide, like(rows, width), like(rows, width)]
@@ -581,12 +699,12 @@
             pltpu.VMEM((rows, width), jnp.float32),
         ],
         compiler_params=params(),
-    )(grad, x, branch, hidden, mlp, table, late[1], late[0], late[1])
-
-
-def call_front_back(keep, grad_qkv, grad_middle, x, table, early):
+        cost_estimate=takes(16),
+    )(grad, x, branch, hidden, mlp, table, late, late, late)
+
+
+def call_front_back(keep, core, grad_qkv, grad_middle, x, table, early):
     rows, width = x.shape
-    devices = early[0].shape[0]
     out_shape, out_specs = [like(rows, width)], [whole_block(x)]
     if keep:
         out_shape += [like(*table.shape, dtype=jnp.float32)]
@@ -594,50 +712,46 @@
     return pl.pallas_call(
         functools.partial(front_back_kernel, keep),
         grid=(1,),
-        in_specs=[
-            whole_block(grad_qkv),
-            whole_block(grad_middle),
-            whole_block(x),
-            whole_block(table),
-            whole_block(early[0]),
-            pl.BlockSpec((devices, SLAB, width), lambda i: (0, 0, 0)),
-        ],
+        in_specs=[SCALARS]
+        + [whole_block(member) for member in (grad_qkv, grad_middle, x, table)]
+        + early_specs(early),
         out_specs=out_specs,
         out_shape=out_shape,
         compiler_params=params(),
-    )(grad_qkv, grad_middle, x, table, *early)
-
-
-def call_mlp_weights(core, normed, hidden_low, active, mlp_low, late):
+        cost_estimate=takes(7),
+    )(core, grad_qkv, grad_middle, x, table, *early)
+
+
+def call_mlp_weights(core, normed, hidden_low, active, mlp_low, attn, branch_low, devices, owned):
     rows, width = normed.shape
-    chips = late[0].shape[0] // 2
-    steps = late[0].shape[1] // SLAB
-    owned = late[0].shape[1]
+    steps = owned // SLAB
+    half = width // 2
     column = pl.BlockSpec((rows, width), lambda j: (0, j))
-    fc1_spec = pl.BlockSpec((chips, SLAB, width), lambda j: (0, j, 0))
-    fc2_spec = pl.BlockSpec((chips // steps, owned, width), lambda j: (j, 0, 0))
+    fc1_spec = pl.BlockSpec((devices, SLAB, half), lambda j: (0, j, 0))
+    fc2_spec = pl.BlockSpec((devices // steps, owned, half), lambda j: (j, 0, 0))
+    proj_spec = pl.BlockSpec((devices, SLAB, half), lambda j: (0, 0, 0))
     return pl.pallas_call(
         mlp_weights_kernel,
         grid=(steps,),
-        in_specs=[SCALARS, whole_block(normed), column, column, whole_block(mlp_low)],
-        out_specs=[fc1_spec, fc1_spec, fc2_spec, fc2_spec],
-        out_shape=[like(chips, owned, width)] * 4,
+        in_specs=[SCALARS, whole_block(normed), column, column]
+        + [whole_block(member) for member in (mlp_low, attn, branch_low)],
+        out_specs=[fc1_spec, fc1_spec, fc2_spec, fc2_spec, proj_spec, proj_spec],
+        out_shape=[like(devices, owned, half)] * 4 + [like(devices, SLAB, half)] * 2,
         compiler_params=params(),
-    )(core, normed, hidden_low, active, mlp_low)
-
-
-def call_attn_weights(core, x, table, grad_qkv, attn, branch_low, small):
-    width = x.shape[1]
-    chips = small.shape[0] // 2
-    first, second = like(chips, 2 * SLAB, width), like(chips, 3 * SLAB, width)
-    operands = (x, table, grad_qkv, attn, branch_low, small)
+        cost_estimate=takes(11),
+    )(core, normed, hidden_low, active, mlp_low, attn, branch_low)
+
+
+def call_attn_weights(kernel, core, devices, *operands):
+    shape = like(devices, 2 * SLAB, operands[0].shape[1] // 2)
     return pl.pallas_call(
-        attn_weights_kernel,
+        kernel,
         grid=(1,),
         in_specs=[SCALARS] + [whole_block(operand) for operand in operands],
-        out_specs=[whole_block(shape) for shape in (first, first, second, second)],
-        out_shape=[first, first, second, second],
+        out_specs=[whole_block(shape)] * 2,
+        out_shape=[shape] * 2,
         compiler_params=params(),
+        cost_estimate=takes(4),
     )(core, *operands)
 
 
@@ -645,12 +759,12 @@
     lead = vectors.shape[:-2]
     row = jnp.concatenate([vectors.reshape(lead + (-1,)), hidden_vector], axis=-1)
     return jnp.pad(
-        row[..., None, :], [(0, 0)] * len(lead) + [(0, SLAB - 1), (0, 1024 - row.shape[-1])]
+        row[..., None, :], [(0, 0)] * len(lead) + [(0, SLAB - 1), (0, SMALL_WIDTH - row.shape[-1])]
     )
 
 
 def table_of(slabs):
-    row = slabs[:, 0, :].astype(jnp.float32)
+    row = slabs.astype(jnp.float32)
     vectors = row[:, : HIDDEN_ROW * SLAB].reshape(-1, HIDDEN_ROW, SLAB)
     vectors = vectors.transpose(1, 0, 2).reshape(HIDDEN_ROW, -1)
     start = HIDDEN_ROW * SLAB
@@ -718,67 +832,94 @@
             mlp_scale,
         ]
     )
-    qkv_slabs = column_slabs(qkv_weight[0])
-    early = (
-        spread(qkv_slabs[: 2 * SLAB], "dp"),
-        spread(
-            jnp.concatenate([qkv_slabs[2 * SLAB :], small_slab(vectors, fc1_bias[0])]), "head"
-        ),
-    )
-    late = (
-        spread(column_slabs(fc1_weight[0]), "dp"),
-        spread(jnp.concatenate([fc2_weight[0], proj_weight[0]]), "head"),
-    )
-    table = table_of(early[1][:, SLAB:])
-    devices = early[0].shape[0]
+    late_shard = jnp.concatenate([fc2_weight[0], column_slabs(fc1_weight[0]), proj_weight[0]])
+    late = lax.all_gather(late_shard, ("dp", "head"), axis=0)
+    devices = late.shape[0]
+    small_shard = jnp.pad(
+        small_slab(vectors, fc1_bias[0]), [(0, 0), (0, features - SMALL_WIDTH)]
+    )
+    early_shard = jnp.concatenate([column_slabs(qkv_weight[0]), small_shard])
+    ways = ("dp", "head")
+    chip = spread_chip(early_shard)
+    lanes = [
+        spread_lane(chip[:, :, : 2 * SLAB], "dp"),
+        spread_lane(chip[:, :, 2 * SLAB :], "head"),
+    ]
+    ends = [spread_ends(lane, way) for lane, way in zip(lanes, ways)]
+    spread_parts = [spread_rest(*item) for item in zip(lanes, ends, ways)]
+    early = [part[at] for at in range(2) for part in spread_parts]
+    table = table_of(jnp.where(core == 0, early[1][:, SLAB], early[3][:, SLAB]))
 
     own_images = jnp.where(reversed_order, images[::-1], images).reshape(rows, features)
     counts = jnp.sum(key_mask, axis=1, dtype=jnp.int32)
     counts = jnp.where(reversed_order, counts[::-1], counts)
 
-    def forward(x, keep):
-        heads = to_peers(call_front(x, table, early))
-        attn_heads, lse = call_attend(counts, heads)
-        attn = to_peers(attn_heads)
-        return (heads, lse, attn), call_rear(keep, x, attn, table, late)
-
-    def backward(grad, x, attn_state, rear_state, keep):
-        heads, lse, _ = attn_state
-        _, branch, hidden, mlp = rear_state
-        rear = call_rear_back(keep, grad, x, branch, hidden, mlp, table, late)
-        grad_heads = to_peers(rear[0])
-        grad_qkv = to_peers(call_attend_back(counts, grad_heads, heads, lse))
-        front = call_front_back(keep, grad_qkv, rear[1], x, table, early)
-        return rear, grad_qkv, front
-
-    _, (passed,) = forward(own_images, False)
+    def attention(x):
+        heads = to_peers(call_front(core, x, table, early))
+        attn, lse = call_attend(counts, heads)
+        return heads, lse, to_peers(attn)
+
+    (passed,) = call_rear(False, own_images, attention(own_images)[2], table, late)
     x = jnp.where(section_index == 0, own_images, shifted(passed, 1))
-    attn_state, rear_state = forward(x, True)
+    heads, lse, attn = attention(x)
+    result, *rear_state = call_rear(True, x, attn, table, late)
 
     own_grad = cotangent.reshape(rows, features)
-    _, _, (passed_back,) = backward(own_grad, x, attn_state, rear_state, False)
+    rear = call_rear_back(False, own_grad, x, *rear_state, table, late)
+    grad_qkv = to_peers(call_attend_back(counts, to_peers(rear[0]), heads, lse))
+    (passed_back,) = call_front_back(False, core, grad_qkv, rear[1], x, table, early)
     grad = jnp.where(section_index == 0, shifted(passed_back, -1), own_grad)
-    rear, grad_qkv, (input_grad, front_sums) = backward(grad, x, attn_state, rear_state, True)
-    _, _, mlp_low, hidden_low, active, normed, branch_low, rear_sums = rear
-
-    fc1_mine, fc1_other, fc2_mine, fc2_other = call_mlp_weights(
-        core, normed, hidden_low, active, mlp_low, late
-    )
-    fc1_grad = collect(fc1_mine, fc1_other, "dp")
-    fc2_grad = collect(fc2_mine, fc2_other, "head")
+
+    rear = call_rear_back(True, grad, x, *rear_state, table, late)
+    grad_attn, grad_middle, mlp_low, hidden_low, active, normed, branch_low, rear_sums = rear
+    fc1_mine, fc1_other, fc2_mine, fc2_other, proj_mine, proj_other = call_mlp_weights(
+        core, normed, hidden_low, active, mlp_low, attn, branch_low, devices, 4 * SLAB
+    )
+    grad_heads = after(to_peers(grad_attn), fc1_mine)
+    mlp_terms = [
+        core_sum(fc1_mine, fc1_other),
+        jnp.concatenate(
+            [core_sum(fc2_mine, fc2_other), core_sum(proj_mine, proj_other)], axis=4
+        ),
+    ]
+    grad_qkv = to_peers(call_attend_back(counts, grad_heads, heads, lse))
+    grad_qkv = after(grad_qkv, *mlp_terms)
+    mlp_halves = [ring_halves(terms, way) for terms, way in zip(mlp_terms, ways)]
+    mlp_terms = [ring_rest(*item) for item in zip(mlp_terms, mlp_halves, ways)]
+
+    attn_parts = call_attn_weights(query_key_weights_kernel, core, devices, x, table, grad_qkv)
+    input_grad, front_sums = call_front_back(
+        True, core, after(grad_qkv, attn_parts, mlp_halves), grad_middle, x, table, early
+    )
     small = slabs_of(rear_sums + front_sums, devices)
-    first_mine, first_other, second_mine, second_other = call_attn_weights(
-        core, x, table, grad_qkv, attn_state[2], branch_low, small
-    )
-    first_grad = collect(first_mine, first_other, "dp")
-    second_grad = collect(second_mine, second_other, "head")
-    qkv_grad = from_column_slabs(jnp.concatenate([first_grad, second_grad[:SLAB]]))
-    proj_grad = second_grad[SLAB : 2 * SLAB]
-    row = second_grad[2 * SLAB]
+    value_parts = call_attn_weights(
+        value_weights_kernel, core, devices, x, table, grad_qkv, small
+    )
+    attn_terms = [core_sum(*attn_parts), core_sum(*value_parts)]
+    attn_terms = [
+        ring_rest(terms, ring_halves(terms, way), way) for terms, way in zip(attn_terms, ways)
+    ]
+    ring_sums = [
+        second_ring(terms, way)
+        for terms, way in zip(mlp_terms + attn_terms, ways + ways)
+    ]
+    shard_grad = collect_rest(jnp.concatenate(ring_sums, axis=2))
+    fc1_grad, fc2_grad, proj_grad, qkv_grad, small_row = (
+        shard_grad[start:stop]
+        for start, stop in (
+            (0, 4 * SLAB),
+            (4 * SLAB, 8 * SLAB),
+            (8 * SLAB, 9 * SLAB),
+            (9 * SLAB, 12 * SLAB),
+            (12 * SLAB, 12 * SLAB + 1),
+        )
+    )
+    qkv_grad = from_column_slabs(qkv_grad)
+    row = small_row[0]
     small_grads = row[: HIDDEN_ROW * SLAB].reshape(HIDDEN_ROW, SLAB)
     fc1_bias_grad = row[HIDDEN_ROW * SLAB : HIDDEN_ROW * SLAB + 64]
 
-    layer_out = rear_state[0].reshape(images.shape)
+    layer_out = result.reshape(images.shape)
     input_grad = input_grad.reshape(images.shape)
     input_grad = jnp.where(
         (section_index == 0) & reversed_order, input_grad[::-1], input_grad

time: 732 us -> 634 us (0.87)
  waiting for transfers between devices: 236 us -> 153 us
  local copies, waits for them, and re-layouts: 76 us -> 41.2 us
  other arithmetic: 30.4 us -> 47.6 us
  between operations: 3.28 us -> 16.4 us
  starting transfers between devices: 116 us -> 103 us
    ppermute x48 -> x42, waiting for transfers between devices: 190 us -> 76.6 us  [hop(): lax.ppermute(block, axis, [(i, (i + 2 * places) % size) for i in range(si...]
    dynamic_update_slice x44 -> x18, local copies, waits for them, and re-layouts: 42.4 us -> 13.7 us  [the longest x5 6.07 us: spread_rest(): near = lax.dynamic_update_slice(near, block[None], (source, at, 0) + zeros)]
    all_to_all x3, waiting for transfers between devices: 11 us -> 39.1 us  [to_peers(): lax.all_to_all(blocks, 'head', split_axis=0, concat_axis=0, tiled=True)]
    broadcast_in_dim x6 -> x0, local copies, waits for them, and re-layouts: 11 us -> none  [the longest x2 9.59 us: spread(): whole = jnp.zeros((x_size, 2, y_size, 2) + shard.shape, shard.dtype)]
    all_to_all x3, starting transfers between devices: 21.6 us -> 12.4 us  [to_peers(): lax.all_to_all(blocks, 'head', split_axis=0, concat_axis=0, tiled=True)]
    convert_element_type x9 -> x11, other arithmetic: 18.6 us -> 25.7 us  [the longest x5 20.8 us: core_sum(): total.astype(jnp.bfloat16).reshape((x_size, 2, y_size, 2) + mine.shape[1:])]
    ppermute x28 -> x11, starting transfers between devices: 36.2 us -> 31.3 us  [swap(): return lax.ppermute(block, axis, [(i, i ^ 1) for i in range(size)])]
    ppermute x48 -> x42, starting transfers between devices: 53.5 us -> 56.4 us  [hop(): lax.ppermute(block, axis, [(i, (i + 2 * places) % size) for i in range(si...]
  transfers between devices with their start and end apart: 81 -> 59, of which waited for: 33 -> 24; matrix products, arithmetic and copies ran while one was open for 13% -> 11% of each run, Pallas kernels for 6% -> 9%
where the time goes in v2:
time: 634 us; the launch traced here: 625 us
  Pallas kernels  166 us (26%)
  waiting for transfers between devices  153 us (24%)
  starting transfers between devices  103 us (16%)
  blocking collectives  97.7 us (15%)
  other arithmetic  47.6 us (8%)
  local copies, waits for them, and re-layouts  41.2 us (6%)
  between operations  16.4 us (3%)
    all_to_all x5, blocking collectives, to_peers(): lax.all_to_all(blocks, 'head', split_axis=0, concat_axis=0, tiled=True)  97.7 us
    ppermute x42, waiting for transfers between devices, hop(): lax.ppermute(block, axis, [(i, (i + 2 * places) % size) for i in range(si...  76.6 us
    ppermute x42, starting transfers between devices, hop(): lax.ppermute(block, axis, [(i, (i + 2 * places) % size) for i in range(si...  56.4 us
    all_to_all x3, waiting for transfers between devices, to_peers(): lax.all_to_all(blocks, 'head', split_axis=0, concat_axis=0, tiled=True)  39.1 us
    pallas_call x2, Pallas kernels, call_attend_back(): pl.pallas_call(attend_back_kernel, grid=(images,), in_specs=[SCALARS, pl....  33.2 us
    ppermute x11, starting transfers between devices, swap(): return lax.ppermute(block, axis, [(i, i ^ 1) for i in range(size)])  31.3 us
    pallas_call x2, Pallas kernels, call_rear_back(): pl.pallas_call(functools.partial(rear_back_kernel, keep), grid=(steps,),...  30.6 us
    pallas_call x2, Pallas kernels, call_attend(): pl.pallas_call(attend_kernel, grid=(images,), in_specs=[SCALARS, pl.Block...  28.9 us
  transfers between devices with their start and end apart: 59, of which 24 were waited for; matrix products, arithmetic and copies ran while one was open for 11% of the time, Pallas kernels for 9%

profile of v2, /device:TPU:1, one launch (start us, length us, event | category | flops | bytes accessed | tf_op | source)
XLA Modules:
  0.0 625.2 jit_solution(2355968692882616006)
XLA Ops:
  15.9 3.8 collective-permute-start.1
  19.6 3.6 collective-permute-done.1
  48.2 3.4 collective-permute-done.5
  59.8 3.4 collective-permute-start.16
  69.3 7.9 %collective-permute-start.9 = (bf16[64,32,512]{2,1,0:T(8,128)(2,1)S(1)}, bf16[64,32,512]{2,1,0:T(8,128)(2,1)S(1)}, u32[]{:S(2)}, u32[]{:S(2)}) collective-permute-start(bf16[64,32,512]{2,1,0:T(8,128)(2,1)S(1)} %bitcast.304), channel_id=1, source_target_pairs={{0,1},{1,0},{2,3},{3,2},{4,5},{5,4},{6,7},{7,6},{8,9},{9,8},{10,11... | collective-permute-start | bytes 6291464 | tf_op jit(solution)/shard_map/ppermute | solution.py:44
  87.3 6.2 shard_map.318
  93.6 4.2 all-to-all-start
  98.5 25.8 %all-to-all-done = bf16[8,256,384]{2,1,0:T(8,128)(2,1)S(1)} async-done(((bf16[8,256,384]{2,1,0:T(8,128)(2,1)}), bf16[8,256,384]{2,1,0:T(8,128)(2,1)S(1)}, u32[]{:S(2)}, u32[]{:S(2)}) %all-to-all-start) | async-done | bytes 1572896 | tf_op jit(solution)/shard_map/all_to_all | solution.py:191
  125.5 14.6 %shard_map.319 = (bf16[8,2,128,128]{3,2,1,0:T(8,128)(2,1)}, f32[2,2,1024]{2,1,0:T(2,128)}) custom-call(s32[2]{0:T(128)} %broadcast_select_fusion.5.count_ref, bf16[8,2,128,384]{3,2,1,0:T(8,128)(2,1)} %bitcast.314), custom_call_target="tpu_custom_call" | custom-call | flops 16444999680 | bytes 42900000 | tf_op jit(solution)/shard_map/pallas_call | solution.py:595
  140.1 15.1 %all_to_all.40.attn_ref = bf16[8,256,128]{2,1,0:T(8,128)(2,1)} all-to-all(bf16[8,256,128]{2,1,0:T(8,128)(2,1)} %bitcast.323), channel_id=1, replica_groups=mesh['section'=2,'dp'=8,'head'=8] {'head'}, dimensions={0} | all-to-all | bytes 1048576 | tf_op jit(solution)/shard_map/all_to_all | solution.py:191
  155.1 11.9 %shard_map.320 = bf16[256,1024]{1,0:T(8,128)(2,1)} custom-call(bf16[256,1024]{1,0:T(8,128)(2,1)} %bitcast.303, bf16[8,256,128]{2,1,0:T(8,128)(2,1)} %all_to_all.40.attn_ref, f32[16,1024]{1,0:T(8,128)} %select_maximum_fusion.table_ref, bf16[64,144,1024]{2,1,0:T(8,128)(2,1)} %bitcast.273, bf16[64,144,1024]{2,1,0:T(8,128)(2,1)} %bitcast.274, ...), custom_call_target="tpu_custom_call" | custom-call | flops 14949999616 | bytes 39000000 | tf_op jit(solution)/shard_map/pallas_call | solution.py:654
  169.1 10.4 %collective-permute-done.18 = bf16[256,1024]{1,0:T(8,128)(2,1)S(1)} collective-permute-done((bf16[256,1024]{1,0:T(8,128)(2,1)}, bf16[256,1024]{1,0:T(8,128)(2,1)S(1)}, u32[]{:S(2)}, u32[]{:S(2)}) %collective-permute-start.18) | collective-permute-done | bytes 524320 | tf_op jit(solution)/shard_map/ppermute | solution.py:197
  180.5 6.2 shard_map.321
  186.7 27.4 %all_to_all.41 = bf16[8,256,384]{2,1,0:T(8,128)(2,1)} all-to-all(bf16[8,256,384]{2,1,0:T(8,128)(2,1)} %shard_map.321), channel_id=1, replica_groups=mesh['section'=2,'dp'=8,'head'=8] {'head'}, dimensions={0} | all-to-all | bytes 3145728 | tf_op jit(solution)/shard_map/all_to_all | solution.py:191
  214.1 14.4 %shard_map.322 = (bf16[8,2,128,128]{3,2,1,0:T(8,128)(2,1)}, f32[2,2,1024]{2,1,0:T(2,128)}) custom-call(s32[2]{0:T(128)} %broadcast_select_fusion.5.count_ref, bf16[8,2,128,384]{3,2,1,0:T(8,128)(2,1)} %bitcast.310), custom_call_target="tpu_custom_call" | custom-call | flops 16444999680 | bytes 42900000 | tf_op jit(solution)/shard_map/pallas_call | solution.py:595
  228.4 14.5 %all_to_all.42.attn_ref = bf16[8,256,128]{2,1,0:T(8,128)(2,1)} all-to-all(bf16[8,256,128]{2,1,0:T(8,128)(2,1)} %bitcast.324), channel_id=1, replica_groups=mesh['section'=2,'dp'=8,'head'=8] {'head'}, dimensions={0} | all-to-all | bytes 1048576 | tf_op jit(solution)/shard_map/all_to_all | solution.py:191
  242.9 13.5 %shard_map.323 = (bf16[256,1024]{1,0:T(8,128)(2,1)}, f32[256,1024]{1,0:T(8,128)}, f32[256,4096]{1,0:T(8,128)}, f32[256,1024]{1,0:T(8,128)}) custom-call(bf16[256,1024]{1,0:T(8,128)(2,1)} %broadcast_select_fusion.1.x_ref, bf16[8,256,128]{2,1,0:T(8,128)(2,1)} %all_to_all.42.attn_ref, f32[16,1024]{1,0:T(8,128)} %select_maximum_fusion.table_ref, ...), custom_call_target="tpu_custom_call" | custom-call | flops 14949999616 | bytes 39000000 | tf_op jit(solution)/shard_map/pallas_call | solution.py:654
  256.5 14.1 %shard_map.324 = (bf16[8,256,128]{2,1,0:T(8,128)(2,1)}, f32[256,1024]{1,0:T(8,128)}) custom-call(bf16[256,1024]{1,0:T(8,128)(2,1)} %bitcast.321, bf16[256,1024]{1,0:T(8,128)(2,1)} %broadcast_select_fusion.1.x_ref, f32[256,1024]{1,0:T(8,128)} %get-tuple-element.52.branch_ref, f32[256,4096]{1,0:T(8,128)} %get-tuple-element.53.hidden_ref, ...), custom_call_target="tpu_custom_call" | custom-call | flops 18400000000 | bytes 48000000 | tf_op jit(solution)/shard_map/pallas_call | solution.py:683
  270.6 14.7 %all_to_all.43 = bf16[8,256,128]{2,1,0:T(8,128)(2,1)} all-to-all(bf16[8,256,128]{2,1,0:T(8,128)(2,1)} %get-tuple-element.55), channel_id=1, replica_groups=mesh['section'=2,'dp'=8,'head'=8] {'head'}, dimensions={0} | all-to-all | bytes 1048576 | tf_op jit(solution)/shard_map/all_to_all | solution.py:191
  285.3 16.6 %shard_map.325 = bf16[8,2,128,384]{3,2,1,0:T(8,128)(2,1)} custom-call(s32[2]{0:T(128)} %broadcast_select_fusion.5.count_ref, bf16[8,2,128,128]{3,2,1,0:T(8,128)(2,1)} %bitcast.325, bf16[8,2,128,384]{3,2,1,0:T(8,128)(2,1)} %bitcast.311, f32[2,2,1024]{2,1,0:T(2,128)} %get-tuple-element.56.lse_ref), custom_call_target="tpu_custom_call" | custom-call | flops 18975000576 | bytes 49500000 | tf_op jit(solution)/shard_map/pallas_call | solution.py:617
  301.9 26.1 %all_to_all.44.grad_ref = bf16[8,256,384]{2,1,0:T(8,128)(2,1)} all-to-all(bf16[8,256,384]{2,1,0:T(8,128)(2,1)} %bitcast.315), channel_id=1, replica_groups=mesh['section'=2,'dp'=8,'head'=8] {'head'}, dimensions={0} | all-to-all | bytes 3145728 | tf_op jit(solution)/shard_map/all_to_all | solution.py:191
  327.9 6.7 %shard_map.326 = bf16[256,1024]{1,0:T(8,128)(2,1)} custom-call(s32[1]{0:T(128)} %bitcast.2.core_ref, bf16[8,256,384]{2,1,0:T(8,128)(2,1)} %all_to_all.44.grad_ref, f32[256,1024]{1,0:T(8,128)} %get-tuple-element.57.middle_grad_ref, bf16[256,1024]{1,0:T(8,128)(2,1)} %broadcast_select_fusion.1.x_ref, f32[16,1024]{1,0:T(8,128)} %select_maximum_fusion.table_ref, ...), custom_call_target="tpu_custom_call" | custom-call | flops 8049999872 | bytes 21000000 | tf_op jit(solution)/shard_map/pallas_call | solution.py:712
  335.9 13.2 %collective-permute-done.19 = bf16[256,1024]{1,0:T(8,128)(2,1)S(1)} collective-permute-done((bf16[256,1024]{1,0:T(8,128)(2,1)}, bf16[256,1024]{1,0:T(8,128)(2,1)S(1)}, u32[]{:S(2)}, u32[]{:S(2)}) %collective-permute-start.19) | collective-permute-done | bytes 524320 | tf_op jit(solution)/shard_map/ppermute | solution.py:197
  350.0 16.5 %shard_map.327 = (bf16[8,256,128]{2,1,0:T(8,128)(2,1)}, f32[256,1024]{1,0:T(8,128)}, bf16[256,1024]{1,0:T(8,128)(2,1)}, bf16[256,4096]{1,0:T(8,128)(2,1)}, bf16[...) custom-call(bf16[256,1024]{1,0:T(8,128)(2,1)} %broadcast_select_fusion.grad_re, ...), custom_call_target="tpu_custom_call" | custom-call | flops 18400000000 | bytes 48000000 | tf_op jit(solution)/shard_map/pallas_call | solution.py:683
  366.6 11.8 %shard_map.328 = (bf16[64,64,512]{2,1,0:T(8,128)(2,1)}, bf16[64,64,512]{2,1,0:T(8,128)(2,1)}, bf16[64,64,512]{2,1,0:T(8,128)(2,1)}, bf16[64,64,512]{2,1,0:T(8,12...) custom-call(s32[1]{0:T(128)} %bitcast.2.core_ref, bf16[256,1024]{1,0:T(8,128)(2,1)} %get-tuple-element.59.normed_ref, ...), custom_call_target="tpu_custom_call" | custom-call | flops 12650000384 | bytes 33000000 | tf_op jit(solution)/shard_map/pallas_call | solution.py:733
  380.5 3.8 all-to-all-start.6
  385.0 8.8 %all-to-all-done.6 = bf16[8,256,128]{2,1,0:T(8,128)(2,1)S(1)} async-done(((bf16[8,256,128]{2,1,0:T(8,128)(2,1)}), bf16[8,256,128]{2,1,0:T(8,128)(2,1)S(1)}, u32[]{:S(2)}, u32[]{:S(2)}) %all-to-all-start.6) | async-done | bytes 524320 | tf_op jit(solution)/shard_map/all_to_all | solution.py:191
  394.7 16.6 %shard_map.329 = bf16[8,2,128,384]{3,2,1,0:T(8,128)(2,1)} custom-call(s32[2]{0:T(128)} %broadcast_select_fusion.5.count_ref, bf16[8,2,128,128]{3,2,1,0:T(8,128)(2,1)} %bitcast.322, bf16[8,2,128,384]{3,2,1,0:T(8,128)(2,1)} %bitcast.312, f32[2,2,1024]{2,1,0:T(2,128)} %get-tuple-element.56.lse_ref), custom_call_target="tpu_custom_call" | custom-call | flops 18975000576 | bytes 49500000 | tf_op jit(solution)/shard_map/pallas_call | solution.py:617
  411.3 4.3 all-to-all-start.7
  418.6 7.5 %add_convert_fusion = bf16[64,64,512]{2,1,0:T(8,128)(2,1)} fusion(bf16[64,64,512]{2,1,0:T(8,128)(2,1)} %collective-permute-done.21, bf16[64,64,512]{2,1,0:T(8,128)(2,1)} %get-tuple-element.67), kind=kLoop, calls=%fused_computation | loop fusion | flops 8388608 | bytes 12582912 | tf_op jit(solution)/shard_map/convert_element_type | solution.py:142
  426.1 5.8 add_convert_fusion.1
  431.9 4.5 all-to-all-done.7.grad_ref
  442.9 5.0 shard_map.330
  461.5 4.4 collective-permute-done.25
  465.8 7.0 %shard_map.331 = (bf16[256,1024]{1,0:T(8,128)(2,1)}, f32[16,1024]{1,0:T(8,128)}) custom-call(s32[1]{0:T(128)} %bitcast.2.core_ref, bf16[8,256,384]{2,1,0:T(8,128)(2,1)} %copy-done.8, f32[256,1024]{1,0:T(8,128)} %get-tuple-element.75.middle_grad_ref, bf16[256,1024]{1,0:T(8,128)(2,1)} %broadcast_select_fusion.1.x_ref, ...), custom_call_target="tpu_custom_call" | custom-call | flops 8049999872 | bytes 21000000 | tf_op jit(solution)/shard_map/pallas_call | solution.py:712
  475.5 4.9 shard_map.332
  496.2 29.7 %collective-permute-done.30 = bf16[2,2,64,512]{3,2,1,0:T(8,128)(2,1)S(1)} collective-permute-done((bf16[2,2,64,512]{3,2,1,0:T(8,128)(2,1)S(1)}, bf16[2,2,64,512]{3,2,1,0:T(8,128)(2,1)S(1)}, u32[]{:S(2)}, u32[]{:S(2)}) %collective-permute-start.30) | collective-permute-done | bytes 262176 | tf_op jit(solution)/shard_map/ppermute | solution.py:39
  526.6 3.6 collective-permute-start.29
  530.2 5.2 collective-permute-done.29
  549.2 14.0 %collective-permute-done.38 = bf16[1,4,2,32,512]{4,3,2,1,0:T(8,128)(2,1)S(1)} collective-permute-done((bf16[1,4,2,32,512]{4,3,2,1,0:T(8,128)(2,1)S(1)}, bf16[1,4,2,32,512]{4,3,2,1,0:T(8,128)(2,1)S(1)}, u32[]{:S(2)}, u32[]{:S(2)}) %collective-permute-start.38) | collective-permute-done | bytes 262176 | tf_op jit(solution)/shard_map/ppermute | solution.py:39
  564.7 4.9 collective-permute-done.48
  573.9 6.8 %collective-permute-done.39 = bf16[2,4,2,32,512]{4,3,2,1,0:T(8,128)(2,1)S(1)} collective-permute-done((bf16[2,4,2,32,512]{4,3,2,1,0:T(8,128)(2,1)S(1)}, bf16[2,4,2,32,512]{4,3,2,1,0:T(8,128)(2,1)S(1)}, u32[]{:S(2)}, u32[]{:S(2)}) %collective-permute-start.39) | collective-permute-done | bytes 524320 | tf_op jit(solution)/shard_map/ppermute | solution.py:39
  581.0 4.0 collective-permute-start.43
  585.3 3.4 collective-permute-start.52
  590.8 3.3 collective-permute-done.51
  595.8 5.4 collective-permute-start.53
  601.2 5.5 collective-permute-done.53
  606.9 5.4 collective-permute-start.54
  (251 shorter events, 139.2 us)
Async XLA Ops:
  7.2 147.9 %all-gather.3.cloned.1.call-start = ((), (), s32[]{:S(2)}) async-start(), calls=%async_computation.8 | async-start | bytes 19169280 | tf_op jit(solution)/shard_map/all_gather | solution.py:836
  24.0 10.1 %collective-permute-start.2 = (bf16[2,2,32,512]{3,2,1,0:T(8,128)(2,1)}, bf16[2,2,32,512]{3,2,1,0:T(8,128)(2,1)S(1)}, u32[]{:S(2)}, u32[]{:S(2)}) collective-permute-start(bf16[2,2,32,512]{3,2,1,0:T(8,128)(2,1)} %get-tuple-element.126.given_ref), channel_id=1, source_target_pairs={{0,16},{8,24},{16,32},{24,40},{32,48},{40,56},{48,0},{56,8},{1,17}... | collective-permute-start | bytes 393224 | tf_op jit(solution)/shard_map/ppermute | solution.py:39
  25.2 11.3 %collective-permute-start.3 = (bf16[2,2,32,512]{3,2,1,0:T(8,128)(2,1)}, bf16[2,2,32,512]{3,2,1,0:T(8,128)(2,1)S(1)}, u32[]{:S(2)}, u32[]{:S(2)}) collective-permute-start(bf16[2,2,32,512]{3,2,1,0:T(8,128)(2,1)} %get-tuple-element.126.given_ref), channel_id=1, source_target_pairs={{0,32},{8,40},{16,48},{24,56},{32,0},{40,8},{48,16},{56,24},{1,33}... | collective-permute-start | bytes 393224 | tf_op jit(solution)/shard_map/ppermute | solution.py:39
  27.6 9.5 %collective-permute-start.4 = (bf16[2,2,32,512]{3,2,1,0:T(8,128)(2,1)}, bf16[2,2,32,512]{3,2,1,0:T(8,128)(2,1)S(1)}, u32[]{:S(2)}, u32[]{:S(2)}) collective-permute-start(bf16[2,2,32,512]{3,2,1,0:T(8,128)(2,1)} %get-tuple-element.126.given_ref), channel_id=1, source_target_pairs={{0,48},{8,56},{16,0},{24,8},{32,16},{40,24},{48,32},{56,40},{1,49}... | collective-permute-start | bytes 393224 | tf_op jit(solution)/shard_map/ppermute | solution.py:39
  28.8 12.0 %collective-permute-start.10 = (bf16[2,2,32,512]{3,2,1,0:T(8,128)(2,1)}, bf16[2,2,32,512]{3,2,1,0:T(8,128)(2,1)S(1)}, u32[]{:S(2)}, u32[]{:S(2)}) collective-permute-start(bf16[2,2,32,512]{3,2,1,0:T(8,128)(2,1)} %get-tuple-element.125.given_ref), channel_id=1, source_target_pairs={{0,2},{1,3},{2,4},{3,5},{4,6},{5,7},{6,0},{7,1},{8,10},{9,11},{10,... | collective-permute-start | bytes 393224 | tf_op jit(solution)/shard_map/ppermute | solution.py:39
  30.1 11.4 %collective-permute-start.11 = (bf16[2,2,32,512]{3,2,1,0:T(8,128)(2,1)}, bf16[2,2,32,512]{3,2,1,0:T(8,128)(2,1)S(1)}, u32[]{:S(2)}, u32[]{:S(2)}) collective-permute-start(bf16[2,2,32,512]{3,2,1,0:T(8,128)(2,1)} %get-tuple-element.125.given_ref), channel_id=1, source_target_pairs={{0,4},{1,5},{2,6},{3,7},{4,0},{5,1},{6,2},{7,3},{8,12},{9,13},{10,... | collective-permute-start | bytes 393224 | tf_op jit(solution)/shard_map/ppermute | solution.py:39
  37.8 13.7 %collective-permute-start.5 = (bf16[4,2,2,32,512]{4,3,2,1,0:T(8,128)(2,1)}, bf16[4,2,2,32,512]{4,3,2,1,0:T(8,128)(2,1)}, u32[]{:S(2)}, u32[]{:S(2)}) collective-permute-start(bf16[4,2,2,32,512]{4,3,2,1,0:T(8,128)(2,1)} %bitcast_dynamic-update-slice_fusion.14.given_ref), channel_id=1, source_target_pairs={{0,2},{1,3},{2,4},{3,5},{4,6},{5,7},{6,0},{7,1},{8,10},{9,11},{10,... | collective-permute-start | bytes 1572872 | tf_op jit(solution)/shard_map/ppermute | solution.py:39
  39.2 15.2 %collective-permute-start.6 = (bf16[4,2,2,32,512]{4,3,2,1,0:T(8,128)(2,1)}, bf16[4,2,2,32,512]{4,3,2,1,0:T(8,128)(2,1)}, u32[]{:S(2)}, u32[]{:S(2)}) collective-permute-start(bf16[4,2,2,32,512]{4,3,2,1,0:T(8,128)(2,1)} %bitcast_dynamic-update-slice_fusion.14.given_ref), channel_id=1, source_target_pairs={{0,6},{1,7},{2,0},{3,1},{4,2},{5,3},{6,4},{7,5},{8,14},{9,15},{10,... | collective-permute-start | bytes 1572872 | tf_op jit(solution)/shard_map/ppermute | solution.py:39
  42.8 15.0 %collective-permute-start.13 = (bf16[2,4,2,32,512]{4,3,2,1,0:T(8,128)(2,1)}, bf16[2,4,2,32,512]{4,3,2,1,0:T(8,128)(2,1)}, u32[]{:S(2)}, u32[]{:S(2)}) collective-permute-start(bf16[2,4,2,32,512]{4,3,2,1,0:T(8,128)(2,1)} %bitcast_dynamic-update-slice_fusion.13.given_ref), channel_id=1, source_target_pairs={{0,16},{8,24},{16,32},{24,40},{32,48},{40,56},{48,0},{56,8},{1,17}... | collective-permute-start | bytes 1572872 | tf_op jit(solution)/shard_map/ppermute | solution.py:39
  42.8 16.0 %collective-permute-start.14 = (bf16[2,4,2,32,512]{4,3,2,1,0:T(8,128)(2,1)}, bf16[2,4,2,32,512]{4,3,2,1,0:T(8,128)(2,1)}, u32[]{:S(2)}, u32[]{:S(2)}) collective-permute-start(bf16[2,4,2,32,512]{4,3,2,1,0:T(8,128)(2,1)} %bitcast_dynamic-update-slice_fusion.13.given_ref), channel_id=1, source_target_pairs={{0,48},{8,56},{16,0},{24,8},{32,16},{40,24},{48,32},{56,40},{1,49}... | collective-permute-start | bytes 1572872 | tf_op jit(solution)/shard_map/ppermute | solution.py:39
  52.5 16.7 %collective-permute-start.7 = (bf16[2,2,2,32,512]{4,3,2,1,0:T(8,128)(2,1)S(1)}, bf16[2,2,2,32,512]{4,3,2,1,0:T(8,128)(2,1)S(1)}, u32[]{:S(2)}, u32[]{:S(2)}) collective-permute-start(bf16[2,2,2,32,512]{4,3,2,1,0:T(8,128)(2,1)S(1)} %slice.395), channel_id=1, source_target_pairs={{0,2},{1,3},{2,4},{3,5},{4,6},{5,7},{6,0},{7,1},{8,10},{9,11},{10,... | collective-permute-start | bytes 786440 | tf_op jit(solution)/shard_map/ppermute | solution.py:39
  55.4 13.9 %collective-permute-start.8 = (bf16[2,2,2,32,512]{4,3,2,1,0:T(8,128)(2,1)S(1)}, bf16[2,2,2,32,512]{4,3,2,1,0:T(8,128)(2,1)S(1)}, u32[]{:S(2)}, u32[]{:S(2)}) collective-permute-start(bf16[2,2,2,32,512]{4,3,2,1,0:T(8,128)(2,1)S(1)} %slice.396), channel_id=1, source_target_pairs={{0,6},{1,7},{2,0},{3,1},{4,2},{5,3},{6,4},{7,5},{8,14},{9,15},{10,... | collective-permute-start | bytes 786440 | tf_op jit(solution)/shard_map/ppermute | solution.py:39
  58.7 18.5 %collective-permute-start.15 = (bf16[1,4,2,32,512]{4,3,2,1,0:T(8,128)(2,1)S(1)}, bf16[1,4,2,32,512]{4,3,2,1,0:T(8,128)(2,1)S(1)}, u32[]{:S(2)}, u32[]{:S(2)}) collective-permute-start(bf16[1,4,2,32,512]{4,3,2,1,0:T(8,128)(2,1)S(1)} %slice.402), channel_id=1, source_target_pairs={{0,16},{8,24},{16,32},{24,40},{32,48},{40,56},{48,0},{56,8},{1,17}... | collective-permute-start | bytes 786440 | tf_op jit(solution)/shard_map/ppermute | solution.py:39
  59.8 18.1 %collective-permute-start.16 = (bf16[1,4,2,32,512]{4,3,2,1,0:T(8,128)(2,1)S(1)}, bf16[1,4,2,32,512]{4,3,2,1,0:T(8,128)(2,1)S(1)}, u32[]{:S(2)}, u32[]{:S(2)}) collective-permute-start(bf16[1,4,2,32,512]{4,3,2,1,0:T(8,128)(2,1)S(1)} %slice.403), channel_id=1, source_target_pairs={{0,48},{8,56},{16,0},{24,8},{32,16},{40,24},{48,32},{56,40},{1,49}... | collective-permute-start | bytes 786440 | tf_op jit(solution)/shard_map/ppermute | solution.py:39
  69.3 12.4 %collective-permute-start.9 = (bf16[64,32,512]{2,1,0:T(8,128)(2,1)S(1)}, bf16[64,32,512]{2,1,0:T(8,128)(2,1)S(1)}, u32[]{:S(2)}, u32[]{:S(2)}) collective-permute-start(bf16[64,32,512]{2,1,0:T(8,128)(2,1)S(1)} %bitcast.304), channel_id=1, source_target_pairs={{0,1},{1,0},{2,3},{3,2},{4,5},{5,4},{6,7},{7,6},{8,9},{9,8},{10,11... | collective-permute-start | bytes 6291464 | tf_op jit(solution)/shard_map/ppermute | solution.py:44
  78.6 8.7 %collective-permute-start.17 = (bf16[64,32,512]{2,1,0:T(8,128)(2,1)}, bf16[64,32,512]{2,1,0:T(8,128)(2,1)}, u32[]{:S(2)}, u32[]{:S(2)}) collective-permute-start(bf16[64,32,512]{2,1,0:T(8,128)(2,1)} %bitcast.41.qk_mine_ref), channel_id=1, source_target_pairs={{0,1},{1,0},{2,3},{3,2},{4,5},{5,4},{6,7},{7,6},{8,9},{9,8},{10,11... | collective-permute-start | bytes 6291464 | tf_op jit(solution)/shard_map/ppermute | solution.py:44
  93.6 30.7 %all-to-all-start = ((bf16[8,256,384]{2,1,0:T(8,128)(2,1)}), bf16[8,256,384]{2,1,0:T(8,128)(2,1)S(1)}, u32[]{:S(2)}, u32[]{:S(2)}) async-start(bf16[8,256,384]{2,1,0:T(8,128)(2,1)} %shard_map.318), calls=%async_computation | async-start | bytes 3145728 | tf_op jit(solution)/shard_map/all_to_all | solution.py:191
  167.0 12.6 %collective-permute-start.18 = (bf16[256,1024]{1,0:T(8,128)(2,1)}, bf16[256,1024]{1,0:T(8,128)(2,1)S(1)}, u32[]{:S(2)}, u32[]{:S(2)}) collective-permute-start(bf16[256,1024]{1,0:T(8,128)(2,1)} %shard_map.320), channel_id=1, source_target_pairs={{0,64},{1,65},{2,66},{3,67},{4,68},{5,69},{6,70},{7,71},{8,72},{9,... | collective-permute-start | bytes 1572872 | tf_op jit(solution)/shard_map/ppermute | solution.py:197
  334.6 14.5 %collective-permute-start.19 = (bf16[256,1024]{1,0:T(8,128)(2,1)}, bf16[256,1024]{1,0:T(8,128)(2,1)S(1)}, u32[]{:S(2)}, u32[]{:S(2)}) collective-permute-start(bf16[256,1024]{1,0:T(8,128)(2,1)} %shard_map.326), channel_id=1, source_target_pairs={{64,0},{65,1},{66,2},{67,3},{68,4},{69,5},{70,6},{71,7},{72,8},{73... | collective-permute-start | bytes 1572872 | tf_op jit(solution)/shard_map/ppermute | solution.py:197
  378.4 40.2 %collective-permute-start.21 = (bf16[64,64,512]{2,1,0:T(8,128)(2,1)}, bf16[64,64,512]{2,1,0:T(8,128)(2,1)}, u32[]{:S(2)}, u32[]{:S(2)}) collective-permute-start(bf16[64,64,512]{2,1,0:T(8,128)(2,1)} %get-tuple-element.68), channel_id=1, source_target_pairs={{0,1},{1,0},{2,3},{3,2},{4,5},{5,4},{6,7},{7,6},{8,9},{9,8},{10,11... | collective-permute-start | bytes 12582920 | tf_op jit(solution)/shard_map/ppermute | solution.py:44
  380.4 45.6 %collective-permute-start.20 = (bf16[64,64,512]{2,1,0:T(8,128)(2,1)}, bf16[64,64,512]{2,1,0:T(8,128)(2,1)}, u32[]{:S(2)}, u32[]{:S(2)}) collective-permute-start(bf16[64,64,512]{2,1,0:T(8,128)(2,1)} %get-tuple-element.66), channel_id=1, source_target_pairs={{0,1},{1,0},{2,3},{3,2},{4,5},{5,4},{6,7},{7,6},{8,9},{9,8},{10,11... | collective-permute-start | bytes 12582920 | tf_op jit(solution)/shard_map/ppermute | solution.py:44
  380.5 13.3 %all-to-all-start.6 = ((bf16[8,256,128]{2,1,0:T(8,128)(2,1)}), bf16[8,256,128]{2,1,0:T(8,128)(2,1)S(1)}, u32[]{:S(2)}, u32[]{:S(2)}) async-start(bf16[8,256,128]{2,1,0:T(8,128)(2,1)} %get-tuple-element.58), calls=%async_computation.6 | async-start | bytes 1048576 | tf_op jit(solution)/shard_map/all_to_all | solution.py:191
  384.4 31.3 %collective-permute-start.22 = (bf16[64,16,512]{2,1,0:T(8,128)(2,1)}, bf16[64,16,512]{2,1,0:T(8,128)(2,1)S(1)}, u32[]{:S(2)}, u32[]{:S(2)}) collective-permute-start(bf16[64,16,512]{2,1,0:T(8,128)(2,1)} %get-tuple-element.70), channel_id=1, source_target_pairs={{0,1},{1,0},{2,3},{3,2},{4,5},{5,4},{6,7},{7,6},{8,9},{9,8},{10,11... | collective-permute-start | bytes 3145736 | tf_op jit(solution)/shard_map/ppermute | solution.py:44
  411.3 25.1 %all-to-all-start.7 = ((bf16[8,256,384]{2,1,0:T(8,128)(2,1)}), bf16[8,256,384]{2,1,0:T(8,128)(2,1)S(1)}, u32[]{:S(2)}, u32[]{:S(2)}) async-start(bf16[8,256,384]{2,1,0:T(8,128)(2,1)} %bitcast.313), calls=%async_computation.7 | async-start | bytes 3145728 | tf_op jit(solution)/shard_map/all_to_all | solution.py:191
  440.1 18.8 %collective-permute-start.23 = (bf16[1,4,2,64,512]{4,3,2,1,0:T(8,128)(2,1)}, bf16[1,4,2,64,512]{4,3,2,1,0:T(8,128)(2,1)}, u32[]{:S(2)}, u32[]{:S(2)}) collective-permute-start(bf16[1,4,2,64,512]{4,3,2,1,0:T(8,128)(2,1)} %get-tuple-element.88), channel_id=1, source_target_pairs={{0,16},{8,24},{16,32},{24,40},{32,48},{40,56},{48,0},{56,8},{1,17}... | collective-permute-start | bytes 1572872 | tf_op jit(solution)/shard_map/ppermute | solution.py:39
  440.1 14.3 %collective-permute-start.24 = (bf16[1,4,2,64,512]{4,3,2,0,1:T(8,128)(2,1)S(1)}, bf16[1,4,2,64,512]{4,3,2,0,1:T(8,128)(2,1)}, u32[]{:S(2)}, u32[]{:S(2)}) collective-permute-start(bf16[1,4,2,64,512]{4,3,2,0,1:T(8,128)(2,1)S(1)} %get-tuple-element.90), channel_id=1, source_target_pairs={{0,48},{8,56},{16,0},{24,8},{32,16},{40,24},{48,32},{56,40},{1,49}... | collective-permute-start | bytes 1572872 | tf_op jit(solution)/shard_map/ppermute | solution.py:39
  449.6 16.2 %collective-permute-start.25 = (bf16[2,2,2,80,512]{4,3,2,1,0:T(8,128)(2,1)S(1)}, bf16[2,2,2,80,512]{4,3,2,1,0:T(8,128)(2,1)}, u32[]{:S(2)}, u32[]{:S(2)}) collective-permute-start(bf16[2,2,2,80,512]{4,3,2,1,0:T(8,128)(2,1)S(1)} %get-tuple-element.85), channel_id=1, source_target_pairs={{0,2},{1,3},{2,4},{3,5},{4,6},{5,7},{6,0},{7,1},{8,10},{9,11},{10,... | collective-permute-start | bytes 1966088 | tf_op jit(solution)/shard_map/ppermute | solution.py:39
  450.0 15.8 %collective-permute-start.26 = (bf16[2,2,2,80,512]{4,3,2,1,0:T(8,128)(2,1)S(1)}, bf16[2,2,2,80,512]{4,3,2,1,0:T(8,128)(2,1)}, u32[]{:S(2)}, u32[]{:S(2)}) collective-permute-start(bf16[2,2,2,80,512]{4,3,2,1,0:T(8,128)(2,1)S(1)} %get-tuple-element.86), channel_id=1, source_target_pairs={{0,6},{1,7},{2,0},{3,1},{4,2},{5,3},{6,4},{7,5},{8,14},{9,15},{10,... | collective-permute-start | bytes 1966088 | tf_op jit(solution)/shard_map/ppermute | solution.py:39
  452.4 84.3 %collective-permute-start.37 = (bf16[64,32,512]{2,1,0:T(8,128)(2,1)}, bf16[64,32,512]{2,1,0:T(8,128)(2,1)}, u32[]{:S(2)}, u32[]{:S(2)}) collective-permute-start(bf16[64,32,512]{2,1,0:T(8,128)(2,1)} %get-tuple-element.73), channel_id=1, source_target_pairs={{0,1},{1,0},{2,3},{3,2},{4,5},{5,4},{6,7},{7,6},{8,9},{9,8},{10,11... | collective-permute-start | bytes 6291464 | tf_op jit(solution)/shard_map/ppermute | solution.py:44
  456.8 28.0 %collective-permute-start.28 = (bf16[2,4,2,64,512]{4,3,2,0,1:T(8,128)(2,1)}, bf16[2,4,2,64,512]{4,3,2,0,1:T(8,128)(2,1)}, u32[]{:S(2)}, u32[]{:S(2)}) collective-permute-start(bf16[2,4,2,64,512]{4,3,2,0,1:T(8,128)(2,1)} %pad_maximum_fusion.5), channel_id=1, source_target_pairs={{0,48},{8,56},{16,0},{24,8},{32,16},{40,24},{48,32},{56,40},{1,49}... | collective-permute-start | bytes 3145736 | tf_op jit(solution)/shard_map/ppermute | solution.py:39
  461.5 23.8 %collective-permute-start.27 = (bf16[2,4,2,64,512]{4,3,2,1,0:T(8,128)(2,1)}, bf16[2,4,2,64,512]{4,3,2,1,0:T(8,128)(2,1)}, u32[]{:S(2)}, u32[]{:S(2)}) collective-permute-start(bf16[2,4,2,64,512]{4,3,2,1,0:T(8,128)(2,1)} %pad_maximum_fusion.4), channel_id=1, source_target_pairs={{0,16},{8,24},{16,32},{24,40},{32,48},{40,56},{48,0},{56,8},{1,17}... | collective-permute-start | bytes 3145736 | tf_op jit(solution)/shard_map/ppermute | solution.py:39
  480.4 65.1 %collective-permute-start.45 = (bf16[64,32,512]{2,1,0:T(8,128)(2,1)}, bf16[64,32,512]{2,1,0:T(8,128)(2,1)}, u32[]{:S(2)}, u32[]{:S(2)}) collective-permute-start(bf16[64,32,512]{2,1,0:T(8,128)(2,1)} %get-tuple-element.80), channel_id=1, source_target_pairs={{0,1},{1,0},{2,3},{3,2},{4,5},{5,4},{6,7},{7,6},{8,9},{9,8},{10,11... | collective-permute-start | bytes 6291464 | tf_op jit(solution)/shard_map/ppermute | solution.py:44
  491.8 48.6 %collective-permute-start.33 = (bf16[4,2,2,80,512]{4,3,2,1,0:T(8,128)(2,1)}, bf16[4,2,2,80,512]{4,3,2,1,0:T(8,128)(2,1)}, u32[]{:S(2)}, u32[]{:S(2)}) collective-permute-start(bf16[4,2,2,80,512]{4,3,2,1,0:T(8,128)(2,1)} %pad_maximum_fusion.3), channel_id=1, source_target_pairs={{0,6},{1,7},{2,0},{3,1},{4,2},{5,3},{6,4},{7,5},{8,14},{9,15},{10,... | collective-permute-start | bytes 3932168 | tf_op jit(solution)/shard_map/ppermute | solution.py:39
  493.1 47.4 %collective-permute-start.32 = (bf16[4,2,2,80,512]{4,3,2,1,0:T(8,128)(2,1)}, bf16[4,2,2,80,512]{4,3,2,1,0:T(8,128)(2,1)S(1)}, u32[]{:S(2)}, u32[]{:S(2)}) collective-permute-start(bf16[4,2,2,80,512]{4,3,2,1,0:T(8,128)(2,1)} %pad_maximum_fusion.2), channel_id=1, source_target_pairs={{0,2},{1,3},{2,4},{3,5},{4,6},{5,7},{6,0},{7,1},{8,10},{9,11},{10,... | collective-permute-start | bytes 3932168 | tf_op jit(solution)/shard_map/ppermute | solution.py:39
  494.6 31.4 %collective-permute-start.30 = (bf16[2,2,64,512]{3,2,1,0:T(8,128)(2,1)S(1)}, bf16[2,2,64,512]{3,2,1,0:T(8,128)(2,1)S(1)}, u32[]{:S(2)}, u32[]{:S(2)}) collective-permute-start(bf16[2,2,64,512]{3,2,1,0:T(8,128)(2,1)S(1)} %get-tuple-element.106), channel_id=1, source_target_pairs={{0,4},{1,5},{2,6},{3,7},{4,0},{5,1},{6,2},{7,3},{8,12},{9,13},{10,... | collective-permute-start | bytes 786440 | tf_op jit(solution)/shard_map/ppermute | solution.py:39
  526.6 8.8 %collective-permute-start.29 = (bf16[2,2,64,512]{3,2,1,0:T(8,128)(2,1)}, bf16[2,2,64,512]{3,2,1,0:T(8,128)(2,1)}, u32[]{:S(2)}, u32[]{:S(2)}) collective-permute-start(bf16[2,2,64,512]{3,2,1,0:T(8,128)(2,1)} %get-tuple-element.104), channel_id=1, source_target_pairs={{0,2},{1,3},{2,4},{3,5},{4,6},{5,7},{6,0},{7,1},{8,10},{9,11},{10,... | collective-permute-start | bytes 786440 | tf_op jit(solution)/shard_map/ppermute | solution.py:39
  542.5 27.7 %collective-permute-start.36 = (bf16[2,2,80,512]{3,2,1,0:T(8,128)(2,1)S(1)}, bf16[2,2,80,512]{3,2,1,0:T(8,128)(2,1)S(1)}, u32[]{:S(2)}, u32[]{:S(2)}) collective-permute-start(bf16[2,2,80,512]{3,2,1,0:T(8,128)(2,1)S(1)} %get-tuple-element.102), channel_id=1, source_target_pairs={{0,48},{8,56},{16,0},{24,8},{32,16},{40,24},{48,32},{56,40},{1,49}... | collective-permute-start | bytes 983048 | tf_op jit(solution)/shard_map/ppermute | solution.py:39
  542.6 28.9 %collective-permute-start.35 = (bf16[2,2,80,512]{3,2,1,0:T(8,128)(2,1)S(1)}, bf16[2,2,80,512]{3,2,1,0:T(8,128)(2,1)S(1)}, u32[]{:S(2)}, u32[]{:S(2)}) collective-permute-start(bf16[2,2,80,512]{3,2,1,0:T(8,128)(2,1)S(1)} %get-tuple-element.103), channel_id=1, source_target_pairs={{0,32},{8,40},{16,48},{24,56},{32,0},{40,8},{48,16},{56,24},{1,33}... | collective-permute-start | bytes 983048 | tf_op jit(solution)/shard_map/ppermute | solution.py:39
  545.4 26.4 %collective-permute-start.34 = (bf16[2,2,80,512]{3,2,1,0:T(8,128)(2,1)S(1)}, bf16[2,2,80,512]{3,2,1,0:T(8,128)(2,1)S(1)}, u32[]{:S(2)}, u32[]{:S(2)}) collective-permute-start(bf16[2,2,80,512]{3,2,1,0:T(8,128)(2,1)S(1)} %get-tuple-element.101), channel_id=1, source_target_pairs={{0,16},{8,24},{16,32},{24,40},{32,48},{40,56},{48,0},{56,8},{1,17}... | collective-permute-start | bytes 983048 | tf_op jit(solution)/shard_map/ppermute | solution.py:39
  545.4 17.8 %collective-permute-start.38 = (bf16[1,4,2,32,512]{4,3,2,1,0:T(8,128)(2,1)S(1)}, bf16[1,4,2,32,512]{4,3,2,1,0:T(8,128)(2,1)S(1)}, u32[]{:S(2)}, u32[]{:S(2)}) collective-permute-start(bf16[1,4,2,32,512]{4,3,2,1,0:T(8,128)(2,1)S(1)} %get-tuple-element.92), channel_id=1, source_target_pairs={{0,16},{8,24},{16,32},{24,40},{32,48},{40,56},{48,0},{56,8},{1,17}... | collective-permute-start | bytes 786440 | tf_op jit(solution)/shard_map/ppermute | solution.py:39
  548.1 16.6 %collective-permute-start.46 = (bf16[2,2,2,32,512]{4,3,2,1,0:T(8,128)(2,1)S(1)}, bf16[2,2,2,32,512]{4,3,2,1,0:T(8,128)(2,1)S(1)}, u32[]{:S(2)}, u32[]{:S(2)}) collective-permute-start(bf16[2,2,2,32,512]{4,3,2,1,0:T(8,128)(2,1)S(1)} %get-tuple-element.97), channel_id=1, source_target_pairs={{0,2},{1,3},{2,4},{3,5},{4,6},{5,7},{6,0},{7,1},{8,10},{9,11},{10,... | collective-permute-start | bytes 786440 | tf_op jit(solution)/shard_map/ppermute | solution.py:39
  564.6 9.2 %collective-permute-start.41 = (bf16[2,4,2,32,512]{4,3,2,0,1:T(8,128)(2,1)S(1)}, bf16[2,4,2,32,512]{4,3,2,0,1:T(8,128)(2,1)S(1)}, u32[]{:S(2)}, u32[]{:S(2)}) collective-permute-start(bf16[2,4,2,32,512]{4,3,2,0,1:T(8,128)(2,1)S(1)} %pad_maximum_fusion.7), channel_id=1, source_target_pairs={{0,48},{8,56},{16,0},{24,8},{32,16},{40,24},{48,32},{56,40},{1,49}... | collective-permute-start | bytes 1572872 | tf_op jit(solution)/shard_map/ppermute | solution.py:39
  569.7 11.0 %collective-permute-start.39 = (bf16[2,4,2,32,512]{4,3,2,1,0:T(8,128)(2,1)S(1)}, bf16[2,4,2,32,512]{4,3,2,1,0:T(8,128)(2,1)S(1)}, u32[]{:S(2)}, u32[]{:S(2)}) collective-permute-start(bf16[2,4,2,32,512]{4,3,2,1,0:T(8,128)(2,1)S(1)} %pad_maximum_fusion.6), channel_id=1, source_target_pairs={{0,16},{8,24},{16,32},{24,40},{32,48},{40,56},{48,0},{56,8},{1,17}... | collective-permute-start | bytes 1572872 | tf_op jit(solution)/shard_map/ppermute | solution.py:39
  570.2 14.8 %collective-permute-start.49 = (bf16[4,2,2,32,512]{4,3,2,1,0:T(8,128)(2,1)S(1)}, bf16[4,2,2,32,512]{4,3,2,1,0:T(8,128)(2,1)S(1)}, u32[]{:S(2)}, u32[]{:S(2)}) collective-permute-start(bf16[4,2,2,32,512]{4,3,2,1,0:T(8,128)(2,1)S(1)} %pad_maximum_fusion.9), channel_id=1, source_target_pairs={{0,6},{1,7},{2,0},{3,1},{4,2},{5,3},{6,4},{7,5},{8,14},{9,15},{10,... | collective-permute-start | bytes 1572872 | tf_op jit(solution)/shard_map/ppermute | solution.py:39
  571.5 13.5 %collective-permute-start.47 = (bf16[4,2,2,32,512]{4,3,2,1,0:T(8,128)(2,1)S(1)}, bf16[4,2,2,32,512]{4,3,2,1,0:T(8,128)(2,1)S(1)}, u32[]{:S(2)}, u32[]{:S(2)}) collective-permute-start(bf16[4,2,2,32,512]{4,3,2,1,0:T(8,128)(2,1)S(1)} %pad_maximum_fusion.8), channel_id=1, source_target_pairs={{0,2},{1,3},{2,4},{3,5},{4,6},{5,7},{6,0},{7,1},{8,10},{9,11},{10,... | collective-permute-start | bytes 1572872 | tf_op jit(solution)/shard_map/ppermute | solution.py:39
  580.9 8.8 %collective-permute-start.44 = (bf16[2,2,32,512]{3,2,1,0:T(8,128)(2,1)S(1)}, bf16[2,2,32,512]{3,2,1,0:T(8,128)(2,1)S(1)}, u32[]{:S(2)}, u32[]{:S(2)}) collective-permute-start(bf16[2,2,32,512]{3,2,1,0:T(8,128)(2,1)S(1)} %get-tuple-element.120), channel_id=1, source_target_pairs={{0,6},{1,7},{2,0},{3,1},{4,2},{5,3},{6,4},{7,5},{8,14},{9,15},{10,... | collective-permute-start | bytes 393224 | tf_op jit(solution)/shard_map/ppermute | solution.py:39
  581.0 9.4 %collective-permute-start.43 = (bf16[2,2,32,512]{3,2,1,0:T(8,128)(2,1)S(1)}, bf16[2,2,32,512]{3,2,1,0:T(8,128)(2,1)S(1)}, u32[]{:S(2)}, u32[]{:S(2)}) collective-permute-start(bf16[2,2,32,512]{3,2,1,0:T(8,128)(2,1)S(1)} %get-tuple-element.121), channel_id=1, source_target_pairs={{0,4},{1,5},{2,6},{3,7},{4,0},{5,1},{6,2},{7,3},{8,12},{9,13},{10,... | collective-permute-start | bytes 393224 | tf_op jit(solution)/shard_map/ppermute | solution.py:39
  595.8 10.9 %collective-permute-start.53 = (bf16[2,208,512]{2,1,0:T(8,128)(2,1)S(1)}, bf16[2,208,512]{2,1,0:T(8,128)(2,1)S(1)}, u32[]{:S(2)}, u32[]{:S(2)}) collective-permute-start(bf16[2,208,512]{2,1,0:T(8,128)(2,1)S(1)} %fusion.19), channel_id=1, source_target_pairs={{0,8},{8,0},{16,24},{24,16},{32,40},{40,32},{48,56},{56,48},{1,9},... | collective-permute-start | bytes 1277960 | tf_op jit(solution)/shard_map/ppermute | solution.py:44
  (32 other events, 240.1 us)
Sparse Core Ops, SparseCore 0:
  11.1 124.5 all-gather.2

commit v3 on v2

--- a/solution.py
+++ b/solution.py
@@ -32,6 +32,9 @@
 ) = range(10)
 HIDDEN_ROW = 10
 TABLE_ROWS = 16
+
+MLP_NORMED, ATTN_NORMED, ATTN_OUT = 4, 5, 6
+MLP_GRAD, BRANCH_GRAD = 4, 5
 
 
 def hop(block, axis, places):
@@ -136,10 +139,9 @@
     return lax.dynamic_index_in_dim(terms, at, dim, keepdims=False)
 
 
-def core_sum(mine, other):
+def by_chip(terms):
     x_size, y_size = lax.axis_size("dp") // 2, lax.axis_size("head") // 2
-    total = mine.astype(jnp.float32) + swap(other, "head").astype(jnp.float32)
-    return total.astype(jnp.bfloat16).reshape((x_size, 2, y_size, 2) + mine.shape[1:])
+    return terms.reshape((x_size, 2, y_size, 2) + terms.shape[1:])
 
 
 def ring_halves(terms, axis):
@@ -150,18 +152,22 @@
     return hop(far[:half], axis, 1), hop(far[half:], axis, -1)
 
 
-def ring_rest(terms, halves, axis):
+def ring_ends(terms, passed, axis):
     x_me, _, y_me, _ = coordinates()
     dim, me, size = (0, x_me, 4) if axis == "dp" else (2, y_me, 4)
-    low, high = (part.astype(jnp.float32) for part in halves)
+    low, high = (part.astype(jnp.float32) for part in passed)
     up = piece(terms, (me + 1) % size, dim).astype(jnp.float32)
     down = piece(terms, (me - 1) % size, dim).astype(jnp.float32)
     half = up.shape[0] // 2
     up = jnp.concatenate([up[:half] + low, up[half:]]).astype(jnp.bfloat16)
     down = jnp.concatenate([down[:half], down[half:] + high]).astype(jnp.bfloat16)
-    total = piece(terms, me, dim).astype(jnp.float32)
-    total = total + hop(up, axis, 1).astype(jnp.float32)
-    return total + hop(down, axis, -1).astype(jnp.float32)
+    return hop(up, axis, 1), hop(down, axis, -1)
+
+
+def ring_total(terms, ends, axis):
+    x_me, _, y_me, _ = coordinates()
+    own = piece(terms, x_me, 0) if axis == "dp" else piece(terms, y_me, 2)
+    return sum((end.astype(jnp.float32) for end in ends), own.astype(jnp.float32))
 
 
 def ring_direct(terms, axis, dim, me):
@@ -248,6 +254,12 @@
         blocks_ref[first + peer, :, start : start + 128] = rows[
             :, peer * 128 : (peer + 1) * 128
         ].astype(blocks_ref.dtype)
+
+
+def put_column(ref, at, rows):
+    width = rows.shape[1]
+    start = at * width if isinstance(at, int) else pl.multiple_of(at * width, width)
+    ref[:, pl.ds(start, width)] = rows
 
 
 def halves(core, rows):
@@ -294,28 +306,38 @@
         put_side_by_side(out_ref, values, 256, first)
 
 
-def valid_rows(count, like):
-    return lax.broadcasted_iota(jnp.int32, like.shape, 0) < count
+def marked(rows, mark):
+    first = lax.broadcasted_iota(jnp.int32, rows.shape, 1) == 0
+    return jnp.concatenate([rows, jnp.where(first, mark, 0.0).astype(jnp.bfloat16)], axis=1)
+
+
+def masked_keys(block, count, head):
+    keys = block[:, 128 + head * DH : 128 + (head + 1) * DH]
+    valid = lax.broadcasted_iota(jnp.int32, keys.shape, 0) < count
+    return marked(keys, jnp.where(valid, 0.0, MASKED_SCORE))
+
+
+def scaled_queries(block, start, head):
+    queries = block[start : start + QUERY_ROWS, head * DH : (head + 1) * DH]
+    return marked((queries.astype(jnp.float32) * SCORE_SCALE).astype(jnp.bfloat16), 1.0)
 
 
 def attend_kernel(count_ref, heads_ref, out_ref, lse_ref):
     count = count_ref[pl.program_id(0)]
     block = flat(heads_ref[:, 0])
     seq_len = block.shape[0]
+    keys = [masked_keys(block, count, head) for head in range(2)]
+    values = [block[:, 256 + head * DH : 256 + (head + 1) * DH] for head in range(2)]
+    values = [jnp.concatenate([part, jnp.ones_like(part)], axis=1) for part in values]
     for start in range(0, seq_len, QUERY_ROWS):
         outs = []
         for head in range(2):
-            low = head * DH
-            keys = block[:, 128 + low : 128 + low + DH]
-            values = block[:, 256 + low : 256 + low + DH]
-            queries = block[start : start + QUERY_ROWS, low : low + DH]
-            scores = product_nt(keys, queries)
-            scores = jnp.where(valid_rows(count, scores), scores * SCORE_SCALE, MASKED_SCORE)
+            scores = product_nt(keys[head], scaled_queries(block, start, head))
             largest = jnp.max(scores, axis=0, keepdims=True)
             weights = jnp.exp(scores - largest)
-            total = jnp.sum(weights, axis=0, keepdims=True)
-            mixed = product_tn(values, weights.astype(jnp.bfloat16)) / total
-            outs.append(mixed.T)
+            mixed = product_tn(values[head], weights.astype(jnp.bfloat16))
+            total = mixed[DH : DH + 1]
+            outs.append((mixed[:DH] / total).T)
             lse_ref[0, head : head + 1, start : start + QUERY_ROWS] = largest + jnp.log(total)
         rows = jnp.concatenate(outs, axis=1).astype(jnp.bfloat16)
         peers = QUERY_ROWS // 128
@@ -328,55 +350,70 @@
     grads = flat(grad_ref[:, 0])
     seq_len = block.shape[0]
     peers = QUERY_ROWS // 128
+    keys = [masked_keys(block, count, head) for head in range(2)]
+    values = [block[:, 256 + head * DH : 256 + (head + 1) * DH] for head in range(2)]
     key_sums = [jnp.zeros((seq_len, DH), jnp.float32) for _ in range(2)]
     value_sums = [jnp.zeros((seq_len, DH), jnp.float32) for _ in range(2)]
     for start in range(0, seq_len, QUERY_ROWS):
         outs = []
         for head in range(2):
-            low = head * DH
-            keys = block[:, 128 + low : 128 + low + DH]
-            values = block[:, 256 + low : 256 + low + DH]
-            queries = block[start : start + QUERY_ROWS, low : low + DH]
-            grad_rows = grads[start : start + QUERY_ROWS, low : low + DH]
+            queries = scaled_queries(block, start, head)
+            grad_rows = grads[start : start + QUERY_ROWS, head * DH : (head + 1) * DH]
             lse = lse_ref[0, head : head + 1, start : start + QUERY_ROWS]
-            scores = product_nt(keys, queries)
-            scores = jnp.where(valid_rows(count, scores), scores * SCORE_SCALE, MASKED_SCORE)
-            weights = jnp.exp(scores - lse)
-            grad_weights = product_nt(values, grad_rows)
+            weights = jnp.exp(product_nt(keys[head], queries) - lse)
+            grad_weights = product_nt(values[head], grad_rows)
             dots = jnp.sum(weights * grad_weights, axis=0, keepdims=True)
             grad_scores = (weights * (grad_weights - dots)).astype(jnp.bfloat16)
             value_sums[head] += product(weights.astype(jnp.bfloat16), grad_rows)
-            key_sums[head] += product(grad_scores, queries)
-            outs.append((product_tn(keys, grad_scores) * SCORE_SCALE).T)
+            key_sums[head] += product(grad_scores, queries[:, :DH])
+            outs.append((product_tn(keys[head][:, :DH], grad_scores) * SCORE_SCALE).T)
         rows = jnp.concatenate(outs, axis=1).astype(jnp.bfloat16)
         out_ref[start // 128 : start // 128 + peers, 0, :, :128] = rows.reshape(peers, 128, 128)
-    key_rows = (jnp.concatenate(key_sums, axis=1) * SCORE_SCALE).astype(jnp.bfloat16)
+    key_rows = jnp.concatenate(key_sums, axis=1).astype(jnp.bfloat16)
     value_rows = jnp.concatenate(value_sums, axis=1).astype(jnp.bfloat16)
     out_ref[:, 0, :, 128:256] = key_rows.reshape(-1, 128, 128)
     out_ref[:, 0, :, 256:] = value_rows.reshape(-1, 128, 128)
 
 
+def hidden_halves(fc1_ref, fc2_ref):
+    columns, owners = fc1_ref.shape[2] // 2, fc2_ref.shape[0] // 2
+    return [
+        (at * columns, (at + 1) * columns, at * owners, (at + 1) * owners) for at in range(2)
+    ]
+
+
 def rear_kernel(keep, x_ref, attn_ref, table_ref, proj_ref, fc1_ref, fc2_ref, *rest):
     if keep:
-        result_ref, branch_ref, hidden_ref, mlp_ref, normed, middle, total = rest
+        result_ref, branch_ref, hidden_ref, mlp_ref, left_ref, normed, middle, total = rest
     else:
         result_ref, normed, middle, total = rest
     step = pl.program_id(0)
 
     @pl.when(step == 0)
     def _():
-        branch = product(side_by_side(attn_ref), flat(proj_ref[...])) + vector(table_ref, PROJ_ADD)
+        attn = side_by_side(attn_ref)
+        branch = product(attn, flat(proj_ref[...])) + vector(table_ref, PROJ_ADD)
+        rows = x_ref[...].astype(jnp.float32)
+        middle[...] = rows + vector(table_ref, ATTN_LAYER) * branch
+        normed[...] = mlp_normed(middle[...], table_ref)[0]
         if keep:
             branch_ref[...] = branch
-        middle[...] = x_ref[...].astype(jnp.float32) + vector(table_ref, ATTN_LAYER) * branch
-        normed[...] = mlp_normed(middle[...], table_ref)[0]
+            put_column(left_ref, MLP_NORMED, normed[...])
+            put_column(left_ref, ATTN_NORMED, attn_normed(rows, table_ref)[0])
+            put_column(left_ref, ATTN_OUT, attn)
         total[...] = jnp.broadcast_to(vector(table_ref, FC2_ADD), total.shape)
 
-    hidden = product(normed[...], flat(fc1_ref[...])) + table_ref[pl.ds(HIDDEN_ROW + step, 1), :]
+    adds = table_ref[pl.ds(HIDDEN_ROW + step, 1), :]
+    actives, mixed = [], 0.0
+    for low, high, rows_from, rows_to in hidden_halves(fc1_ref, fc2_ref):
+        hidden = product(normed[...], flat(fc1_ref[:, :, low:high])) + adds[:, low:high]
+        if keep:
+            hidden_ref[:, low:high] = hidden
+        actives.append((hidden * cumulative(hidden)).astype(jnp.bfloat16))
+        mixed += product(actives[-1], flat(fc2_ref[rows_from:rows_to]))
     if keep:
-        hidden_ref[...] = hidden
-    active = (hidden * cumulative(hidden)).astype(jnp.bfloat16)
-    total[...] += product(active, flat(fc2_ref[...]))
+        put_column(left_ref, step, jnp.concatenate(actives, axis=1))
+    total[...] += mixed
 
     @pl.when(step == pl.num_programs(0) - 1)
     def _():
@@ -388,6 +425,7 @@
 
 def rear_back_kernel(
     keep,
+    core_ref,
     grad_ref,
     x_ref,
     branch_ref,
@@ -402,9 +440,14 @@
     *rest,
 ):
     if keep:
-        mlp_low_ref, hidden_low_ref, active_ref, normed_ref, branch_low_ref, sums_ref = rest[:6]
+        mine_ref, other_ref, sums_ref = rest[:3]
     mlp_low, total = rest[-2:]
     step = pl.program_id(0)
+
+    def put_right(at, rows):
+        mine, other = halves(core_ref[0], rows)
+        put_column(mine_ref, at, mine)
+        put_column(other_ref, at, other)
 
     @pl.when(step == 0)
     def _():
@@ -414,25 +457,27 @@
         if keep:
             sums_ref[...] = jnp.zeros_like(sums_ref)
             sums_ref[FC2_ADD : FC2_ADD + 1, :] = column_sum(grad_mlp)
-            mlp_low_ref[...] = mlp_low[...]
-
-    hidden = hidden_ref[...]
-    below = cumulative(hidden)
-    slope = below + hidden * (jnp.exp(-0.5 * hidden * hidden) * DENSITY_SCALE)
-    grad_hidden = product_nt(mlp_low[...], flat(fc2_ref[...])) * slope
-    hidden_low = grad_hidden.astype(jnp.bfloat16)
-    total[...] += product_nt(hidden_low, flat(fc1_ref[...]))
+            put_right(MLP_GRAD, mlp_low[...])
+
+    lows, sums, mixed = [], [], 0.0
+    for low, high, rows_from, rows_to in hidden_halves(fc1_ref, fc2_ref):
+        hidden = hidden_ref[:, low:high]
+        slope = cumulative(hidden) + hidden * (jnp.exp(-0.5 * hidden * hidden) * DENSITY_SCALE)
+        grad_hidden = product_nt(mlp_low[...], flat(fc2_ref[rows_from:rows_to])) * slope
+        lows.append(grad_hidden.astype(jnp.bfloat16))
+        sums.append(column_sum(grad_hidden))
+        mixed += product_nt(lows[-1], flat(fc1_ref[:, :, low:high]))
+    total[...] += mixed
     if keep:
-        sums_ref[pl.ds(HIDDEN_ROW + step, 1), :] = column_sum(grad_hidden)
-        hidden_low_ref[...] = hidden_low
-        active_ref[...] = (hidden * below).astype(jnp.bfloat16)
+        sums_ref[pl.ds(HIDDEN_ROW + step, 1), :] = jnp.concatenate(sums, axis=1)
+        put_right(step, jnp.concatenate(lows, axis=1))
 
     @pl.when(step == pl.num_programs(0) - 1)
     def _():
         grad_rows = grad_ref[...].astype(jnp.float32)
         branch = branch_ref[...]
         middle = x_ref[...].astype(jnp.float32) + vector(table_ref, ATTN_LAYER) * branch
-        normed, scaled, inverse = mlp_normed(middle, table_ref)
+        _, scaled, inverse = mlp_normed(middle, table_ref)
         grad_normed = total[...]
         grad_middle = grad_rows + norm_back(
             grad_normed * vector(table_ref, MLP_GAIN), scaled, inverse
@@ -442,8 +487,7 @@
         branch_low = grad_branch.astype(jnp.bfloat16)
         put_side_by_side(attn_grad_ref, product_nt(branch_low, flat(proj_ref[...])))
         if keep:
-            normed_ref[...] = normed
-            branch_low_ref[...] = branch_low
+            put_right(BRANCH_GRAD, branch_low)
             for row, rows in (
                 (MLP_LAYER, grad_rows * mlp_ref[...]),
                 (MLP_GAIN, grad_normed * scaled),
@@ -499,52 +543,52 @@
             sums_ref[row : row + 1, :] = column_sum(rows)
 
 
-def put_products(core, mine_ref, other_ref, left, right, start, count):
-    for ref, part in zip((mine_ref, other_ref), halves(core, right)):
-        grad = product_tn(left, part).astype(jnp.bfloat16)
-        ref[:, start : start + count] = grad.reshape(-1, count, part.shape[1])
+def both_products(left_ref, left_other_ref, right, right_other):
+    grad = product_tn(left_ref[...], right) + product_tn(left_other_ref[...], right_other)
+    return grad.astype(jnp.bfloat16)
 
 
 def mlp_weights_kernel(
-    core_ref,
+    active_ref,
+    active_other_ref,
     normed_ref,
-    hidden_low_ref,
-    active_ref,
-    mlp_low_ref,
+    normed_other_ref,
     attn_ref,
-    branch_low_ref,
-    fc1_mine_ref,
-    fc1_other_ref,
-    fc2_mine_ref,
-    fc2_other_ref,
-    proj_mine_ref,
-    proj_other_ref,
+    attn_other_ref,
+    hidden_ref,
+    hidden_other_ref,
+    mlp_ref,
+    mlp_other_ref,
+    branch_ref,
+    branch_other_ref,
+    fc1_proj_ref,
+    fc2_ref,
 ):
-    core = core_ref[0]
-    owned = fc2_mine_ref.shape[1]
-    put_products(core, fc2_mine_ref, fc2_other_ref, active_ref[...], mlp_low_ref[...], 0, owned)
-    put_products(core, fc1_mine_ref, fc1_other_ref, normed_ref[...], hidden_low_ref[...], 0, SLAB)
-
-    @pl.when(pl.program_id(0) == 0)
+    step = pl.program_id(0)
+    devices, _, half = fc1_proj_ref.shape
+    fc2 = both_products(active_ref, active_other_ref, mlp_ref[...], mlp_other_ref[...])
+    fc2_ref[...] = fc2.reshape(fc2_ref.shape)
+    fc1 = both_products(normed_ref, normed_other_ref, hidden_ref[...], hidden_other_ref[...])
+    start = pl.multiple_of(step * SLAB, SLAB)
+    fc1_proj_ref[:, pl.ds(start, SLAB)] = fc1.reshape(devices, SLAB, half)
+
+    @pl.when(step == 0)
     def _():
-        attn = side_by_side(attn_ref)
-        put_products(core, proj_mine_ref, proj_other_ref, attn, branch_low_ref[...], 0, SLAB)
-
-
-def query_key_weights_kernel(core_ref, x_ref, table_ref, grad_ref, mine_ref, other_ref):
-    normed, _, _ = attn_normed(x_ref[...].astype(jnp.float32), table_ref)
-    for at in range(2):
-        grads = side_by_side(grad_ref, at * 128)
-        put_products(core_ref[0], mine_ref, other_ref, normed, grads, at * SLAB, SLAB)
-
-
-def value_weights_kernel(core_ref, x_ref, table_ref, grad_ref, small_ref, mine_ref, other_ref):
-    core = core_ref[0]
-    normed, _, _ = attn_normed(x_ref[...].astype(jnp.float32), table_ref)
-    put_products(core, mine_ref, other_ref, normed, side_by_side(grad_ref, 256), 0, SLAB)
-    small = small_ref[...]
-    mine_ref[:, SLAB:] = jnp.where(core == 0, small, jnp.zeros_like(small))
-    other_ref[:, SLAB:] = jnp.where(core == 0, jnp.zeros_like(small), small)
+        proj = both_products(attn_ref, attn_other_ref, branch_ref[...], branch_other_ref[...])
+        start = pl.num_programs(0) * SLAB
+        fc1_proj_ref[:, start:] = proj.reshape(devices, SLAB, half)
+
+
+def attn_weights_kernel(parts, core_ref, left_ref, left_other_ref, grad_ref, got_ref, *rest):
+    out_ref = rest[-1]
+    devices, _, half = out_ref.shape
+    for at, part in enumerate(parts):
+        right = side_by_side(grad_ref, part * 128, core_ref[0] * 4, 4)
+        right_other = side_by_side(got_ref, part * 128, 0, 4)
+        grad = both_products(left_ref, left_other_ref, right, right_other)
+        out_ref[:, at * SLAB : (at + 1) * SLAB] = grad.reshape(devices, SLAB, half)
+    if len(rest) > 1:
+        out_ref[:, len(parts) * SLAB :] = rest[0][...]
 
 
 def like(*shape, dtype=jnp.bfloat16):
@@ -649,8 +693,9 @@
     column = pl.BlockSpec((rows, width), lambda j: (0, j))
     out_shape, out_specs = [like(rows, width)], [whole_block(x)]
     if keep:
-        out_shape += [full, like(rows, steps * width, dtype=jnp.float32), full]
-        out_specs += [whole_block(x), column, whole_block(x)]
+        left = like(rows, (steps + 3) * width)
+        out_shape += [full, like(rows, steps * width, dtype=jnp.float32), full, left]
+        out_specs += [whole_block(x), column, whole_block(x), whole_block(left)]
     return pl.pallas_call(
         functools.partial(rear_kernel, keep),
         grid=(steps,),
@@ -667,7 +712,7 @@
     )(x, attn, table, late, late, late)
 
 
-def call_rear_back(keep, grad, x, branch, hidden, mlp, table, late):
+def call_rear_back(keep, core, grad, x, branch, hidden, mlp, table, late):
     rows, width = x.shape
     steps, weight_specs = rear_weight_specs(late)
     column = pl.BlockSpec((rows, width), lambda j: (0, j))
@@ -675,15 +720,16 @@
     out_shape = [attn_grad, like(rows, width, dtype=jnp.float32)]
     out_specs = [whole_block(attn_grad), whole_block(x)]
     if keep:
-        wide = like(rows, steps * width)
-        out_shape += [like(rows, width), wide, wide, like(rows, width), like(rows, width)]
-        out_specs += [whole_block(x), column, column, whole_block(x), whole_block(x)]
+        right = like(rows, (steps + 2) * width // 2)
+        out_shape += [right, right]
+        out_specs += [whole_block(right), whole_block(right)]
         out_shape += [like(*table.shape, dtype=jnp.float32)]
         out_specs += [whole_block(table)]
     return pl.pallas_call(
         functools.partial(rear_back_kernel, keep),
         grid=(steps,),
         in_specs=[
+            SCALARS,
             whole_block(grad),
             whole_block(x),
             whole_block(branch),
@@ -700,7 +746,7 @@
         ],
         compiler_params=params(),
         cost_estimate=takes(16),
-    )(grad, x, branch, hidden, mlp, table, late, late, late)
+    )(core, grad, x, branch, hidden, mlp, table, late, late, late)
 
 
 def call_front_back(keep, core, grad_qkv, grad_middle, x, table, early):
@@ -722,37 +768,48 @@
     )(core, grad_qkv, grad_middle, x, table, *early)
 
 
-def call_mlp_weights(core, normed, hidden_low, active, mlp_low, attn, branch_low, devices, owned):
-    rows, width = normed.shape
+def call_mlp_weights(left, left_other, right, right_other, devices, owned):
+    rows = left.shape[0]
     steps = owned // SLAB
-    half = width // 2
-    column = pl.BlockSpec((rows, width), lambda j: (0, j))
-    fc1_spec = pl.BlockSpec((devices, SLAB, half), lambda j: (0, j, 0))
-    fc2_spec = pl.BlockSpec((devices // steps, owned, half), lambda j: (j, 0, 0))
-    proj_spec = pl.BlockSpec((devices, SLAB, half), lambda j: (0, 0, 0))
+    width, half = 1024, 512
+
+    def column(size, at):
+        return pl.BlockSpec((rows, size), lambda j: (0, at))
+
+    by_step = [pl.BlockSpec((rows, size), lambda j: (0, j)) for size in (width, half)]
+    out_shape = [like(devices, owned + SLAB, half), like(devices, owned, half)]
     return pl.pallas_call(
         mlp_weights_kernel,
         grid=(steps,),
-        in_specs=[SCALARS, whole_block(normed), column, column]
-        + [whole_block(member) for member in (mlp_low, attn, branch_low)],
-        out_specs=[fc1_spec, fc1_spec, fc2_spec, fc2_spec, proj_spec, proj_spec],
-        out_shape=[like(devices, owned, half)] * 4 + [like(devices, SLAB, half)] * 2,
+        in_specs=[by_step[0]] * 2
+        + [column(width, MLP_NORMED)] * 2
+        + [column(width, ATTN_OUT)] * 2
+        + [by_step[1]] * 2
+        + [column(half, MLP_GRAD)] * 2
+        + [column(half, BRANCH_GRAD)] * 2,
+        out_specs=[
+            whole_block(out_shape[0]),
+            pl.BlockSpec((devices // steps, owned, half), lambda j: (j, 0, 0)),
+        ],
+        out_shape=out_shape,
         compiler_params=params(),
-        cost_estimate=takes(11),
-    )(core, normed, hidden_low, active, mlp_low, attn, branch_low)
-
-
-def call_attn_weights(kernel, core, devices, *operands):
-    shape = like(devices, 2 * SLAB, operands[0].shape[1] // 2)
+        cost_estimate=takes(9),
+    )(*(left, left_other) * 3, *(right, right_other) * 3)
+
+
+def call_attn_weights(parts, core, devices, left, left_other, grads, got, *small):
+    column = pl.BlockSpec((left.shape[0], 1024), lambda i: (0, ATTN_NORMED))
+    shape = like(devices, (len(parts) + len(small)) * SLAB, 512)
     return pl.pallas_call(
-        kernel,
+        functools.partial(attn_weights_kernel, parts),
         grid=(1,),
-        in_specs=[SCALARS] + [whole_block(operand) for operand in operands],
-        out_specs=[whole_block(shape)] * 2,
-        out_shape=[shape] * 2,
+        in_specs=[SCALARS, column, column]
+        + [whole_block(operand) for operand in (grads, got, *small)],
+        out_specs=whole_block(shape),
+        out_shape=shape,
         compiler_params=params(),
-        cost_estimate=takes(4),
-    )(core, *operands)
+        cost_estimate=takes(3),
+    )(core, left, left_other, grads, got, *small)
 
 
 def small_slab(vectors, hidden_vector):
@@ -862,43 +919,42 @@
     (passed,) = call_rear(False, own_images, attention(own_images)[2], table, late)
     x = jnp.where(section_index == 0, own_images, shifted(passed, 1))
     heads, lse, attn = attention(x)
-    result, *rear_state = call_rear(True, x, attn, table, late)
+    result, *rear_state, left = call_rear(True, x, attn, table, late)
+    left_other = swap(left, "head")
 
     own_grad = cotangent.reshape(rows, features)
-    rear = call_rear_back(False, own_grad, x, *rear_state, table, late)
+    rear = call_rear_back(False, core, own_grad, x, *rear_state, table, late)
     grad_qkv = to_peers(call_attend_back(counts, to_peers(rear[0]), heads, lse))
     (passed_back,) = call_front_back(False, core, grad_qkv, rear[1], x, table, early)
+    passed_back = after(passed_back, left_other)
     grad = jnp.where(section_index == 0, shifted(passed_back, -1), own_grad)
 
-    rear = call_rear_back(True, grad, x, *rear_state, table, late)
-    grad_attn, grad_middle, mlp_low, hidden_low, active, normed, branch_low, rear_sums = rear
-    fc1_mine, fc1_other, fc2_mine, fc2_other, proj_mine, proj_other = call_mlp_weights(
-        core, normed, hidden_low, active, mlp_low, attn, branch_low, devices, 4 * SLAB
-    )
-    grad_heads = after(to_peers(grad_attn), fc1_mine)
-    mlp_terms = [
-        core_sum(fc1_mine, fc1_other),
-        jnp.concatenate(
-            [core_sum(fc2_mine, fc2_other), core_sum(proj_mine, proj_other)], axis=4
-        ),
-    ]
-    grad_qkv = to_peers(call_attend_back(counts, grad_heads, heads, lse))
-    grad_qkv = after(grad_qkv, *mlp_terms)
+    rear = call_rear_back(True, core, grad, x, *rear_state, table, late)
+    grad_attn, grad_middle, right, right_other, rear_sums = rear
+    fc1_proj, fc2 = call_mlp_weights(
+        left, left_other, right, swap(right_other, "head"), devices, 4 * SLAB
+    )
+    grad_heads = after(to_peers(grad_attn), fc2)
+    mlp_terms = [by_chip(fc1_proj), by_chip(fc2)]
     mlp_halves = [ring_halves(terms, way) for terms, way in zip(mlp_terms, ways)]
-    mlp_terms = [ring_rest(*item) for item in zip(mlp_terms, mlp_halves, ways)]
-
-    attn_parts = call_attn_weights(query_key_weights_kernel, core, devices, x, table, grad_qkv)
+    grad_qkv = call_attend_back(counts, grad_heads, heads, lse)
+    grad_qkv = to_peers(after(grad_qkv, mlp_halves))
+    mlp_ends = [ring_ends(*item) for item in zip(mlp_terms, mlp_halves, ways)]
+
+    got = swap(lax.dynamic_slice_in_dim(grad_qkv, (1 - core[0]) * 4, 4), "head")
+    query_key = call_attn_weights((0, 1), core, devices, left, left_other, grad_qkv, got)
     input_grad, front_sums = call_front_back(
-        True, core, after(grad_qkv, attn_parts, mlp_halves), grad_middle, x, table, early
+        True, core, after(grad_qkv, query_key), grad_middle, x, table, early
     )
     small = slabs_of(rear_sums + front_sums, devices)
-    value_parts = call_attn_weights(
-        value_weights_kernel, core, devices, x, table, grad_qkv, small
-    )
-    attn_terms = [core_sum(*attn_parts), core_sum(*value_parts)]
-    attn_terms = [
-        ring_rest(terms, ring_halves(terms, way), way) for terms, way in zip(attn_terms, ways)
-    ]
+    value = call_attn_weights((2,), core, devices, left, left_other, grad_qkv, got, small)
+    attn_terms = [by_chip(query_key), by_chip(value)]
+    attn_halves = [ring_halves(terms, way) for terms, way in zip(attn_terms, ways)]
+    mlp_ends = after(mlp_ends, attn_terms)
+    mlp_terms = [ring_total(*item) for item in zip(mlp_terms, mlp_ends, ways)]
+    attn_ends = [ring_ends(*item) for item in zip(attn_terms, attn_halves, ways)]
+    mlp_terms = after(mlp_terms, attn_halves)
+    attn_terms = [ring_total(*item) for item in zip(attn_terms, attn_ends, ways)]
     ring_sums = [
         second_ring(terms, way)
         for terms, way in zip(mlp_terms + attn_terms, ways + ways)
@@ -908,14 +964,14 @@
         shard_grad[start:stop]
         for start, stop in (
             (0, 4 * SLAB),
-            (4 * SLAB, 8 * SLAB),
-            (8 * SLAB, 9 * SLAB),
+            (5 * SLAB, 9 * SLAB),
+            (4 * SLAB, 5 * SLAB),
             (9 * SLAB, 12 * SLAB),
             (12 * SLAB, 12 * SLAB + 1),
         )
     )
     qkv_grad = from_column_slabs(qkv_grad)
-    row = small_row[0]
+    row = small_row[0, :SMALL_WIDTH] + small_row[0, SMALL_WIDTH:]
     small_grads = row[: HIDDEN_ROW * SLAB].reshape(HIDDEN_ROW, SLAB)
     fc1_bias_grad = row[HIDDEN_ROW * SLAB : HIDDEN_ROW * SLAB + 64]
 

time: 634 us -> 579 us (0.913)
  other arithmetic: 47.6 us -> 23.3 us
  waiting for transfers between devices: 153 us -> 129 us
  blocking collectives: 97.7 us -> 82.9 us
  starting transfers between devices: 103 us -> 111 us
    ppermute x42, waiting for transfers between devices: 76.6 us -> 43.7 us  [hop(): lax.ppermute(block, axis, [(i, (i + 2 * places) % size) for i in range(si...]
    convert_element_type x5 -> x0, other arithmetic: 20.8 us -> none  [core_sum(): total.astype(jnp.bfloat16).reshape((x_size, 2, y_size, 2) + mine.shape[1:])]
    all_to_all x5 -> x4, blocking collectives: 97.7 us -> 82.9 us  [to_peers(): lax.all_to_all(blocks, 'head', split_axis=0, concat_axis=0, tiled=True)]
    all_to_all x3 -> x4, waiting for transfers between devices: 39.1 us -> 49 us  [to_peers(): lax.all_to_all(blocks, 'head', split_axis=0, concat_axis=0, tiled=True)]
    all_to_all x3 -> x4, starting transfers between devices: 12.4 us -> 16.9 us  [to_peers(): lax.all_to_all(blocks, 'head', split_axis=0, concat_axis=0, tiled=True)]
    ppermute x11 -> x9, starting transfers between devices: 31.3 us -> 30.3 us  [swap(): return lax.ppermute(block, axis, [(i, i ^ 1) for i in range(size)])]
    ppermute x11 -> x9, waiting for transfers between devices: 13.3 us -> 13.3 us  [swap(): return lax.ppermute(block, axis, [(i, i ^ 1) for i in range(size)])]
  transfers between devices with their start and end apart: 59 -> 58, of which waited for: 24 -> 25; matrix products, arithmetic and copies ran while one was open for 11% -> 8% of each run, Pallas kernels for 9% -> 15%
where the time goes in v3:
time: 579 us; the launch traced here: 570 us
  Pallas kernels  165 us (28%)
  waiting for transfers between devices  129 us (22%)
  starting transfers between devices  111 us (19%)
  blocking collectives  82.9 us (14%)
  local copies, waits for them, and re-layouts  42.7 us (7%)
  other arithmetic  23.3 us (4%)
  between operations  16.3 us (3%)
    all_to_all x4, blocking collectives, to_peers(): lax.all_to_all(blocks, 'head', split_axis=0, concat_axis=0, tiled=True)  82.9 us
    ppermute x42, starting transfers between devices, hop(): lax.ppermute(block, axis, [(i, (i + 2 * places) % size) for i in range(si...  59.9 us
    all_to_all x4, waiting for transfers between devices, to_peers(): lax.all_to_all(blocks, 'head', split_axis=0, concat_axis=0, tiled=True)  49 us
    ppermute x42, waiting for transfers between devices, hop(): lax.ppermute(block, axis, [(i, (i + 2 * places) % size) for i in range(si...  43.7 us
    pallas_call x2, Pallas kernels, call_attend_back(): pl.pallas_call(attend_back_kernel, grid=(images,), in_specs=[SCALARS, pl....  32.5 us
    pallas_call x2, Pallas kernels, call_rear_back(): pl.pallas_call(functools.partial(rear_back_kernel, keep), grid=(steps,),...  30.3 us
    ppermute x9, starting transfers between devices, swap(): return lax.ppermute(block, axis, [(i, i ^ 1) for i in range(size)])  30.3 us
    pallas_call x2, Pallas kernels, call_attend(): pl.pallas_call(attend_kernel, grid=(images,), in_specs=[SCALARS, pl.Block...  28 us
  transfers between devices with their start and end apart: 58, of which 25 were waited for; matrix products, arithmetic and copies ran while one was open for 8% of the time, Pallas kernels for 15%

profile of v3, /device:TPU:1, one launch (start us, length us, event | category | flops | bytes accessed | tf_op | source)
XLA Modules:
  0.0 570.0 jit_solution(3517677048341152486)
XLA Ops:
  15.9 3.8 collective-permute-start.1
  19.6 3.6 collective-permute-done.1
  48.2 3.4 collective-permute-done.5
  59.8 3.4 collective-permute-start.16
  69.3 7.9 %collective-permute-start.9 = (bf16[64,32,512]{2,1,0:T(8,128)(2,1)S(1)}, bf16[64,32,512]{2,1,0:T(8,128)(2,1)S(1)}, u32[]{:S(2)}, u32[]{:S(2)}) collective-permute-start(bf16[64,32,512]{2,1,0:T(8,128)(2,1)S(1)} %bitcast.313), channel_id=1, source_target_pairs={{0,1},{1,0},{2,3},{3,2},{4,5},{5,4},{6,7},{7,6},{8,9},{9,8},{10,11... | collective-permute-start | bytes 6291464 | tf_op jit(solution)/shard_map/ppermute | solution.py:47
  84.1 3.2 collective-permute-done.17.qk_other_ref
  87.3 6.2 %shard_map.318 = bf16[8,256,384]{2,1,0:T(8,128)(2,1)} custom-call(s32[1]{0:T(128)} %bitcast.2.core_ref, bf16[256,1024]{1,0:T(8,128)(2,1)} %bitcast.308, f32[16,1024]{1,0:T(8,128)} %select_maximum_fusion.table_ref, bf16[64,32,512]{2,1,0:T(8,128)(2,1)} %bitcast.41.qk_mine_ref, bf16[64,32,512]{2,1,0:T(8,128)(2,1)} %bitcast.315, ...), custom_call_target="tpu_custom_call" | custom-call | flops 7474999808 | bytes 19500000 | tf_op jit(solution)/shard_map/pallas_call | solution.py:624
  93.5 4.2 all-to-all-start
  98.5 25.8 %all-to-all-done = bf16[8,256,384]{2,1,0:T(8,128)(2,1)S(1)} async-done(((bf16[8,256,384]{2,1,0:T(8,128)(2,1)}), bf16[8,256,384]{2,1,0:T(8,128)(2,1)S(1)}, u32[]{:S(2)}, u32[]{:S(2)}) %all-to-all-start) | async-done | bytes 1572896 | tf_op jit(solution)/shard_map/all_to_all | solution.py:197
  125.4 14.1 %shard_map.319 = (bf16[8,2,128,128]{3,2,1,0:T(8,128)(2,1)}, f32[2,2,1024]{2,1,0:T(2,128)}) custom-call(s32[2]{0:T(128)} %broadcast_select_fusion.5.count_ref, bf16[8,2,128,384]{3,2,1,0:T(8,128)(2,1)} %bitcast.327), custom_call_target="tpu_custom_call" | custom-call | flops 16444999680 | bytes 42900000 | tf_op jit(solution)/shard_map/pallas_call | solution.py:639
  139.6 15.1 %all_to_all.40.attn_ref = bf16[8,256,128]{2,1,0:T(8,128)(2,1)} all-to-all(bf16[8,256,128]{2,1,0:T(8,128)(2,1)} %bitcast.337), channel_id=1, replica_groups=mesh['section'=2,'dp'=8,'head'=8] {'head'}, dimensions={0} | all-to-all | bytes 1048576 | tf_op jit(solution)/shard_map/all_to_all | solution.py:197
  154.6 12.0 %shard_map.320 = bf16[256,1024]{1,0:T(8,128)(2,1)} custom-call(bf16[256,1024]{1,0:T(8,128)(2,1)} %bitcast.309, bf16[8,256,128]{2,1,0:T(8,128)(2,1)} %all_to_all.40.attn_ref, f32[16,1024]{1,0:T(8,128)} %select_maximum_fusion.table_ref, bf16[64,144,1024]{2,1,0:T(8,128)(2,1)} %bitcast.289, bf16[64,144,1024]{2,1,0:T(8,128)(2,1)} %bitcast.290, ...), custom_call_target="tpu_custom_call" | custom-call | flops 14949999616 | bytes 39000000 | tf_op jit(solution)/shard_map/pallas_call | solution.py:699
  168.7 10.4 %collective-permute-done.18 = bf16[256,1024]{1,0:T(8,128)(2,1)S(1)} collective-permute-done((bf16[256,1024]{1,0:T(8,128)(2,1)}, bf16[256,1024]{1,0:T(8,128)(2,1)S(1)}, u32[]{:S(2)}, u32[]{:S(2)}) %collective-permute-start.18) | collective-permute-done | bytes 524320 | tf_op jit(solution)/shard_map/ppermute | solution.py:203
  180.0 6.2 %shard_map.321 = bf16[8,256,384]{2,1,0:T(8,128)(2,1)} custom-call(s32[1]{0:T(128)} %bitcast.2.core_ref, bf16[256,1024]{1,0:T(8,128)(2,1)} %broadcast_select_fusion.1.x_ref, f32[16,1024]{1,0:T(8,128)} %select_maximum_fusion.table_ref, bf16[64,32,512]{2,1,0:T(8,128)(2,1)} %bitcast.41.qk_mine_ref, bf16[64,32,512]{2,1,0:T(8,128)(2,1)} %bitcast.316, ...), custom_call_target="tpu_custom_call" | custom-call | flops 7474999808 | bytes 19500000 | tf_op jit(solution)/shard_map/pallas_call | solution.py:624
  186.2 27.4 %all_to_all.41 = bf16[8,256,384]{2,1,0:T(8,128)(2,1)} all-to-all(bf16[8,256,384]{2,1,0:T(8,128)(2,1)} %shard_map.321), channel_id=1, replica_groups=mesh['section'=2,'dp'=8,'head'=8] {'head'}, dimensions={0} | all-to-all | bytes 3145728 | tf_op jit(solution)/shard_map/all_to_all | solution.py:197
  213.6 13.9 %shard_map.322 = (bf16[8,2,128,128]{3,2,1,0:T(8,128)(2,1)}, f32[2,2,1024]{2,1,0:T(2,128)}) custom-call(s32[2]{0:T(128)} %broadcast_select_fusion.5.count_ref, bf16[8,2,128,384]{3,2,1,0:T(8,128)(2,1)} %bitcast.323), custom_call_target="tpu_custom_call" | custom-call | flops 16444999680 | bytes 42900000 | tf_op jit(solution)/shard_map/pallas_call | solution.py:639
  227.5 14.5 %all_to_all.42.attn_ref = bf16[8,256,128]{2,1,0:T(8,128)(2,1)} all-to-all(bf16[8,256,128]{2,1,0:T(8,128)(2,1)} %bitcast.338), channel_id=1, replica_groups=mesh['section'=2,'dp'=8,'head'=8] {'head'}, dimensions={0} | all-to-all | bytes 1048576 | tf_op jit(solution)/shard_map/all_to_all | solution.py:197
  242.0 15.2 %shard_map.323 = (bf16[256,1024]{1,0:T(8,128)(2,1)}, f32[256,1024]{1,0:T(8,128)}, f32[256,4096]{1,0:T(8,128)}, f32[256,1024]{1,0:T(8,128)}, bf16[256,7168]{1,0:T(8,128)(2,1)}) custom-call(bf16[256,1024]{1,0:T(8,128)(2,1)} %broadcast_select_fusion.1.x_ref, bf16[8,256,128]{2,1,0:T(8,128)(2,1)} %all_to_all.42.attn_ref, ...), custom_call_target="tpu_custom_call" | custom-call | flops 14949999616 | bytes 39000000 | tf_op jit(solution)/shard_map/pallas_call | solution.py:699
  257.3 14.3 %shard_map.324 = (bf16[8,256,128]{2,1,0:T(8,128)(2,1)}, f32[256,1024]{1,0:T(8,128)}) custom-call(s32[1]{0:T(128)} %bitcast.2.core_ref, bf16[256,1024]{1,0:T(8,128)(2,1)} %bitcast.334, bf16[256,1024]{1,0:T(8,128)(2,1)} %broadcast_select_fusion.1.x_ref, f32[256,1024]{1,0:T(8,128)} %get-tuple-element.49.branch_ref, f32[256,4096]{1,0:T(8,128)} %get-tuple-element.50.hidden_ref, ...), custom_call_target="tpu_custom_call" | custom-call | flops 18400000000 | bytes 48000000 | tf_op jit(solution)/shard_map/pallas_call | solution.py:728
  271.6 4.4 all-to-all-start.4
  276.4 9.1 %all-to-all-done.4 = bf16[8,256,128]{2,1,0:T(8,128)(2,1)S(1)} async-done(((bf16[8,256,128]{2,1,0:T(8,128)(2,1)}), bf16[8,256,128]{2,1,0:T(8,128)(2,1)S(1)}, u32[]{:S(2)}, u32[]{:S(2)}) %all-to-all-start.4) | async-done | bytes 524320 | tf_op jit(solution)/shard_map/all_to_all | solution.py:197
  286.3 16.2 %shard_map.325 = bf16[8,2,128,384]{3,2,1,0:T(8,128)(2,1)} custom-call(s32[2]{0:T(128)} %broadcast_select_fusion.5.count_ref, bf16[8,2,128,128]{3,2,1,0:T(8,128)(2,1)} %bitcast.336, bf16[8,2,128,384]{3,2,1,0:T(8,128)(2,1)} %bitcast.324, f32[2,2,1024]{2,1,0:T(2,128)} %get-tuple-element.53.lse_ref), custom_call_target="tpu_custom_call" | custom-call | flops 18975000576 | bytes 49500000 | tf_op jit(solution)/shard_map/pallas_call | solution.py:661
  302.5 25.9 %all_to_all.43.grad_ref = bf16[8,256,384]{2,1,0:T(8,128)(2,1)} all-to-all(bf16[8,256,384]{2,1,0:T(8,128)(2,1)} %bitcast.328), channel_id=1, replica_groups=mesh['section'=2,'dp'=8,'head'=8] {'head'}, dimensions={0} | all-to-all | bytes 3145728 | tf_op jit(solution)/shard_map/all_to_all | solution.py:197
  328.5 6.7 %shard_map.326 = bf16[256,1024]{1,0:T(8,128)(2,1)} custom-call(s32[1]{0:T(128)} %bitcast.2.core_ref, bf16[8,256,384]{2,1,0:T(8,128)(2,1)} %all_to_all.43.grad_ref, f32[256,1024]{1,0:T(8,128)} %get-tuple-element.54.middle_grad_ref, bf16[256,1024]{1,0:T(8,128)(2,1)} %broadcast_select_fusion.1.x_ref, f32[16,1024]{1,0:T(8,128)} %select_maximum_fusion.table_ref, ...), custom_call_target="tpu_custom_call" | custom-call | flops 8049999872 | bytes 21000000 | tf_op jit(solution)/shard_map/pallas_call | solution.py:758
  336.7 13.0 %collective-permute-done.20 = bf16[256,1024]{1,0:T(8,128)(2,1)S(1)} collective-permute-done((bf16[256,1024]{1,0:T(8,128)(2,1)}, bf16[256,1024]{1,0:T(8,128)(2,1)S(1)}, u32[]{:S(2)}, u32[]{:S(2)}) %collective-permute-start.20) | collective-permute-done | bytes 524320 | tf_op jit(solution)/shard_map/ppermute | solution.py:203
  350.6 16.0 %shard_map.327 = (bf16[8,256,128]{2,1,0:T(8,128)(2,1)}, f32[256,1024]{1,0:T(8,128)}, bf16[256,3072]{1,0:T(8,128)(2,1)}, bf16[256,3072]{1,0:T(8,128)(2,1)}, f32[16,1024]{1,0:T(8,128)}) custom-call(s32[1]{0:T(128)} %bitcast.2.core_ref, bf16[256,1024]{1,0:T(8,128)(2,1)} %broadcast_select_fusion.grad_ref, bf16[256,1024]{1,0:T(8,128)(2,1)} %broadcast_select_fusion.1.x_ref, ...), custom_call_target="tpu_custom_call" | custom-call | flops 18400000000 | bytes 48000000 | tf_op jit(solution)/shard_map/pallas_call | solution.py:728
  368.6 3.5 all-to-all-start.6
  373.2 11.7 %shard_map.328 = (bf16[64,80,512]{2,1,0:T(8,128)(2,1)}, bf16[64,64,512]{2,1,0:T(8,128)(2,1)}) custom-call(bf16[256,7168]{1,0:T(8,128)(2,1)} %get-tuple-element.55.active_ref.normed_ref.attn_ref.left_ref, bf16[256,7168]{1,0:T(8,128)(2,1)} %collective-permute-done.19.active_other_ref.normed_other_ref.attn_other_ref.left_other_ref, ...), custom_call_target="tpu_custom_call" | custom-call | flops 10350000128 | bytes 27000000 | tf_op jit(solution)/shard_map/pallas_call | solution.py:781
  394.8 16.3 %shard_map.329 = bf16[8,2,128,384]{3,2,1,0:T(8,128)(2,1)} custom-call(s32[2]{0:T(128)} %broadcast_select_fusion.5.count_ref, bf16[8,2,128,128]{3,2,1,0:T(8,128)(2,1)} %bitcast.335, bf16[8,2,128,384]{3,2,1,0:T(8,128)(2,1)} %bitcast.325, f32[2,2,1024]{2,1,0:T(2,128)} %get-tuple-element.53.lse_ref), custom_call_target="tpu_custom_call" | custom-call | flops 18975000576 | bytes 49500000 | tf_op jit(solution)/shard_map/pallas_call | solution.py:661
  412.0 4.8 all-to-all-start.7
  423.5 14.0 %all-to-all-done.7.grad_ref = bf16[8,256,384]{2,1,0:T(8,128)(2,1)S(1)} async-done(((bf16[8,256,384]{2,1,0:T(8,128)(2,1)}), bf16[8,256,384]{2,1,0:T(8,128)(2,1)S(1)}, u32[]{:S(2)}, u32[]{:S(2)}) %all-to-all-start.7) | async-done | bytes 1572896 | tf_op jit(solution)/shard_map/all_to_all | solution.py:197
  443.3 2.9 collective-permute-start.28
  446.2 4.5 shard_map.330
  450.7 7.0 %shard_map.331 = (bf16[256,1024]{1,0:T(8,128)(2,1)}, f32[16,1024]{1,0:T(8,128)}) custom-call(s32[1]{0:T(128)} %bitcast.2.core_ref, bf16[8,256,384]{2,1,0:T(8,128)(2,1)} %copy-done, f32[256,1024]{1,0:T(8,128)} %get-tuple-element.65.middle_grad_ref, bf16[256,1024]{1,0:T(8,128)(2,1)} %broadcast_select_fusion.1.x_ref, f32[16,1024]{1,0:T(8,128)} %select_maximum_fusion.table_ref, ...), custom_call_target="tpu_custom_call" | custom-call | flops 8049999872 | bytes 21000000 | tf_op jit(solution)/shard_map/pallas_call | solution.py:758
  460.3 4.4 shard_map.332
  469.1 4.0 collective-permute-done.27
  480.9 3.1 collective-permute-start.40
  485.0 5.7 collective-permute-done.40
  490.7 5.3 collective-permute-start.37
  498.4 11.3 %collective-permute-done.37 = bf16[2,2,80,512]{3,2,1,0:T(8,128)(2,1)S(1)} collective-permute-done((bf16[2,2,80,512]{3,2,1,0:T(8,128)(2,1)S(1)}, bf16[2,2,80,512]{3,2,1,0:T(8,128)(2,1)S(1)}, u32[]{:S(2)}, u32[]{:S(2)}) %collective-permute-start.37) | collective-permute-done | bytes 327712 | tf_op jit(solution)/shard_map/ppermute | solution.py:42
  509.7 3.5 collective-permute-start.42
  514.7 3.4 collective-permute-start.50
  518.7 4.5 collective-permute-done.42
  523.3 4.3 collective-permute-done.41
  527.9 3.5 collective-permute-start.45
  538.1 5.4 collective-permute-start.51
  543.5 5.5 collective-permute-done.51
  549.2 7.8 %collective-permute-start.52 = (bf16[208,512]{1,0:T(8,128)(2,1)S(1)}, bf16[208,512]{1,0:T(8,128)(2,1)S(1)}, u32[]{:S(2)}, u32[]{:S(2)}) collective-permute-start(bf16[208,512]{1,0:T(8,128)(2,1)S(1)} %fusion.23), channel_id=1, source_target_pairs={{0,1},{1,0},{2,3},{3,2},{4,5},{5,4},{6,7},{7,6},{8,9},{9,8},{10,11... | collective-permute-start | bytes 638984 | tf_op jit(solution)/shard_map/ppermute | solution.py:47
  (247 shorter events, 121.2 us)
Async XLA Ops:
  7.2 147.4 %all-gather.3.cloned.1.call-start = ((), (), s32[]{:S(2)}) async-start(), calls=%async_computation.8 | async-start | bytes 19169280 | tf_op jit(solution)/shard_map/all_gather | solution.py:893
  24.0 10.1 %collective-permute-start.2 = (bf16[2,2,32,512]{3,2,1,0:T(8,128)(2,1)}, bf16[2,2,32,512]{3,2,1,0:T(8,128)(2,1)S(1)}, u32[]{:S(2)}, u32[]{:S(2)}) collective-permute-start(bf16[2,2,32,512]{3,2,1,0:T(8,128)(2,1)} %get-tuple-element.110.given_ref), channel_id=1, source_target_pairs={{0,16},{8,24},{16,32},{24,40},{32,48},{40,56},{48,0},{56,8},{1,17}... | collective-permute-start | bytes 393224 | tf_op jit(solution)/shard_map/ppermute | solution.py:42
  25.2 11.3 %collective-permute-start.3 = (bf16[2,2,32,512]{3,2,1,0:T(8,128)(2,1)}, bf16[2,2,32,512]{3,2,1,0:T(8,128)(2,1)S(1)}, u32[]{:S(2)}, u32[]{:S(2)}) collective-permute-start(bf16[2,2,32,512]{3,2,1,0:T(8,128)(2,1)} %get-tuple-element.110.given_ref), channel_id=1, source_target_pairs={{0,32},{8,40},{16,48},{24,56},{32,0},{40,8},{48,16},{56,24},{1,33}... | collective-permute-start | bytes 393224 | tf_op jit(solution)/shard_map/ppermute | solution.py:42
  27.6 9.5 %collective-permute-start.4 = (bf16[2,2,32,512]{3,2,1,0:T(8,128)(2,1)}, bf16[2,2,32,512]{3,2,1,0:T(8,128)(2,1)S(1)}, u32[]{:S(2)}, u32[]{:S(2)}) collective-permute-start(bf16[2,2,32,512]{3,2,1,0:T(8,128)(2,1)} %get-tuple-element.110.given_ref), channel_id=1, source_target_pairs={{0,48},{8,56},{16,0},{24,8},{32,16},{40,24},{48,32},{56,40},{1,49}... | collective-permute-start | bytes 393224 | tf_op jit(solution)/shard_map/ppermute | solution.py:42
  28.8 12.0 %collective-permute-start.10 = (bf16[2,2,32,512]{3,2,1,0:T(8,128)(2,1)}, bf16[2,2,32,512]{3,2,1,0:T(8,128)(2,1)S(1)}, u32[]{:S(2)}, u32[]{:S(2)}) collective-permute-start(bf16[2,2,32,512]{3,2,1,0:T(8,128)(2,1)} %get-tuple-element.109.given_ref), channel_id=1, source_target_pairs={{0,2},{1,3},{2,4},{3,5},{4,6},{5,7},{6,0},{7,1},{8,10},{9,11},{10,... | collective-permute-start | bytes 393224 | tf_op jit(solution)/shard_map/ppermute | solution.py:42
  30.1 11.4 %collective-permute-start.11 = (bf16[2,2,32,512]{3,2,1,0:T(8,128)(2,1)}, bf16[2,2,32,512]{3,2,1,0:T(8,128)(2,1)S(1)}, u32[]{:S(2)}, u32[]{:S(2)}) collective-permute-start(bf16[2,2,32,512]{3,2,1,0:T(8,128)(2,1)} %get-tuple-element.109.given_ref), channel_id=1, source_target_pairs={{0,4},{1,5},{2,6},{3,7},{4,0},{5,1},{6,2},{7,3},{8,12},{9,13},{10,... | collective-permute-start | bytes 393224 | tf_op jit(solution)/shard_map/ppermute | solution.py:42
  37.8 13.8 %collective-permute-start.5 = (bf16[4,2,2,32,512]{4,3,2,1,0:T(8,128)(2,1)}, bf16[4,2,2,32,512]{4,3,2,1,0:T(8,128)(2,1)}, u32[]{:S(2)}, u32[]{:S(2)}) collective-permute-start(bf16[4,2,2,32,512]{4,3,2,1,0:T(8,128)(2,1)} %bitcast_dynamic-update-slice_fusion.14.given_ref), channel_id=1, source_target_pairs={{0,2},{1,3},{2,4},{3,5},{4,6},{5,7},{6,0},{7,1},{8,10},{9,11},{10,... | collective-permute-start | bytes 1572872 | tf_op jit(solution)/shard_map/ppermute | solution.py:42
  39.1 15.2 %collective-permute-start.6 = (bf16[4,2,2,32,512]{4,3,2,1,0:T(8,128)(2,1)}, bf16[4,2,2,32,512]{4,3,2,1,0:T(8,128)(2,1)}, u32[]{:S(2)}, u32[]{:S(2)}) collective-permute-start(bf16[4,2,2,32,512]{4,3,2,1,0:T(8,128)(2,1)} %bitcast_dynamic-update-slice_fusion.14.given_ref), channel_id=1, source_target_pairs={{0,6},{1,7},{2,0},{3,1},{4,2},{5,3},{6,4},{7,5},{8,14},{9,15},{10,... | collective-permute-start | bytes 1572872 | tf_op jit(solution)/shard_map/ppermute | solution.py:42
  42.8 15.0 %collective-permute-start.13 = (bf16[2,4,2,32,512]{4,3,2,1,0:T(8,128)(2,1)}, bf16[2,4,2,32,512]{4,3,2,1,0:T(8,128)(2,1)}, u32[]{:S(2)}, u32[]{:S(2)}) collective-permute-start(bf16[2,4,2,32,512]{4,3,2,1,0:T(8,128)(2,1)} %bitcast_dynamic-update-slice_fusion.13.given_ref), channel_id=1, source_target_pairs={{0,16},{8,24},{16,32},{24,40},{32,48},{40,56},{48,0},{56,8},{1,17}... | collective-permute-start | bytes 1572872 | tf_op jit(solution)/shard_map/ppermute | solution.py:42
  42.8 16.0 %collective-permute-start.14 = (bf16[2,4,2,32,512]{4,3,2,1,0:T(8,128)(2,1)}, bf16[2,4,2,32,512]{4,3,2,1,0:T(8,128)(2,1)}, u32[]{:S(2)}, u32[]{:S(2)}) collective-permute-start(bf16[2,4,2,32,512]{4,3,2,1,0:T(8,128)(2,1)} %bitcast_dynamic-update-slice_fusion.13.given_ref), channel_id=1, source_target_pairs={{0,48},{8,56},{16,0},{24,8},{32,16},{40,24},{48,32},{56,40},{1,49}... | collective-permute-start | bytes 1572872 | tf_op jit(solution)/shard_map/ppermute | solution.py:42
  52.5 16.7 %collective-permute-start.7 = (bf16[2,2,2,32,512]{4,3,2,1,0:T(8,128)(2,1)S(1)}, bf16[2,2,2,32,512]{4,3,2,1,0:T(8,128)(2,1)S(1)}, u32[]{:S(2)}, u32[]{:S(2)}) collective-permute-start(bf16[2,2,2,32,512]{4,3,2,1,0:T(8,128)(2,1)S(1)} %slice.412), channel_id=1, source_target_pairs={{0,2},{1,3},{2,4},{3,5},{4,6},{5,7},{6,0},{7,1},{8,10},{9,11},{10,... | collective-permute-start | bytes 786440 | tf_op jit(solution)/shard_map/ppermute | solution.py:42
  55.3 13.9 %collective-permute-start.8 = (bf16[2,2,2,32,512]{4,3,2,1,0:T(8,128)(2,1)S(1)}, bf16[2,2,2,32,512]{4,3,2,1,0:T(8,128)(2,1)S(1)}, u32[]{:S(2)}, u32[]{:S(2)}) collective-permute-start(bf16[2,2,2,32,512]{4,3,2,1,0:T(8,128)(2,1)S(1)} %slice.413), channel_id=1, source_target_pairs={{0,6},{1,7},{2,0},{3,1},{4,2},{5,3},{6,4},{7,5},{8,14},{9,15},{10,... | collective-permute-start | bytes 786440 | tf_op jit(solution)/shard_map/ppermute | solution.py:42
  58.7 18.5 %collective-permute-start.15 = (bf16[1,4,2,32,512]{4,3,2,1,0:T(8,128)(2,1)S(1)}, bf16[1,4,2,32,512]{4,3,2,1,0:T(8,128)(2,1)S(1)}, u32[]{:S(2)}, u32[]{:S(2)}) collective-permute-start(bf16[1,4,2,32,512]{4,3,2,1,0:T(8,128)(2,1)S(1)} %slice.419), channel_id=1, source_target_pairs={{0,16},{8,24},{16,32},{24,40},{32,48},{40,56},{48,0},{56,8},{1,17}... | collective-permute-start | bytes 786440 | tf_op jit(solution)/shard_map/ppermute | solution.py:42
  59.8 18.1 %collective-permute-start.16 = (bf16[1,4,2,32,512]{4,3,2,1,0:T(8,128)(2,1)S(1)}, bf16[1,4,2,32,512]{4,3,2,1,0:T(8,128)(2,1)S(1)}, u32[]{:S(2)}, u32[]{:S(2)}) collective-permute-start(bf16[1,4,2,32,512]{4,3,2,1,0:T(8,128)(2,1)S(1)} %slice.420), channel_id=1, source_target_pairs={{0,48},{8,56},{16,0},{24,8},{32,16},{40,24},{48,32},{56,40},{1,49}... | collective-permute-start | bytes 786440 | tf_op jit(solution)/shard_map/ppermute | solution.py:42
  69.3 12.3 %collective-permute-start.9 = (bf16[64,32,512]{2,1,0:T(8,128)(2,1)S(1)}, bf16[64,32,512]{2,1,0:T(8,128)(2,1)S(1)}, u32[]{:S(2)}, u32[]{:S(2)}) collective-permute-start(bf16[64,32,512]{2,1,0:T(8,128)(2,1)S(1)} %bitcast.313), channel_id=1, source_target_pairs={{0,1},{1,0},{2,3},{3,2},{4,5},{5,4},{6,7},{7,6},{8,9},{9,8},{10,11... | collective-permute-start | bytes 6291464 | tf_op jit(solution)/shard_map/ppermute | solution.py:47
  93.5 30.8 %all-to-all-start = ((bf16[8,256,384]{2,1,0:T(8,128)(2,1)}), bf16[8,256,384]{2,1,0:T(8,128)(2,1)S(1)}, u32[]{:S(2)}, u32[]{:S(2)}) async-start(bf16[8,256,384]{2,1,0:T(8,128)(2,1)} %shard_map.318), calls=%async_computation | async-start | bytes 3145728 | tf_op jit(solution)/shard_map/all_to_all | solution.py:197
  166.7 12.5 %collective-permute-start.18 = (bf16[256,1024]{1,0:T(8,128)(2,1)}, bf16[256,1024]{1,0:T(8,128)(2,1)S(1)}, u32[]{:S(2)}, u32[]{:S(2)}) collective-permute-start(bf16[256,1024]{1,0:T(8,128)(2,1)} %shard_map.320), channel_id=1, source_target_pairs={{0,64},{1,65},{2,66},{3,67},{4,68},{5,69},{6,70},{7,71},{8,72},{9,... | collective-permute-start | bytes 1572872 | tf_op jit(solution)/shard_map/ppermute | solution.py:203
  271.6 13.9 %all-to-all-start.4 = ((bf16[8,256,128]{2,1,0:T(8,128)(2,1)}), bf16[8,256,128]{2,1,0:T(8,128)(2,1)S(1)}, u32[]{:S(2)}, u32[]{:S(2)}) async-start(bf16[8,256,128]{2,1,0:T(8,128)(2,1)} %get-tuple-element.52), calls=%async_computation.4 | async-start | bytes 1048576 | tf_op jit(solution)/shard_map/all_to_all | solution.py:197
  276.0 59.2 %collective-permute-start.19 = (bf16[256,7168]{1,0:T(8,128)(2,1)}, bf16[256,7168]{1,0:T(8,128)(2,1)}, u32[]{:S(2)}, u32[]{:S(2)}) collective-permute-start(bf16[256,7168]{1,0:T(8,128)(2,1)} %get-tuple-element.55.active_ref.normed_ref.attn_ref.left_ref), channel_id=1, source_target_pairs={{0,1},{1,0},{2,3},{3,2},{4,5},{5,4},{6,7},{7,6},{8,9},{9,8},{10,11... | collective-permute-start | bytes 11010056 | tf_op jit(solution)/shard_map/ppermute | solution.py:47
  335.2 14.5 %collective-permute-start.20 = (bf16[256,1024]{1,0:T(8,128)(2,1)}, bf16[256,1024]{1,0:T(8,128)(2,1)S(1)}, u32[]{:S(2)}, u32[]{:S(2)}) collective-permute-start(bf16[256,1024]{1,0:T(8,128)(2,1)} %shard_map.326), channel_id=1, source_target_pairs={{64,0},{65,1},{66,2},{67,3},{68,4},{69,5},{70,6},{71,7},{72,8},{73... | collective-permute-start | bytes 1572872 | tf_op jit(solution)/shard_map/ppermute | solution.py:203
  368.6 16.3 %all-to-all-start.6 = ((bf16[8,256,128]{2,1,0:T(8,128)(2,1)}), bf16[8,256,128]{2,1,0:T(8,128)(2,1)S(1)}, u32[]{:S(2)}, u32[]{:S(2)}) async-start(bf16[8,256,128]{2,1,0:T(8,128)(2,1)} %get-tuple-element.57), calls=%async_computation.6 | async-start | bytes 1048576 | tf_op jit(solution)/shard_map/all_to_all | solution.py:197
  387.8 23.3 %collective-permute-start.22 = (bf16[1,4,2,80,512]{4,3,2,1,0:T(8,128)(2,1)S(1)}, bf16[1,4,2,80,512]{4,3,2,1,0:T(8,128)(2,1)S(1)}, u32[]{:S(2)}, u32[]{:S(2)}) collective-permute-start(bf16[1,4,2,80,512]{4,3,2,1,0:T(8,128)(2,1)S(1)} %get-tuple-element.76), channel_id=1, source_target_pairs={{0,16},{8,24},{16,32},{24,40},{32,48},{40,56},{48,0},{56,8},{1,17}... | collective-permute-start | bytes 1966088 | tf_op jit(solution)/shard_map/ppermute | solution.py:42
  387.9 23.3 %collective-permute-start.23 = (bf16[1,4,2,80,512]{4,3,2,0,1:T(8,128)(2,1)S(1)}, bf16[1,4,2,80,512]{4,3,2,0,1:T(8,128)(2,1)}, u32[]{:S(2)}, u32[]{:S(2)}) collective-permute-start(bf16[1,4,2,80,512]{4,3,2,0,1:T(8,128)(2,1)S(1)} %get-tuple-element.78), channel_id=1, source_target_pairs={{0,48},{8,56},{16,0},{24,8},{32,16},{40,24},{48,32},{56,40},{1,49}... | collective-permute-start | bytes 1966088 | tf_op jit(solution)/shard_map/ppermute | solution.py:42
  391.8 19.3 %collective-permute-start.24 = (bf16[2,2,2,64,512]{4,3,2,1,0:T(8,128)(2,1)}, bf16[2,2,2,64,512]{4,3,2,1,0:T(8,128)(2,1)}, u32[]{:S(2)}, u32[]{:S(2)}) collective-permute-start(bf16[2,2,2,64,512]{4,3,2,1,0:T(8,128)(2,1)} %get-tuple-element.80), channel_id=1, source_target_pairs={{0,2},{1,3},{2,4},{3,5},{4,6},{5,7},{6,0},{7,1},{8,10},{9,11},{10,... | collective-permute-start | bytes 1572872 | tf_op jit(solution)/shard_map/ppermute | solution.py:42
  393.2 17.9 %collective-permute-start.25 = (bf16[2,2,2,64,512]{4,3,2,1,0:T(8,128)(2,1)}, bf16[2,2,2,64,512]{4,3,2,1,0:T(8,128)(2,1)}, u32[]{:S(2)}, u32[]{:S(2)}) collective-permute-start(bf16[2,2,2,64,512]{4,3,2,1,0:T(8,128)(2,1)} %get-tuple-element.82), channel_id=1, source_target_pairs={{0,6},{1,7},{2,0},{3,1},{4,2},{5,3},{6,4},{7,5},{8,14},{9,15},{10,... | collective-permute-start | bytes 1572872 | tf_op jit(solution)/shard_map/ppermute | solution.py:42
  412.0 25.5 %all-to-all-start.7 = ((bf16[8,256,384]{2,1,0:T(8,128)(2,1)}), bf16[8,256,384]{2,1,0:T(8,128)(2,1)S(1)}, u32[]{:S(2)}, u32[]{:S(2)}) async-start(bf16[8,256,384]{2,1,0:T(8,128)(2,1)} %bitcast.326), calls=%async_computation.7 | async-start | bytes 3145728 | tf_op jit(solution)/shard_map/all_to_all | solution.py:197
  419.7 47.0 %collective-permute-start.29 = (bf16[4,2,2,64,512]{4,3,2,1,0:T(8,128)(2,1)}, bf16[4,2,2,64,512]{4,3,2,1,0:T(8,128)(2,1)}, u32[]{:S(2)}, u32[]{:S(2)}) collective-permute-start(bf16[4,2,2,64,512]{4,3,2,1,0:T(8,128)(2,1)} %pad_maximum_fusion.3), channel_id=1, source_target_pairs={{0,2},{1,3},{2,4},{3,5},{4,6},{5,7},{6,0},{7,1},{8,10},{9,11},{10,... | collective-permute-start | bytes 3145736 | tf_op jit(solution)/shard_map/ppermute | solution.py:42
  422.2 46.8 %collective-permute-start.30 = (bf16[4,2,2,64,512]{4,3,2,1,0:T(8,128)(2,1)}, bf16[4,2,2,64,512]{4,3,2,1,0:T(8,128)(2,1)}, u32[]{:S(2)}, u32[]{:S(2)}) collective-permute-start(bf16[4,2,2,64,512]{4,3,2,1,0:T(8,128)(2,1)} %pad_maximum_fusion.4), channel_id=1, source_target_pairs={{0,6},{1,7},{2,0},{3,1},{4,2},{5,3},{6,4},{7,5},{8,14},{9,15},{10,... | collective-permute-start | bytes 3145736 | tf_op jit(solution)/shard_map/ppermute | solution.py:42
  441.7 31.4 %collective-permute-start.27 = (bf16[2,4,2,80,512]{4,3,2,1,0:T(8,128)(2,1)}, bf16[2,4,2,80,512]{4,3,2,1,0:T(8,128)(2,1)S(1)}, u32[]{:S(2)}, u32[]{:S(2)}) collective-permute-start(bf16[2,4,2,80,512]{4,3,2,1,0:T(8,128)(2,1)} %pad_maximum_fusion.1), channel_id=1, source_target_pairs={{0,16},{8,24},{16,32},{24,40},{32,48},{40,56},{48,0},{56,8},{1,17}... | collective-permute-start | bytes 3932168 | tf_op jit(solution)/shard_map/ppermute | solution.py:42
  443.3 30.3 %collective-permute-start.28 = (bf16[2,4,2,80,512]{4,3,2,0,1:T(8,128)(2,1)S(1)}, bf16[2,4,2,80,512]{4,3,2,0,1:T(8,128)(2,1)}, u32[]{:S(2)}, u32[]{:S(2)}) collective-permute-start(bf16[2,4,2,80,512]{4,3,2,0,1:T(8,128)(2,1)S(1)} %pad_maximum_fusion.2), channel_id=1, source_target_pairs={{0,48},{8,56},{16,0},{24,8},{32,16},{40,24},{48,32},{56,40},{1,49}... | collective-permute-start | bytes 3932168 | tf_op jit(solution)/shard_map/ppermute | solution.py:42
  466.1 12.3 %collective-permute-start.33 = (bf16[2,2,2,32,512]{4,3,2,1,0:T(8,128)(2,1)S(1)}, bf16[2,2,2,32,512]{4,3,2,1,0:T(8,128)(2,1)S(1)}, u32[]{:S(2)}, u32[]{:S(2)}) collective-permute-start(bf16[2,2,2,32,512]{4,3,2,1,0:T(8,128)(2,1)S(1)} %get-tuple-element.91), channel_id=1, source_target_pairs={{0,2},{1,3},{2,4},{3,5},{4,6},{5,7},{6,0},{7,1},{8,10},{9,11},{10,... | collective-permute-start | bytes 786440 | tf_op jit(solution)/shard_map/ppermute | solution.py:42
  466.7 11.8 %collective-permute-start.34 = (bf16[2,2,2,32,512]{4,3,2,1,0:T(8,128)(2,1)S(1)}, bf16[2,2,2,32,512]{4,3,2,1,0:T(8,128)(2,1)S(1)}, u32[]{:S(2)}, u32[]{:S(2)}) collective-permute-start(bf16[2,2,2,32,512]{4,3,2,1,0:T(8,128)(2,1)S(1)} %get-tuple-element.94), channel_id=1, source_target_pairs={{0,6},{1,7},{2,0},{3,1},{4,2},{5,3},{6,4},{7,5},{8,14},{9,15},{10,... | collective-permute-start | bytes 786440 | tf_op jit(solution)/shard_map/ppermute | solution.py:42
  469.0 11.3 %collective-permute-start.32 = (bf16[1,4,2,32,512]{4,3,2,0,1:T(8,128)(2,1)S(1)}, bf16[1,4,2,32,512]{4,3,2,0,1:T(8,128)(2,1)S(1)}, u32[]{:S(2)}, u32[]{:S(2)}) collective-permute-start(bf16[1,4,2,32,512]{4,3,2,0,1:T(8,128)(2,1)S(1)} %get-tuple-element.88), channel_id=1, source_target_pairs={{0,48},{8,56},{16,0},{24,8},{32,16},{40,24},{48,32},{56,40},{1,49}... | collective-permute-start | bytes 786440 | tf_op jit(solution)/shard_map/ppermute | solution.py:42
  478.7 35.7 %collective-permute-start.47 = (bf16[4,2,2,32,512]{4,3,2,1,0:T(8,128)(2,1)S(1)}, bf16[4,2,2,32,512]{4,3,2,1,0:T(8,128)(2,1)S(1)}, u32[]{:S(2)}, u32[]{:S(2)}) collective-permute-start(bf16[4,2,2,32,512]{4,3,2,1,0:T(8,128)(2,1)S(1)} %pad_maximum_fusion.8), channel_id=1, source_target_pairs={{0,6},{1,7},{2,0},{3,1},{4,2},{5,3},{6,4},{7,5},{8,14},{9,15},{10,... | collective-permute-start | bytes 1572872 | tf_op jit(solution)/shard_map/ppermute | solution.py:42
  479.7 34.7 %collective-permute-start.46 = (bf16[4,2,2,32,512]{4,3,2,1,0:T(8,128)(2,1)S(1)}, bf16[4,2,2,32,512]{4,3,2,1,0:T(8,128)(2,1)S(1)}, u32[]{:S(2)}, u32[]{:S(2)}) collective-permute-start(bf16[4,2,2,32,512]{4,3,2,1,0:T(8,128)(2,1)S(1)} %pad_maximum_fusion.7), channel_id=1, source_target_pairs={{0,2},{1,3},{2,4},{3,5},{4,6},{5,7},{6,0},{7,1},{8,10},{9,11},{10,... | collective-permute-start | bytes 1572872 | tf_op jit(solution)/shard_map/ppermute | solution.py:42
  480.9 9.8 %collective-permute-start.40 = (bf16[2,2,64,512]{3,2,1,0:T(8,128)(2,1)S(1)}, bf16[2,2,64,512]{3,2,1,0:T(8,128)(2,1)S(1)}, u32[]{:S(2)}, u32[]{:S(2)}) collective-permute-start(bf16[2,2,64,512]{3,2,1,0:T(8,128)(2,1)S(1)} %get-tuple-element.100), channel_id=1, source_target_pairs={{0,48},{8,56},{16,0},{24,8},{32,16},{40,24},{48,32},{56,40},{1,49}... | collective-permute-start | bytes 786440 | tf_op jit(solution)/shard_map/ppermute | solution.py:42
  484.0 12.0 %collective-permute-start.39 = (bf16[2,2,64,512]{3,2,1,0:T(8,128)(2,1)S(1)}, bf16[2,2,64,512]{3,2,1,0:T(8,128)(2,1)S(1)}, u32[]{:S(2)}, u32[]{:S(2)}) collective-permute-start(bf16[2,2,64,512]{3,2,1,0:T(8,128)(2,1)S(1)} %get-tuple-element.99), channel_id=1, source_target_pairs={{0,32},{8,40},{16,48},{24,56},{32,0},{40,8},{48,16},{56,24},{1,33}... | collective-permute-start | bytes 786440 | tf_op jit(solution)/shard_map/ppermute | solution.py:42
  484.0 13.9 %collective-permute-start.38 = (bf16[2,2,64,512]{3,2,1,0:T(8,128)(2,1)S(1)}, bf16[2,2,64,512]{3,2,1,0:T(8,128)(2,1)S(1)}, u32[]{:S(2)}, u32[]{:S(2)}) collective-permute-start(bf16[2,2,64,512]{3,2,1,0:T(8,128)(2,1)S(1)} %get-tuple-element.98), channel_id=1, source_target_pairs={{0,16},{8,24},{16,32},{24,40},{32,48},{40,56},{48,0},{56,8},{1,17}... | collective-permute-start | bytes 786440 | tf_op jit(solution)/shard_map/ppermute | solution.py:42
  490.7 19.1 %collective-permute-start.37 = (bf16[2,2,80,512]{3,2,1,0:T(8,128)(2,1)S(1)}, bf16[2,2,80,512]{3,2,1,0:T(8,128)(2,1)S(1)}, u32[]{:S(2)}, u32[]{:S(2)}) collective-permute-start(bf16[2,2,80,512]{3,2,1,0:T(8,128)(2,1)S(1)} %get-tuple-element.97), channel_id=1, source_target_pairs={{0,6},{1,7},{2,0},{3,1},{4,2},{5,3},{6,4},{7,5},{8,14},{9,15},{10,... | collective-permute-start | bytes 983048 | tf_op jit(solution)/shard_map/ppermute | solution.py:42
  496.0 17.3 %collective-permute-start.36 = (bf16[2,2,80,512]{3,2,1,0:T(8,128)(2,1)S(1)}, bf16[2,2,80,512]{3,2,1,0:T(8,128)(2,1)S(1)}, u32[]{:S(2)}, u32[]{:S(2)}) collective-permute-start(bf16[2,2,80,512]{3,2,1,0:T(8,128)(2,1)S(1)} %get-tuple-element.96), channel_id=1, source_target_pairs={{0,4},{1,5},{2,6},{3,7},{4,0},{5,1},{6,2},{7,3},{8,12},{9,13},{10,... | collective-permute-start | bytes 983048 | tf_op jit(solution)/shard_map/ppermute | solution.py:42
  497.9 16.3 %collective-permute-start.35 = (bf16[2,2,80,512]{3,2,1,0:T(8,128)(2,1)S(1)}, bf16[2,2,80,512]{3,2,1,0:T(8,128)(2,1)S(1)}, u32[]{:S(2)}, u32[]{:S(2)}) collective-permute-start(bf16[2,2,80,512]{3,2,1,0:T(8,128)(2,1)S(1)} %get-tuple-element.95), channel_id=1, source_target_pairs={{0,2},{1,3},{2,4},{3,5},{4,6},{5,7},{6,0},{7,1},{8,10},{9,11},{10,... | collective-permute-start | bytes 983048 | tf_op jit(solution)/shard_map/ppermute | solution.py:42
  509.7 13.5 %collective-permute-start.42 = (bf16[2,4,2,32,512]{4,3,2,0,1:T(8,128)(2,1)S(1)}, bf16[2,4,2,32,512]{4,3,2,0,1:T(8,128)(2,1)S(1)}, u32[]{:S(2)}, u32[]{:S(2)}) collective-permute-start(bf16[2,4,2,32,512]{4,3,2,0,1:T(8,128)(2,1)S(1)} %pad_maximum_fusion.6), channel_id=1, source_target_pairs={{0,48},{8,56},{16,0},{24,8},{32,16},{40,24},{48,32},{56,40},{1,49}... | collective-permute-start | bytes 1572872 | tf_op jit(solution)/shard_map/ppermute | solution.py:42
  513.3 14.3 %collective-permute-start.41 = (bf16[2,4,2,32,512]{4,3,2,1,0:T(8,128)(2,1)S(1)}, bf16[2,4,2,32,512]{4,3,2,1,0:T(8,128)(2,1)S(1)}, u32[]{:S(2)}, u32[]{:S(2)}) collective-permute-start(bf16[2,4,2,32,512]{4,3,2,1,0:T(8,128)(2,1)S(1)} %pad_maximum_fusion.5), channel_id=1, source_target_pairs={{0,16},{8,24},{16,32},{24,40},{32,48},{40,56},{48,0},{56,8},{1,17}... | collective-permute-start | bytes 1572872 | tf_op jit(solution)/shard_map/ppermute | solution.py:42
  514.7 16.7 %collective-permute-start.50 = (bf16[2,2,32,512]{3,2,1,0:T(8,128)(2,1)S(1)}, bf16[2,2,32,512]{3,2,1,0:T(8,128)(2,1)S(1)}, u32[]{:S(2)}, u32[]{:S(2)}) collective-permute-start(bf16[2,2,32,512]{3,2,1,0:T(8,128)(2,1)S(1)} %get-tuple-element.107), channel_id=1, source_target_pairs={{0,48},{8,56},{16,0},{24,8},{32,16},{40,24},{48,32},{56,40},{1,49}... | collective-permute-start | bytes 393224 | tf_op jit(solution)/shard_map/ppermute | solution.py:42
  518.1 14.0 %collective-permute-start.49 = (bf16[2,2,32,512]{3,2,1,0:T(8,128)(2,1)S(1)}, bf16[2,2,32,512]{3,2,1,0:T(8,128)(2,1)S(1)}, u32[]{:S(2)}, u32[]{:S(2)}) collective-permute-start(bf16[2,2,32,512]{3,2,1,0:T(8,128)(2,1)S(1)} %get-tuple-element.108), channel_id=1, source_target_pairs={{0,32},{8,40},{16,48},{24,56},{32,0},{40,8},{48,16},{56,24},{1,33}... | collective-permute-start | bytes 393224 | tf_op jit(solution)/shard_map/ppermute | solution.py:42
  518.1 14.0 %collective-permute-start.48 = (bf16[2,2,32,512]{3,2,1,0:T(8,128)(2,1)S(1)}, bf16[2,2,32,512]{3,2,1,0:T(8,128)(2,1)S(1)}, u32[]{:S(2)}, u32[]{:S(2)}) collective-permute-start(bf16[2,2,32,512]{3,2,1,0:T(8,128)(2,1)S(1)} %get-tuple-element.106), channel_id=1, source_target_pairs={{0,16},{8,24},{16,32},{24,40},{32,48},{40,56},{48,0},{56,8},{1,17}... | collective-permute-start | bytes 393224 | tf_op jit(solution)/shard_map/ppermute | solution.py:42
  538.1 10.9 %collective-permute-start.51 = (bf16[2,208,512]{2,1,0:T(8,128)(2,1)S(1)}, bf16[2,208,512]{2,1,0:T(8,128)(2,1)S(1)}, u32[]{:S(2)}, u32[]{:S(2)}) collective-permute-start(bf16[2,208,512]{2,1,0:T(8,128)(2,1)S(1)} %fusion.17), channel_id=1, source_target_pairs={{0,8},{8,0},{16,24},{24,16},{32,40},{40,32},{48,56},{56,48},{1,9},... | collective-permute-start | bytes 1277960 | tf_op jit(solution)/shard_map/ppermute | solution.py:47
  549.2 8.9 %collective-permute-start.52 = (bf16[208,512]{1,0:T(8,128)(2,1)S(1)}, bf16[208,512]{1,0:T(8,128)(2,1)S(1)}, u32[]{:S(2)}, u32[]{:S(2)}) collective-permute-start(bf16[208,512]{1,0:T(8,128)(2,1)S(1)} %fusion.23), channel_id=1, source_target_pairs={{0,1},{1,0},{2,3},{3,2},{4,5},{5,4},{6,7},{7,6},{8,9},{9,8},{10,11... | collective-permute-start | bytes 638984 | tf_op jit(solution)/shard_map/ppermute | solution.py:47
  (32 other events, 214.2 us)
Sparse Core Ops, SparseCore 0:
  11.1 124.4 all-gather.2

commit v4 on v3

--- a/solution.py
+++ b/solution.py
@@ -15,7 +15,9 @@
 SCORE_SCALE = DH ** (-0.5)
 SLAB = 16
 SMALL_WIDTH = 512
-QUERY_ROWS = 256
+QUERY_ROWS = 512
+BACK_ROWS = 128
+PIECES = 1
 VMEM_LIMIT = 60 * 1024 * 1024
 
 (
@@ -167,7 +169,8 @@
 def ring_total(terms, ends, axis):
     x_me, _, y_me, _ = coordinates()
     own = piece(terms, x_me, 0) if axis == "dp" else piece(terms, y_me, 2)
-    return sum((end.astype(jnp.float32) for end in ends), own.astype(jnp.float32))
+    total = sum((end.astype(jnp.float32) for end in ends), own.astype(jnp.float32))
+    return total.astype(jnp.bfloat16)
 
 
 def ring_direct(terms, axis, dim, me):
@@ -177,9 +180,14 @@
     return own
 
 
+def ring_first(terms, axis):
+    x_me, _, y_me, _ = coordinates()
+    dim, me = (0, x_me) if axis == "dp" else (2, y_me)
+    return ring_direct(terms, axis, dim, me).astype(jnp.bfloat16)
+
+
 def second_ring(terms, first_axis):
     x_me, _, y_me, _ = coordinates()
-    terms = terms.astype(jnp.bfloat16)
     if first_axis == "dp":
         return ring_direct(terms, "head", 1, y_me)
     return ring_direct(terms, "dp", 0, x_me)
@@ -201,6 +209,14 @@
     size = lax.axis_size("section")
     route = [(i, i + distance) for i in range(size) if 0 <= i + distance < size]
     return lax.ppermute(block, "section", route)
+
+
+def ahead(items, function):
+    value = function(items[0])
+    for at, item in enumerate(items):
+        later = function(items[at + 1]) if at + 1 < len(items) else None
+        yield item, value
+        value = later
 
 
 def norm_stats(rows):
@@ -317,8 +333,8 @@
     return marked(keys, jnp.where(valid, 0.0, MASKED_SCORE))
 
 
-def scaled_queries(block, start, head):
-    queries = block[start : start + QUERY_ROWS, head * DH : (head + 1) * DH]
+def scaled_queries(block, start, count, head):
+    queries = block[start : start + count, head * DH : (head + 1) * DH]
     return marked((queries.astype(jnp.float32) * SCORE_SCALE).astype(jnp.bfloat16), 1.0)
 
 
@@ -329,19 +345,24 @@
     keys = [masked_keys(block, count, head) for head in range(2)]
     values = [block[:, 256 + head * DH : 256 + (head + 1) * DH] for head in range(2)]
     values = [jnp.concatenate([part, jnp.ones_like(part)], axis=1) for part in values]
-    for start in range(0, seq_len, QUERY_ROWS):
-        outs = []
-        for head in range(2):
-            scores = product_nt(keys[head], scaled_queries(block, start, head))
-            largest = jnp.max(scores, axis=0, keepdims=True)
-            weights = jnp.exp(scores - largest)
-            mixed = product_tn(values[head], weights.astype(jnp.bfloat16))
-            total = mixed[DH : DH + 1]
-            outs.append((mixed[:DH] / total).T)
-            lse_ref[0, head : head + 1, start : start + QUERY_ROWS] = largest + jnp.log(total)
-        rows = jnp.concatenate(outs, axis=1).astype(jnp.bfloat16)
-        peers = QUERY_ROWS // 128
-        out_ref[start // 128 : start // 128 + peers, 0] = rows.reshape(peers, 128, 128)
+    outs = []
+
+    def scores_of(item):
+        start, head = item
+        return product_nt(keys[head], scaled_queries(block, start, QUERY_ROWS, head))
+
+    items = [(start, head) for start in range(0, seq_len, QUERY_ROWS) for head in range(2)]
+    for (start, head), scores in ahead(items, scores_of):
+        largest = jnp.max(scores, axis=0, keepdims=True)
+        weights = jnp.exp(scores - largest)
+        mixed = product_tn(values[head], weights.astype(jnp.bfloat16))
+        total = mixed[DH : DH + 1]
+        outs.append((mixed[:DH] / total).T)
+        lse_ref[0, head : head + 1, start : start + QUERY_ROWS] = largest + jnp.log(total)
+        if head == 1:
+            rows = jnp.concatenate(outs[-2:], axis=1).astype(jnp.bfloat16)
+            peers = QUERY_ROWS // 128
+            out_ref[start // 128 : start // 128 + peers, 0] = rows.reshape(peers, 128, 128)
 
 
 def attend_back_kernel(count_ref, grad_ref, heads_ref, lse_ref, out_ref):
@@ -349,36 +370,45 @@
     block = flat(heads_ref[:, 0])
     grads = flat(grad_ref[:, 0])
     seq_len = block.shape[0]
-    peers = QUERY_ROWS // 128
+    peers = BACK_ROWS // 128
     keys = [masked_keys(block, count, head) for head in range(2)]
     values = [block[:, 256 + head * DH : 256 + (head + 1) * DH] for head in range(2)]
     key_sums = [jnp.zeros((seq_len, DH), jnp.float32) for _ in range(2)]
     value_sums = [jnp.zeros((seq_len, DH), jnp.float32) for _ in range(2)]
-    for start in range(0, seq_len, QUERY_ROWS):
-        outs = []
-        for head in range(2):
-            queries = scaled_queries(block, start, head)
-            grad_rows = grads[start : start + QUERY_ROWS, head * DH : (head + 1) * DH]
-            lse = lse_ref[0, head : head + 1, start : start + QUERY_ROWS]
-            weights = jnp.exp(product_nt(keys[head], queries) - lse)
-            grad_weights = product_nt(values[head], grad_rows)
-            dots = jnp.sum(weights * grad_weights, axis=0, keepdims=True)
-            grad_scores = (weights * (grad_weights - dots)).astype(jnp.bfloat16)
-            value_sums[head] += product(weights.astype(jnp.bfloat16), grad_rows)
-            key_sums[head] += product(grad_scores, queries[:, :DH])
-            outs.append((product_tn(keys[head][:, :DH], grad_scores) * SCORE_SCALE).T)
-        rows = jnp.concatenate(outs, axis=1).astype(jnp.bfloat16)
-        out_ref[start // 128 : start // 128 + peers, 0, :, :128] = rows.reshape(peers, 128, 128)
+    outs = []
+
+    def products_of(item):
+        start, head = item
+        queries = scaled_queries(block, start, BACK_ROWS, head)
+        grad_rows = grads[start : start + BACK_ROWS, head * DH : (head + 1) * DH]
+        scores = product_nt(keys[head], queries)
+        return queries, grad_rows, scores, product_nt(values[head], grad_rows)
+
+    items = [(start, head) for start in range(0, seq_len, BACK_ROWS) for head in range(2)]
+    for (start, head), members in ahead(items, products_of):
+        queries, grad_rows, scores, grad_weights = members
+        weights = jnp.exp(scores - lse_ref[0, head : head + 1, start : start + BACK_ROWS])
+        shares = weights * grad_weights
+        dots = jnp.sum(shares, axis=0, keepdims=True)
+        grad_scores = (shares - weights * dots).astype(jnp.bfloat16)
+        value_sums[head] += product(weights.astype(jnp.bfloat16), grad_rows)
+        key_sums[head] += product(grad_scores, queries[:, :DH])
+        outs.append((product_tn(keys[head][:, :DH], grad_scores) * SCORE_SCALE).T)
+        if head == 1:
+            rows = jnp.concatenate(outs[-2:], axis=1).astype(jnp.bfloat16)
+            at = start // 128
+            out_ref[at : at + peers, 0, :, :128] = rows.reshape(peers, 128, 128)
     key_rows = jnp.concatenate(key_sums, axis=1).astype(jnp.bfloat16)
     value_rows = jnp.concatenate(value_sums, axis=1).astype(jnp.bfloat16)
     out_ref[:, 0, :, 128:256] = key_rows.reshape(-1, 128, 128)
     out_ref[:, 0, :, 256:] = value_rows.reshape(-1, 128, 128)
 
 
-def hidden_halves(fc1_ref, fc2_ref):
-    columns, owners = fc1_ref.shape[2] // 2, fc2_ref.shape[0] // 2
+def hidden_pieces(fc1_ref, fc2_ref):
+    columns, owners = fc1_ref.shape[2] // PIECES, fc2_ref.shape[0] // PIECES
     return [
-        (at * columns, (at + 1) * columns, at * owners, (at + 1) * owners) for at in range(2)
+        (slice(at * columns, (at + 1) * columns), slice(at * owners, (at + 1) * owners))
+        for at in range(PIECES)
     ]
 
 
@@ -405,12 +435,15 @@
 
     adds = table_ref[pl.ds(HIDDEN_ROW + step, 1), :]
     actives, mixed = [], 0.0
-    for low, high, rows_from, rows_to in hidden_halves(fc1_ref, fc2_ref):
-        hidden = product(normed[...], flat(fc1_ref[:, :, low:high])) + adds[:, low:high]
+
+    def hidden_of(item):
+        return product(normed[...], flat(fc1_ref[:, :, item[0]])) + adds[:, item[0]]
+
+    for (columns, owners), hidden in ahead(hidden_pieces(fc1_ref, fc2_ref), hidden_of):
         if keep:
-            hidden_ref[:, low:high] = hidden
+            hidden_ref[:, columns] = hidden
         actives.append((hidden * cumulative(hidden)).astype(jnp.bfloat16))
-        mixed += product(actives[-1], flat(fc2_ref[rows_from:rows_to]))
+        mixed += product(actives[-1], flat(fc2_ref[owners]))
     if keep:
         put_column(left_ref, step, jnp.concatenate(actives, axis=1))
     total[...] += mixed
@@ -460,13 +493,17 @@
             put_right(MLP_GRAD, mlp_low[...])
 
     lows, sums, mixed = [], [], 0.0
-    for low, high, rows_from, rows_to in hidden_halves(fc1_ref, fc2_ref):
-        hidden = hidden_ref[:, low:high]
+
+    def active_grad_of(item):
+        return product_nt(mlp_low[...], flat(fc2_ref[item[1]]))
+
+    for (columns, _), grad in ahead(hidden_pieces(fc1_ref, fc2_ref), active_grad_of):
+        hidden = hidden_ref[:, columns]
         slope = cumulative(hidden) + hidden * (jnp.exp(-0.5 * hidden * hidden) * DENSITY_SCALE)
-        grad_hidden = product_nt(mlp_low[...], flat(fc2_ref[rows_from:rows_to])) * slope
+        grad_hidden = grad * slope
         lows.append(grad_hidden.astype(jnp.bfloat16))
         sums.append(column_sum(grad_hidden))
-        mixed += product_nt(lows[-1], flat(fc1_ref[:, :, low:high]))
+        mixed += product_nt(lows[-1], flat(fc1_ref[:, :, columns]))
     total[...] += mixed
     if keep:
         sums_ref[pl.ds(HIDDEN_ROW + step, 1), :] = jnp.concatenate(sums, axis=1)
@@ -579,16 +616,16 @@
         fc1_proj_ref[:, start:] = proj.reshape(devices, SLAB, half)
 
 
-def attn_weights_kernel(parts, core_ref, left_ref, left_other_ref, grad_ref, got_ref, *rest):
-    out_ref = rest[-1]
-    devices, _, half = out_ref.shape
-    for at, part in enumerate(parts):
+def attn_weights_kernel(
+    core_ref, left_ref, left_other_ref, grad_ref, got_ref, small_ref, query_key_ref, value_ref
+):
+    devices, _, half = value_ref.shape
+    for part, ref, start in ((0, query_key_ref, 0), (1, query_key_ref, SLAB), (2, value_ref, 0)):
         right = side_by_side(grad_ref, part * 128, core_ref[0] * 4, 4)
         right_other = side_by_side(got_ref, part * 128, 0, 4)
         grad = both_products(left_ref, left_other_ref, right, right_other)
-        out_ref[:, at * SLAB : (at + 1) * SLAB] = grad.reshape(devices, SLAB, half)
-    if len(rest) > 1:
-        out_ref[:, len(parts) * SLAB :] = rest[0][...]
+        ref[:, start : start + SLAB] = grad.reshape(devices, SLAB, half)
+    value_ref[:, SLAB:] = small_ref[...]
 
 
 def like(*shape, dtype=jnp.bfloat16):
@@ -797,19 +834,19 @@
     )(*(left, left_other) * 3, *(right, right_other) * 3)
 
 
-def call_attn_weights(parts, core, devices, left, left_other, grads, got, *small):
+def call_attn_weights(core, left, left_other, grads, got, small):
     column = pl.BlockSpec((left.shape[0], 1024), lambda i: (0, ATTN_NORMED))
-    shape = like(devices, (len(parts) + len(small)) * SLAB, 512)
+    shape = like(small.shape[0], 2 * SLAB, 512)
     return pl.pallas_call(
-        functools.partial(attn_weights_kernel, parts),
+        attn_weights_kernel,
         grid=(1,),
         in_specs=[SCALARS, column, column]
-        + [whole_block(operand) for operand in (grads, got, *small)],
-        out_specs=whole_block(shape),
-        out_shape=shape,
+        + [whole_block(operand) for operand in (grads, got, small)],
+        out_specs=[whole_block(shape), whole_block(shape)],
+        out_shape=[shape, shape],
         compiler_params=params(),
-        cost_estimate=takes(3),
-    )(core, left, left_other, grads, got, *small)
+        cost_estimate=takes(8),
+    )(core, left, left_other, grads, got, small)
 
 
 def small_slab(vectors, hidden_vector):
@@ -942,35 +979,25 @@
     mlp_ends = [ring_ends(*item) for item in zip(mlp_terms, mlp_halves, ways)]
 
     got = swap(lax.dynamic_slice_in_dim(grad_qkv, (1 - core[0]) * 4, 4), "head")
-    query_key = call_attn_weights((0, 1), core, devices, left, left_other, grad_qkv, got)
     input_grad, front_sums = call_front_back(
-        True, core, after(grad_qkv, query_key), grad_middle, x, table, early
+        True, core, grad_qkv, grad_middle, x, table, early
     )
     small = slabs_of(rear_sums + front_sums, devices)
-    value = call_attn_weights((2,), core, devices, left, left_other, grad_qkv, got, small)
-    attn_terms = [by_chip(query_key), by_chip(value)]
-    attn_halves = [ring_halves(terms, way) for terms, way in zip(attn_terms, ways)]
+    attn_terms = call_attn_weights(core, left, left_other, grad_qkv, got, small)
+    attn_terms = [by_chip(terms) for terms in attn_terms]
     mlp_ends = after(mlp_ends, attn_terms)
-    mlp_terms = [ring_total(*item) for item in zip(mlp_terms, mlp_ends, ways)]
-    attn_ends = [ring_ends(*item) for item in zip(attn_terms, attn_halves, ways)]
-    mlp_terms = after(mlp_terms, attn_halves)
-    attn_terms = [ring_total(*item) for item in zip(attn_terms, attn_ends, ways)]
+    attn_totals = [ring_first(*item) for item in zip(attn_terms, ways)]
+    mlp_totals = [ring_total(*item) for item in zip(mlp_terms, mlp_ends, ways)]
     ring_sums = [
-        second_ring(terms, way)
-        for terms, way in zip(mlp_terms + attn_terms, ways + ways)
+        second_ring(jnp.concatenate(totals, axis=3), way)
+        for *totals, way in zip(mlp_totals, attn_totals, ways)
     ]
     shard_grad = collect_rest(jnp.concatenate(ring_sums, axis=2))
-    fc1_grad, fc2_grad, proj_grad, qkv_grad, small_row = (
-        shard_grad[start:stop]
-        for start, stop in (
-            (0, 4 * SLAB),
-            (5 * SLAB, 9 * SLAB),
-            (4 * SLAB, 5 * SLAB),
-            (9 * SLAB, 12 * SLAB),
-            (12 * SLAB, 12 * SLAB + 1),
-        )
-    )
-    qkv_grad = from_column_slabs(qkv_grad)
+    fc1_grad, proj_grad, query_key_grad, fc2_grad, value_grad, small_row = (
+        shard_grad[start * SLAB : stop * SLAB]
+        for start, stop in ((0, 4), (4, 5), (5, 7), (7, 11), (11, 12), (12, 13))
+    )
+    qkv_grad = from_column_slabs(jnp.concatenate([query_key_grad, value_grad]))
     row = small_row[0, :SMALL_WIDTH] + small_row[0, SMALL_WIDTH:]
     small_grads = row[: HIDDEN_ROW * SLAB].reshape(HIDDEN_ROW, SLAB)
     fc1_bias_grad = row[HIDDEN_ROW * SLAB : HIDDEN_ROW * SLAB + 64]

time: 579 us -> 548 us (0.946)
  starting transfers between devices: 111 us -> 88.9 us
  Pallas kernels: 165 us -> 146 us
  other arithmetic: 23.3 us -> 29.4 us
    ppermute x42 -> x34, starting transfers between devices: 59.9 us -> 43 us  [hop(): lax.ppermute(block, axis, [(i, (i + 2 * places) % size) for i in range(si...]
    pallas_call x2, Pallas kernels: 28 us -> 15.9 us  [call_attend(): pl.pallas_call(attend_kernel, grid=(images,), in_specs=[SCALARS, pl.Block...]
    convert_element_type x2 -> x5, other arithmetic: 0.5 us -> 7.83 us  [the longest x2 5.12 us: ring_total(): return total.astype(jnp.bfloat16)]
    all_to_all x4, waiting for transfers between devices: 49 us -> 42.3 us  [to_peers(): lax.all_to_all(blocks, 'head', split_axis=0, concat_axis=0, tiled=True)]
    ppermute x42 -> x34, waiting for transfers between devices: 43.7 us -> 46.6 us  [hop(): lax.ppermute(block, axis, [(i, (i + 2 * places) % size) for i in range(si...]
  transfers between devices with their start and end apart: 58 -> 50, of which waited for: 25 -> 19; matrix products, arithmetic and copies ran while one was open for 8% -> 10% of each run, Pallas kernels for 15% -> 14%
where the time goes in v4:
time: 548 us; the launch traced here: 539 us
  Pallas kernels  146 us (27%)
  waiting for transfers between devices  128 us (23%)
  starting transfers between devices  88.9 us (16%)
  blocking collectives  83.1 us (15%)
  local copies, waits for them, and re-layouts  46.5 us (8%)
  other arithmetic  29.4 us (5%)
  between operations  16.5 us (3%)
    all_to_all x4, blocking collectives, to_peers(): lax.all_to_all(blocks, 'head', split_axis=0, concat_axis=0, tiled=True)  83.1 us
    ppermute x34, waiting for transfers between devices, hop(): lax.ppermute(block, axis, [(i, (i + 2 * places) % size) for i in range(si...  46.6 us
    ppermute x34, starting transfers between devices, hop(): lax.ppermute(block, axis, [(i, (i + 2 * places) % size) for i in range(si...  43 us
    all_to_all x4, waiting for transfers between devices, to_peers(): lax.all_to_all(blocks, 'head', split_axis=0, concat_axis=0, tiled=True)  42.3 us
    pallas_call x2, Pallas kernels, call_attend_back(): pl.pallas_call(attend_back_kernel, grid=(images,), in_specs=[SCALARS, pl....  30.1 us
    pallas_call x2, Pallas kernels, call_rear_back(): pl.pallas_call(functools.partial(rear_back_kernel, keep), grid=(steps,),...  29.9 us
    pallas_call x2, Pallas kernels, call_rear(): pl.pallas_call(functools.partial(rear_kernel, keep), grid=(steps,), in_sp...  26.9 us
    ppermute x9, starting transfers between devices, swap(): return lax.ppermute(block, axis, [(i, i ^ 1) for i in range(size)])  25.6 us
  transfers between devices with their start and end apart: 50, of which 19 were waited for; matrix products, arithmetic and copies ran while one was open for 10% of the time, Pallas kernels for 14%

profile of v4, /device:TPU:1, one launch (start us, length us, event | category | flops | bytes accessed | tf_op | source)
XLA Modules:
  0.0 538.8 jit_solution(3336274076059546335)
XLA Ops:
  15.9 3.8 collective-permute-start.1
  19.6 3.6 collective-permute-done.1
  30.1 2.6 collective-permute-start.11
  42.8 2.7 collective-permute-start.14
  48.2 3.4 collective-permute-done.5
  59.8 3.3 collective-permute-start.16
  69.3 7.9 %collective-permute-start.9 = (bf16[64,32,512]{2,1,0:T(8,128)(2,1)S(1)}, bf16[64,32,512]{2,1,0:T(8,128)(2,1)S(1)}, u32[]{:S(2)}, u32[]{:S(2)}) collective-permute-start(bf16[64,32,512]{2,1,0:T(8,128)(2,1)S(1)} %bitcast.258), channel_id=1, source_target_pairs={{0,1},{1,0},{2,3},{3,2},{4,5},{5,4},{6,7},{7,6},{8,9},{9,8},{10,11... | collective-permute-start | bytes 6291464 | tf_op jit(solution)/shard_map/ppermute | solution.py:49
  84.2 3.2 collective-permute-done.17.qk_other_ref
  87.3 6.2 %shard_map.318 = bf16[8,256,384]{2,1,0:T(8,128)(2,1)} custom-call(s32[1]{0:T(128)} %bitcast.2.core_ref, bf16[256,1024]{1,0:T(8,128)(2,1)} %bitcast.253, f32[16,1024]{1,0:T(8,128)} %select_maximum_fusion.table_ref, bf16[64,32,512]{2,1,0:T(8,128)(2,1)} %bitcast.41.qk_mine_ref, bf16[64,32,512]{2,1,0:T(8,128)(2,1)} %bitcast.260, ...), custom_call_target="tpu_custom_call" | custom-call | flops 7474999808 | bytes 19500000 | tf_op jit(solution)/shard_map/pallas_call | solution.py:661
  93.5 4.2 all-to-all-start
  98.5 25.8 %all-to-all-done = bf16[8,256,384]{2,1,0:T(8,128)(2,1)S(1)} async-done(((bf16[8,256,384]{2,1,0:T(8,128)(2,1)}), bf16[8,256,384]{2,1,0:T(8,128)(2,1)S(1)}, u32[]{:S(2)}, u32[]{:S(2)}) %all-to-all-start) | async-done | bytes 1572896 | tf_op jit(solution)/shard_map/all_to_all | solution.py:205
  125.4 8.1 %shard_map.319 = (bf16[8,2,128,128]{3,2,1,0:T(8,128)(2,1)}, f32[2,2,1024]{2,1,0:T(2,128)}) custom-call(s32[2]{0:T(128)} %broadcast_select_fusion.5.count_ref, bf16[8,2,128,384]{3,2,1,0:T(8,128)(2,1)} %bitcast.271), custom_call_target="tpu_custom_call" | custom-call | flops 16444999680 | bytes 42900000 | tf_op jit(solution)/shard_map/pallas_call | solution.py:676
  133.5 15.1 %all_to_all.40.attn_ref = bf16[8,256,128]{2,1,0:T(8,128)(2,1)} all-to-all(bf16[8,256,128]{2,1,0:T(8,128)(2,1)} %bitcast.284), channel_id=1, replica_groups=mesh['section'=2,'dp'=8,'head'=8] {'head'}, dimensions={0} | all-to-all | bytes 1048576 | tf_op jit(solution)/shard_map/all_to_all | solution.py:205
  148.6 11.9 %shard_map.320 = bf16[256,1024]{1,0:T(8,128)(2,1)} custom-call(bf16[256,1024]{1,0:T(8,128)(2,1)} %bitcast.254, bf16[8,256,128]{2,1,0:T(8,128)(2,1)} %all_to_all.40.attn_ref, f32[16,1024]{1,0:T(8,128)} %select_maximum_fusion.table_ref, bf16[64,144,1024]{2,1,0:T(8,128)(2,1)} %bitcast.237, bf16[64,144,1024]{2,1,0:T(8,128)(2,1)} %bitcast.238, ...), custom_call_target="tpu_custom_call" | custom-call | flops 14949999616 | bytes 39000000 | tf_op jit(solution)/shard_map/pallas_call | solution.py:736
  162.5 10.4 %collective-permute-done.18 = bf16[256,1024]{1,0:T(8,128)(2,1)S(1)} collective-permute-done((bf16[256,1024]{1,0:T(8,128)(2,1)}, bf16[256,1024]{1,0:T(8,128)(2,1)S(1)}, u32[]{:S(2)}, u32[]{:S(2)}) %collective-permute-start.18) | collective-permute-done | bytes 524320 | tf_op jit(solution)/shard_map/ppermute | solution.py:211
  173.8 6.2 %shard_map.321 = bf16[8,256,384]{2,1,0:T(8,128)(2,1)} custom-call(s32[1]{0:T(128)} %bitcast.2.core_ref, bf16[256,1024]{1,0:T(8,128)(2,1)} %broadcast_select_fusion.1.x_ref, f32[16,1024]{1,0:T(8,128)} %select_maximum_fusion.table_ref, bf16[64,32,512]{2,1,0:T(8,128)(2,1)} %bitcast.41.qk_mine_ref, bf16[64,32,512]{2,1,0:T(8,128)(2,1)} %bitcast.261, ...), custom_call_target="tpu_custom_call" | custom-call | flops 7474999808 | bytes 19500000 | tf_op jit(solution)/shard_map/pallas_call | solution.py:661
  180.1 27.0 %all_to_all.41 = bf16[8,256,384]{2,1,0:T(8,128)(2,1)} all-to-all(bf16[8,256,384]{2,1,0:T(8,128)(2,1)} %shard_map.321), channel_id=1, replica_groups=mesh['section'=2,'dp'=8,'head'=8] {'head'}, dimensions={0} | all-to-all | bytes 3145728 | tf_op jit(solution)/shard_map/all_to_all | solution.py:205
  207.0 7.8 %shard_map.322 = (bf16[8,2,128,128]{3,2,1,0:T(8,128)(2,1)}, f32[2,2,1024]{2,1,0:T(2,128)}) custom-call(s32[2]{0:T(128)} %broadcast_select_fusion.5.count_ref, bf16[8,2,128,384]{3,2,1,0:T(8,128)(2,1)} %bitcast.267), custom_call_target="tpu_custom_call" | custom-call | flops 16444999680 | bytes 42900000 | tf_op jit(solution)/shard_map/pallas_call | solution.py:676
  214.9 14.9 %all_to_all.42.attn_ref = bf16[8,256,128]{2,1,0:T(8,128)(2,1)} all-to-all(bf16[8,256,128]{2,1,0:T(8,128)(2,1)} %bitcast.285), channel_id=1, replica_groups=mesh['section'=2,'dp'=8,'head'=8] {'head'}, dimensions={0} | all-to-all | bytes 1048576 | tf_op jit(solution)/shard_map/all_to_all | solution.py:205
  229.8 15.0 %shard_map.323 = (bf16[256,1024]{1,0:T(8,128)(2,1)}, f32[256,1024]{1,0:T(8,128)}, f32[256,4096]{1,0:T(8,128)}, f32[256,1024]{1,0:T(8,128)}, bf16[256,7168]{1,0:T(8,128)(2,1)}) custom-call(bf16[256,1024]{1,0:T(8,128)(2,1)} %broadcast_select_fusion.1.x_ref, bf16[8,256,128]{2,1,0:T(8,128)(2,1)} %all_to_all.42.attn_ref, ...), custom_call_target="tpu_custom_call" | custom-call | flops 14949999616 | bytes 39000000 | tf_op jit(solution)/shard_map/pallas_call | solution.py:736
  244.9 14.1 %shard_map.324 = (bf16[8,256,128]{2,1,0:T(8,128)(2,1)}, f32[256,1024]{1,0:T(8,128)}) custom-call(s32[1]{0:T(128)} %bitcast.2.core_ref, bf16[256,1024]{1,0:T(8,128)(2,1)} %bitcast.278, bf16[256,1024]{1,0:T(8,128)(2,1)} %broadcast_select_fusion.1.x_ref, f32[256,1024]{1,0:T(8,128)} %get-tuple-element.48.branch_ref, f32[256,4096]{1,0:T(8,128)} %get-tuple-element.49.hidden_ref, ...), custom_call_target="tpu_custom_call" | custom-call | flops 18400000000 | bytes 48000000 | tf_op jit(solution)/shard_map/pallas_call | solution.py:765
  259.0 4.4 all-to-all-start.4
  263.6 9.3 %all-to-all-done.4 = bf16[8,256,128]{2,1,0:T(8,128)(2,1)S(1)} async-done(((bf16[8,256,128]{2,1,0:T(8,128)(2,1)}), bf16[8,256,128]{2,1,0:T(8,128)(2,1)S(1)}, u32[]{:S(2)}, u32[]{:S(2)}) %all-to-all-start.4) | async-done | bytes 524320 | tf_op jit(solution)/shard_map/all_to_all | solution.py:205
  273.7 15.0 %shard_map.325 = bf16[8,2,128,384]{3,2,1,0:T(8,128)(2,1)} custom-call(s32[2]{0:T(128)} %broadcast_select_fusion.5.count_ref, bf16[8,2,128,128]{3,2,1,0:T(8,128)(2,1)} %bitcast.283, bf16[8,2,128,384]{3,2,1,0:T(8,128)(2,1)} %bitcast.268, f32[2,2,1024]{2,1,0:T(2,128)} %get-tuple-element.52.lse_ref), custom_call_target="tpu_custom_call" | custom-call | flops 18975000576 | bytes 49500000 | tf_op jit(solution)/shard_map/pallas_call | solution.py:698
  288.8 26.1 %all_to_all.43.grad_ref = bf16[8,256,384]{2,1,0:T(8,128)(2,1)} all-to-all(bf16[8,256,384]{2,1,0:T(8,128)(2,1)} %bitcast.272), channel_id=1, replica_groups=mesh['section'=2,'dp'=8,'head'=8] {'head'}, dimensions={0} | all-to-all | bytes 3145728 | tf_op jit(solution)/shard_map/all_to_all | solution.py:205
  314.9 6.7 %shard_map.326 = bf16[256,1024]{1,0:T(8,128)(2,1)} custom-call(s32[1]{0:T(128)} %bitcast.2.core_ref, bf16[8,256,384]{2,1,0:T(8,128)(2,1)} %all_to_all.43.grad_ref, f32[256,1024]{1,0:T(8,128)} %get-tuple-element.53.middle_grad_ref, bf16[256,1024]{1,0:T(8,128)(2,1)} %broadcast_select_fusion.1.x_ref, f32[16,1024]{1,0:T(8,128)} %select_maximum_fusion.table_ref, ...), custom_call_target="tpu_custom_call" | custom-call | flops 8049999872 | bytes 21000000 | tf_op jit(solution)/shard_map/pallas_call | solution.py:795
  322.9 13.2 %collective-permute-done.20 = bf16[256,1024]{1,0:T(8,128)(2,1)S(1)} collective-permute-done((bf16[256,1024]{1,0:T(8,128)(2,1)}, bf16[256,1024]{1,0:T(8,128)(2,1)S(1)}, u32[]{:S(2)}, u32[]{:S(2)}) %collective-permute-start.20) | collective-permute-done | bytes 524320 | tf_op jit(solution)/shard_map/ppermute | solution.py:211
  337.0 15.8 %shard_map.327 = (bf16[8,256,128]{2,1,0:T(8,128)(2,1)}, f32[256,1024]{1,0:T(8,128)}, bf16[256,3072]{1,0:T(8,128)(2,1)}, bf16[256,3072]{1,0:T(8,128)(2,1)}, f32[16,1024]{1,0:T(8,128)}) custom-call(s32[1]{0:T(128)} %bitcast.2.core_ref, bf16[256,1024]{1,0:T(8,128)(2,1)} %broadcast_select_fusion.grad_ref, bf16[256,1024]{1,0:T(8,128)(2,1)} %broadcast_select_fusion.1.x_ref, ...), custom_call_target="tpu_custom_call" | custom-call | flops 18400000000 | bytes 48000000 | tf_op jit(solution)/shard_map/pallas_call | solution.py:765
  354.7 3.5 all-to-all-start.6
  359.4 11.7 %shard_map.328 = (bf16[64,80,512]{2,1,0:T(8,128)(2,1)}, bf16[64,64,512]{2,1,0:T(8,128)(2,1)}) custom-call(bf16[256,7168]{1,0:T(8,128)(2,1)} %get-tuple-element.54.active_ref.normed_ref.attn_ref.left_ref, bf16[256,7168]{1,0:T(8,128)(2,1)} %collective-permute-done.19.active_other_ref.normed_other_ref.attn_other_ref.left_other_ref, ...), custom_call_target="tpu_custom_call" | custom-call | flops 10350000128 | bytes 27000000 | tf_op jit(solution)/shard_map/pallas_call | solution.py:818
  374.1 2.7 collective-permute-start.23
  380.9 15.1 %shard_map.329 = bf16[8,2,128,384]{3,2,1,0:T(8,128)(2,1)} custom-call(s32[2]{0:T(128)} %broadcast_select_fusion.5.count_ref, bf16[8,2,128,128]{3,2,1,0:T(8,128)(2,1)} %bitcast.282, bf16[8,2,128,384]{3,2,1,0:T(8,128)(2,1)} %bitcast.269, f32[2,2,1024]{2,1,0:T(2,128)} %get-tuple-element.52.lse_ref), custom_call_target="tpu_custom_call" | custom-call | flops 18975000576 | bytes 49500000 | tf_op jit(solution)/shard_map/pallas_call | solution.py:698
  396.8 4.8 all-to-all-start.7
  412.4 2.7 collective-permute-start.27
  415.1 7.2 %all-to-all-done.7.grad_ref = bf16[8,256,384]{2,1,0:T(8,128)(2,1)S(1)} async-done(((bf16[8,256,384]{2,1,0:T(8,128)(2,1)}), bf16[8,256,384]{2,1,0:T(8,128)(2,1)S(1)}, u32[]{:S(2)}, u32[]{:S(2)}) %all-to-all-start.7) | async-done | bytes 1572896 | tf_op jit(solution)/shard_map/all_to_all | solution.py:205
  425.0 7.0 %shard_map.330 = (bf16[256,1024]{1,0:T(8,128)(2,1)}, f32[16,1024]{1,0:T(8,128)}) custom-call(s32[1]{0:T(128)} %bitcast.2.core_ref, bf16[8,256,384]{2,1,0:T(8,128)(2,1)} %copy-done.7, f32[256,1024]{1,0:T(8,128)} %get-tuple-element.63.middle_grad_ref, bf16[256,1024]{1,0:T(8,128)(2,1)} %broadcast_select_fusion.1.x_ref, ...), custom_call_target="tpu_custom_call" | custom-call | flops 8049999872 | bytes 21000000 | tf_op jit(solution)/shard_map/pallas_call | solution.py:795
  434.6 5.6 %shard_map.331 = (bf16[64,32,512]{2,1,0:T(8,128)(2,1)}, bf16[64,32,512]{2,1,0:T(8,128)(2,1)}) custom-call(s32[1]{0:T(128)} %bitcast.2.core_ref, bf16[256,7168]{1,0:T(8,128)(2,1)} %get-tuple-element.54.active_ref.normed_ref.attn_ref.left_ref, bf16[256,7168]{1,0:T(8,128)(2,1)} %collective-permute-done.19.active_other_ref.normed_other_ref.attn_other_ref.left_other_ref, ...), custom_call_target="tpu_custom_call" | custom-call | flops 9200000000 | bytes 24000000 | tf_op jit(solution)/shard_map/pallas_call | solution.py:840
  440.2 2.7 dynamic-slice_bitcast_fusion.14
  448.1 2.7 fusion
  450.9 5.9 %collective-permute-done.39 = bf16[4,2,2,32,512]{4,3,2,1,0:T(8,128)(2,1)} collective-permute-done((bf16[4,2,2,32,512]{4,3,2,1,0:T(8,128)(2,1)}, bf16[4,2,2,32,512]{4,3,2,1,0:T(8,128)(2,1)}, u32[]{:S(2)}, u32[]{:S(2)}) %collective-permute-start.39) | collective-permute-done | bytes 524320 | tf_op jit(solution)/shard_map/ppermute | solution.py:44
  459.1 13.7 %collective-permute-done.37 = bf16[4,2,2,32,512]{4,3,2,1,0:T(8,128)(2,1)S(1)} collective-permute-done((bf16[4,2,2,32,512]{4,3,2,1,0:T(8,128)(2,1)S(1)}, bf16[4,2,2,32,512]{4,3,2,1,0:T(8,128)(2,1)S(1)}, u32[]{:S(2)}, u32[]{:S(2)}) %collective-permute-start.37) | collective-permute-done | bytes 524320 | tf_op jit(solution)/shard_map/ppermute | solution.py:44
  475.4 3.0 collective-permute-start.42
  482.9 11.7 %collective-permute-done.42 = bf16[2,2,96,512]{3,2,1,0:T(8,128)(2,1)S(1)} collective-permute-done((bf16[2,2,96,512]{3,2,1,0:T(8,128)(2,1)S(1)}, bf16[2,2,96,512]{3,2,1,0:T(8,128)(2,1)S(1)}, u32[]{:S(2)}, u32[]{:S(2)}) %collective-permute-start.42) | collective-permute-done | bytes 393248 | tf_op jit(solution)/shard_map/ppermute | solution.py:44
  495.4 3.2 collective-permute-done.40
  499.9 6.7 %collective-permute-done.34 = bf16[2,2,112,512]{3,2,1,0:T(8,128)(2,1)} collective-permute-done((bf16[2,2,112,512]{3,2,1,0:T(8,128)(2,1)}, bf16[2,2,112,512]{3,2,1,0:T(8,128)(2,1)}, u32[]{:S(2)}, u32[]{:S(2)}) %collective-permute-start.34) | collective-permute-done | bytes 458784 | tf_op jit(solution)/shard_map/ppermute | solution.py:44
  509.0 5.4 %collective-permute-start.43 = (bf16[2,208,512]{2,1,0:T(8,128)(2,1)}, bf16[2,208,512]{2,1,0:T(8,128)(2,1)S(1)}, u32[]{:S(2)}, u32[]{:S(2)}) collective-permute-start(bf16[2,208,512]{2,1,0:T(8,128)(2,1)} %fusion.31), channel_id=1, source_target_pairs={{0,8},{8,0},{16,24},{24,16},{32,40},{40,32},{48,56},{56,48},{1,9},... | collective-permute-start | bytes 1277960 | tf_op jit(solution)/shard_map/ppermute | solution.py:49
  514.4 7.9 %collective-permute-done.43 = bf16[2,208,512]{2,1,0:T(8,128)(2,1)S(1)} collective-permute-done((bf16[2,208,512]{2,1,0:T(8,128)(2,1)}, bf16[2,208,512]{2,1,0:T(8,128)(2,1)S(1)}, u32[]{:S(2)}, u32[]{:S(2)}) %collective-permute-start.43) | collective-permute-done | bytes 426016 | tf_op jit(solution)/shard_map/ppermute | solution.py:49
  522.5 3.1 collective-permute-start.44
  (234 shorter events, 108.3 us)
Async XLA Ops:
  7.2 141.4 %all-gather.3.cloned.1.call-start = ((), (), s32[]{:S(2)}) async-start(), calls=%async_computation.8 | async-start | bytes 19169280 | tf_op jit(solution)/shard_map/all_gather | solution.py:930
  15.9 7.3 %collective-permute-start.1 = (bf16[2,64,512]{2,1,0:T(8,128)(2,1)S(1)}, bf16[2,64,512]{2,1,0:T(8,128)(2,1)S(1)}, u32[]{:S(2)}, u32[]{:S(2)}) collective-permute-start(bf16[2,64,512]{2,1,0:T(8,128)(2,1)S(1)} %maximum_select_fusion.3), channel_id=1, source_target_pairs={{0,8},{8,0},{16,24},{24,16},{32,40},{40,32},{48,56},{56,48},{1,9},... | collective-permute-start | bytes 393224 | tf_op jit(solution)/shard_map/ppermute | solution.py:49
  24.0 10.1 %collective-permute-start.2 = (bf16[2,2,32,512]{3,2,1,0:T(8,128)(2,1)}, bf16[2,2,32,512]{3,2,1,0:T(8,128)(2,1)S(1)}, u32[]{:S(2)}, u32[]{:S(2)}) collective-permute-start(bf16[2,2,32,512]{3,2,1,0:T(8,128)(2,1)} %get-tuple-element.101.given_ref), channel_id=1, source_target_pairs={{0,16},{8,24},{16,32},{24,40},{32,48},{40,56},{48,0},{56,8},{1,17}... | collective-permute-start | bytes 393224 | tf_op jit(solution)/shard_map/ppermute | solution.py:44
  25.2 11.3 %collective-permute-start.3 = (bf16[2,2,32,512]{3,2,1,0:T(8,128)(2,1)}, bf16[2,2,32,512]{3,2,1,0:T(8,128)(2,1)S(1)}, u32[]{:S(2)}, u32[]{:S(2)}) collective-permute-start(bf16[2,2,32,512]{3,2,1,0:T(8,128)(2,1)} %get-tuple-element.101.given_ref), channel_id=1, source_target_pairs={{0,32},{8,40},{16,48},{24,56},{32,0},{40,8},{48,16},{56,24},{1,33}... | collective-permute-start | bytes 393224 | tf_op jit(solution)/shard_map/ppermute | solution.py:44
  27.6 9.5 %collective-permute-start.4 = (bf16[2,2,32,512]{3,2,1,0:T(8,128)(2,1)}, bf16[2,2,32,512]{3,2,1,0:T(8,128)(2,1)S(1)}, u32[]{:S(2)}, u32[]{:S(2)}) collective-permute-start(bf16[2,2,32,512]{3,2,1,0:T(8,128)(2,1)} %get-tuple-element.101.given_ref), channel_id=1, source_target_pairs={{0,48},{8,56},{16,0},{24,8},{32,16},{40,24},{48,32},{56,40},{1,49}... | collective-permute-start | bytes 393224 | tf_op jit(solution)/shard_map/ppermute | solution.py:44
  28.8 12.0 %collective-permute-start.10 = (bf16[2,2,32,512]{3,2,1,0:T(8,128)(2,1)}, bf16[2,2,32,512]{3,2,1,0:T(8,128)(2,1)S(1)}, u32[]{:S(2)}, u32[]{:S(2)}) collective-permute-start(bf16[2,2,32,512]{3,2,1,0:T(8,128)(2,1)} %get-tuple-element.100.given_ref), channel_id=1, source_target_pairs={{0,2},{1,3},{2,4},{3,5},{4,6},{5,7},{6,0},{7,1},{8,10},{9,11},{10,... | collective-permute-start | bytes 393224 | tf_op jit(solution)/shard_map/ppermute | solution.py:44
  30.1 11.4 %collective-permute-start.11 = (bf16[2,2,32,512]{3,2,1,0:T(8,128)(2,1)}, bf16[2,2,32,512]{3,2,1,0:T(8,128)(2,1)S(1)}, u32[]{:S(2)}, u32[]{:S(2)}) collective-permute-start(bf16[2,2,32,512]{3,2,1,0:T(8,128)(2,1)} %get-tuple-element.100.given_ref), channel_id=1, source_target_pairs={{0,4},{1,5},{2,6},{3,7},{4,0},{5,1},{6,2},{7,3},{8,12},{9,13},{10,... | collective-permute-start | bytes 393224 | tf_op jit(solution)/shard_map/ppermute | solution.py:44
  34.0 8.1 %collective-permute-start.12 = (bf16[2,2,32,512]{3,2,1,0:T(8,128)(2,1)}, bf16[2,2,32,512]{3,2,1,0:T(8,128)(2,1)S(1)}, u32[]{:S(2)}, u32[]{:S(2)}) collective-permute-start(bf16[2,2,32,512]{3,2,1,0:T(8,128)(2,1)} %get-tuple-element.100.given_ref), channel_id=1, source_target_pairs={{0,6},{1,7},{2,0},{3,1},{4,2},{5,3},{6,4},{7,5},{8,14},{9,15},{10,... | collective-permute-start | bytes 393224 | tf_op jit(solution)/shard_map/ppermute | solution.py:44
  37.8 13.8 %collective-permute-start.5 = (bf16[4,2,2,32,512]{4,3,2,1,0:T(8,128)(2,1)}, bf16[4,2,2,32,512]{4,3,2,1,0:T(8,128)(2,1)}, u32[]{:S(2)}, u32[]{:S(2)}) collective-permute-start(bf16[4,2,2,32,512]{4,3,2,1,0:T(8,128)(2,1)} %bitcast_dynamic-update-slice_fusion.14.given_ref), channel_id=1, source_target_pairs={{0,2},{1,3},{2,4},{3,5},{4,6},{5,7},{6,0},{7,1},{8,10},{9,11},{10,... | collective-permute-start | bytes 1572872 | tf_op jit(solution)/shard_map/ppermute | solution.py:44
  39.1 15.2 %collective-permute-start.6 = (bf16[4,2,2,32,512]{4,3,2,1,0:T(8,128)(2,1)}, bf16[4,2,2,32,512]{4,3,2,1,0:T(8,128)(2,1)}, u32[]{:S(2)}, u32[]{:S(2)}) collective-permute-start(bf16[4,2,2,32,512]{4,3,2,1,0:T(8,128)(2,1)} %bitcast_dynamic-update-slice_fusion.14.given_ref), channel_id=1, source_target_pairs={{0,6},{1,7},{2,0},{3,1},{4,2},{5,3},{6,4},{7,5},{8,14},{9,15},{10,... | collective-permute-start | bytes 1572872 | tf_op jit(solution)/shard_map/ppermute | solution.py:44
  42.8 15.0 %collective-permute-start.13 = (bf16[2,4,2,32,512]{4,3,2,1,0:T(8,128)(2,1)}, bf16[2,4,2,32,512]{4,3,2,1,0:T(8,128)(2,1)}, u32[]{:S(2)}, u32[]{:S(2)}) collective-permute-start(bf16[2,4,2,32,512]{4,3,2,1,0:T(8,128)(2,1)} %bitcast_dynamic-update-slice_fusion.13.given_ref), channel_id=1, source_target_pairs={{0,16},{8,24},{16,32},{24,40},{32,48},{40,56},{48,0},{56,8},{1,17}... | collective-permute-start | bytes 1572872 | tf_op jit(solution)/shard_map/ppermute | solution.py:44
  42.8 16.0 %collective-permute-start.14 = (bf16[2,4,2,32,512]{4,3,2,1,0:T(8,128)(2,1)}, bf16[2,4,2,32,512]{4,3,2,1,0:T(8,128)(2,1)}, u32[]{:S(2)}, u32[]{:S(2)}) collective-permute-start(bf16[2,4,2,32,512]{4,3,2,1,0:T(8,128)(2,1)} %bitcast_dynamic-update-slice_fusion.13.given_ref), channel_id=1, source_target_pairs={{0,48},{8,56},{16,0},{24,8},{32,16},{40,24},{48,32},{56,40},{1,49}... | collective-permute-start | bytes 1572872 | tf_op jit(solution)/shard_map/ppermute | solution.py:44
  52.5 16.7 %collective-permute-start.7 = (bf16[2,2,2,32,512]{4,3,2,1,0:T(8,128)(2,1)S(1)}, bf16[2,2,2,32,512]{4,3,2,1,0:T(8,128)(2,1)S(1)}, u32[]{:S(2)}, u32[]{:S(2)}) collective-permute-start(bf16[2,2,2,32,512]{4,3,2,1,0:T(8,128)(2,1)S(1)} %slice.296), channel_id=1, source_target_pairs={{0,2},{1,3},{2,4},{3,5},{4,6},{5,7},{6,0},{7,1},{8,10},{9,11},{10,... | collective-permute-start | bytes 786440 | tf_op jit(solution)/shard_map/ppermute | solution.py:44
  55.3 13.9 %collective-permute-start.8 = (bf16[2,2,2,32,512]{4,3,2,1,0:T(8,128)(2,1)S(1)}, bf16[2,2,2,32,512]{4,3,2,1,0:T(8,128)(2,1)S(1)}, u32[]{:S(2)}, u32[]{:S(2)}) collective-permute-start(bf16[2,2,2,32,512]{4,3,2,1,0:T(8,128)(2,1)S(1)} %slice.297), channel_id=1, source_target_pairs={{0,6},{1,7},{2,0},{3,1},{4,2},{5,3},{6,4},{7,5},{8,14},{9,15},{10,... | collective-permute-start | bytes 786440 | tf_op jit(solution)/shard_map/ppermute | solution.py:44
  58.7 18.4 %collective-permute-start.15 = (bf16[1,4,2,32,512]{4,3,2,1,0:T(8,128)(2,1)S(1)}, bf16[1,4,2,32,512]{4,3,2,1,0:T(8,128)(2,1)S(1)}, u32[]{:S(2)}, u32[]{:S(2)}) collective-permute-start(bf16[1,4,2,32,512]{4,3,2,1,0:T(8,128)(2,1)S(1)} %slice.303), channel_id=1, source_target_pairs={{0,16},{8,24},{16,32},{24,40},{32,48},{40,56},{48,0},{56,8},{1,17}... | collective-permute-start | bytes 786440 | tf_op jit(solution)/shard_map/ppermute | solution.py:44
  59.8 18.1 %collective-permute-start.16 = (bf16[1,4,2,32,512]{4,3,2,1,0:T(8,128)(2,1)S(1)}, bf16[1,4,2,32,512]{4,3,2,1,0:T(8,128)(2,1)S(1)}, u32[]{:S(2)}, u32[]{:S(2)}) collective-permute-start(bf16[1,4,2,32,512]{4,3,2,1,0:T(8,128)(2,1)S(1)} %slice.304), channel_id=1, source_target_pairs={{0,48},{8,56},{16,0},{24,8},{32,16},{40,24},{48,32},{56,40},{1,49}... | collective-permute-start | bytes 786440 | tf_op jit(solution)/shard_map/ppermute | solution.py:44
  69.3 12.4 %collective-permute-start.9 = (bf16[64,32,512]{2,1,0:T(8,128)(2,1)S(1)}, bf16[64,32,512]{2,1,0:T(8,128)(2,1)S(1)}, u32[]{:S(2)}, u32[]{:S(2)}) collective-permute-start(bf16[64,32,512]{2,1,0:T(8,128)(2,1)S(1)} %bitcast.258), channel_id=1, source_target_pairs={{0,1},{1,0},{2,3},{3,2},{4,5},{5,4},{6,7},{7,6},{8,9},{9,8},{10,11... | collective-permute-start | bytes 6291464 | tf_op jit(solution)/shard_map/ppermute | solution.py:49
  78.6 8.7 %collective-permute-start.17 = (bf16[64,32,512]{2,1,0:T(8,128)(2,1)}, bf16[64,32,512]{2,1,0:T(8,128)(2,1)}, u32[]{:S(2)}, u32[]{:S(2)}) collective-permute-start(bf16[64,32,512]{2,1,0:T(8,128)(2,1)} %bitcast.41.qk_mine_ref), channel_id=1, source_target_pairs={{0,1},{1,0},{2,3},{3,2},{4,5},{5,4},{6,7},{7,6},{8,9},{9,8},{10,11... | collective-permute-start | bytes 6291464 | tf_op jit(solution)/shard_map/ppermute | solution.py:49
  93.5 30.7 %all-to-all-start = ((bf16[8,256,384]{2,1,0:T(8,128)(2,1)}), bf16[8,256,384]{2,1,0:T(8,128)(2,1)S(1)}, u32[]{:S(2)}, u32[]{:S(2)}) async-start(bf16[8,256,384]{2,1,0:T(8,128)(2,1)} %shard_map.318), calls=%async_computation | async-start | bytes 3145728 | tf_op jit(solution)/shard_map/all_to_all | solution.py:205
  160.4 12.5 %collective-permute-start.18 = (bf16[256,1024]{1,0:T(8,128)(2,1)}, bf16[256,1024]{1,0:T(8,128)(2,1)S(1)}, u32[]{:S(2)}, u32[]{:S(2)}) collective-permute-start(bf16[256,1024]{1,0:T(8,128)(2,1)} %shard_map.320), channel_id=1, source_target_pairs={{0,64},{1,65},{2,66},{3,67},{4,68},{5,69},{6,70},{7,71},{8,72},{9,... | collective-permute-start | bytes 1572872 | tf_op jit(solution)/shard_map/ppermute | solution.py:211
  259.0 13.9 %all-to-all-start.4 = ((bf16[8,256,128]{2,1,0:T(8,128)(2,1)}), bf16[8,256,128]{2,1,0:T(8,128)(2,1)S(1)}, u32[]{:S(2)}, u32[]{:S(2)}) async-start(bf16[8,256,128]{2,1,0:T(8,128)(2,1)} %get-tuple-element.51), calls=%async_computation.4 | async-start | bytes 1048576 | tf_op jit(solution)/shard_map/all_to_all | solution.py:205
  263.4 58.2 %collective-permute-start.19 = (bf16[256,7168]{1,0:T(8,128)(2,1)}, bf16[256,7168]{1,0:T(8,128)(2,1)}, u32[]{:S(2)}, u32[]{:S(2)}) collective-permute-start(bf16[256,7168]{1,0:T(8,128)(2,1)} %get-tuple-element.54.active_ref.normed_ref.attn_ref.left_ref), channel_id=1, source_target_pairs={{0,1},{1,0},{2,3},{3,2},{4,5},{5,4},{6,7},{7,6},{8,9},{9,8},{10,11... | collective-permute-start | bytes 11010056 | tf_op jit(solution)/shard_map/ppermute | solution.py:49
  321.6 14.5 %collective-permute-start.20 = (bf16[256,1024]{1,0:T(8,128)(2,1)}, bf16[256,1024]{1,0:T(8,128)(2,1)S(1)}, u32[]{:S(2)}, u32[]{:S(2)}) collective-permute-start(bf16[256,1024]{1,0:T(8,128)(2,1)} %shard_map.326), channel_id=1, source_target_pairs={{64,0},{65,1},{66,2},{67,3},{68,4},{69,5},{70,6},{71,7},{72,8},{73... | collective-permute-start | bytes 1572872 | tf_op jit(solution)/shard_map/ppermute | solution.py:211
  352.8 5.4 %collective-permute-start.21 = (bf16[256,3072]{1,0:T(8,128)(2,1)}, bf16[256,3072]{1,0:T(8,128)(2,1)S(1)}, u32[]{:S(2)}, u32[]{:S(2)}) collective-permute-start(bf16[256,3072]{1,0:T(8,128)(2,1)} %get-tuple-element.58), channel_id=1, source_target_pairs={{0,1},{1,0},{2,3},{3,2},{4,5},{5,4},{6,7},{7,6},{8,9},{9,8},{10,11... | collective-permute-start | bytes 4718600 | tf_op jit(solution)/shard_map/ppermute | solution.py:49
  354.7 16.3 %all-to-all-start.6 = ((bf16[8,256,128]{2,1,0:T(8,128)(2,1)}), bf16[8,256,128]{2,1,0:T(8,128)(2,1)S(1)}, u32[]{:S(2)}, u32[]{:S(2)}) async-start(bf16[8,256,128]{2,1,0:T(8,128)(2,1)} %get-tuple-element.56), calls=%async_computation.6 | async-start | bytes 1048576 | tf_op jit(solution)/shard_map/all_to_all | solution.py:205
  374.0 21.9 %collective-permute-start.22 = (bf16[1,4,2,80,512]{4,3,2,1,0:T(8,128)(2,1)S(1)}, bf16[1,4,2,80,512]{4,3,2,1,0:T(8,128)(2,1)S(1)}, u32[]{:S(2)}, u32[]{:S(2)}) collective-permute-start(bf16[1,4,2,80,512]{4,3,2,1,0:T(8,128)(2,1)S(1)} %get-tuple-element.74), channel_id=1, source_target_pairs={{0,16},{8,24},{16,32},{24,40},{32,48},{40,56},{48,0},{56,8},{1,17}... | collective-permute-start | bytes 1966088 | tf_op jit(solution)/shard_map/ppermute | solution.py:44
  374.1 21.9 %collective-permute-start.23 = (bf16[1,4,2,80,512]{4,3,2,0,1:T(8,128)(2,1)S(1)}, bf16[1,4,2,80,512]{4,3,2,0,1:T(8,128)(2,1)}, u32[]{:S(2)}, u32[]{:S(2)}) collective-permute-start(bf16[1,4,2,80,512]{4,3,2,0,1:T(8,128)(2,1)S(1)} %get-tuple-element.76), channel_id=1, source_target_pairs={{0,48},{8,56},{16,0},{24,8},{32,16},{40,24},{48,32},{56,40},{1,49}... | collective-permute-start | bytes 1966088 | tf_op jit(solution)/shard_map/ppermute | solution.py:44
  378.0 17.9 %collective-permute-start.24 = (bf16[2,2,2,64,512]{4,3,2,1,0:T(8,128)(2,1)}, bf16[2,2,2,64,512]{4,3,2,1,0:T(8,128)(2,1)}, u32[]{:S(2)}, u32[]{:S(2)}) collective-permute-start(bf16[2,2,2,64,512]{4,3,2,1,0:T(8,128)(2,1)} %get-tuple-element.78), channel_id=1, source_target_pairs={{0,2},{1,3},{2,4},{3,5},{4,6},{5,7},{6,0},{7,1},{8,10},{9,11},{10,... | collective-permute-start | bytes 1572872 | tf_op jit(solution)/shard_map/ppermute | solution.py:44
  379.4 16.5 %collective-permute-start.25 = (bf16[2,2,2,64,512]{4,3,2,1,0:T(8,128)(2,1)}, bf16[2,2,2,64,512]{4,3,2,1,0:T(8,128)(2,1)}, u32[]{:S(2)}, u32[]{:S(2)}) collective-permute-start(bf16[2,2,2,64,512]{4,3,2,1,0:T(8,128)(2,1)} %get-tuple-element.80), channel_id=1, source_target_pairs={{0,6},{1,7},{2,0},{3,1},{4,2},{5,3},{6,4},{7,5},{8,14},{9,15},{10,... | collective-permute-start | bytes 1572872 | tf_op jit(solution)/shard_map/ppermute | solution.py:44
  396.8 25.5 %all-to-all-start.7 = ((bf16[8,256,384]{2,1,0:T(8,128)(2,1)}), bf16[8,256,384]{2,1,0:T(8,128)(2,1)S(1)}, u32[]{:S(2)}, u32[]{:S(2)}) async-start(bf16[8,256,384]{2,1,0:T(8,128)(2,1)} %bitcast.270), calls=%async_computation.7 | async-start | bytes 3145728 | tf_op jit(solution)/shard_map/all_to_all | solution.py:205
  404.6 40.2 %collective-permute-start.28 = (bf16[4,2,2,64,512]{4,3,2,1,0:T(8,128)(2,1)}, bf16[4,2,2,64,512]{4,3,2,1,0:T(8,128)(2,1)}, u32[]{:S(2)}, u32[]{:S(2)}) collective-permute-start(bf16[4,2,2,64,512]{4,3,2,1,0:T(8,128)(2,1)} %pad_maximum_fusion.2), channel_id=1, source_target_pairs={{0,2},{1,3},{2,4},{3,5},{4,6},{5,7},{6,0},{7,1},{8,10},{9,11},{10,... | collective-permute-start | bytes 3145736 | tf_op jit(solution)/shard_map/ppermute | solution.py:44
  407.0 37.7 %collective-permute-start.29 = (bf16[4,2,2,64,512]{4,3,2,1,0:T(8,128)(2,1)}, bf16[4,2,2,64,512]{4,3,2,1,0:T(8,128)(2,1)}, u32[]{:S(2)}, u32[]{:S(2)}) collective-permute-start(bf16[4,2,2,64,512]{4,3,2,1,0:T(8,128)(2,1)} %pad_maximum_fusion.3), channel_id=1, source_target_pairs={{0,6},{1,7},{2,0},{3,1},{4,2},{5,3},{6,4},{7,5},{8,14},{9,15},{10,... | collective-permute-start | bytes 3145736 | tf_op jit(solution)/shard_map/ppermute | solution.py:44
  410.8 34.0 %collective-permute-start.26 = (bf16[2,4,2,80,512]{4,3,2,1,0:T(8,128)(2,1)}, bf16[2,4,2,80,512]{4,3,2,1,0:T(8,128)(2,1)}, u32[]{:S(2)}, u32[]{:S(2)}) collective-permute-start(bf16[2,4,2,80,512]{4,3,2,1,0:T(8,128)(2,1)} %pad_maximum_fusion), channel_id=1, source_target_pairs={{0,16},{8,24},{16,32},{24,40},{32,48},{40,56},{48,0},{56,8},{1,17}... | collective-permute-start | bytes 3932168 | tf_op jit(solution)/shard_map/ppermute | solution.py:44
  412.4 32.4 %collective-permute-start.27 = (bf16[2,4,2,80,512]{4,3,2,0,1:T(8,128)(2,1)S(1)}, bf16[2,4,2,80,512]{4,3,2,0,1:T(8,128)(2,1)}, u32[]{:S(2)}, u32[]{:S(2)}) collective-permute-start(bf16[2,4,2,80,512]{4,3,2,0,1:T(8,128)(2,1)S(1)} %pad_maximum_fusion.1), channel_id=1, source_target_pairs={{0,48},{8,56},{16,0},{24,8},{32,16},{40,24},{48,32},{56,40},{1,49}... | collective-permute-start | bytes 3932168 | tf_op jit(solution)/shard_map/ppermute | solution.py:44
  423.5 11.2 %collective-permute-start.30 = (bf16[4,256,384]{2,1,0:T(8,128)(2,1)}, bf16[4,256,384]{2,1,0:T(8,128)(2,1)}, u32[]{:S(2)}, u32[]{:S(2)}) collective-permute-start(bf16[4,256,384]{2,1,0:T(8,128)(2,1)} %constant_dynamic-slice_fusion.4), channel_id=1, source_target_pairs={{0,1},{1,0},{2,3},{3,2},{4,5},{5,4},{6,7},{7,6},{8,9},{9,8},{10,11... | collective-permute-start | bytes 2359304 | tf_op jit(solution)/shard_map/ppermute | solution.py:49
  442.9 13.8 %collective-permute-start.39 = (bf16[4,2,2,32,512]{4,3,2,1,0:T(8,128)(2,1)}, bf16[4,2,2,32,512]{4,3,2,1,0:T(8,128)(2,1)}, u32[]{:S(2)}, u32[]{:S(2)}) collective-permute-start(bf16[4,2,2,32,512]{4,3,2,1,0:T(8,128)(2,1)} %get-tuple-element.84), channel_id=1, source_target_pairs={{0,6},{1,7},{2,0},{3,1},{4,2},{5,3},{6,4},{7,5},{8,14},{9,15},{10,... | collective-permute-start | bytes 1572872 | tf_op jit(solution)/shard_map/ppermute | solution.py:44
  445.1 33.3 %collective-permute-start.33 = (bf16[2,4,2,32,512]{4,3,2,0,1:T(8,128)(2,1)S(1)}, bf16[2,4,2,32,512]{4,3,2,0,1:T(8,128)(2,1)S(1)}, u32[]{:S(2)}, u32[]{:S(2)}) collective-permute-start(bf16[2,4,2,32,512]{4,3,2,0,1:T(8,128)(2,1)S(1)} %bitcast.281), channel_id=1, source_target_pairs={{0,48},{8,56},{16,0},{24,8},{32,16},{40,24},{48,32},{56,40},{1,49}... | collective-permute-start | bytes 1572872 | tf_op jit(solution)/shard_map/ppermute | solution.py:44
  446.1 33.1 %collective-permute-start.32 = (bf16[2,4,2,32,512]{4,3,2,0,1:T(8,128)(2,1)S(1)}, bf16[2,4,2,32,512]{4,3,2,0,1:T(8,128)(2,1)S(1)}, u32[]{:S(2)}, u32[]{:S(2)}) collective-permute-start(bf16[2,4,2,32,512]{4,3,2,0,1:T(8,128)(2,1)S(1)} %bitcast.279), channel_id=1, source_target_pairs={{0,32},{8,40},{16,48},{24,56},{32,0},{40,8},{48,16},{56,24},{1,33}... | collective-permute-start | bytes 1572872 | tf_op jit(solution)/shard_map/ppermute | solution.py:44
  446.2 12.9 %collective-permute-start.38 = (bf16[4,2,2,32,512]{4,3,2,1,0:T(8,128)(2,1)S(1)}, bf16[4,2,2,32,512]{4,3,2,1,0:T(8,128)(2,1)S(1)}, u32[]{:S(2)}, u32[]{:S(2)}) collective-permute-start(bf16[4,2,2,32,512]{4,3,2,1,0:T(8,128)(2,1)S(1)} %copy-done.16), channel_id=1, source_target_pairs={{0,4},{1,5},{2,6},{3,7},{4,0},{5,1},{6,2},{7,3},{8,12},{9,13},{10,... | collective-permute-start | bytes 1572872 | tf_op jit(solution)/shard_map/ppermute | solution.py:44
  447.8 25.1 %collective-permute-start.37 = (bf16[4,2,2,32,512]{4,3,2,1,0:T(8,128)(2,1)S(1)}, bf16[4,2,2,32,512]{4,3,2,1,0:T(8,128)(2,1)S(1)}, u32[]{:S(2)}, u32[]{:S(2)}) collective-permute-start(bf16[4,2,2,32,512]{4,3,2,1,0:T(8,128)(2,1)S(1)} %copy-done.15), channel_id=1, source_target_pairs={{0,2},{1,3},{2,4},{3,5},{4,6},{5,7},{6,0},{7,1},{8,10},{9,11},{10,... | collective-permute-start | bytes 1572872 | tf_op jit(solution)/shard_map/ppermute | solution.py:44
  456.7 22.5 %collective-permute-start.31 = (bf16[2,4,2,32,512]{4,3,2,0,1:T(8,128)(2,1)S(1)}, bf16[2,4,2,32,512]{4,3,2,0,1:T(8,128)(2,1)S(1)}, u32[]{:S(2)}, u32[]{:S(2)}) collective-permute-start(bf16[2,4,2,32,512]{4,3,2,0,1:T(8,128)(2,1)S(1)} %bitcast.280), channel_id=1, source_target_pairs={{0,16},{8,24},{16,32},{24,40},{32,48},{40,56},{48,0},{56,8},{1,17}... | collective-permute-start | bytes 1572872 | tf_op jit(solution)/shard_map/ppermute | solution.py:44
  475.4 19.2 %collective-permute-start.42 = (bf16[2,2,96,512]{3,2,1,0:T(8,128)(2,1)S(1)}, bf16[2,2,96,512]{3,2,1,0:T(8,128)(2,1)S(1)}, u32[]{:S(2)}, u32[]{:S(2)}) collective-permute-start(bf16[2,2,96,512]{3,2,1,0:T(8,128)(2,1)S(1)} %get-tuple-element.95), channel_id=1, source_target_pairs={{0,48},{8,56},{16,0},{24,8},{32,16},{40,24},{48,32},{56,40},{1,49}... | collective-permute-start | bytes 1179656 | tf_op jit(solution)/shard_map/ppermute | solution.py:44
  478.3 16.3 %collective-permute-start.41 = (bf16[2,2,96,512]{3,2,1,0:T(8,128)(2,1)}, bf16[2,2,96,512]{3,2,1,0:T(8,128)(2,1)S(1)}, u32[]{:S(2)}, u32[]{:S(2)}) collective-permute-start(bf16[2,2,96,512]{3,2,1,0:T(8,128)(2,1)} %get-tuple-element.94), channel_id=1, source_target_pairs={{0,32},{8,40},{16,48},{24,56},{32,0},{40,8},{48,16},{56,24},{1,33}... | collective-permute-start | bytes 1179656 | tf_op jit(solution)/shard_map/ppermute | solution.py:44
  478.3 20.2 %collective-permute-start.40 = (bf16[2,2,96,512]{3,2,1,0:T(8,128)(2,1)S(1)}, bf16[2,2,96,512]{3,2,1,0:T(8,128)(2,1)}, u32[]{:S(2)}, u32[]{:S(2)}) collective-permute-start(bf16[2,2,96,512]{3,2,1,0:T(8,128)(2,1)S(1)} %get-tuple-element.93), channel_id=1, source_target_pairs={{0,16},{8,24},{16,32},{24,40},{32,48},{40,56},{48,0},{56,8},{1,17}... | collective-permute-start | bytes 1179656 | tf_op jit(solution)/shard_map/ppermute | solution.py:44
  481.5 18.4 %collective-permute-start.36 = (bf16[2,2,112,512]{3,2,1,0:T(8,128)(2,1)}, bf16[2,2,112,512]{3,2,1,0:T(8,128)(2,1)}, u32[]{:S(2)}, u32[]{:S(2)}) collective-permute-start(bf16[2,2,112,512]{3,2,1,0:T(8,128)(2,1)} %get-tuple-element.92), channel_id=1, source_target_pairs={{0,6},{1,7},{2,0},{3,1},{4,2},{5,3},{6,4},{7,5},{8,14},{9,15},{10,... | collective-permute-start | bytes 1376264 | tf_op jit(solution)/shard_map/ppermute | solution.py:44
  481.5 18.4 %collective-permute-start.35 = (bf16[2,2,112,512]{3,2,1,0:T(8,128)(2,1)}, bf16[2,2,112,512]{3,2,1,0:T(8,128)(2,1)}, u32[]{:S(2)}, u32[]{:S(2)}) collective-permute-start(bf16[2,2,112,512]{3,2,1,0:T(8,128)(2,1)} %get-tuple-element.91), channel_id=1, source_target_pairs={{0,4},{1,5},{2,6},{3,7},{4,0},{5,1},{6,2},{7,3},{8,12},{9,13},{10,... | collective-permute-start | bytes 1376264 | tf_op jit(solution)/shard_map/ppermute | solution.py:44
  494.6 12.1 %collective-permute-start.34 = (bf16[2,2,112,512]{3,2,1,0:T(8,128)(2,1)}, bf16[2,2,112,512]{3,2,1,0:T(8,128)(2,1)}, u32[]{:S(2)}, u32[]{:S(2)}) collective-permute-start(bf16[2,2,112,512]{3,2,1,0:T(8,128)(2,1)} %get-tuple-element.90), channel_id=1, source_target_pairs={{0,2},{1,3},{2,4},{3,5},{4,6},{5,7},{6,0},{7,1},{8,10},{9,11},{10,... | collective-permute-start | bytes 1376264 | tf_op jit(solution)/shard_map/ppermute | solution.py:44
  509.0 13.3 %collective-permute-start.43 = (bf16[2,208,512]{2,1,0:T(8,128)(2,1)}, bf16[2,208,512]{2,1,0:T(8,128)(2,1)S(1)}, u32[]{:S(2)}, u32[]{:S(2)}) collective-permute-start(bf16[2,208,512]{2,1,0:T(8,128)(2,1)} %fusion.31), channel_id=1, source_target_pairs={{0,8},{8,0},{16,24},{24,16},{32,40},{40,32},{48,56},{56,48},{1,9},... | collective-permute-start | bytes 1277960 | tf_op jit(solution)/shard_map/ppermute | solution.py:49
  (30 other events, 177.4 us)
Sparse Core Ops, SparseCore 0:
  11.1 124.4 all-gather.2

commit v5 on v4

--- a/solution.py
+++ b/solution.py
@@ -35,7 +35,7 @@
 HIDDEN_ROW = 10
 TABLE_ROWS = 16
 
-MLP_NORMED, ATTN_NORMED, ATTN_OUT = 4, 5, 6
+MLP_NORMED, ATTN_OUT = 4, 5
 MLP_GRAD, BRANCH_GRAD = 4, 5
 
 
@@ -201,6 +201,19 @@
     return by_core(core_me, piece(cores, core_me, 0), got, 1)
 
 
+def collect_heads(terms):
+    x_me, z_me, _, _ = coordinates()
+    peers = lax.axis_size("head")
+    blocks = terms.reshape(lax.axis_size("dp") // 2, 2, -1, terms.shape[1])
+    blocks = ring_direct(blocks, "dp", 0, x_me)
+    away = piece(blocks, 1 - z_me, 0).astype(jnp.bfloat16)
+    total = piece(blocks, z_me, 0) + swap(away, "dp").astype(jnp.float32)
+    parts = to_peers(total.astype(jnp.bfloat16).reshape(peers, -1, terms.shape[1]))
+    rows = parts.shape[1]
+    parts = parts.reshape(peers, rows, 3, -1).transpose(1, 2, 0, 3)
+    return parts.reshape(rows, -1).astype(jnp.float32)
+
+
 def to_peers(blocks):
     return lax.all_to_all(blocks, "head", split_axis=0, concat_axis=0, tiled=True)
 
@@ -305,10 +318,11 @@
 
 
 def front_kernel(
-    core_ref, x_ref, table_ref, qk_mine_ref, v_mine_ref, qk_other_ref, v_other_ref, out_ref
+    core_ref, x_ref, table_ref, qk_mine_ref, v_mine_ref, qk_other_ref, v_other_ref, out_ref, normed_ref
 ):
     core = core_ref[0]
     normed, _, _ = attn_normed(x_ref[...].astype(jnp.float32), table_ref)
+    normed_ref[...] = normed
     query_adds = halves(core, vector(table_ref, QUERY_ADD))
     value_adds = halves(core, vector(table_ref, VALUE_ADD))
     for at, (qk_ref, v_ref) in enumerate(
@@ -429,7 +443,6 @@
         if keep:
             branch_ref[...] = branch
             put_column(left_ref, MLP_NORMED, normed[...])
-            put_column(left_ref, ATTN_NORMED, attn_normed(rows, table_ref)[0])
             put_column(left_ref, ATTN_OUT, attn)
         total[...] = jnp.broadcast_to(vector(table_ref, FC2_ADD), total.shape)
 
@@ -616,16 +629,8 @@
         fc1_proj_ref[:, start:] = proj.reshape(devices, SLAB, half)
 
 
-def attn_weights_kernel(
-    core_ref, left_ref, left_other_ref, grad_ref, got_ref, small_ref, query_key_ref, value_ref
-):
-    devices, _, half = value_ref.shape
-    for part, ref, start in ((0, query_key_ref, 0), (1, query_key_ref, SLAB), (2, value_ref, 0)):
-        right = side_by_side(grad_ref, part * 128, core_ref[0] * 4, 4)
-        right_other = side_by_side(got_ref, part * 128, 0, 4)
-        grad = both_products(left_ref, left_other_ref, right, right_other)
-        ref[:, start : start + SLAB] = grad.reshape(devices, SLAB, half)
-    value_ref[:, SLAB:] = small_ref[...]
+def attn_weights_kernel(normed_ref, grad_ref, out_ref):
+    out_ref[...] = product_tn(flat(normed_ref[...]), flat(grad_ref[...])).astype(jnp.bfloat16)
 
 
 def like(*shape, dtype=jnp.bfloat16):
@@ -662,8 +667,8 @@
         front_kernel,
         grid=(1,),
         in_specs=[SCALARS, whole_block(x), whole_block(table)] + early_specs(early),
-        out_specs=pl.BlockSpec((8, rows, 384), lambda i: (0, 0, 0)),
-        out_shape=like(8, rows, 384),
+        out_specs=[pl.BlockSpec((8, rows, 384), lambda i: (0, 0, 0)), whole_block(x)],
+        out_shape=[like(8, rows, 384), like(*x.shape)],
         compiler_params=params(),
         cost_estimate=takes(6.5),
     )(core, x, table, *early)
@@ -730,7 +735,7 @@
     column = pl.BlockSpec((rows, width), lambda j: (0, j))
     out_shape, out_specs = [like(rows, width)], [whole_block(x)]
     if keep:
-        left = like(rows, (steps + 3) * width)
+        left = like(rows, (steps + 2) * width)
         out_shape += [full, like(rows, steps * width, dtype=jnp.float32), full, left]
         out_specs += [whole_block(x), column, whole_block(x), whole_block(left)]
     return pl.pallas_call(
@@ -834,19 +839,17 @@
     )(*(left, left_other) * 3, *(right, right_other) * 3)
 
 
-def call_attn_weights(core, left, left_other, grads, got, small):
-    column = pl.BlockSpec((left.shape[0], 1024), lambda i: (0, ATTN_NORMED))
-    shape = like(small.shape[0], 2 * SLAB, 512)
+def call_attn_weights(normed, grads):
+    width, columns = normed.shape[2], grads.shape[2]
     return pl.pallas_call(
         attn_weights_kernel,
         grid=(1,),
-        in_specs=[SCALARS, column, column]
-        + [whole_block(operand) for operand in (grads, got, small)],
-        out_specs=[whole_block(shape), whole_block(shape)],
-        out_shape=[shape, shape],
+        in_specs=[whole_block(normed), whole_block(grads)],
+        out_specs=pl.BlockSpec((width, columns), lambda i: (0, 0)),
+        out_shape=like(width, columns),
         compiler_params=params(),
-        cost_estimate=takes(8),
-    )(core, left, left_other, grads, got, small)
+        cost_estimate=takes(6),
+    )(normed, grads)
 
 
 def small_slab(vectors, hidden_vector):
@@ -949,13 +952,15 @@
     counts = jnp.where(reversed_order, counts[::-1], counts)
 
     def attention(x):
-        heads = to_peers(call_front(core, x, table, early))
+        heads, normed = call_front(core, x, table, early)
+        heads = to_peers(heads)
         attn, lse = call_attend(counts, heads)
-        return heads, lse, to_peers(attn)
+        return heads, lse, to_peers(attn), normed
 
     (passed,) = call_rear(False, own_images, attention(own_images)[2], table, late)
     x = jnp.where(section_index == 0, own_images, shifted(passed, 1))
-    heads, lse, attn = attention(x)
+    heads, lse, attn, normed = attention(x)
+    normed = lax.all_gather(after(normed, attn), "head", axis=0)
     result, *rear_state, left = call_rear(True, x, attn, table, late)
     left_other = swap(left, "head")
 
@@ -974,30 +979,25 @@
     grad_heads = after(to_peers(grad_attn), fc2)
     mlp_terms = [by_chip(fc1_proj), by_chip(fc2)]
     mlp_halves = [ring_halves(terms, way) for terms, way in zip(mlp_terms, ways)]
-    grad_qkv = call_attend_back(counts, grad_heads, heads, lse)
-    grad_qkv = to_peers(after(grad_qkv, mlp_halves))
+    grad_own_heads = call_attend_back(counts, grad_heads, heads, lse)
+    grad_qkv = to_peers(after(grad_own_heads, mlp_halves))
     mlp_ends = [ring_ends(*item) for item in zip(mlp_terms, mlp_halves, ways)]
-
-    got = swap(lax.dynamic_slice_in_dim(grad_qkv, (1 - core[0]) * 4, 4), "head")
+    qkv_terms = call_attn_weights(normed, grad_own_heads)
+    qkv_grad = collect_heads(qkv_terms)
+
     input_grad, front_sums = call_front_back(
-        True, core, grad_qkv, grad_middle, x, table, early
-    )
-    small = slabs_of(rear_sums + front_sums, devices)
-    attn_terms = call_attn_weights(core, left, left_other, grad_qkv, got, small)
-    attn_terms = [by_chip(terms) for terms in attn_terms]
-    mlp_ends = after(mlp_ends, attn_terms)
-    attn_totals = [ring_first(*item) for item in zip(attn_terms, ways)]
+        True, core, after(grad_qkv, qkv_terms), grad_middle, x, table, early
+    )
+    small = ring_first(by_chip(slabs_of(rear_sums + front_sums, devices)), "dp")
     mlp_totals = [ring_total(*item) for item in zip(mlp_terms, mlp_ends, ways)]
     ring_sums = [
-        second_ring(jnp.concatenate(totals, axis=3), way)
-        for *totals, way in zip(mlp_totals, attn_totals, ways)
+        second_ring(jnp.concatenate([mlp_totals[0], small], axis=3), "dp"),
+        second_ring(mlp_totals[1], "head"),
     ]
     shard_grad = collect_rest(jnp.concatenate(ring_sums, axis=2))
-    fc1_grad, proj_grad, query_key_grad, fc2_grad, value_grad, small_row = (
-        shard_grad[start * SLAB : stop * SLAB]
-        for start, stop in ((0, 4), (4, 5), (5, 7), (7, 11), (11, 12), (12, 13))
-    )
-    qkv_grad = from_column_slabs(jnp.concatenate([query_key_grad, value_grad]))
+    fc1_grad, proj_grad, small_row, fc2_grad = (
+        shard_grad[start * SLAB : stop * SLAB] for start, stop in ((0, 4), (4, 5), (5, 6), (6, 10))
+    )
     row = small_row[0, :SMALL_WIDTH] + small_row[0, SMALL_WIDTH:]
     small_grads = row[: HIDDEN_ROW * SLAB].reshape(HIDDEN_ROW, SLAB)
     fc1_bias_grad = row[HIDDEN_ROW * SLAB : HIDDEN_ROW * SLAB + 64]

time: 548 us -> 545 us (level)
  starting transfers between devices: 88.9 us -> 103 us
  waiting for transfers between devices: 128 us -> 117 us
    all_to_all x4 -> x5, starting transfers between devices: 16.9 us -> 31.5 us  [to_peers(): lax.all_to_all(blocks, 'head', split_axis=0, concat_axis=0, tiled=True)]
    ppermute x34, waiting for transfers between devices: 46.6 us -> 38.3 us  [hop(): lax.ppermute(block, axis, [(i, (i + 2 * places) % size) for i in range(si...]
    all_to_all x4 -> x5, waiting for transfers between devices: 42.3 us -> 41.9 us  [to_peers(): lax.all_to_all(blocks, 'head', split_axis=0, concat_axis=0, tiled=True)]
  transfers between devices with their start and end apart: 50 -> 52, of which waited for: 19 -> 20; matrix products, arithmetic and copies ran while one was open for 10% -> 10% of each run, Pallas kernels for 14% -> 17%
where the time goes in v5:
time: 545 us; the launch traced here: 534 us
  Pallas kernels  147 us (27%)
  waiting for transfers between devices  117 us (21%)
  starting transfers between devices  103 us (19%)
  blocking collectives  83.1 us (15%)
  local copies, waits for them, and re-layouts  43.3 us (8%)
  other arithmetic  25 us (5%)
  between operations  16.5 us (3%)
    all_to_all x4, blocking collectives, to_peers(): lax.all_to_all(blocks, 'head', split_axis=0, concat_axis=0, tiled=True)  83.1 us
    ppermute x34, starting transfers between devices, hop(): lax.ppermute(block, axis, [(i, (i + 2 * places) % size) for i in range(si...  46.7 us
    all_to_all x5, waiting for transfers between devices, to_peers(): lax.all_to_all(blocks, 'head', split_axis=0, concat_axis=0, tiled=True)  41.9 us
    ppermute x34, waiting for transfers between devices, hop(): lax.ppermute(block, axis, [(i, (i + 2 * places) % size) for i in range(si...  38.3 us
    all_to_all x5, starting transfers between devices, to_peers(): lax.all_to_all(blocks, 'head', split_axis=0, concat_axis=0, tiled=True)  31.5 us
    pallas_call x2, Pallas kernels, call_attend_back(): pl.pallas_call(attend_back_kernel, grid=(images,), in_specs=[SCALARS, pl....  30.2 us
    pallas_call x2, Pallas kernels, call_rear_back(): pl.pallas_call(functools.partial(rear_back_kernel, keep), grid=(steps,),...  30.1 us
    pallas_call x2, Pallas kernels, call_rear(): pl.pallas_call(functools.partial(rear_kernel, keep), grid=(steps,), in_sp...  26.5 us
  transfers between devices with their start and end apart: 52, of which 20 were waited for; matrix products, arithmetic and copies ran while one was open for 10% of the time, Pallas kernels for 17%

profile of v5, /device:TPU:1, one launch (start us, length us, event | category | flops | bytes accessed | tf_op | source)
XLA Modules:
  0.0 534.0 jit_solution(1670671036858721969)
XLA Ops:
  15.9 3.8 collective-permute-start.1
  19.6 3.6 collective-permute-done.1
  30.1 2.6 collective-permute-start.11
  42.8 2.7 collective-permute-start.14
  48.2 3.4 collective-permute-done.5
  59.8 3.4 collective-permute-start.16
  69.3 7.9 %collective-permute-start.9 = (bf16[64,32,512]{2,1,0:T(8,128)(2,1)S(1)}, bf16[64,32,512]{2,1,0:T(8,128)(2,1)S(1)}, u32[]{:S(2)}, u32[]{:S(2)}) collective-permute-start(bf16[64,32,512]{2,1,0:T(8,128)(2,1)S(1)} %bitcast.258), channel_id=1, source_target_pairs={{0,1},{1,0},{2,3},{3,2},{4,5},{5,4},{6,7},{7,6},{8,9},{9,8},{10,11... | collective-permute-start | bytes 6291464 | tf_op jit(solution)/shard_map/ppermute | solution.py:49
  84.1 3.2 collective-permute-done.17.qk_other_ref
  87.3 6.2 %shard_map.318 = (bf16[8,256,384]{2,1,0:T(8,128)(2,1)}, bf16[256,1024]{1,0:T(8,128)(2,1)}) custom-call(s32[1]{0:T(128)} %bitcast.2.core_ref, bf16[256,1024]{1,0:T(8,128)(2,1)} %bitcast.251, f32[16,1024]{1,0:T(8,128)} %select_maximum_fusion.table_ref, bf16[64,32,512]{2,1,0:T(8,128)(2,1)} %bitcast.41.qk_mine_ref, bf16[64,32,512]{2,1,0:T(8,128)(2,1)} %bitcast.260, ...), custom_call_target="tpu_custom_call" | custom-call | flops 7474999808 | bytes 19500000 | tf_op jit(solution)/shard_map/pallas_call | solution.py:666
  93.6 4.2 all-to-all-start
  98.6 25.8 %all-to-all-done = bf16[8,256,384]{2,1,0:T(8,128)(2,1)S(1)} async-done(((bf16[8,256,384]{2,1,0:T(8,128)(2,1)}), bf16[8,256,384]{2,1,0:T(8,128)(2,1)S(1)}, u32[]{:S(2)}, u32[]{:S(2)}) %all-to-all-start) | async-done | bytes 1572896 | tf_op jit(solution)/shard_map/all_to_all | solution.py:218
  125.5 8.1 %shard_map.319 = (bf16[8,2,128,128]{3,2,1,0:T(8,128)(2,1)}, f32[2,2,1024]{2,1,0:T(2,128)}) custom-call(s32[2]{0:T(128)} %broadcast_select_fusion.5.count_ref, bf16[8,2,128,384]{3,2,1,0:T(8,128)(2,1)} %bitcast.269), custom_call_target="tpu_custom_call" | custom-call | flops 16444999680 | bytes 42900000 | tf_op jit(solution)/shard_map/pallas_call | solution.py:681
  133.6 15.1 %all_to_all.45.attn_ref = bf16[8,256,128]{2,1,0:T(8,128)(2,1)} all-to-all(bf16[8,256,128]{2,1,0:T(8,128)(2,1)} %bitcast.280), channel_id=1, replica_groups=mesh['section'=2,'dp'=8,'head'=8] {'head'}, dimensions={0} | all-to-all | bytes 1048576 | tf_op jit(solution)/shard_map/all_to_all | solution.py:218
  148.7 11.9 %shard_map.320 = bf16[256,1024]{1,0:T(8,128)(2,1)} custom-call(bf16[256,1024]{1,0:T(8,128)(2,1)} %bitcast.252, bf16[8,256,128]{2,1,0:T(8,128)(2,1)} %all_to_all.45.attn_ref, f32[16,1024]{1,0:T(8,128)} %select_maximum_fusion.table_ref, bf16[64,144,1024]{2,1,0:T(8,128)(2,1)} %bitcast.235, bf16[64,144,1024]{2,1,0:T(8,128)(2,1)} %bitcast.236, ...), custom_call_target="tpu_custom_call" | custom-call | flops 14949999616 | bytes 39000000 | tf_op jit(solution)/shard_map/pallas_call | solution.py:741
  162.6 10.4 %collective-permute-done.18 = bf16[256,1024]{1,0:T(8,128)(2,1)S(1)} collective-permute-done((bf16[256,1024]{1,0:T(8,128)(2,1)}, bf16[256,1024]{1,0:T(8,128)(2,1)S(1)}, u32[]{:S(2)}, u32[]{:S(2)}) %collective-permute-start.18) | collective-permute-done | bytes 524320 | tf_op jit(solution)/shard_map/ppermute | solution.py:224
  173.9 6.2 %shard_map.321 = (bf16[8,256,384]{2,1,0:T(8,128)(2,1)}, bf16[256,1024]{1,0:T(8,128)(2,1)}) custom-call(s32[1]{0:T(128)} %bitcast.2.core_ref, bf16[256,1024]{1,0:T(8,128)(2,1)} %broadcast_select_fusion.1.x_ref, f32[16,1024]{1,0:T(8,128)} %select_maximum_fusion.table_ref, bf16[64,32,512]{2,1,0:T(8,128)(2,1)} %bitcast.41.qk_mine_ref, ...), custom_call_target="tpu_custom_call" | custom-call | flops 7474999808 | bytes 19500000 | tf_op jit(solution)/shard_map/pallas_call | solution.py:666
  180.2 27.0 %all_to_all.46 = bf16[8,256,384]{2,1,0:T(8,128)(2,1)} all-to-all(bf16[8,256,384]{2,1,0:T(8,128)(2,1)} %get-tuple-element.46), channel_id=1, replica_groups=mesh['section'=2,'dp'=8,'head'=8] {'head'}, dimensions={0} | all-to-all | bytes 3145728 | tf_op jit(solution)/shard_map/all_to_all | solution.py:218
  207.2 7.8 %shard_map.322 = (bf16[8,2,128,128]{3,2,1,0:T(8,128)(2,1)}, f32[2,2,1024]{2,1,0:T(2,128)}) custom-call(s32[2]{0:T(128)} %broadcast_select_fusion.5.count_ref, bf16[8,2,128,384]{3,2,1,0:T(8,128)(2,1)} %bitcast.264), custom_call_target="tpu_custom_call" | custom-call | flops 16444999680 | bytes 42900000 | tf_op jit(solution)/shard_map/pallas_call | solution.py:681
  215.0 14.9 %all_to_all.47.attn_ref = bf16[8,256,128]{2,1,0:T(8,128)(2,1)} all-to-all(bf16[8,256,128]{2,1,0:T(8,128)(2,1)} %bitcast.281), channel_id=1, replica_groups=mesh['section'=2,'dp'=8,'head'=8] {'head'}, dimensions={0} | all-to-all | bytes 1048576 | tf_op jit(solution)/shard_map/all_to_all | solution.py:218
  229.9 14.6 %shard_map.323 = (bf16[256,1024]{1,0:T(8,128)(2,1)}, f32[256,1024]{1,0:T(8,128)}, f32[256,4096]{1,0:T(8,128)}, f32[256,1024]{1,0:T(8,128)}, bf16[256,6144]{1,0:T(8,128)(2,1)}) custom-call(bf16[256,1024]{1,0:T(8,128)(2,1)} %broadcast_select_fusion.1.x_ref, bf16[8,256,128]{2,1,0:T(8,128)(2,1)} %all_to_all.47.attn_ref, ...), custom_call_target="tpu_custom_call" | custom-call | flops 14949999616 | bytes 39000000 | tf_op jit(solution)/shard_map/pallas_call | solution.py:741
  244.5 14.1 %shard_map.324 = (bf16[8,256,128]{2,1,0:T(8,128)(2,1)}, f32[256,1024]{1,0:T(8,128)}) custom-call(s32[1]{0:T(128)} %bitcast.2.core_ref, bf16[256,1024]{1,0:T(8,128)(2,1)} %bitcast.277, bf16[256,1024]{1,0:T(8,128)(2,1)} %broadcast_select_fusion.1.x_ref, f32[256,1024]{1,0:T(8,128)} %get-tuple-element.49.branch_ref, f32[256,4096]{1,0:T(8,128)} %get-tuple-element.50.hidden_ref, ...), custom_call_target="tpu_custom_call" | custom-call | flops 18400000000 | bytes 48000000 | tf_op jit(solution)/shard_map/pallas_call | solution.py:770
  258.7 4.4 all-to-all-start.4
  263.3 9.3 %all-to-all-done.4 = bf16[8,256,128]{2,1,0:T(8,128)(2,1)S(1)} async-done(((bf16[8,256,128]{2,1,0:T(8,128)(2,1)}), bf16[8,256,128]{2,1,0:T(8,128)(2,1)S(1)}, u32[]{:S(2)}, u32[]{:S(2)}) %all-to-all-start.4) | async-done | bytes 524320 | tf_op jit(solution)/shard_map/all_to_all | solution.py:218
  273.4 15.1 %shard_map.325 = bf16[8,2,128,384]{3,2,1,0:T(8,128)(2,1)} custom-call(s32[2]{0:T(128)} %broadcast_select_fusion.5.count_ref, bf16[8,2,128,128]{3,2,1,0:T(8,128)(2,1)} %bitcast.279, bf16[8,2,128,384]{3,2,1,0:T(8,128)(2,1)} %bitcast.265, f32[2,2,1024]{2,1,0:T(2,128)} %get-tuple-element.53.lse_ref), custom_call_target="tpu_custom_call" | custom-call | flops 18975000576 | bytes 49500000 | tf_op jit(solution)/shard_map/pallas_call | solution.py:703
  288.5 26.1 %all_to_all.48.grad_ref = bf16[8,256,384]{2,1,0:T(8,128)(2,1)} all-to-all(bf16[8,256,384]{2,1,0:T(8,128)(2,1)} %bitcast.270), channel_id=1, replica_groups=mesh['section'=2,'dp'=8,'head'=8] {'head'}, dimensions={0} | all-to-all | bytes 3145728 | tf_op jit(solution)/shard_map/all_to_all | solution.py:218
  314.6 6.7 %shard_map.326 = bf16[256,1024]{1,0:T(8,128)(2,1)} custom-call(s32[1]{0:T(128)} %bitcast.2.core_ref, bf16[8,256,384]{2,1,0:T(8,128)(2,1)} %all_to_all.48.grad_ref, f32[256,1024]{1,0:T(8,128)} %get-tuple-element.54.middle_grad_ref, bf16[256,1024]{1,0:T(8,128)(2,1)} %broadcast_select_fusion.1.x_ref, f32[16,1024]{1,0:T(8,128)} %select_maximum_fusion.table_ref, ...), custom_call_target="tpu_custom_call" | custom-call | flops 8049999872 | bytes 21000000 | tf_op jit(solution)/shard_map/pallas_call | solution.py:800
  322.6 13.2 %collective-permute-done.20 = bf16[256,1024]{1,0:T(8,128)(2,1)S(1)} collective-permute-done((bf16[256,1024]{1,0:T(8,128)(2,1)}, bf16[256,1024]{1,0:T(8,128)(2,1)S(1)}, u32[]{:S(2)}, u32[]{:S(2)}) %collective-permute-start.20) | collective-permute-done | bytes 524320 | tf_op jit(solution)/shard_map/ppermute | solution.py:224
  336.7 16.0 %shard_map.327 = (bf16[8,256,128]{2,1,0:T(8,128)(2,1)}, f32[256,1024]{1,0:T(8,128)}, bf16[256,3072]{1,0:T(8,128)(2,1)}, bf16[256,3072]{1,0:T(8,128)(2,1)}, f32[16,1024]{1,0:T(8,128)}) custom-call(s32[1]{0:T(128)} %bitcast.2.core_ref, bf16[256,1024]{1,0:T(8,128)(2,1)} %broadcast_select_fusion.grad_ref, bf16[256,1024]{1,0:T(8,128)(2,1)} %broadcast_select_fusion.1.x_ref, ...), custom_call_target="tpu_custom_call" | custom-call | flops 18400000000 | bytes 48000000 | tf_op jit(solution)/shard_map/pallas_call | solution.py:770
  354.7 3.4 all-to-all-start.6
  359.4 11.7 %shard_map.328 = (bf16[64,80,512]{2,1,0:T(8,128)(2,1)}, bf16[64,64,512]{2,1,0:T(8,128)(2,1)}) custom-call(bf16[256,6144]{1,0:T(8,128)(2,1)} %get-tuple-element.55.active_ref.normed_ref.attn_ref, bf16[256,6144]{1,0:T(8,128)(2,1)} %collective-permute-done.19.active_other_ref.normed_other_ref.attn_other_ref, ...), custom_call_target="tpu_custom_call" | custom-call | flops 10350000128 | bytes 27000000 | tf_op jit(solution)/shard_map/pallas_call | solution.py:823
  371.1 2.7 dynamic-slice_bitcast_fusion.8
  377.2 3.0 dynamic-slice_bitcast_fusion.1
  380.3 2.7 collective-permute-start.23
  383.0 5.7 %collective-permute-done.24 = bf16[2,2,2,64,512]{4,3,2,1,0:T(8,128)(2,1)S(1)} collective-permute-done((bf16[2,2,2,64,512]{4,3,2,1,0:T(8,128)(2,1)}, bf16[2,2,2,64,512]{4,3,2,1,0:T(8,128)(2,1)S(1)}, u32[]{:S(2)}, u32[]{:S(2)}) %collective-permute-start.24) | collective-permute-done | bytes 524320 | tf_op jit(solution)/shard_map/ppermute | solution.py:44
  395.0 15.1 %shard_map.329 = bf16[8,2,128,384]{3,2,1,0:T(8,128)(2,1)} custom-call(s32[2]{0:T(128)} %broadcast_select_fusion.5.count_ref, bf16[8,2,128,128]{3,2,1,0:T(8,128)(2,1)} %bitcast.278, bf16[8,2,128,384]{3,2,1,0:T(8,128)(2,1)} %bitcast.266, f32[2,2,1024]{2,1,0:T(2,128)} %get-tuple-element.53.lse_ref), custom_call_target="tpu_custom_call" | custom-call | flops 18975000576 | bytes 49500000 | tf_op jit(solution)/shard_map/pallas_call | solution.py:703
  410.1 6.1 %all-to-all-start.7 = ((bf16[8,256,384]{2,1,0:T(8,128)(2,1)}), bf16[8,256,384]{2,1,0:T(8,128)(2,1)S(1)}, u32[]{:S(2)}, u32[]{:S(2)}) async-start(bf16[8,256,384]{2,1,0:T(8,128)(2,1)} %bitcast.267), calls=%async_computation.7 | async-start | bytes 3145728 | tf_op jit(solution)/shard_map/all_to_all | solution.py:218
  427.9 6.0 %shard_map.330 = bf16[1024,384]{1,0:T(8,128)(2,1)} custom-call(bf16[8,256,1024]{2,1,0:T(8,128)(2,1)} %bitcast.295, bf16[8,256,384]{2,1,0:T(8,128)(2,1)} %bitcast.268), custom_call_target="tpu_custom_call" | custom-call | flops 6899999744 | bytes 18000000 | tf_op jit(solution)/shard_map/pallas_call | solution.py:844
  433.9 3.0 all-to-all-done.7.grad_ref
  438.1 7.0 %shard_map.331 = (bf16[256,1024]{1,0:T(8,128)(2,1)}, f32[16,1024]{1,0:T(8,128)}) custom-call(s32[1]{0:T(128)} %bitcast.2.core_ref, bf16[8,256,384]{2,1,0:T(8,128)(2,1)} %copy-done.5, f32[256,1024]{1,0:T(8,128)} %get-tuple-element.67.middle_grad_ref, bf16[256,1024]{1,0:T(8,128)(2,1)} %broadcast_select_fusion.1.x_ref, ...), custom_call_target="tpu_custom_call" | custom-call | flops 8049999872 | bytes 21000000 | tf_op jit(solution)/shard_map/pallas_call | solution.py:800
  449.4 15.1 %collective-permute-done.26 = bf16[2,4,2,80,512]{4,3,2,1,0:T(8,128)(2,1)} collective-permute-done((bf16[2,4,2,80,512]{4,3,2,1,0:T(8,128)(2,1)}, bf16[2,4,2,80,512]{4,3,2,1,0:T(8,128)(2,1)}, u32[]{:S(2)}, u32[]{:S(2)}) %collective-permute-start.26) | collective-permute-done | bytes 1310752 | tf_op jit(solution)/shard_map/ppermute | solution.py:44
  464.5 2.8 fusion
  467.5 6.7 %collective-permute-start.43 = (bf16[2,128,384]{2,1,0:T(8,128)(2,1)S(1)}, bf16[2,128,384]{2,1,0:T(8,128)(2,1)S(1)}, u32[]{:S(2)}, u32[]{:S(2)}) collective-permute-start(bf16[2,128,384]{2,1,0:T(8,128)(2,1)S(1)} %get-tuple-element.91), channel_id=1, source_target_pairs={{0,48},{8,56},{16,0},{24,8},{32,16},{40,24},{48,32},{56,40},{1,49}... | collective-permute-start | bytes 589832 | tf_op jit(solution)/shard_map/ppermute | solution.py:44
  484.0 2.9 collective-permute-done.41
  487.1 4.8 collective-permute-done.31
  492.2 5.4 %collective-permute-start.39 = (bf16[2,160,512]{2,1,0:T(8,128)(2,1)S(1)}, bf16[2,160,512]{2,1,0:T(8,128)(2,1)S(1)}, u32[]{:S(2)}, u32[]{:S(2)}) collective-permute-start(bf16[2,160,512]{2,1,0:T(8,128)(2,1)S(1)} %fusion.30), channel_id=1, source_target_pairs={{0,8},{8,0},{16,24},{24,16},{32,40},{40,32},{48,56},{56,48},{1,9},... | collective-permute-start | bytes 983048 | tf_op jit(solution)/shard_map/ppermute | solution.py:49
  497.7 5.4 %collective-permute-done.44 = bf16[128,384]{1,0:T(8,128)(2,1)S(1)} collective-permute-done((bf16[128,384]{1,0:T(8,128)(2,1)S(1)}, bf16[128,384]{1,0:T(8,128)(2,1)S(1)}, u32[]{:S(2)}, u32[]{:S(2)}) %collective-permute-start.44) | collective-permute-done | bytes 98336 | tf_op jit(solution)/shard_map/ppermute | solution.py:49
  503.7 13.4 %all-to-all-start.8 = ((bf16[8,16,384]{2,1,0:T(8,128)(2,1)}), bf16[8,16,384]{2,1,0:T(8,128)(2,1)S(1)}, u32[]{:S(2)}, u32[]{:S(2)}) async-start(bf16[8,16,384]{2,1,0:T(8,128)(2,1)} %bitcast.105), calls=%async_computation.8 | async-start | bytes 196608 | tf_op jit(solution)/shard_map/all_to_all | solution.py:218
  518.2 3.8 all-to-all-done.8
  (216 shorter events, 103.3 us)
Async XLA Ops:
  7.2 141.5 %all-gather.5.cloned.1.call-start = ((), (), s32[]{:S(2)}) async-start(), calls=%async_computation.9 | async-start | bytes 19169280 | tf_op jit(solution)/shard_map/all_gather | solution.py:933
  15.9 7.3 %collective-permute-start.1 = (bf16[2,64,512]{2,1,0:T(8,128)(2,1)S(1)}, bf16[2,64,512]{2,1,0:T(8,128)(2,1)S(1)}, u32[]{:S(2)}, u32[]{:S(2)}) collective-permute-start(bf16[2,64,512]{2,1,0:T(8,128)(2,1)S(1)} %maximum_select_fusion.3), channel_id=1, source_target_pairs={{0,8},{8,0},{16,24},{24,16},{32,40},{40,32},{48,56},{56,48},{1,9},... | collective-permute-start | bytes 393224 | tf_op jit(solution)/shard_map/ppermute | solution.py:49
  24.0 10.1 %collective-permute-start.2 = (bf16[2,2,32,512]{3,2,1,0:T(8,128)(2,1)}, bf16[2,2,32,512]{3,2,1,0:T(8,128)(2,1)S(1)}, u32[]{:S(2)}, u32[]{:S(2)}) collective-permute-start(bf16[2,2,32,512]{3,2,1,0:T(8,128)(2,1)} %get-tuple-element.96.given_ref), channel_id=1, source_target_pairs={{0,16},{8,24},{16,32},{24,40},{32,48},{40,56},{48,0},{56,8},{1,17}... | collective-permute-start | bytes 393224 | tf_op jit(solution)/shard_map/ppermute | solution.py:44
  25.2 11.3 %collective-permute-start.3 = (bf16[2,2,32,512]{3,2,1,0:T(8,128)(2,1)}, bf16[2,2,32,512]{3,2,1,0:T(8,128)(2,1)S(1)}, u32[]{:S(2)}, u32[]{:S(2)}) collective-permute-start(bf16[2,2,32,512]{3,2,1,0:T(8,128)(2,1)} %get-tuple-element.96.given_ref), channel_id=1, source_target_pairs={{0,32},{8,40},{16,48},{24,56},{32,0},{40,8},{48,16},{56,24},{1,33}... | collective-permute-start | bytes 393224 | tf_op jit(solution)/shard_map/ppermute | solution.py:44
  27.6 9.5 %collective-permute-start.4 = (bf16[2,2,32,512]{3,2,1,0:T(8,128)(2,1)}, bf16[2,2,32,512]{3,2,1,0:T(8,128)(2,1)S(1)}, u32[]{:S(2)}, u32[]{:S(2)}) collective-permute-start(bf16[2,2,32,512]{3,2,1,0:T(8,128)(2,1)} %get-tuple-element.96.given_ref), channel_id=1, source_target_pairs={{0,48},{8,56},{16,0},{24,8},{32,16},{40,24},{48,32},{56,40},{1,49}... | collective-permute-start | bytes 393224 | tf_op jit(solution)/shard_map/ppermute | solution.py:44
  28.8 12.0 %collective-permute-start.10 = (bf16[2,2,32,512]{3,2,1,0:T(8,128)(2,1)}, bf16[2,2,32,512]{3,2,1,0:T(8,128)(2,1)S(1)}, u32[]{:S(2)}, u32[]{:S(2)}) collective-permute-start(bf16[2,2,32,512]{3,2,1,0:T(8,128)(2,1)} %get-tuple-element.95.given_ref), channel_id=1, source_target_pairs={{0,2},{1,3},{2,4},{3,5},{4,6},{5,7},{6,0},{7,1},{8,10},{9,11},{10,... | collective-permute-start | bytes 393224 | tf_op jit(solution)/shard_map/ppermute | solution.py:44
  30.1 11.4 %collective-permute-start.11 = (bf16[2,2,32,512]{3,2,1,0:T(8,128)(2,1)}, bf16[2,2,32,512]{3,2,1,0:T(8,128)(2,1)S(1)}, u32[]{:S(2)}, u32[]{:S(2)}) collective-permute-start(bf16[2,2,32,512]{3,2,1,0:T(8,128)(2,1)} %get-tuple-element.95.given_ref), channel_id=1, source_target_pairs={{0,4},{1,5},{2,6},{3,7},{4,0},{5,1},{6,2},{7,3},{8,12},{9,13},{10,... | collective-permute-start | bytes 393224 | tf_op jit(solution)/shard_map/ppermute | solution.py:44
  34.0 8.1 %collective-permute-start.12 = (bf16[2,2,32,512]{3,2,1,0:T(8,128)(2,1)}, bf16[2,2,32,512]{3,2,1,0:T(8,128)(2,1)S(1)}, u32[]{:S(2)}, u32[]{:S(2)}) collective-permute-start(bf16[2,2,32,512]{3,2,1,0:T(8,128)(2,1)} %get-tuple-element.95.given_ref), channel_id=1, source_target_pairs={{0,6},{1,7},{2,0},{3,1},{4,2},{5,3},{6,4},{7,5},{8,14},{9,15},{10,... | collective-permute-start | bytes 393224 | tf_op jit(solution)/shard_map/ppermute | solution.py:44
  37.8 13.8 %collective-permute-start.5 = (bf16[4,2,2,32,512]{4,3,2,1,0:T(8,128)(2,1)}, bf16[4,2,2,32,512]{4,3,2,1,0:T(8,128)(2,1)}, u32[]{:S(2)}, u32[]{:S(2)}) collective-permute-start(bf16[4,2,2,32,512]{4,3,2,1,0:T(8,128)(2,1)} %bitcast_dynamic-update-slice_fusion.14.given_ref), channel_id=1, source_target_pairs={{0,2},{1,3},{2,4},{3,5},{4,6},{5,7},{6,0},{7,1},{8,10},{9,11},{10,... | collective-permute-start | bytes 1572872 | tf_op jit(solution)/shard_map/ppermute | solution.py:44
  39.1 15.2 %collective-permute-start.6 = (bf16[4,2,2,32,512]{4,3,2,1,0:T(8,128)(2,1)}, bf16[4,2,2,32,512]{4,3,2,1,0:T(8,128)(2,1)}, u32[]{:S(2)}, u32[]{:S(2)}) collective-permute-start(bf16[4,2,2,32,512]{4,3,2,1,0:T(8,128)(2,1)} %bitcast_dynamic-update-slice_fusion.14.given_ref), channel_id=1, source_target_pairs={{0,6},{1,7},{2,0},{3,1},{4,2},{5,3},{6,4},{7,5},{8,14},{9,15},{10,... | collective-permute-start | bytes 1572872 | tf_op jit(solution)/shard_map/ppermute | solution.py:44
  42.8 15.0 %collective-permute-start.13 = (bf16[2,4,2,32,512]{4,3,2,1,0:T(8,128)(2,1)}, bf16[2,4,2,32,512]{4,3,2,1,0:T(8,128)(2,1)}, u32[]{:S(2)}, u32[]{:S(2)}) collective-permute-start(bf16[2,4,2,32,512]{4,3,2,1,0:T(8,128)(2,1)} %bitcast_dynamic-update-slice_fusion.13.given_ref), channel_id=1, source_target_pairs={{0,16},{8,24},{16,32},{24,40},{32,48},{40,56},{48,0},{56,8},{1,17}... | collective-permute-start | bytes 1572872 | tf_op jit(solution)/shard_map/ppermute | solution.py:44
  42.8 16.0 %collective-permute-start.14 = (bf16[2,4,2,32,512]{4,3,2,1,0:T(8,128)(2,1)}, bf16[2,4,2,32,512]{4,3,2,1,0:T(8,128)(2,1)}, u32[]{:S(2)}, u32[]{:S(2)}) collective-permute-start(bf16[2,4,2,32,512]{4,3,2,1,0:T(8,128)(2,1)} %bitcast_dynamic-update-slice_fusion.13.given_ref), channel_id=1, source_target_pairs={{0,48},{8,56},{16,0},{24,8},{32,16},{40,24},{48,32},{56,40},{1,49}... | collective-permute-start | bytes 1572872 | tf_op jit(solution)/shard_map/ppermute | solution.py:44
  52.5 16.7 %collective-permute-start.7 = (bf16[2,2,2,32,512]{4,3,2,1,0:T(8,128)(2,1)S(1)}, bf16[2,2,2,32,512]{4,3,2,1,0:T(8,128)(2,1)S(1)}, u32[]{:S(2)}, u32[]{:S(2)}) collective-permute-start(bf16[2,2,2,32,512]{4,3,2,1,0:T(8,128)(2,1)S(1)} %slice.288), channel_id=1, source_target_pairs={{0,2},{1,3},{2,4},{3,5},{4,6},{5,7},{6,0},{7,1},{8,10},{9,11},{10,... | collective-permute-start | bytes 786440 | tf_op jit(solution)/shard_map/ppermute | solution.py:44
  55.3 13.9 %collective-permute-start.8 = (bf16[2,2,2,32,512]{4,3,2,1,0:T(8,128)(2,1)S(1)}, bf16[2,2,2,32,512]{4,3,2,1,0:T(8,128)(2,1)S(1)}, u32[]{:S(2)}, u32[]{:S(2)}) collective-permute-start(bf16[2,2,2,32,512]{4,3,2,1,0:T(8,128)(2,1)S(1)} %slice.289), channel_id=1, source_target_pairs={{0,6},{1,7},{2,0},{3,1},{4,2},{5,3},{6,4},{7,5},{8,14},{9,15},{10,... | collective-permute-start | bytes 786440 | tf_op jit(solution)/shard_map/ppermute | solution.py:44
  58.7 18.5 %collective-permute-start.15 = (bf16[1,4,2,32,512]{4,3,2,1,0:T(8,128)(2,1)S(1)}, bf16[1,4,2,32,512]{4,3,2,1,0:T(8,128)(2,1)S(1)}, u32[]{:S(2)}, u32[]{:S(2)}) collective-permute-start(bf16[1,4,2,32,512]{4,3,2,1,0:T(8,128)(2,1)S(1)} %slice.295), channel_id=1, source_target_pairs={{0,16},{8,24},{16,32},{24,40},{32,48},{40,56},{48,0},{56,8},{1,17}... | collective-permute-start | bytes 786440 | tf_op jit(solution)/shard_map/ppermute | solution.py:44
  59.8 18.1 %collective-permute-start.16 = (bf16[1,4,2,32,512]{4,3,2,1,0:T(8,128)(2,1)S(1)}, bf16[1,4,2,32,512]{4,3,2,1,0:T(8,128)(2,1)S(1)}, u32[]{:S(2)}, u32[]{:S(2)}) collective-permute-start(bf16[1,4,2,32,512]{4,3,2,1,0:T(8,128)(2,1)S(1)} %slice.296), channel_id=1, source_target_pairs={{0,48},{8,56},{16,0},{24,8},{32,16},{40,24},{48,32},{56,40},{1,49}... | collective-permute-start | bytes 786440 | tf_op jit(solution)/shard_map/ppermute | solution.py:44
  69.3 12.4 %collective-permute-start.9 = (bf16[64,32,512]{2,1,0:T(8,128)(2,1)S(1)}, bf16[64,32,512]{2,1,0:T(8,128)(2,1)S(1)}, u32[]{:S(2)}, u32[]{:S(2)}) collective-permute-start(bf16[64,32,512]{2,1,0:T(8,128)(2,1)S(1)} %bitcast.258), channel_id=1, source_target_pairs={{0,1},{1,0},{2,3},{3,2},{4,5},{5,4},{6,7},{7,6},{8,9},{9,8},{10,11... | collective-permute-start | bytes 6291464 | tf_op jit(solution)/shard_map/ppermute | solution.py:49
  78.7 8.7 %collective-permute-start.17 = (bf16[64,32,512]{2,1,0:T(8,128)(2,1)}, bf16[64,32,512]{2,1,0:T(8,128)(2,1)}, u32[]{:S(2)}, u32[]{:S(2)}) collective-permute-start(bf16[64,32,512]{2,1,0:T(8,128)(2,1)} %bitcast.41.qk_mine_ref), channel_id=1, source_target_pairs={{0,1},{1,0},{2,3},{3,2},{4,5},{5,4},{6,7},{7,6},{8,9},{9,8},{10,11... | collective-permute-start | bytes 6291464 | tf_op jit(solution)/shard_map/ppermute | solution.py:49
  93.6 30.8 %all-to-all-start = ((bf16[8,256,384]{2,1,0:T(8,128)(2,1)}), bf16[8,256,384]{2,1,0:T(8,128)(2,1)S(1)}, u32[]{:S(2)}, u32[]{:S(2)}) async-start(bf16[8,256,384]{2,1,0:T(8,128)(2,1)} %get-tuple-element.44), calls=%async_computation | async-start | bytes 3145728 | tf_op jit(solution)/shard_map/all_to_all | solution.py:218
  160.6 12.5 %collective-permute-start.18 = (bf16[256,1024]{1,0:T(8,128)(2,1)}, bf16[256,1024]{1,0:T(8,128)(2,1)S(1)}, u32[]{:S(2)}, u32[]{:S(2)}) collective-permute-start(bf16[256,1024]{1,0:T(8,128)(2,1)} %shard_map.320), channel_id=1, source_target_pairs={{0,64},{1,65},{2,66},{3,67},{4,68},{5,69},{6,70},{7,71},{8,72},{9,... | collective-permute-start | bytes 1572872 | tf_op jit(solution)/shard_map/ppermute | solution.py:224
  258.7 13.9 %all-to-all-start.4 = ((bf16[8,256,128]{2,1,0:T(8,128)(2,1)}), bf16[8,256,128]{2,1,0:T(8,128)(2,1)S(1)}, u32[]{:S(2)}, u32[]{:S(2)}) async-start(bf16[8,256,128]{2,1,0:T(8,128)(2,1)} %get-tuple-element.52), calls=%async_computation.4 | async-start | bytes 1048576 | tf_op jit(solution)/shard_map/all_to_all | solution.py:218
  263.1 164.8 %all-gather.7.cloned.1.call-start = ((), (), s32[]{:S(2)}) async-start(), calls=%async_computation.10 | async-start | bytes 4718592 | tf_op jit(solution)/shard_map/all_gather | solution.py:963
  263.1 58.1 %collective-permute-start.19 = (bf16[256,6144]{1,0:T(8,128)(2,1)}, bf16[256,6144]{1,0:T(8,128)(2,1)}, u32[]{:S(2)}, u32[]{:S(2)}) collective-permute-start(bf16[256,6144]{1,0:T(8,128)(2,1)} %get-tuple-element.55.active_ref.normed_ref.attn_ref), channel_id=1, source_target_pairs={{0,1},{1,0},{2,3},{3,2},{4,5},{5,4},{6,7},{7,6},{8,9},{9,8},{10,11... | collective-permute-start | bytes 9437192 | tf_op jit(solution)/shard_map/ppermute | solution.py:49
  321.2 14.5 %collective-permute-start.20 = (bf16[256,1024]{1,0:T(8,128)(2,1)}, bf16[256,1024]{1,0:T(8,128)(2,1)S(1)}, u32[]{:S(2)}, u32[]{:S(2)}) collective-permute-start(bf16[256,1024]{1,0:T(8,128)(2,1)} %shard_map.326), channel_id=1, source_target_pairs={{64,0},{65,1},{66,2},{67,3},{68,4},{69,5},{70,6},{71,7},{72,8},{73... | collective-permute-start | bytes 1572872 | tf_op jit(solution)/shard_map/ppermute | solution.py:224
  354.7 21.8 %all-to-all-start.6 = ((bf16[8,256,128]{2,1,0:T(8,128)(2,1)}), bf16[8,256,128]{2,1,0:T(8,128)(2,1)S(1)}, u32[]{:S(2)}, u32[]{:S(2)}) async-start(bf16[8,256,128]{2,1,0:T(8,128)(2,1)} %get-tuple-element.57), calls=%async_computation.6 | async-start | bytes 1048576 | tf_op jit(solution)/shard_map/all_to_all | solution.py:218
  373.8 14.9 %collective-permute-start.24 = (bf16[2,2,2,64,512]{4,3,2,1,0:T(8,128)(2,1)}, bf16[2,2,2,64,512]{4,3,2,1,0:T(8,128)(2,1)S(1)}, u32[]{:S(2)}, u32[]{:S(2)}) collective-permute-start(bf16[2,2,2,64,512]{4,3,2,1,0:T(8,128)(2,1)} %get-tuple-element.79), channel_id=1, source_target_pairs={{0,2},{1,3},{2,4},{3,5},{4,6},{5,7},{6,0},{7,1},{8,10},{9,11},{10,... | collective-permute-start | bytes 1572872 | tf_op jit(solution)/shard_map/ppermute | solution.py:44
  375.2 13.5 %collective-permute-start.25 = (bf16[2,2,2,64,512]{4,3,2,1,0:T(8,128)(2,1)}, bf16[2,2,2,64,512]{4,3,2,1,0:T(8,128)(2,1)}, u32[]{:S(2)}, u32[]{:S(2)}) collective-permute-start(bf16[2,2,2,64,512]{4,3,2,1,0:T(8,128)(2,1)} %get-tuple-element.80), channel_id=1, source_target_pairs={{0,6},{1,7},{2,0},{3,1},{4,2},{5,3},{6,4},{7,5},{8,14},{9,15},{10,... | collective-permute-start | bytes 1572872 | tf_op jit(solution)/shard_map/ppermute | solution.py:44
  380.3 29.8 %collective-permute-start.22 = (bf16[1,4,2,80,512]{4,3,2,1,0:T(8,128)(2,1)}, bf16[1,4,2,80,512]{4,3,2,1,0:T(8,128)(2,1)}, u32[]{:S(2)}, u32[]{:S(2)}) collective-permute-start(bf16[1,4,2,80,512]{4,3,2,1,0:T(8,128)(2,1)} %get-tuple-element.72), channel_id=1, source_target_pairs={{0,16},{8,24},{16,32},{24,40},{32,48},{40,56},{48,0},{56,8},{1,17}... | collective-permute-start | bytes 1966088 | tf_op jit(solution)/shard_map/ppermute | solution.py:44
  380.3 29.8 %collective-permute-start.23 = (bf16[1,4,2,80,512]{4,3,2,0,1:T(8,128)(2,1)}, bf16[1,4,2,80,512]{4,3,2,0,1:T(8,128)(2,1)S(1)}, u32[]{:S(2)}, u32[]{:S(2)}) collective-permute-start(bf16[1,4,2,80,512]{4,3,2,0,1:T(8,128)(2,1)} %get-tuple-element.74), channel_id=1, source_target_pairs={{0,48},{8,56},{16,0},{24,8},{32,16},{40,24},{48,32},{56,40},{1,49}... | collective-permute-start | bytes 1966088 | tf_op jit(solution)/shard_map/ppermute | solution.py:44
  391.4 31.4 %collective-permute-start.35 = (bf16[4,2,2,64,512]{4,3,2,1,0:T(8,128)(2,1)}, bf16[4,2,2,64,512]{4,3,2,1,0:T(8,128)(2,1)}, u32[]{:S(2)}, u32[]{:S(2)}) collective-permute-start(bf16[4,2,2,64,512]{4,3,2,1,0:T(8,128)(2,1)} %pad_maximum_fusion.3), channel_id=1, source_target_pairs={{0,6},{1,7},{2,0},{3,1},{4,2},{5,3},{6,4},{7,5},{8,14},{9,15},{10,... | collective-permute-start | bytes 3145736 | tf_op jit(solution)/shard_map/ppermute | solution.py:44
  394.8 27.9 %collective-permute-start.34 = (bf16[4,2,2,64,512]{4,3,2,1,0:T(8,128)(2,1)}, bf16[4,2,2,64,512]{4,3,2,1,0:T(8,128)(2,1)}, u32[]{:S(2)}, u32[]{:S(2)}) collective-permute-start(bf16[4,2,2,64,512]{4,3,2,1,0:T(8,128)(2,1)} %pad_maximum_fusion.2), channel_id=1, source_target_pairs={{0,2},{1,3},{2,4},{3,5},{4,6},{5,7},{6,0},{7,1},{8,10},{9,11},{10,... | collective-permute-start | bytes 3145736 | tf_op jit(solution)/shard_map/ppermute | solution.py:44
  410.1 26.8 %all-to-all-start.7 = ((bf16[8,256,384]{2,1,0:T(8,128)(2,1)}), bf16[8,256,384]{2,1,0:T(8,128)(2,1)S(1)}, u32[]{:S(2)}, u32[]{:S(2)}) async-start(bf16[8,256,384]{2,1,0:T(8,128)(2,1)} %bitcast.267), calls=%async_computation.7 | async-start | bytes 3145728 | tf_op jit(solution)/shard_map/all_to_all | solution.py:218
  418.6 30.7 %collective-permute-start.27 = (bf16[2,4,2,80,512]{4,3,2,0,1:T(8,128)(2,1)}, bf16[2,4,2,80,512]{4,3,2,0,1:T(8,128)(2,1)}, u32[]{:S(2)}, u32[]{:S(2)}) collective-permute-start(bf16[2,4,2,80,512]{4,3,2,0,1:T(8,128)(2,1)} %pad_maximum_fusion.1), channel_id=1, source_target_pairs={{0,48},{8,56},{16,0},{24,8},{32,16},{40,24},{48,32},{56,40},{1,49}... | collective-permute-start | bytes 3932168 | tf_op jit(solution)/shard_map/ppermute | solution.py:44
  421.3 43.2 %collective-permute-start.26 = (bf16[2,4,2,80,512]{4,3,2,1,0:T(8,128)(2,1)}, bf16[2,4,2,80,512]{4,3,2,1,0:T(8,128)(2,1)}, u32[]{:S(2)}, u32[]{:S(2)}) collective-permute-start(bf16[2,4,2,80,512]{4,3,2,1,0:T(8,128)(2,1)} %pad_maximum_fusion), channel_id=1, source_target_pairs={{0,16},{8,24},{16,32},{24,40},{32,48},{40,56},{48,0},{56,8},{1,17}... | collective-permute-start | bytes 3932168 | tf_op jit(solution)/shard_map/ppermute | solution.py:44
  425.9 48.6 %collective-permute-start.38 = (bf16[2,2,64,512]{3,2,1,0:T(8,128)(2,1)}, bf16[2,2,64,512]{3,2,1,0:T(8,128)(2,1)}, u32[]{:S(2)}, u32[]{:S(2)}) collective-permute-start(bf16[2,2,64,512]{3,2,1,0:T(8,128)(2,1)} %get-tuple-element.85), channel_id=1, source_target_pairs={{0,48},{8,56},{16,0},{24,8},{32,16},{40,24},{48,32},{56,40},{1,49}... | collective-permute-start | bytes 786440 | tf_op jit(solution)/shard_map/ppermute | solution.py:44
  427.1 48.0 %collective-permute-start.37 = (bf16[2,2,64,512]{3,2,1,0:T(8,128)(2,1)S(1)}, bf16[2,2,64,512]{3,2,1,0:T(8,128)(2,1)}, u32[]{:S(2)}, u32[]{:S(2)}) collective-permute-start(bf16[2,2,64,512]{3,2,1,0:T(8,128)(2,1)S(1)} %get-tuple-element.86), channel_id=1, source_target_pairs={{0,32},{8,40},{16,48},{24,56},{32,0},{40,8},{48,16},{56,24},{1,33}... | collective-permute-start | bytes 786440 | tf_op jit(solution)/shard_map/ppermute | solution.py:44
  446.8 20.6 %collective-permute-start.30 = (bf16[2,4,2,16,512]{4,3,2,1,0:T(8,128)(2,1)S(1)}, bf16[2,4,2,16,512]{4,3,2,1,0:T(8,128)(2,1)S(1)}, u32[]{:S(2)}, u32[]{:S(2)}) collective-permute-start(bf16[2,4,2,16,512]{4,3,2,1,0:T(8,128)(2,1)S(1)} %get-tuple-element.88), channel_id=1, source_target_pairs={{0,48},{8,56},{16,0},{24,8},{32,16},{40,24},{48,32},{56,40},{1,49}... | collective-permute-start | bytes 786440 | tf_op jit(solution)/shard_map/ppermute | solution.py:44
  449.4 18.1 %collective-permute-start.29 = (bf16[2,4,2,16,512]{4,3,2,1,0:T(8,128)(2,1)S(1)}, bf16[2,4,2,16,512]{4,3,2,1,0:T(8,128)(2,1)S(1)}, u32[]{:S(2)}, u32[]{:S(2)}) collective-permute-start(bf16[2,4,2,16,512]{4,3,2,1,0:T(8,128)(2,1)S(1)} %get-tuple-element.89), channel_id=1, source_target_pairs={{0,32},{8,40},{16,48},{24,56},{32,0},{40,8},{48,16},{56,24},{1,33}... | collective-permute-start | bytes 786440 | tf_op jit(solution)/shard_map/ppermute | solution.py:44
  464.5 9.7 %collective-permute-start.28 = (bf16[2,4,2,16,512]{4,3,2,1,0:T(8,128)(2,1)S(1)}, bf16[2,4,2,16,512]{4,3,2,1,0:T(8,128)(2,1)S(1)}, u32[]{:S(2)}, u32[]{:S(2)}) collective-permute-start(bf16[2,4,2,16,512]{4,3,2,1,0:T(8,128)(2,1)S(1)} %get-tuple-element.87), channel_id=1, source_target_pairs={{0,16},{8,24},{16,32},{24,40},{32,48},{40,56},{48,0},{56,8},{1,17}... | collective-permute-start | bytes 786440 | tf_op jit(solution)/shard_map/ppermute | solution.py:44
  467.4 11.0 %collective-permute-start.36 = (bf16[2,2,64,512]{3,2,1,0:T(8,128)(2,1)S(1)}, bf16[2,2,64,512]{3,2,1,0:T(8,128)(2,1)S(1)}, u32[]{:S(2)}, u32[]{:S(2)}) collective-permute-start(bf16[2,2,64,512]{3,2,1,0:T(8,128)(2,1)S(1)} %get-tuple-element.84), channel_id=1, source_target_pairs={{0,16},{8,24},{16,32},{24,40},{32,48},{40,56},{48,0},{56,8},{1,17}... | collective-permute-start | bytes 786440 | tf_op jit(solution)/shard_map/ppermute | solution.py:44
  467.5 14.8 %collective-permute-start.43 = (bf16[2,128,384]{2,1,0:T(8,128)(2,1)S(1)}, bf16[2,128,384]{2,1,0:T(8,128)(2,1)S(1)}, u32[]{:S(2)}, u32[]{:S(2)}) collective-permute-start(bf16[2,128,384]{2,1,0:T(8,128)(2,1)S(1)} %get-tuple-element.91), channel_id=1, source_target_pairs={{0,48},{8,56},{16,0},{24,8},{32,16},{40,24},{48,32},{56,40},{1,49}... | collective-permute-start | bytes 589832 | tf_op jit(solution)/shard_map/ppermute | solution.py:44
  474.2 9.9 %collective-permute-start.42 = (bf16[2,128,384]{2,1,0:T(8,128)(2,1)S(1)}, bf16[2,128,384]{2,1,0:T(8,128)(2,1)S(1)}, u32[]{:S(2)}, u32[]{:S(2)}) collective-permute-start(bf16[2,128,384]{2,1,0:T(8,128)(2,1)S(1)} %get-tuple-element.92), channel_id=1, source_target_pairs={{0,32},{8,40},{16,48},{24,56},{32,0},{40,8},{48,16},{56,24},{1,33}... | collective-permute-start | bytes 589832 | tf_op jit(solution)/shard_map/ppermute | solution.py:44
  474.5 12.5 %collective-permute-start.41 = (bf16[2,128,384]{2,1,0:T(8,128)(2,1)S(1)}, bf16[2,128,384]{2,1,0:T(8,128)(2,1)S(1)}, u32[]{:S(2)}, u32[]{:S(2)}) collective-permute-start(bf16[2,128,384]{2,1,0:T(8,128)(2,1)S(1)} %get-tuple-element.90), channel_id=1, source_target_pairs={{0,16},{8,24},{16,32},{24,40},{32,48},{40,56},{48,0},{56,8},{1,17}... | collective-permute-start | bytes 589832 | tf_op jit(solution)/shard_map/ppermute | solution.py:44
  475.1 11.9 %collective-permute-start.33 = (bf16[2,2,96,512]{3,2,1,0:T(8,128)(2,1)S(1)}, bf16[2,2,96,512]{3,2,1,0:T(8,128)(2,1)S(1)}, u32[]{:S(2)}, u32[]{:S(2)}) collective-permute-start(bf16[2,2,96,512]{3,2,1,0:T(8,128)(2,1)S(1)} %get-tuple-element.83), channel_id=1, source_target_pairs={{0,6},{1,7},{2,0},{3,1},{4,2},{5,3},{6,4},{7,5},{8,14},{9,15},{10,... | collective-permute-start | bytes 1179656 | tf_op jit(solution)/shard_map/ppermute | solution.py:44
  478.3 8.7 %collective-permute-start.32 = (bf16[2,2,96,512]{3,2,1,0:T(8,128)(2,1)S(1)}, bf16[2,2,96,512]{3,2,1,0:T(8,128)(2,1)S(1)}, u32[]{:S(2)}, u32[]{:S(2)}) collective-permute-start(bf16[2,2,96,512]{3,2,1,0:T(8,128)(2,1)S(1)} %get-tuple-element.82), channel_id=1, source_target_pairs={{0,4},{1,5},{2,6},{3,7},{4,0},{5,1},{6,2},{7,3},{8,12},{9,13},{10,... | collective-permute-start | bytes 1179656 | tf_op jit(solution)/shard_map/ppermute | solution.py:44
  482.3 9.6 %collective-permute-start.31 = (bf16[2,2,96,512]{3,2,1,0:T(8,128)(2,1)S(1)}, bf16[2,2,96,512]{3,2,1,0:T(8,128)(2,1)S(1)}, u32[]{:S(2)}, u32[]{:S(2)}) collective-permute-start(bf16[2,2,96,512]{3,2,1,0:T(8,128)(2,1)S(1)} %get-tuple-element.81), channel_id=1, source_target_pairs={{0,2},{1,3},{2,4},{3,5},{4,6},{5,7},{6,0},{7,1},{8,10},{9,11},{10,... | collective-permute-start | bytes 1179656 | tf_op jit(solution)/shard_map/ppermute | solution.py:44
  492.2 24.9 %collective-permute-start.39 = (bf16[2,160,512]{2,1,0:T(8,128)(2,1)S(1)}, bf16[2,160,512]{2,1,0:T(8,128)(2,1)S(1)}, u32[]{:S(2)}, u32[]{:S(2)}) collective-permute-start(bf16[2,160,512]{2,1,0:T(8,128)(2,1)S(1)} %fusion.30), channel_id=1, source_target_pairs={{0,8},{8,0},{16,24},{24,16},{32,40},{40,32},{48,56},{56,48},{1,9},... | collective-permute-start | bytes 983048 | tf_op jit(solution)/shard_map/ppermute | solution.py:49
  503.7 18.3 %all-to-all-start.8 = ((bf16[8,16,384]{2,1,0:T(8,128)(2,1)}), bf16[8,16,384]{2,1,0:T(8,128)(2,1)S(1)}, u32[]{:S(2)}, u32[]{:S(2)}) async-start(bf16[8,16,384]{2,1,0:T(8,128)(2,1)} %bitcast.105), calls=%async_computation.8 | async-start | bytes 196608 | tf_op jit(solution)/shard_map/all_to_all | solution.py:218
  (22 other events, 160.3 us)
Sparse Core Ops, SparseCore 0:
  11.1 124.5 all-gather.4
  322.7 35.2 all-gather.6

commit v6 on v5

--- a/solution.py
+++ b/solution.py
@@ -980,6 +980,7 @@
     mlp_terms = [by_chip(fc1_proj), by_chip(fc2)]
     mlp_halves = [ring_halves(terms, way) for terms, way in zip(mlp_terms, ways)]
     grad_own_heads = call_attend_back(counts, grad_heads, heads, lse)
+    mlp_halves = after(mlp_halves, grad_own_heads)
     grad_qkv = to_peers(after(grad_own_heads, mlp_halves))
     mlp_ends = [ring_ends(*item) for item in zip(mlp_terms, mlp_halves, ways)]
     qkv_terms = call_attn_weights(normed, grad_own_heads)
@@ -994,6 +995,7 @@
         second_ring(jnp.concatenate([mlp_totals[0], small], axis=3), "dp"),
         second_ring(mlp_totals[1], "head"),
     ]
+    ring_sums = after(ring_sums, qkv_grad)
     shard_grad = collect_rest(jnp.concatenate(ring_sums, axis=2))
     fc1_grad, proj_grad, small_row, fc2_grad = (
         shard_grad[start * SLAB : stop * SLAB] for start, stop in ((0, 4), (4, 5), (5, 6), (6, 10))

time: 545 us -> 539 us (0.989)
  starting transfers between devices: 103 us -> 93.8 us
  waiting for transfers between devices: 117 us -> 123 us
    all_to_all x5, starting transfers between devices: 31.5 us -> 24.7 us  [to_peers(): lax.all_to_all(blocks, 'head', split_axis=0, concat_axis=0, tiled=True)]
  transfers between devices with their start and end apart: 52 -> 52, of which waited for: 20 -> 21; matrix products, arithmetic and copies ran while one was open for 10% -> 10% of each run, Pallas kernels for 17% -> 17%
where the time goes in v6:
time: 539 us; the launch traced here: 530 us
  Pallas kernels  146 us (27%)
  waiting for transfers between devices  123 us (23%)
  starting transfers between devices  93.8 us (17%)
  blocking collectives  83.1 us (15%)
  local copies, waits for them, and re-layouts  41.9 us (8%)
  other arithmetic  25.1 us (5%)
  between operations  16.4 us (3%)
    all_to_all x4, blocking collectives, to_peers(): lax.all_to_all(blocks, 'head', split_axis=0, concat_axis=0, tiled=True)  83.1 us
    ppermute x34, starting transfers between devices, hop(): lax.ppermute(block, axis, [(i, (i + 2 * places) % size) for i in range(si...  44.6 us
    all_to_all x5, waiting for transfers between devices, to_peers(): lax.all_to_all(blocks, 'head', split_axis=0, concat_axis=0, tiled=True)  43.6 us
    ppermute x34, waiting for transfers between devices, hop(): lax.ppermute(block, axis, [(i, (i + 2 * places) % size) for i in range(si...  40.7 us
    pallas_call x2, Pallas kernels, call_attend_back(): pl.pallas_call(attend_back_kernel, grid=(images,), in_specs=[SCALARS, pl....  30.1 us
    pallas_call x2, Pallas kernels, call_rear_back(): pl.pallas_call(functools.partial(rear_back_kernel, keep), grid=(steps,),...  30.1 us
    pallas_call x2, Pallas kernels, call_rear(): pl.pallas_call(functools.partial(rear_kernel, keep), grid=(steps,), in_sp...  26.5 us
    all_to_all x5, starting transfers between devices, to_peers(): lax.all_to_all(blocks, 'head', split_axis=0, concat_axis=0, tiled=True)  24.7 us
  transfers between devices with their start and end apart: 52, of which 21 were waited for; matrix products, arithmetic and copies ran while one was open for 10% of the time, Pallas kernels for 17%

profile of v6, /device:TPU:1, one launch (start us, length us, event | category | flops | bytes accessed | tf_op | source)
XLA Modules:
  0.0 530.2 jit_solution(8819150075860764931)
XLA Ops:
  15.9 3.8 collective-permute-start.1
  19.6 3.6 collective-permute-done.1
  30.1 2.6 collective-permute-start.11
  42.8 2.7 collective-permute-start.14
  48.1 3.4 collective-permute-done.5
  59.8 3.4 collective-permute-start.16
  69.3 7.9 %collective-permute-start.9 = (bf16[64,32,512]{2,1,0:T(8,128)(2,1)S(1)}, bf16[64,32,512]{2,1,0:T(8,128)(2,1)S(1)}, u32[]{:S(2)}, u32[]{:S(2)}) collective-permute-start(bf16[64,32,512]{2,1,0:T(8,128)(2,1)S(1)} %bitcast.256), channel_id=1, source_target_pairs={{0,1},{1,0},{2,3},{3,2},{4,5},{5,4},{6,7},{7,6},{8,9},{9,8},{10,11... | collective-permute-start | bytes 6291464 | tf_op jit(solution)/shard_map/ppermute | solution.py:49
  84.1 3.2 collective-permute-done.17.qk_other_ref
  87.3 6.2 %shard_map.318 = (bf16[8,256,384]{2,1,0:T(8,128)(2,1)}, bf16[256,1024]{1,0:T(8,128)(2,1)}) custom-call(s32[1]{0:T(128)} %bitcast.2.core_ref, bf16[256,1024]{1,0:T(8,128)(2,1)} %bitcast.249, f32[16,1024]{1,0:T(8,128)} %select_maximum_fusion.table_ref, bf16[64,32,512]{2,1,0:T(8,128)(2,1)} %bitcast.41.qk_mine_ref, bf16[64,32,512]{2,1,0:T(8,128)(2,1)} %bitcast.258, ...), custom_call_target="tpu_custom_call" | custom-call | flops 7474999808 | bytes 19500000 | tf_op jit(solution)/shard_map/pallas_call | solution.py:666
  93.6 4.2 all-to-all-start
  98.5 25.8 %all-to-all-done = bf16[8,256,384]{2,1,0:T(8,128)(2,1)S(1)} async-done(((bf16[8,256,384]{2,1,0:T(8,128)(2,1)}), bf16[8,256,384]{2,1,0:T(8,128)(2,1)S(1)}, u32[]{:S(2)}, u32[]{:S(2)}) %all-to-all-start) | async-done | bytes 1572896 | tf_op jit(solution)/shard_map/all_to_all | solution.py:218
  125.5 8.1 %shard_map.319 = (bf16[8,2,128,128]{3,2,1,0:T(8,128)(2,1)}, f32[2,2,1024]{2,1,0:T(2,128)}) custom-call(s32[2]{0:T(128)} %broadcast_select_fusion.5.count_ref, bf16[8,2,128,384]{3,2,1,0:T(8,128)(2,1)} %bitcast.265), custom_call_target="tpu_custom_call" | custom-call | flops 16444999680 | bytes 42900000 | tf_op jit(solution)/shard_map/pallas_call | solution.py:681
  133.6 15.1 %all_to_all.45.attn_ref = bf16[8,256,128]{2,1,0:T(8,128)(2,1)} all-to-all(bf16[8,256,128]{2,1,0:T(8,128)(2,1)} %bitcast.276), channel_id=1, replica_groups=mesh['section'=2,'dp'=8,'head'=8] {'head'}, dimensions={0} | all-to-all | bytes 1048576 | tf_op jit(solution)/shard_map/all_to_all | solution.py:218
  148.6 11.9 %shard_map.320 = bf16[256,1024]{1,0:T(8,128)(2,1)} custom-call(bf16[256,1024]{1,0:T(8,128)(2,1)} %bitcast.250, bf16[8,256,128]{2,1,0:T(8,128)(2,1)} %all_to_all.45.attn_ref, f32[16,1024]{1,0:T(8,128)} %select_maximum_fusion.table_ref, bf16[64,144,1024]{2,1,0:T(8,128)(2,1)} %bitcast.233, bf16[64,144,1024]{2,1,0:T(8,128)(2,1)} %bitcast.234, ...), custom_call_target="tpu_custom_call" | custom-call | flops 14949999616 | bytes 39000000 | tf_op jit(solution)/shard_map/pallas_call | solution.py:741
  162.6 10.4 %collective-permute-done.18 = bf16[256,1024]{1,0:T(8,128)(2,1)S(1)} collective-permute-done((bf16[256,1024]{1,0:T(8,128)(2,1)}, bf16[256,1024]{1,0:T(8,128)(2,1)S(1)}, u32[]{:S(2)}, u32[]{:S(2)}) %collective-permute-start.18) | collective-permute-done | bytes 524320 | tf_op jit(solution)/shard_map/ppermute | solution.py:224
  173.9 6.2 %shard_map.321 = (bf16[8,256,384]{2,1,0:T(8,128)(2,1)}, bf16[256,1024]{1,0:T(8,128)(2,1)}) custom-call(s32[1]{0:T(128)} %bitcast.2.core_ref, bf16[256,1024]{1,0:T(8,128)(2,1)} %broadcast_select_fusion.1.x_ref, f32[16,1024]{1,0:T(8,128)} %select_maximum_fusion.table_ref, bf16[64,32,512]{2,1,0:T(8,128)(2,1)} %bitcast.41.qk_mine_ref, ...), custom_call_target="tpu_custom_call" | custom-call | flops 7474999808 | bytes 19500000 | tf_op jit(solution)/shard_map/pallas_call | solution.py:666
  180.2 27.0 %all_to_all.46 = bf16[8,256,384]{2,1,0:T(8,128)(2,1)} all-to-all(bf16[8,256,384]{2,1,0:T(8,128)(2,1)} %get-tuple-element.52), channel_id=1, replica_groups=mesh['section'=2,'dp'=8,'head'=8] {'head'}, dimensions={0} | all-to-all | bytes 3145728 | tf_op jit(solution)/shard_map/all_to_all | solution.py:218
  207.2 7.8 %shard_map.322 = (bf16[8,2,128,128]{3,2,1,0:T(8,128)(2,1)}, f32[2,2,1024]{2,1,0:T(2,128)}) custom-call(s32[2]{0:T(128)} %broadcast_select_fusion.5.count_ref, bf16[8,2,128,384]{3,2,1,0:T(8,128)(2,1)} %bitcast.262), custom_call_target="tpu_custom_call" | custom-call | flops 16444999680 | bytes 42900000 | tf_op jit(solution)/shard_map/pallas_call | solution.py:681
  215.0 14.9 %all_to_all.47.attn_ref = bf16[8,256,128]{2,1,0:T(8,128)(2,1)} all-to-all(bf16[8,256,128]{2,1,0:T(8,128)(2,1)} %bitcast.277), channel_id=1, replica_groups=mesh['section'=2,'dp'=8,'head'=8] {'head'}, dimensions={0} | all-to-all | bytes 1048576 | tf_op jit(solution)/shard_map/all_to_all | solution.py:218
  230.0 14.6 %shard_map.323 = (bf16[256,1024]{1,0:T(8,128)(2,1)}, f32[256,1024]{1,0:T(8,128)}, f32[256,4096]{1,0:T(8,128)}, f32[256,1024]{1,0:T(8,128)}, bf16[256,6144]{1,0:T(8,128)(2,1)}) custom-call(bf16[256,1024]{1,0:T(8,128)(2,1)} %broadcast_select_fusion.1.x_ref, bf16[8,256,128]{2,1,0:T(8,128)(2,1)} %all_to_all.47.attn_ref, ...), custom_call_target="tpu_custom_call" | custom-call | flops 14949999616 | bytes 39000000 | tf_op jit(solution)/shard_map/pallas_call | solution.py:741
  244.6 14.1 %shard_map.324 = (bf16[8,256,128]{2,1,0:T(8,128)(2,1)}, f32[256,1024]{1,0:T(8,128)}) custom-call(s32[1]{0:T(128)} %bitcast.2.core_ref, bf16[256,1024]{1,0:T(8,128)(2,1)} %bitcast.273, bf16[256,1024]{1,0:T(8,128)(2,1)} %broadcast_select_fusion.1.x_ref, f32[256,1024]{1,0:T(8,128)} %get-tuple-element.55.branch_ref, f32[256,4096]{1,0:T(8,128)} %get-tuple-element.56.hidden_ref, ...), custom_call_target="tpu_custom_call" | custom-call | flops 18400000000 | bytes 48000000 | tf_op jit(solution)/shard_map/pallas_call | solution.py:770
  258.7 4.4 all-to-all-start.4
  263.4 9.3 %all-to-all-done.4 = bf16[8,256,128]{2,1,0:T(8,128)(2,1)S(1)} async-done(((bf16[8,256,128]{2,1,0:T(8,128)(2,1)}), bf16[8,256,128]{2,1,0:T(8,128)(2,1)S(1)}, u32[]{:S(2)}, u32[]{:S(2)}) %all-to-all-start.4) | async-done | bytes 524320 | tf_op jit(solution)/shard_map/all_to_all | solution.py:218
  273.4 15.1 %shard_map.325 = bf16[8,2,128,384]{3,2,1,0:T(8,128)(2,1)} custom-call(s32[2]{0:T(128)} %broadcast_select_fusion.5.count_ref, bf16[8,2,128,128]{3,2,1,0:T(8,128)(2,1)} %bitcast.275, bf16[8,2,128,384]{3,2,1,0:T(8,128)(2,1)} %bitcast.263, f32[2,2,1024]{2,1,0:T(2,128)} %get-tuple-element.59.lse_ref), custom_call_target="tpu_custom_call" | custom-call | flops 18975000576 | bytes 49500000 | tf_op jit(solution)/shard_map/pallas_call | solution.py:703
  288.5 26.1 %all_to_all.48.grad_ref = bf16[8,256,384]{2,1,0:T(8,128)(2,1)} all-to-all(bf16[8,256,384]{2,1,0:T(8,128)(2,1)} %bitcast.266), channel_id=1, replica_groups=mesh['section'=2,'dp'=8,'head'=8] {'head'}, dimensions={0} | all-to-all | bytes 3145728 | tf_op jit(solution)/shard_map/all_to_all | solution.py:218
  314.6 6.7 %shard_map.326 = bf16[256,1024]{1,0:T(8,128)(2,1)} custom-call(s32[1]{0:T(128)} %bitcast.2.core_ref, bf16[8,256,384]{2,1,0:T(8,128)(2,1)} %all_to_all.48.grad_ref, f32[256,1024]{1,0:T(8,128)} %get-tuple-element.60.middle_grad_ref, bf16[256,1024]{1,0:T(8,128)(2,1)} %broadcast_select_fusion.1.x_ref, f32[16,1024]{1,0:T(8,128)} %select_maximum_fusion.table_ref, ...), custom_call_target="tpu_custom_call" | custom-call | flops 8049999872 | bytes 21000000 | tf_op jit(solution)/shard_map/pallas_call | solution.py:800
  322.6 13.2 %collective-permute-done.20 = bf16[256,1024]{1,0:T(8,128)(2,1)S(1)} collective-permute-done((bf16[256,1024]{1,0:T(8,128)(2,1)}, bf16[256,1024]{1,0:T(8,128)(2,1)S(1)}, u32[]{:S(2)}, u32[]{:S(2)}) %collective-permute-start.20) | collective-permute-done | bytes 524320 | tf_op jit(solution)/shard_map/ppermute | solution.py:224
  336.7 16.0 %shard_map.327 = (bf16[8,256,128]{2,1,0:T(8,128)(2,1)}, f32[256,1024]{1,0:T(8,128)}, bf16[256,3072]{1,0:T(8,128)(2,1)}, bf16[256,3072]{1,0:T(8,128)(2,1)}, f32[16,1024]{1,0:T(8,128)}) custom-call(s32[1]{0:T(128)} %bitcast.2.core_ref, bf16[256,1024]{1,0:T(8,128)(2,1)} %broadcast_select_fusion.grad_ref, bf16[256,1024]{1,0:T(8,128)(2,1)} %broadcast_select_fusion.1.x_ref, ...), custom_call_target="tpu_custom_call" | custom-call | flops 18400000000 | bytes 48000000 | tf_op jit(solution)/shard_map/pallas_call | solution.py:770
  354.7 3.5 all-to-all-start.6
  359.4 11.7 %shard_map.328 = (bf16[64,80,512]{2,1,0:T(8,128)(2,1)}, bf16[64,64,512]{2,1,0:T(8,128)(2,1)}) custom-call(bf16[256,6144]{1,0:T(8,128)(2,1)} %get-tuple-element.61.active_ref.normed_ref.attn_ref, bf16[256,6144]{1,0:T(8,128)(2,1)} %collective-permute-done.19.active_other_ref.normed_other_ref.attn_other_ref, ...), custom_call_target="tpu_custom_call" | custom-call | flops 10350000128 | bytes 27000000 | tf_op jit(solution)/shard_map/pallas_call | solution.py:823
  372.0 2.9 dynamic-slice_bitcast_fusion.1
  374.9 2.7 collective-permute-start.23
  381.6 15.1 %shard_map.329 = bf16[8,2,128,384]{3,2,1,0:T(8,128)(2,1)} custom-call(s32[2]{0:T(128)} %broadcast_select_fusion.5.count_ref, bf16[8,2,128,128]{3,2,1,0:T(8,128)(2,1)} %bitcast.274, bf16[8,2,128,384]{3,2,1,0:T(8,128)(2,1)} %bitcast.264, f32[2,2,1024]{2,1,0:T(2,128)} %get-tuple-element.59.lse_ref), custom_call_target="tpu_custom_call" | custom-call | flops 18975000576 | bytes 49500000 | tf_op jit(solution)/shard_map/pallas_call | solution.py:703
  402.2 6.2 %all-to-all-start.7 = ((bf16[8,256,384]{2,1,0:T(8,128)(2,1)}), bf16[8,256,384]{2,1,0:T(8,128)(2,1)S(1)}, u32[]{:S(2)}, u32[]{:S(2)}) async-start(bf16[8,256,384]{2,1,0:T(8,128)(2,1)} %bitcast.56.grad_ref), calls=%async_computation.7 | async-start | bytes 3145728 | tf_op jit(solution)/shard_map/all_to_all | solution.py:218
  414.9 8.4 %collective-permute-done.35 = bf16[4,2,2,64,512]{4,3,2,1,0:T(8,128)(2,1)} collective-permute-done((bf16[4,2,2,64,512]{4,3,2,1,0:T(8,128)(2,1)}, bf16[4,2,2,64,512]{4,3,2,1,0:T(8,128)(2,1)}, u32[]{:S(2)}, u32[]{:S(2)}) %collective-permute-start.35) | collective-permute-done | bytes 1048608 | tf_op jit(solution)/shard_map/ppermute | solution.py:44
  423.4 4.1 collective-permute-done.34
  431.7 6.0 %shard_map.330 = bf16[1024,384]{1,0:T(8,128)(2,1)} custom-call(bf16[8,256,1024]{2,1,0:T(8,128)(2,1)} %bitcast.291, bf16[8,256,384]{2,1,0:T(8,128)(2,1)} %bitcast.56.grad_ref), custom_call_target="tpu_custom_call" | custom-call | flops 6899999744 | bytes 18000000 | tf_op jit(solution)/shard_map/pallas_call | solution.py:844
  437.6 4.7 all-to-all-done.7.grad_ref
  443.5 7.0 %shard_map.331 = (bf16[256,1024]{1,0:T(8,128)(2,1)}, f32[16,1024]{1,0:T(8,128)}) custom-call(s32[1]{0:T(128)} %bitcast.2.core_ref, bf16[8,256,384]{2,1,0:T(8,128)(2,1)} %copy-done.6, f32[256,1024]{1,0:T(8,128)} %get-tuple-element.77.middle_grad_ref, bf16[256,1024]{1,0:T(8,128)(2,1)} %broadcast_select_fusion.1.x_ref, ...), custom_call_target="tpu_custom_call" | custom-call | flops 8049999872 | bytes 21000000 | tf_op jit(solution)/shard_map/pallas_call | solution.py:800
  453.8 2.7 fusion
  459.4 4.7 collective-permute-start.43
  467.1 6.1 %collective-permute-done.36 = bf16[2,2,64,512]{3,2,1,0:T(8,128)(2,1)S(1)} collective-permute-done((bf16[2,2,64,512]{3,2,1,0:T(8,128)(2,1)S(1)}, bf16[2,2,64,512]{3,2,1,0:T(8,128)(2,1)S(1)}, u32[]{:S(2)}, u32[]{:S(2)}) %collective-permute-start.36) | collective-permute-done | bytes 262176 | tf_op jit(solution)/shard_map/ppermute | solution.py:44
  477.6 3.9 collective-permute-done.32
  481.5 11.0 %collective-permute-done.31 = bf16[2,2,96,512]{3,2,1,0:T(8,128)(2,1)S(1)} collective-permute-done((bf16[2,2,96,512]{3,2,1,0:T(8,128)(2,1)S(1)}, bf16[2,2,96,512]{3,2,1,0:T(8,128)(2,1)S(1)}, u32[]{:S(2)}, u32[]{:S(2)}) %collective-permute-start.31) | collective-permute-done | bytes 393248 | tf_op jit(solution)/shard_map/ppermute | solution.py:44
  492.9 5.3 %collective-permute-start.39 = (bf16[2,160,512]{2,1,0:T(8,128)(2,1)S(1)}, bf16[2,160,512]{2,1,0:T(8,128)(2,1)S(1)}, u32[]{:S(2)}, u32[]{:S(2)}) collective-permute-start(bf16[2,160,512]{2,1,0:T(8,128)(2,1)S(1)} %fusion.25), channel_id=1, source_target_pairs={{0,8},{8,0},{16,24},{24,16},{32,40},{40,32},{48,56},{56,48},{1,9},... | collective-permute-start | bytes 983048 | tf_op jit(solution)/shard_map/ppermute | solution.py:49
  498.4 7.8 %collective-permute-done.44 = bf16[128,384]{1,0:T(8,128)(2,1)S(1)} collective-permute-done((bf16[128,384]{1,0:T(8,128)(2,1)S(1)}, bf16[128,384]{1,0:T(8,128)(2,1)S(1)}, u32[]{:S(2)}, u32[]{:S(2)}) %collective-permute-start.44) | collective-permute-done | bytes 98336 | tf_op jit(solution)/shard_map/ppermute | solution.py:49
  506.8 6.4 %all-to-all-start.8 = ((bf16[8,16,384]{2,1,0:T(8,128)(2,1)}), bf16[8,16,384]{2,1,0:T(8,128)(2,1)S(1)}, u32[]{:S(2)}, u32[]{:S(2)}) async-start(bf16[8,16,384]{2,1,0:T(8,128)(2,1)} %bitcast.105), calls=%async_computation.8 | async-start | bytes 196608 | tf_op jit(solution)/shard_map/all_to_all | solution.py:218
  514.4 3.8 all-to-all-done.8
  (220 shorter events, 102.0 us)
Async XLA Ops:
  7.2 141.4 %all-gather.5.cloned.1.call-start = ((), (), s32[]{:S(2)}) async-start(), calls=%async_computation.9 | async-start | bytes 19169280 | tf_op jit(solution)/shard_map/all_gather | solution.py:933
  15.9 7.3 %collective-permute-start.1 = (bf16[2,64,512]{2,1,0:T(8,128)(2,1)S(1)}, bf16[2,64,512]{2,1,0:T(8,128)(2,1)S(1)}, u32[]{:S(2)}, u32[]{:S(2)}) collective-permute-start(bf16[2,64,512]{2,1,0:T(8,128)(2,1)S(1)} %maximum_select_fusion.3), channel_id=1, source_target_pairs={{0,8},{8,0},{16,24},{24,16},{32,40},{40,32},{48,56},{56,48},{1,9},... | collective-permute-start | bytes 393224 | tf_op jit(solution)/shard_map/ppermute | solution.py:49
  24.0 10.1 %collective-permute-start.2 = (bf16[2,2,32,512]{3,2,1,0:T(8,128)(2,1)}, bf16[2,2,32,512]{3,2,1,0:T(8,128)(2,1)S(1)}, u32[]{:S(2)}, u32[]{:S(2)}) collective-permute-start(bf16[2,2,32,512]{3,2,1,0:T(8,128)(2,1)} %get-tuple-element.108.given_ref), channel_id=1, source_target_pairs={{0,16},{8,24},{16,32},{24,40},{32,48},{40,56},{48,0},{56,8},{1,17}... | collective-permute-start | bytes 393224 | tf_op jit(solution)/shard_map/ppermute | solution.py:44
  25.2 11.3 %collective-permute-start.3 = (bf16[2,2,32,512]{3,2,1,0:T(8,128)(2,1)}, bf16[2,2,32,512]{3,2,1,0:T(8,128)(2,1)S(1)}, u32[]{:S(2)}, u32[]{:S(2)}) collective-permute-start(bf16[2,2,32,512]{3,2,1,0:T(8,128)(2,1)} %get-tuple-element.108.given_ref), channel_id=1, source_target_pairs={{0,32},{8,40},{16,48},{24,56},{32,0},{40,8},{48,16},{56,24},{1,33}... | collective-permute-start | bytes 393224 | tf_op jit(solution)/shard_map/ppermute | solution.py:44
  27.6 9.5 %collective-permute-start.4 = (bf16[2,2,32,512]{3,2,1,0:T(8,128)(2,1)}, bf16[2,2,32,512]{3,2,1,0:T(8,128)(2,1)S(1)}, u32[]{:S(2)}, u32[]{:S(2)}) collective-permute-start(bf16[2,2,32,512]{3,2,1,0:T(8,128)(2,1)} %get-tuple-element.108.given_ref), channel_id=1, source_target_pairs={{0,48},{8,56},{16,0},{24,8},{32,16},{40,24},{48,32},{56,40},{1,49}... | collective-permute-start | bytes 393224 | tf_op jit(solution)/shard_map/ppermute | solution.py:44
  28.8 12.0 %collective-permute-start.10 = (bf16[2,2,32,512]{3,2,1,0:T(8,128)(2,1)}, bf16[2,2,32,512]{3,2,1,0:T(8,128)(2,1)S(1)}, u32[]{:S(2)}, u32[]{:S(2)}) collective-permute-start(bf16[2,2,32,512]{3,2,1,0:T(8,128)(2,1)} %get-tuple-element.107.given_ref), channel_id=1, source_target_pairs={{0,2},{1,3},{2,4},{3,5},{4,6},{5,7},{6,0},{7,1},{8,10},{9,11},{10,... | collective-permute-start | bytes 393224 | tf_op jit(solution)/shard_map/ppermute | solution.py:44
  30.1 11.4 %collective-permute-start.11 = (bf16[2,2,32,512]{3,2,1,0:T(8,128)(2,1)}, bf16[2,2,32,512]{3,2,1,0:T(8,128)(2,1)S(1)}, u32[]{:S(2)}, u32[]{:S(2)}) collective-permute-start(bf16[2,2,32,512]{3,2,1,0:T(8,128)(2,1)} %get-tuple-element.107.given_ref), channel_id=1, source_target_pairs={{0,4},{1,5},{2,6},{3,7},{4,0},{5,1},{6,2},{7,3},{8,12},{9,13},{10,... | collective-permute-start | bytes 393224 | tf_op jit(solution)/shard_map/ppermute | solution.py:44
  34.0 8.1 %collective-permute-start.12 = (bf16[2,2,32,512]{3,2,1,0:T(8,128)(2,1)}, bf16[2,2,32,512]{3,2,1,0:T(8,128)(2,1)S(1)}, u32[]{:S(2)}, u32[]{:S(2)}) collective-permute-start(bf16[2,2,32,512]{3,2,1,0:T(8,128)(2,1)} %get-tuple-element.107.given_ref), channel_id=1, source_target_pairs={{0,6},{1,7},{2,0},{3,1},{4,2},{5,3},{6,4},{7,5},{8,14},{9,15},{10,... | collective-permute-start | bytes 393224 | tf_op jit(solution)/shard_map/ppermute | solution.py:44
  37.8 13.7 %collective-permute-start.5 = (bf16[4,2,2,32,512]{4,3,2,1,0:T(8,128)(2,1)}, bf16[4,2,2,32,512]{4,3,2,1,0:T(8,128)(2,1)}, u32[]{:S(2)}, u32[]{:S(2)}) collective-permute-start(bf16[4,2,2,32,512]{4,3,2,1,0:T(8,128)(2,1)} %bitcast_dynamic-update-slice_fusion.14.given_ref), channel_id=1, source_target_pairs={{0,2},{1,3},{2,4},{3,5},{4,6},{5,7},{6,0},{7,1},{8,10},{9,11},{10,... | collective-permute-start | bytes 1572872 | tf_op jit(solution)/shard_map/ppermute | solution.py:44
  39.2 15.2 %collective-permute-start.6 = (bf16[4,2,2,32,512]{4,3,2,1,0:T(8,128)(2,1)}, bf16[4,2,2,32,512]{4,3,2,1,0:T(8,128)(2,1)}, u32[]{:S(2)}, u32[]{:S(2)}) collective-permute-start(bf16[4,2,2,32,512]{4,3,2,1,0:T(8,128)(2,1)} %bitcast_dynamic-update-slice_fusion.14.given_ref), channel_id=1, source_target_pairs={{0,6},{1,7},{2,0},{3,1},{4,2},{5,3},{6,4},{7,5},{8,14},{9,15},{10,... | collective-permute-start | bytes 1572872 | tf_op jit(solution)/shard_map/ppermute | solution.py:44
  42.8 15.0 %collective-permute-start.13 = (bf16[2,4,2,32,512]{4,3,2,1,0:T(8,128)(2,1)}, bf16[2,4,2,32,512]{4,3,2,1,0:T(8,128)(2,1)}, u32[]{:S(2)}, u32[]{:S(2)}) collective-permute-start(bf16[2,4,2,32,512]{4,3,2,1,0:T(8,128)(2,1)} %bitcast_dynamic-update-slice_fusion.13.given_ref), channel_id=1, source_target_pairs={{0,16},{8,24},{16,32},{24,40},{32,48},{40,56},{48,0},{56,8},{1,17}... | collective-permute-start | bytes 1572872 | tf_op jit(solution)/shard_map/ppermute | solution.py:44
  42.8 16.0 %collective-permute-start.14 = (bf16[2,4,2,32,512]{4,3,2,1,0:T(8,128)(2,1)}, bf16[2,4,2,32,512]{4,3,2,1,0:T(8,128)(2,1)}, u32[]{:S(2)}, u32[]{:S(2)}) collective-permute-start(bf16[2,4,2,32,512]{4,3,2,1,0:T(8,128)(2,1)} %bitcast_dynamic-update-slice_fusion.13.given_ref), channel_id=1, source_target_pairs={{0,48},{8,56},{16,0},{24,8},{32,16},{40,24},{48,32},{56,40},{1,49}... | collective-permute-start | bytes 1572872 | tf_op jit(solution)/shard_map/ppermute | solution.py:44
  52.5 16.7 %collective-permute-start.7 = (bf16[2,2,2,32,512]{4,3,2,1,0:T(8,128)(2,1)S(1)}, bf16[2,2,2,32,512]{4,3,2,1,0:T(8,128)(2,1)S(1)}, u32[]{:S(2)}, u32[]{:S(2)}) collective-permute-start(bf16[2,2,2,32,512]{4,3,2,1,0:T(8,128)(2,1)S(1)} %slice.288), channel_id=1, source_target_pairs={{0,2},{1,3},{2,4},{3,5},{4,6},{5,7},{6,0},{7,1},{8,10},{9,11},{10,... | collective-permute-start | bytes 786440 | tf_op jit(solution)/shard_map/ppermute | solution.py:44
  55.4 13.8 %collective-permute-start.8 = (bf16[2,2,2,32,512]{4,3,2,1,0:T(8,128)(2,1)S(1)}, bf16[2,2,2,32,512]{4,3,2,1,0:T(8,128)(2,1)S(1)}, u32[]{:S(2)}, u32[]{:S(2)}) collective-permute-start(bf16[2,2,2,32,512]{4,3,2,1,0:T(8,128)(2,1)S(1)} %slice.289), channel_id=1, source_target_pairs={{0,6},{1,7},{2,0},{3,1},{4,2},{5,3},{6,4},{7,5},{8,14},{9,15},{10,... | collective-permute-start | bytes 786440 | tf_op jit(solution)/shard_map/ppermute | solution.py:44
  58.7 18.5 %collective-permute-start.15 = (bf16[1,4,2,32,512]{4,3,2,1,0:T(8,128)(2,1)S(1)}, bf16[1,4,2,32,512]{4,3,2,1,0:T(8,128)(2,1)S(1)}, u32[]{:S(2)}, u32[]{:S(2)}) collective-permute-start(bf16[1,4,2,32,512]{4,3,2,1,0:T(8,128)(2,1)S(1)} %slice.295), channel_id=1, source_target_pairs={{0,16},{8,24},{16,32},{24,40},{32,48},{40,56},{48,0},{56,8},{1,17}... | collective-permute-start | bytes 786440 | tf_op jit(solution)/shard_map/ppermute | solution.py:44
  59.8 18.1 %collective-permute-start.16 = (bf16[1,4,2,32,512]{4,3,2,1,0:T(8,128)(2,1)S(1)}, bf16[1,4,2,32,512]{4,3,2,1,0:T(8,128)(2,1)S(1)}, u32[]{:S(2)}, u32[]{:S(2)}) collective-permute-start(bf16[1,4,2,32,512]{4,3,2,1,0:T(8,128)(2,1)S(1)} %slice.296), channel_id=1, source_target_pairs={{0,48},{8,56},{16,0},{24,8},{32,16},{40,24},{48,32},{56,40},{1,49}... | collective-permute-start | bytes 786440 | tf_op jit(solution)/shard_map/ppermute | solution.py:44
  69.3 12.4 %collective-permute-start.9 = (bf16[64,32,512]{2,1,0:T(8,128)(2,1)S(1)}, bf16[64,32,512]{2,1,0:T(8,128)(2,1)S(1)}, u32[]{:S(2)}, u32[]{:S(2)}) collective-permute-start(bf16[64,32,512]{2,1,0:T(8,128)(2,1)S(1)} %bitcast.256), channel_id=1, source_target_pairs={{0,1},{1,0},{2,3},{3,2},{4,5},{5,4},{6,7},{7,6},{8,9},{9,8},{10,11... | collective-permute-start | bytes 6291464 | tf_op jit(solution)/shard_map/ppermute | solution.py:49
  78.7 8.7 %collective-permute-start.17 = (bf16[64,32,512]{2,1,0:T(8,128)(2,1)}, bf16[64,32,512]{2,1,0:T(8,128)(2,1)}, u32[]{:S(2)}, u32[]{:S(2)}) collective-permute-start(bf16[64,32,512]{2,1,0:T(8,128)(2,1)} %bitcast.41.qk_mine_ref), channel_id=1, source_target_pairs={{0,1},{1,0},{2,3},{3,2},{4,5},{5,4},{6,7},{7,6},{8,9},{9,8},{10,11... | collective-permute-start | bytes 6291464 | tf_op jit(solution)/shard_map/ppermute | solution.py:49
  93.6 30.8 %all-to-all-start = ((bf16[8,256,384]{2,1,0:T(8,128)(2,1)}), bf16[8,256,384]{2,1,0:T(8,128)(2,1)S(1)}, u32[]{:S(2)}, u32[]{:S(2)}) async-start(bf16[8,256,384]{2,1,0:T(8,128)(2,1)} %get-tuple-element.50), calls=%async_computation | async-start | bytes 3145728 | tf_op jit(solution)/shard_map/all_to_all | solution.py:218
  160.5 12.5 %collective-permute-start.18 = (bf16[256,1024]{1,0:T(8,128)(2,1)}, bf16[256,1024]{1,0:T(8,128)(2,1)S(1)}, u32[]{:S(2)}, u32[]{:S(2)}) collective-permute-start(bf16[256,1024]{1,0:T(8,128)(2,1)} %shard_map.320), channel_id=1, source_target_pairs={{0,64},{1,65},{2,66},{3,67},{4,68},{5,69},{6,70},{7,71},{8,72},{9,... | collective-permute-start | bytes 1572872 | tf_op jit(solution)/shard_map/ppermute | solution.py:224
  258.7 13.9 %all-to-all-start.4 = ((bf16[8,256,128]{2,1,0:T(8,128)(2,1)}), bf16[8,256,128]{2,1,0:T(8,128)(2,1)S(1)}, u32[]{:S(2)}, u32[]{:S(2)}) async-start(bf16[8,256,128]{2,1,0:T(8,128)(2,1)} %get-tuple-element.58), calls=%async_computation.4 | async-start | bytes 1048576 | tf_op jit(solution)/shard_map/all_to_all | solution.py:218
  263.1 168.5 %all-gather.7.cloned.1.call-start = ((), (), s32[]{:S(2)}) async-start(), calls=%async_computation.10 | async-start | bytes 4718592 | tf_op jit(solution)/shard_map/all_gather | solution.py:963
  263.1 58.2 %collective-permute-start.19 = (bf16[256,6144]{1,0:T(8,128)(2,1)}, bf16[256,6144]{1,0:T(8,128)(2,1)}, u32[]{:S(2)}, u32[]{:S(2)}) collective-permute-start(bf16[256,6144]{1,0:T(8,128)(2,1)} %get-tuple-element.61.active_ref.normed_ref.attn_ref), channel_id=1, source_target_pairs={{0,1},{1,0},{2,3},{3,2},{4,5},{5,4},{6,7},{7,6},{8,9},{9,8},{10,11... | collective-permute-start | bytes 9437192 | tf_op jit(solution)/shard_map/ppermute | solution.py:49
  321.3 14.5 %collective-permute-start.20 = (bf16[256,1024]{1,0:T(8,128)(2,1)}, bf16[256,1024]{1,0:T(8,128)(2,1)S(1)}, u32[]{:S(2)}, u32[]{:S(2)}) collective-permute-start(bf16[256,1024]{1,0:T(8,128)(2,1)} %shard_map.326), channel_id=1, source_target_pairs={{64,0},{65,1},{66,2},{67,3},{68,4},{69,5},{70,6},{71,7},{72,8},{73... | collective-permute-start | bytes 1572872 | tf_op jit(solution)/shard_map/ppermute | solution.py:224
  354.7 16.4 %all-to-all-start.6 = ((bf16[8,256,128]{2,1,0:T(8,128)(2,1)}), bf16[8,256,128]{2,1,0:T(8,128)(2,1)S(1)}, u32[]{:S(2)}, u32[]{:S(2)}) async-start(bf16[8,256,128]{2,1,0:T(8,128)(2,1)} %get-tuple-element.63), calls=%async_computation.6 | async-start | bytes 1048576 | tf_op jit(solution)/shard_map/all_to_all | solution.py:218
  374.9 21.8 %collective-permute-start.22 = (bf16[1,4,2,80,512]{4,3,2,1,0:T(8,128)(2,1)}, bf16[1,4,2,80,512]{4,3,2,1,0:T(8,128)(2,1)}, u32[]{:S(2)}, u32[]{:S(2)}) collective-permute-start(bf16[1,4,2,80,512]{4,3,2,1,0:T(8,128)(2,1)} %get-tuple-element.84), channel_id=1, source_target_pairs={{0,16},{8,24},{16,32},{24,40},{32,48},{40,56},{48,0},{56,8},{1,17}... | collective-permute-start | bytes 1966088 | tf_op jit(solution)/shard_map/ppermute | solution.py:44
  374.9 21.8 %collective-permute-start.23 = (bf16[1,4,2,80,512]{4,3,2,0,1:T(8,128)(2,1)S(1)}, bf16[1,4,2,80,512]{4,3,2,0,1:T(8,128)(2,1)S(1)}, u32[]{:S(2)}, u32[]{:S(2)}) collective-permute-start(bf16[1,4,2,80,512]{4,3,2,0,1:T(8,128)(2,1)S(1)} %get-tuple-element.86), channel_id=1, source_target_pairs={{0,48},{8,56},{16,0},{24,8},{32,16},{40,24},{48,32},{56,40},{1,49}... | collective-permute-start | bytes 1966088 | tf_op jit(solution)/shard_map/ppermute | solution.py:44
  378.8 18.0 %collective-permute-start.24 = (bf16[2,2,2,64,512]{4,3,2,1,0:T(8,128)(2,1)}, bf16[2,2,2,64,512]{4,3,2,1,0:T(8,128)(2,1)}, u32[]{:S(2)}, u32[]{:S(2)}) collective-permute-start(bf16[2,2,2,64,512]{4,3,2,1,0:T(8,128)(2,1)} %get-tuple-element.91), channel_id=1, source_target_pairs={{0,2},{1,3},{2,4},{3,5},{4,6},{5,7},{6,0},{7,1},{8,10},{9,11},{10,... | collective-permute-start | bytes 1572872 | tf_op jit(solution)/shard_map/ppermute | solution.py:44
  380.2 16.6 %collective-permute-start.25 = (bf16[2,2,2,64,512]{4,3,2,1,0:T(8,128)(2,1)}, bf16[2,2,2,64,512]{4,3,2,1,0:T(8,128)(2,1)}, u32[]{:S(2)}, u32[]{:S(2)}) collective-permute-start(bf16[2,2,2,64,512]{4,3,2,1,0:T(8,128)(2,1)} %get-tuple-element.92), channel_id=1, source_target_pairs={{0,6},{1,7},{2,0},{3,1},{4,2},{5,3},{6,4},{7,5},{8,14},{9,15},{10,... | collective-permute-start | bytes 1572872 | tf_op jit(solution)/shard_map/ppermute | solution.py:44
  399.7 23.7 %collective-permute-start.35 = (bf16[4,2,2,64,512]{4,3,2,1,0:T(8,128)(2,1)}, bf16[4,2,2,64,512]{4,3,2,1,0:T(8,128)(2,1)}, u32[]{:S(2)}, u32[]{:S(2)}) collective-permute-start(bf16[4,2,2,64,512]{4,3,2,1,0:T(8,128)(2,1)} %pad_maximum_fusion.3), channel_id=1, source_target_pairs={{0,6},{1,7},{2,0},{3,1},{4,2},{5,3},{6,4},{7,5},{8,14},{9,15},{10,... | collective-permute-start | bytes 3145736 | tf_op jit(solution)/shard_map/ppermute | solution.py:44
  402.1 25.4 %collective-permute-start.34 = (bf16[4,2,2,64,512]{4,3,2,1,0:T(8,128)(2,1)}, bf16[4,2,2,64,512]{4,3,2,1,0:T(8,128)(2,1)}, u32[]{:S(2)}, u32[]{:S(2)}) collective-permute-start(bf16[4,2,2,64,512]{4,3,2,1,0:T(8,128)(2,1)} %pad_maximum_fusion.2), channel_id=1, source_target_pairs={{0,2},{1,3},{2,4},{3,5},{4,6},{5,7},{6,0},{7,1},{8,10},{9,11},{10,... | collective-permute-start | bytes 3145736 | tf_op jit(solution)/shard_map/ppermute | solution.py:44
  402.2 40.2 %all-to-all-start.7 = ((bf16[8,256,384]{2,1,0:T(8,128)(2,1)}), bf16[8,256,384]{2,1,0:T(8,128)(2,1)S(1)}, u32[]{:S(2)}, u32[]{:S(2)}) async-start(bf16[8,256,384]{2,1,0:T(8,128)(2,1)} %bitcast.56.grad_ref), calls=%async_computation.7 | async-start | bytes 3145728 | tf_op jit(solution)/shard_map/all_to_all | solution.py:218
  410.8 41.7 %collective-permute-start.27 = (bf16[2,4,2,80,512]{4,3,2,0,1:T(8,128)(2,1)}, bf16[2,4,2,80,512]{4,3,2,0,1:T(8,128)(2,1)}, u32[]{:S(2)}, u32[]{:S(2)}) collective-permute-start(bf16[2,4,2,80,512]{4,3,2,0,1:T(8,128)(2,1)} %pad_maximum_fusion.1), channel_id=1, source_target_pairs={{0,48},{8,56},{16,0},{24,8},{32,16},{40,24},{48,32},{56,40},{1,49}... | collective-permute-start | bytes 3932168 | tf_op jit(solution)/shard_map/ppermute | solution.py:44
  413.5 39.7 %collective-permute-start.26 = (bf16[2,4,2,80,512]{4,3,2,1,0:T(8,128)(2,1)}, bf16[2,4,2,80,512]{4,3,2,1,0:T(8,128)(2,1)}, u32[]{:S(2)}, u32[]{:S(2)}) collective-permute-start(bf16[2,4,2,80,512]{4,3,2,1,0:T(8,128)(2,1)} %pad_maximum_fusion), channel_id=1, source_target_pairs={{0,16},{8,24},{16,32},{24,40},{32,48},{40,56},{48,0},{56,8},{1,17}... | collective-permute-start | bytes 3932168 | tf_op jit(solution)/shard_map/ppermute | solution.py:44
  430.6 33.8 %collective-permute-start.38 = (bf16[2,2,64,512]{3,2,1,0:T(8,128)(2,1)}, bf16[2,2,64,512]{3,2,1,0:T(8,128)(2,1)}, u32[]{:S(2)}, u32[]{:S(2)}) collective-permute-start(bf16[2,2,64,512]{3,2,1,0:T(8,128)(2,1)} %get-tuple-element.97), channel_id=1, source_target_pairs={{0,48},{8,56},{16,0},{24,8},{32,16},{40,24},{48,32},{56,40},{1,49}... | collective-permute-start | bytes 786440 | tf_op jit(solution)/shard_map/ppermute | solution.py:44
  430.9 34.2 %collective-permute-start.37 = (bf16[2,2,64,512]{3,2,1,0:T(8,128)(2,1)S(1)}, bf16[2,2,64,512]{3,2,1,0:T(8,128)(2,1)}, u32[]{:S(2)}, u32[]{:S(2)}) collective-permute-start(bf16[2,2,64,512]{3,2,1,0:T(8,128)(2,1)S(1)} %get-tuple-element.98), channel_id=1, source_target_pairs={{0,32},{8,40},{16,48},{24,56},{32,0},{40,8},{48,16},{56,24},{1,33}... | collective-permute-start | bytes 786440 | tf_op jit(solution)/shard_map/ppermute | solution.py:44
  452.6 6.8 %collective-permute-start.29 = (bf16[2,4,2,16,512]{4,3,2,1,0:T(8,128)(2,1)S(1)}, bf16[2,4,2,16,512]{4,3,2,1,0:T(8,128)(2,1)S(1)}, u32[]{:S(2)}, u32[]{:S(2)}) collective-permute-start(bf16[2,4,2,16,512]{4,3,2,1,0:T(8,128)(2,1)S(1)} %get-tuple-element.101), channel_id=1, source_target_pairs={{0,32},{8,40},{16,48},{24,56},{32,0},{40,8},{48,16},{56,24},{1,33}... | collective-permute-start | bytes 786440 | tf_op jit(solution)/shard_map/ppermute | solution.py:44
  453.2 11.0 %collective-permute-start.28 = (bf16[2,4,2,16,512]{4,3,2,1,0:T(8,128)(2,1)S(1)}, bf16[2,4,2,16,512]{4,3,2,1,0:T(8,128)(2,1)S(1)}, u32[]{:S(2)}, u32[]{:S(2)}) collective-permute-start(bf16[2,4,2,16,512]{4,3,2,1,0:T(8,128)(2,1)S(1)} %get-tuple-element.99), channel_id=1, source_target_pairs={{0,16},{8,24},{16,32},{24,40},{32,48},{40,56},{48,0},{56,8},{1,17}... | collective-permute-start | bytes 786440 | tf_op jit(solution)/shard_map/ppermute | solution.py:44
  457.5 15.8 %collective-permute-start.36 = (bf16[2,2,64,512]{3,2,1,0:T(8,128)(2,1)S(1)}, bf16[2,2,64,512]{3,2,1,0:T(8,128)(2,1)S(1)}, u32[]{:S(2)}, u32[]{:S(2)}) collective-permute-start(bf16[2,2,64,512]{3,2,1,0:T(8,128)(2,1)S(1)} %get-tuple-element.96), channel_id=1, source_target_pairs={{0,16},{8,24},{16,32},{24,40},{32,48},{40,56},{48,0},{56,8},{1,17}... | collective-permute-start | bytes 786440 | tf_op jit(solution)/shard_map/ppermute | solution.py:44
  459.4 16.3 %collective-permute-start.43 = (bf16[2,128,384]{2,1,0:T(8,128)(2,1)S(1)}, bf16[2,128,384]{2,1,0:T(8,128)(2,1)S(1)}, u32[]{:S(2)}, u32[]{:S(2)}) collective-permute-start(bf16[2,128,384]{2,1,0:T(8,128)(2,1)S(1)} %get-tuple-element.103), channel_id=1, source_target_pairs={{0,48},{8,56},{16,0},{24,8},{32,16},{40,24},{48,32},{56,40},{1,49}... | collective-permute-start | bytes 589832 | tf_op jit(solution)/shard_map/ppermute | solution.py:44
  464.1 12.8 %collective-permute-start.42 = (bf16[2,128,384]{2,1,0:T(8,128)(2,1)S(1)}, bf16[2,128,384]{2,1,0:T(8,128)(2,1)S(1)}, u32[]{:S(2)}, u32[]{:S(2)}) collective-permute-start(bf16[2,128,384]{2,1,0:T(8,128)(2,1)S(1)} %get-tuple-element.104), channel_id=1, source_target_pairs={{0,32},{8,40},{16,48},{24,56},{32,0},{40,8},{48,16},{56,24},{1,33}... | collective-permute-start | bytes 589832 | tf_op jit(solution)/shard_map/ppermute | solution.py:44
  464.5 13.0 %collective-permute-start.41 = (bf16[2,128,384]{2,1,0:T(8,128)(2,1)S(1)}, bf16[2,128,384]{2,1,0:T(8,128)(2,1)S(1)}, u32[]{:S(2)}, u32[]{:S(2)}) collective-permute-start(bf16[2,128,384]{2,1,0:T(8,128)(2,1)S(1)} %get-tuple-element.102), channel_id=1, source_target_pairs={{0,16},{8,24},{16,32},{24,40},{32,48},{40,56},{48,0},{56,8},{1,17}... | collective-permute-start | bytes 589832 | tf_op jit(solution)/shard_map/ppermute | solution.py:44
  465.1 12.5 %collective-permute-start.33 = (bf16[2,2,96,512]{3,2,1,0:T(8,128)(2,1)S(1)}, bf16[2,2,96,512]{3,2,1,0:T(8,128)(2,1)S(1)}, u32[]{:S(2)}, u32[]{:S(2)}) collective-permute-start(bf16[2,2,96,512]{3,2,1,0:T(8,128)(2,1)S(1)} %get-tuple-element.95), channel_id=1, source_target_pairs={{0,6},{1,7},{2,0},{3,1},{4,2},{5,3},{6,4},{7,5},{8,14},{9,15},{10,... | collective-permute-start | bytes 1179656 | tf_op jit(solution)/shard_map/ppermute | solution.py:44
  473.3 8.2 %collective-permute-start.32 = (bf16[2,2,96,512]{3,2,1,0:T(8,128)(2,1)S(1)}, bf16[2,2,96,512]{3,2,1,0:T(8,128)(2,1)S(1)}, u32[]{:S(2)}, u32[]{:S(2)}) collective-permute-start(bf16[2,2,96,512]{3,2,1,0:T(8,128)(2,1)S(1)} %get-tuple-element.94), channel_id=1, source_target_pairs={{0,4},{1,5},{2,6},{3,7},{4,0},{5,1},{6,2},{7,3},{8,12},{9,13},{10,... | collective-permute-start | bytes 1179656 | tf_op jit(solution)/shard_map/ppermute | solution.py:44
  475.7 16.8 %collective-permute-start.31 = (bf16[2,2,96,512]{3,2,1,0:T(8,128)(2,1)S(1)}, bf16[2,2,96,512]{3,2,1,0:T(8,128)(2,1)S(1)}, u32[]{:S(2)}, u32[]{:S(2)}) collective-permute-start(bf16[2,2,96,512]{3,2,1,0:T(8,128)(2,1)S(1)} %get-tuple-element.93), channel_id=1, source_target_pairs={{0,2},{1,3},{2,4},{3,5},{4,6},{5,7},{6,0},{7,1},{8,10},{9,11},{10,... | collective-permute-start | bytes 1179656 | tf_op jit(solution)/shard_map/ppermute | solution.py:44
  492.9 20.4 %collective-permute-start.39 = (bf16[2,160,512]{2,1,0:T(8,128)(2,1)S(1)}, bf16[2,160,512]{2,1,0:T(8,128)(2,1)S(1)}, u32[]{:S(2)}, u32[]{:S(2)}) collective-permute-start(bf16[2,160,512]{2,1,0:T(8,128)(2,1)S(1)} %fusion.25), channel_id=1, source_target_pairs={{0,8},{8,0},{16,24},{24,16},{32,40},{40,32},{48,56},{56,48},{1,9},... | collective-permute-start | bytes 983048 | tf_op jit(solution)/shard_map/ppermute | solution.py:49
  498.3 7.9 %collective-permute-start.44 = (bf16[128,384]{1,0:T(8,128)(2,1)S(1)}, bf16[128,384]{1,0:T(8,128)(2,1)S(1)}, u32[]{:S(2)}, u32[]{:S(2)}) collective-permute-start(bf16[128,384]{1,0:T(8,128)(2,1)S(1)} %fusion.31), channel_id=1, source_target_pairs={{0,8},{8,0},{16,24},{24,16},{32,40},{40,32},{48,56},{56,48},{1,9},... | collective-permute-start | bytes 294920 | tf_op jit(solution)/shard_map/ppermute | solution.py:49
  506.8 11.4 %all-to-all-start.8 = ((bf16[8,16,384]{2,1,0:T(8,128)(2,1)}), bf16[8,16,384]{2,1,0:T(8,128)(2,1)S(1)}, u32[]{:S(2)}, u32[]{:S(2)}) async-start(bf16[8,16,384]{2,1,0:T(8,128)(2,1)} %bitcast.105), calls=%async_computation.8 | async-start | bytes 196608 | tf_op jit(solution)/shard_map/all_to_all | solution.py:218
  (23 other events, 162.0 us)
Sparse Core Ops, SparseCore 0:
  11.1 124.4 all-gather.4
  322.7 35.2 all-gather.6
